TPU v7x, 32 devices: a whole 2x2x4 slice. The times are simulated.
32 devices in a mesh: groups: 2 (over y), bank: 4 (over x, core), query: 4 (over z).
Axes of the slice: x: 2, y: 2, z: 4, core: 2. Of those that a mesh axis runs over, the one named last changes fastest.
Arguments:
- queries: bfloat16 [256, 768], P(('groups', 'bank', 'query')), parts along dimension 0, may hold values from -12 to 12
- bank_keys: bfloat16 [65536, 768], P(('groups', 'bank', 'query')), parts along dimension 0, may hold values from -5 to 5
- bank_labels: bfloat16 [65536, 1000], P(('groups', 'bank', 'query')), parts along dimension 0, may hold values from 0.0009994507 to 1
Outputs:
- log_votes: float32 [256, 1000], P(('groups', 'bank', 'query')), parts along dimension 0
There are 2 independent parts, one for each index of `groups`. A program takes and returns all parts, laid end to end along the dimension named above; each array names one. Nothing has to cross between parts.
All inputs are finite; a program needn't handle non-finite values.
Results may differ from a plain program's by a relative error of at most 0.0003.
Values may be sent and summed in bfloat16 or wider, within the bound.
No kernel may reach another device: no remote copies, remote signals or barrier semaphores. Data moves between devices by JAX's collectives and lax.ppermute only.
A program may use at most 64 MiB of HBM per device.

v0:
```python
import math

import jax
import jax.numpy as jnp
from jax import lax
from jax.sharding import PartitionSpec as P

SCORE_GAIN = 3.0


def partial_stats(query_rows, key_block, label_block):
    score_gain = SCORE_GAIN / math.sqrt(query_rows.shape[1])
    scores = (
        lax.dot_general(
            query_rows, key_block, (((1,), (1,)), ((), ())), preferred_element_type=jnp.float32
        )
        * score_gain
    )
    peaks = jnp.max(scores, axis=1)
    weights = jnp.exp(scores - peaks[:, None])
    totals = jnp.sum(weights, axis=1)
    votes = jnp.dot(weights.astype(jnp.bfloat16), label_block, preferred_element_type=jnp.float32)
    return (peaks, totals, votes)


def local(queries, bank_keys, bank_labels):
    current = partial_stats(
        lax.all_gather(queries, ("bank", "query"), axis=0, tiled=True), bank_keys, bank_labels
    )
    peaks, totals, votes = tuple((latest for latest in current))
    row_top = lax.pmax(peaks, ("bank", "query"))
    factor = jnp.exp(peaks - row_top)
    class_mass, denominator = (
        lax.psum_scatter(
            votes * factor[:, None], ("bank", "query"), scatter_dimension=0, tiled=True
        ),
        lax.psum_scatter(totals * factor, ("bank", "query"), scatter_dimension=0, tiled=True),
    )
    return jnp.log(class_mass / denominator[:, None])


def solution(mesh):
    placed = (
        P(("groups", "bank", "query"), None),
        P(("groups", "bank", "query"), None),
        P(("groups", "bank", "query"), None),
    )
    return jax.shard_map(
        local,
        mesh=mesh,
        in_specs=placed,
        out_specs=P(("groups", "bank", "query"), None),
        check_vma=False,
    )
```

profile of v0, /device:TPU:0, one launch (start us, length us, event | category | flops | bytes accessed | tf_op | source)
XLA Modules:
  0.0 143.8 jit_solution(8183991988119629524)
XLA Ops:
  6.5 0.0 copy-start
  6.5 0.0 reduce-scatter.2.cloned.1.call-start
  6.5 35.9 %all_gather.3 = bf16[128,768]{1,0:T(8,128)(2,1)S(1)} all-gather(bf16[8,768]{1,0:T(8,128)(2,1)} %param.3), channel_id=1, replica_groups=mesh['groups'=2,'bank'=4,'query'=4] {'bank','query'}, dimensions={0}, use_global_device_ids=true | all-gather | bytes 208896 | tf_op jit(solution)/shard_map/all_gather | solution.py:28
  42.4 0.0 copy-done
  42.4 2.1 %fusion.5 = (f32[128]{0:T(128)S(1)}, f32[128,2048]{1,0:T(8,128)}) fusion(bf16[128,768]{1,0:T(8,128)(2,1)S(1)} %all_gather.3, bf16[2048,768]{1,0:T(8,128)(2,1)S(1)} %copy-done), kind=kOutput, calls=%fused_computation.9 | convolution fusion | flops 403177344 | bytes 4391424 | tf_op jit(solution)/shard_map/dot_general | solution.py:14
  44.5 0.0 copy-start.1
  44.5 29.7 %pmax.7 = f32[128]{0:T(128)S(1)} all-reduce(f32[128]{0:T(128)S(1)} %get-tuple-element.7), channel_id=1, replica_groups=mesh['groups'=2,'bank'=4,'query'=4] {'bank','query'}, use_global_device_ids=true, to_apply=%region_1.0 | all-reduce | flops 128 | bytes 1024 | tf_op jit(solution)/shard_map/pmax | solution.py:31
  74.2 1.5 %fusion = f32[128]{0:T(128)S(1)} fusion(f32[128,2048]{1,0:T(8,128)} %get-tuple-element.8, f32[128]{0:T(128)S(1)} %get-tuple-element.7), kind=kLoop, calls=%fused_computation.3 | loop fusion | flops 524160 | bytes 1049600 | tf_op jit(solution)/shard_map/reduce_sum | solution.py:21
  75.8 4.7 %convolution_multiply_fusion.1 = f32[128,1000]{1,0:T(8,128)} fusion(bf16[2048,1000]{0,1:T(8,128)(2,1)} %param.5, f32[128,2048]{1,0:T(8,128)} %get-tuple-element.8, f32[128]{0:T(128)S(1)} %get-tuple-element.7, f32[128]{0:T(128)S(1)} %get-tuple-element.6), kind=kOutput, calls=%fused_computation.1 | convolution fusion | flops 524940288 | bytes 5657600 | tf_op jit(solution)/shard_map/dot_general | solution.py:22
  80.5 0.0 reduce-scatter.2.cloned.1.call-update
  80.5 0.0 copy-done.1
  80.5 0.6 dynamic-slice
  81.8 32.0 %all-reduce = f32[128]{0:T(128)S(1)} all-reduce(f32[128]{0:T(128)S(1)} %get-tuple-element.5), channel_id=3, replica_groups=mesh['groups'=2,'bank'=4,'query'=4] {'bank','query'}, use_global_device_ids=true, to_apply=%region_4.0.clone | all-reduce | flops 128 | bytes 1024
  113.8 0.1 dynamic-slice.1
  113.8 21.7 %reduce-scatter.2.cloned.1.call-done = f32[8,1000]{1,0:T(8,128)} async-done(((f32[128,1000]{1,0:T(8,128)}), f32[8,1000]{1,0:T(8,128)}) %reduce-scatter.2.cloned.1.call-update) | async-done | bytes 32016 | tf_op jit(solution)/shard_map/reduce_scatter | solution.py:34
  135.5 1.5 %divide_log_fusion = f32[8,1000]{1,0:T(8,128)} fusion(f32[8,1000]{1,0:T(8,128)} %reduce-scatter.2.cloned.1.call-done, f32[8]{0:T(128)S(1)} %dynamic-slice.1), kind=kLoop, calls=%fused_computation.6 | loop fusion | flops 8000 | bytes 64032 | tf_op jit(solution)/shard_map/log | solution.py:39
  (1 shorter events, 0.0 us)
Async XLA Ops:
  6.5 35.9 %copy-start = (bf16[2048,768]{1,0:T(8,128)(2,1)S(1)}, bf16[2048,768]{1,0:T(8,128)(2,1)}, u32[]{:S(2)}) copy-start(bf16[2048,768]{1,0:T(8,128)(2,1)} %param.4) | copy-start | bytes 9437188
  6.5 129.0 %reduce-scatter.2.cloned.1.call-start = ((), (), s32[]{:S(2)}) async-start(), calls=%async_computation.1 | async-start | bytes 557056 | tf_op jit(solution)/shard_map/reduce_scatter | solution.py:34
  44.5 36.0 %copy-start.1 = (u32[32]{0:T(128)S(1)}, u32[32]{0:T(128)}, u32[]{:S(2)}) copy-start(u32[32]{0:T(128)} %constant.9) | copy-start | bytes 388
Sparse Core Ops, SparseCore 0:
  80.7 54.7 reduce-scatter.1
where the time goes:
time: 144 us
  blocking collectives  97.5 us (68%)
  waiting for transfers between devices  21.7 us (15%)
  between operations  14.1 us (10%)
  matrix products  6.87 us (5%)
  other arithmetic  2.98 us (2%)
    all_gather x1, blocking collectives, local(): lax.all_gather(queries, ('bank', 'query'), axis=0, tiled=True)  35.9 us
    unnamed x1, blocking collectives  32 us
    pmax x1, blocking collectives, local(): row_top = lax.pmax(peaks, ('bank', 'query'))  29.7 us
    reduce_scatter x1, waiting for transfers between devices, local(): lax.psum_scatter(votes * factor[:, None], ('bank', 'query'), scatter_dime...  21.7 us
    dot_general x1, matrix products, partial_stats(): jnp.dot(weights.astype(jnp.bfloat16), label_block, preferred_element_type...  4.74 us
  transfers between devices with their start and end apart: 1, of which 1 were waited for; matrix products, arithmetic and copies ran while one was open for 0% of the time, Pallas kernels for 0%

commit v1 on v0

v1 whole, which is shorter than its diff:
```python
import functools
import math

import jax
import jax.numpy as jnp
from jax import lax
from jax.experimental import pallas as pl
from jax.experimental.pallas import tpu as pltpu
from jax.sharding import PartitionSpec as P

SCORE_GAIN = 3.0
AXES = ("bank", "query")
LANES = 128
VMEM = pl.BlockSpec(memory_space=pltpu.VMEM)


def pad_lanes(width):
    return -(-(width + 2) // LANES) * LANES


def stats_kernel(q_ref, k_ref, lt_ref, keep_ref, send_ref):
    rows, width = q_ref.shape
    classes = lt_ref.shape[0]
    half = rows // 2
    scores = lax.dot_general(
        q_ref[...], k_ref[...], (((1,), (1,)), ((), ())), preferred_element_type=jnp.float32
    ) * (SCORE_GAIN / math.sqrt(width))
    peaks = jnp.max(scores, axis=1, keepdims=True)
    weights = jnp.exp(scores - peaks)
    totals = jnp.sum(weights, axis=1, keepdims=True)
    votes = lax.dot_general(
        weights.astype(jnp.bfloat16),
        lt_ref[...],
        (((1,), (1,)), ((), ())),
        preferred_element_type=jnp.float32,
    )
    for ref, lo in ((keep_ref, 0), (send_ref, half)):
        ref[:, :classes] = votes[lo : lo + half]
        ref[:, classes : classes + 1] = peaks[lo : lo + half]
        ref[:, classes + 1 : classes + 2] = totals[lo : lo + half]


def stats(queries, keys, labels_t):
    rows, width = queries.shape
    bank = keys.shape[0]
    classes = labels_t.shape[0]
    out = jax.ShapeDtypeStruct((rows // 2, pad_lanes(classes)), jnp.float32)
    return pl.pallas_call(
        stats_kernel,
        out_shape=(out, out),
        in_specs=[VMEM] * 3,
        out_specs=(VMEM, VMEM),
        compiler_params=pltpu.CompilerParams(vmem_limit_bytes=32 * 1024 * 1024),
        cost_estimate=pl.CostEstimate(
            flops=2 * rows * bank * (width + classes),
            bytes_accessed=2 * bank * (width + classes),
            transcendentals=rows * bank,
        ),
    )(queries, keys, labels_t)


def combine(mine, other, classes):
    peak_a, peak_b = mine[:, classes : classes + 1], other[:, classes : classes + 1]
    top = jnp.maximum(peak_a, peak_b)
    factor_a, factor_b = jnp.exp(peak_a - top), jnp.exp(peak_b - top)
    return top, factor_a * mine + factor_b * other


def merge_kernel(classes, mine_ref, other_ref, keep_ref, send_ref):
    half = keep_ref.shape[0]
    for ref, lo in ((keep_ref, 0), (send_ref, half)):
        top, merged = combine(mine_ref[lo : lo + half], other_ref[lo : lo + half], classes)
        ref[...] = merged
        ref[:, classes : classes + 1] = top


def merge(mine, other, classes):
    out = jax.ShapeDtypeStruct((mine.shape[0] // 2, mine.shape[1]), jnp.float32)
    return pl.pallas_call(
        functools.partial(merge_kernel, classes),
        out_shape=(out, out),
        in_specs=[VMEM] * 2,
        out_specs=(VMEM, VMEM),
    )(mine, other)


def finish_kernel(classes, mine_ref, other_ref, out_ref):
    _, merged = combine(mine_ref[...], other_ref[...], classes)
    out_ref[...] = jnp.log(merged[:, :classes] / merged[:, classes + 1 : classes + 2])


def finish(mine, other, classes):
    return pl.pallas_call(
        functools.partial(finish_kernel, classes),
        out_shape=jax.ShapeDtypeStruct((mine.shape[0], classes), jnp.float32),
        in_specs=[VMEM] * 2,
        out_specs=VMEM,
    )(mine, other)


def local(bits, size, queries, bank_keys, bank_labels):
    def swap(block, bit):
        return lax.ppermute(block, AXES, [(i, i ^ bit) for i in range(size)])

    classes = bank_labels.shape[1]
    rows = queries
    for bit in bits:
        rows = jnp.concatenate([rows, swap(rows, bit)], axis=0)
    keep, send = stats(rows, bank_keys, bank_labels.T)
    for bit in bits[:0:-1]:
        keep, send = merge(keep, swap(send, bit), classes)
    return finish(keep, swap(send, bits[0]), classes)


def solution(mesh):
    placed = P(("groups", "bank", "query"), None)
    size = mesh.shape["bank"] * mesh.shape["query"]
    query_bits = [1 << b for b in range(mesh.shape["query"].bit_length() - 1)]
    bank_bits = [mesh.shape["query"] << b for b in range(mesh.shape["bank"].bit_length() - 1)]
    bits = query_bits + bank_bits[1:] + bank_bits[:1]
    return jax.shard_map(
        functools.partial(local, bits, size),
        mesh=mesh,
        in_specs=(placed,) * 3,
        out_specs=placed,
        check_vma=False,
    )
```

time: 144 us -> 51.8 us (0.36)
  blocking collectives: 97.5 us -> 0 us
  starting transfers between devices: 0.01 us -> 14.1 us
  between operations: 14.1 us -> 0.05 us
  Pallas kernels: 0 us -> 9.3 us
  local copies, waits for them, and re-layouts: 0.67 us -> 8.12 us
  matrix products: 6.87 us -> 0 us
  waiting for transfers between devices: 21.7 us -> 17.5 us
    all_gather x1 -> x0, blocking collectives: 35.9 us -> none  [local(): lax.all_gather(queries, ('bank', 'query'), axis=0, tiled=True)]
    unnamed x1 -> x0, blocking collectives: 32 us -> none
    pmax x1 -> x0, blocking collectives: 29.7 us -> none  [local(): row_top = lax.pmax(peaks, ('bank', 'query'))]
    reduce_scatter x1 -> x0, waiting for transfers between devices: 21.7 us -> none  [local(): lax.psum_scatter(votes * factor[:, None], ('bank', 'query'), scatter_dime...]
    ppermute x0 -> x8, waiting for transfers between devices: none -> 17.5 us  [swap(): return lax.ppermute(block, AXES, [(i, i ^ bit) for i in range(size)])]
    ppermute x0 -> x8, starting transfers between devices: none -> 14.1 us  [swap(): return lax.ppermute(block, AXES, [(i, i ^ bit) for i in range(size)])]
    pallas_call x0 -> x5, Pallas kernels: none -> 9.3 us  [the longest x3 5.1 us: merge(): pl.pallas_call(functools.partial(merge_kernel, classes), out_shape=(out,...]
    unnamed x6 -> x18, local copies, waits for them, and re-layouts: 0.67 us -> 8.11 us
  transfers between devices with their start and end apart: 1 -> 8, of which waited for: 1 -> 8; matrix products, arithmetic and copies ran while one was open for 0% -> 1% of each run, Pallas kernels for 0% -> 0%
where the time goes in v1:
time: 51.8 us; the launch traced here: 51.3 us
  waiting for transfers between devices  17.5 us (34%)
  starting transfers between devices  14.1 us (27%)
  Pallas kernels  9.3 us (18%)
  local copies, waits for them, and re-layouts  8.12 us (16%)
  other arithmetic  2.14 us (4%)
    ppermute x8, waiting for transfers between devices, swap(): return lax.ppermute(block, AXES, [(i, i ^ bit) for i in range(size)])  17.5 us
    ppermute x8, starting transfers between devices, swap(): return lax.ppermute(block, AXES, [(i, i ^ bit) for i in range(size)])  14.1 us
    unnamed x18, local copies, waits for them, and re-layouts  8.11 us
    pallas_call x3, Pallas kernels, merge(): pl.pallas_call(functools.partial(merge_kernel, classes), out_shape=(out,...  5.1 us
    pallas_call x1, Pallas kernels, stats(): pl.pallas_call(stats_kernel, out_shape=(out, out), in_specs=[VMEM] * 3, o...  2.64 us
    concatenate x3, other arithmetic, local(): rows = jnp.concatenate([rows, swap(rows, bit)], axis=0)  2.14 us
    pallas_call x1, Pallas kernels, finish(): pl.pallas_call(functools.partial(finish_kernel, classes), out_shape=jax.S...  1.56 us
  transfers between devices with their start and end apart: 8, of which 8 were waited for; matrix products, arithmetic and copies ran while one was open for 1% of the time, Pallas kernels for 0%

profile of v1, /device:TPU:0, one launch (start us, length us, event | category | flops | bytes accessed | tf_op | source)
XLA Modules:
  0.0 51.3 jit_solution(7473167062726186459)
XLA Ops:
  0.0 3.0 %collective-permute-start = (bf16[8,768]{1,0:T(8,128)(2,1)}, bf16[8,768]{1,0:T(8,128)(2,1)S(1)}, u32[]{:S(2)}, u32[]{:S(2)}) collective-permute-start(bf16[8,768]{1,0:T(8,128)(2,1)} %param.3), channel_id=1, source_target_pairs={{0,1},{1,0},{2,3},{3,2},{4,5},{5,4},{6,7},{7,6},{8,9},{9,8},{10,11... | collective-permute-start | bytes 36872 | tf_op jit(solution)/shard_map/ppermute | solution.py:103
  3.0 0.7 %constant_dynamic-update-slice_fusion.4 = bf16[128,768]{1,0:T(8,128)(2,1)S(1)} fusion(bf16[8,768]{1,0:T(8,128)(2,1)} %param.3), kind=kLoop, calls=%fused_computation.7 | loop fusion | bytes 24576
  3.8 1.1 %collective-permute-done = bf16[8,768]{1,0:T(8,128)(2,1)S(1)} collective-permute-done((bf16[8,768]{1,0:T(8,128)(2,1)}, bf16[8,768]{1,0:T(8,128)(2,1)S(1)}, u32[]{:S(2)}, u32[]{:S(2)}) %collective-permute-start) | collective-permute-done | bytes 12320 | tf_op jit(solution)/shard_map/ppermute | solution.py:103
  4.9 0.7 %pad_maximum_fusion.2 = bf16[16,768]{1,0:T(8,128)(2,1)S(1)} fusion(bf16[8,768]{1,0:T(8,128)(2,1)S(1)} %collective-permute-done, bf16[8,768]{1,0:T(8,128)(2,1)} %param.3), kind=kLoop, calls=%fused_computation.2 | loop fusion | flops 49152 | bytes 49152 | tf_op jit(solution)/shard_map/concatenate | solution.py:108
  5.6 3.0 %collective-permute-start.1 = (bf16[16,768]{1,0:T(8,128)(2,1)S(1)}, bf16[16,768]{1,0:T(8,128)(2,1)S(1)}, u32[]{:S(2)}, u32[]{:S(2)}) collective-permute-start(bf16[16,768]{1,0:T(8,128)(2,1)S(1)} %pad_maximum_fusion.2), channel_id=1, source_target_pairs={{0,2},{1,3},{2,0},{3,1},{4,6},{5,7},{6,4},{7,5},{8,10},{9,11},{10,... | collective-permute-start | bytes 73736 | tf_op jit(solution)/shard_map/ppermute | solution.py:103
  8.7 1.8 %collective-permute-done.1 = bf16[16,768]{1,0:T(8,128)(2,1)S(1)} collective-permute-done((bf16[16,768]{1,0:T(8,128)(2,1)S(1)}, bf16[16,768]{1,0:T(8,128)(2,1)S(1)}, u32[]{:S(2)}, u32[]{:S(2)}) %collective-permute-start.1) | collective-permute-done | bytes 24608 | tf_op jit(solution)/shard_map/ppermute | solution.py:103
  10.5 0.7 %pad_maximum_fusion.1 = bf16[32,768]{1,0:T(8,128)(2,1)S(1)} fusion(bf16[16,768]{1,0:T(8,128)(2,1)S(1)} %collective-permute-done.1, bf16[8,768]{1,0:T(8,128)(2,1)S(1)} %collective-permute-done, bf16[8,768]{1,0:T(8,128)(2,1)} %param.3), kind=kLoop, calls=%fused_computation.1 | loop fusion | flops 147456 | bytes 98304 | tf_op jit(solution)/shard_map/concatenate | solution.py:108
  11.2 1.8 %collective-permute-start.2 = (bf16[32,768]{1,0:T(8,128)(2,1)S(1)}, bf16[32,768]{1,0:T(8,128)(2,1)S(1)}, u32[]{:S(2)}, u32[]{:S(2)}) collective-permute-start(bf16[32,768]{1,0:T(8,128)(2,1)S(1)} %pad_maximum_fusion.1), channel_id=1, source_target_pairs={{0,8},{1,9},{2,10},{3,11},{4,12},{5,13},{6,14},{7,15},{8,0},{9,1},... | collective-permute-start | bytes 147464 | tf_op jit(solution)/shard_map/ppermute | solution.py:103
  13.0 2.3 %collective-permute-done.2 = bf16[32,768]{1,0:T(8,128)(2,1)S(1)} collective-permute-done((bf16[32,768]{1,0:T(8,128)(2,1)S(1)}, bf16[32,768]{1,0:T(8,128)(2,1)S(1)}, u32[]{:S(2)}, u32[]{:S(2)}) %collective-permute-start.2) | collective-permute-done | bytes 49184 | tf_op jit(solution)/shard_map/ppermute | solution.py:103
  15.3 0.7 %pad_maximum_fusion = bf16[64,768]{1,0:T(8,128)(2,1)S(1)} fusion(bf16[32,768]{1,0:T(8,128)(2,1)S(1)} %collective-permute-done.2, bf16[16,768]{1,0:T(8,128)(2,1)S(1)} %collective-permute-done.1, bf16[8,768]{1,0:T(8,128)(2,1)S(1)} %collective-permute-done, bf16[8,768]{1,0:T(8,128)(2,1)} %param.3), kind=kLoop, calls=%fused_computation | loop fusion | flops 393216 | bytes 196608 | tf_op jit(solution)/shard_map/concatenate | solution.py:108
  16.0 1.3 %collective-permute-done.3 = bf16[64,768]{1,0:T(8,128)(2,1)S(1)} collective-permute-done((bf16[64,768]{1,0:T(8,128)(2,1)S(1)}, bf16[64,768]{1,0:T(8,128)(2,1)S(1)}, u32[]{:S(2)}, u32[]{:S(2)}) %collective-permute-start.3) | collective-permute-done | bytes 98336 | tf_op jit(solution)/shard_map/ppermute | solution.py:103
  17.3 0.0 copy-start
  17.3 2.2 %copy-done = bf16[2048,1000]{0,1:T(8,128)(2,1)S(1)} copy-done((bf16[2048,1000]{0,1:T(8,128)(2,1)S(1)}, bf16[2048,1000]{0,1:T(8,128)(2,1)}, u32[]{:S(2)}) %copy-start) | copy-done | bytes 4096024
  19.5 1.9 %copy-done.1 = bf16[2048,768]{1,0:T(8,128)(2,1)S(1)} copy-done((bf16[2048,768]{1,0:T(8,128)(2,1)S(1)}, bf16[2048,768]{1,0:T(8,128)(2,1)}, u32[]{:S(2)}) %copy-start.1) | copy-done | bytes 3145752
  21.3 2.6 %shard_map.37 = (f32[64,1024]{1,0:T(8,128)S(1)}, f32[64,1024]{1,0:T(8,128)S(1)}) custom-call(bf16[128,768]{1,0:T(8,128)(2,1)S(1)} %constant_dynamic-update-slice_fusion.q_ref, bf16[2048,768]{1,0:T(8,128)(2,1)S(1)} %copy-done.1, bf16[1000,2048]{1,0:T(8,128)(2,1)S(1)} %bitcast.1), custom_call_target="tpu_custom_call" | custom-call | flops 926941184 | bytes 7241728 | tf_op jit(solution)/shard_map/pallas_call | solution.py:48
  24.0 0.7 %copy-done.2 = f32[64,1024]{1,0:T(8,128)} copy-done((f32[64,1024]{1,0:T(8,128)}, f32[64,1024]{1,0:T(8,128)S(1)}, u32[]{:S(2)}) %copy-start.2) | copy-done | bytes 262168
  24.7 0.1 collective-permute-start.4
  24.8 1.4 %collective-permute-done.4.other_ref = f32[64,1024]{1,0:T(8,128)S(1)} collective-permute-done((f32[64,1024]{1,0:T(8,128)S(1)}, f32[64,1024]{1,0:T(8,128)S(1)}, u32[]{:S(2)}, u32[]{:S(2)}) %collective-permute-start.4) | collective-permute-done | bytes 262176 | tf_op jit(solution)/shard_map/ppermute | solution.py:103
  26.2 0.7 %copy-done.3 = f32[64,1024]{1,0:T(8,128)} copy-done((f32[64,1024]{1,0:T(8,128)}, f32[64,1024]{1,0:T(8,128)S(1)}, u32[]{:S(2)}) %copy-start.3) | copy-done | bytes 262168
  26.9 1.8 %shard_map.38 = (f32[32,1024]{1,0:T(8,128)}, f32[32,1024]{1,0:T(8,128)}) custom-call(f32[64,1024]{1,0:T(8,128)} %copy-done.2, f32[64,1024]{1,0:T(8,128)} %copy-done.3), custom_call_target="tpu_custom_call" | custom-call | tf_op jit(solution)/shard_map/pallas_call | solution.py:79
  28.7 1.8 %collective-permute-start.5 = (f32[32,1024]{1,0:T(8,128)}, f32[32,1024]{1,0:T(8,128)S(1)}, u32[]{:S(2)}, u32[]{:S(2)}) collective-permute-start(f32[32,1024]{1,0:T(8,128)} %get-tuple-element.16), channel_id=1, source_target_pairs={{0,8},{1,9},{2,10},{3,11},{4,12},{5,13},{6,14},{7,15},{8,0},{9,1},... | collective-permute-start | bytes 393224 | tf_op jit(solution)/shard_map/ppermute | solution.py:103
  30.6 4.0 %collective-permute-done.5.other_ref = f32[32,1024]{1,0:T(8,128)S(1)} collective-permute-done((f32[32,1024]{1,0:T(8,128)}, f32[32,1024]{1,0:T(8,128)S(1)}, u32[]{:S(2)}, u32[]{:S(2)}) %collective-permute-start.5) | collective-permute-done | bytes 131104 | tf_op jit(solution)/shard_map/ppermute | solution.py:103
  34.6 0.7 %copy-done.4 = f32[32,1024]{1,0:T(8,128)} copy-done((f32[32,1024]{1,0:T(8,128)}, f32[32,1024]{1,0:T(8,128)S(1)}, u32[]{:S(2)}) %copy-start.4) | copy-done | bytes 131096
  35.2 1.7 %shard_map.39 = (f32[16,1024]{1,0:T(8,128)}, f32[16,1024]{1,0:T(8,128)}) custom-call(f32[32,1024]{1,0:T(8,128)} %get-tuple-element.15.mine_ref, f32[32,1024]{1,0:T(8,128)} %copy-done.4), custom_call_target="tpu_custom_call" | custom-call | tf_op jit(solution)/shard_map/pallas_call | solution.py:79
  37.0 2.9 %collective-permute-start.6 = (f32[16,1024]{1,0:T(8,128)}, f32[16,1024]{1,0:T(8,128)S(1)}, u32[]{:S(2)}, u32[]{:S(2)}) collective-permute-start(f32[16,1024]{1,0:T(8,128)} %get-tuple-element.18), channel_id=1, source_target_pairs={{0,2},{1,3},{2,0},{3,1},{4,6},{5,7},{6,4},{7,5},{8,10},{9,11},{10,... | collective-permute-start | bytes 196616 | tf_op jit(solution)/shard_map/ppermute | solution.py:103
  39.8 2.9 %collective-permute-done.6.other_ref = f32[16,1024]{1,0:T(8,128)S(1)} collective-permute-done((f32[16,1024]{1,0:T(8,128)}, f32[16,1024]{1,0:T(8,128)S(1)}, u32[]{:S(2)}, u32[]{:S(2)}) %collective-permute-start.6) | collective-permute-done | bytes 65568 | tf_op jit(solution)/shard_map/ppermute | solution.py:103
  42.8 0.6 %copy-done.5 = f32[16,1024]{1,0:T(8,128)} copy-done((f32[16,1024]{1,0:T(8,128)}, f32[16,1024]{1,0:T(8,128)S(1)}, u32[]{:S(2)}) %copy-start.5) | copy-done | bytes 65560
  43.4 1.6 %shard_map.40 = (f32[8,1024]{1,0:T(8,128)}, f32[8,1024]{1,0:T(8,128)}) custom-call(f32[16,1024]{1,0:T(8,128)} %get-tuple-element.17.mine_ref, f32[16,1024]{1,0:T(8,128)} %copy-done.5), custom_call_target="tpu_custom_call" | custom-call | tf_op jit(solution)/shard_map/pallas_call | solution.py:79
  45.0 1.4 %collective-permute-start.7 = (f32[8,1024]{1,0:T(8,128)}, f32[8,1024]{1,0:T(8,128)S(1)}, u32[]{:S(2)}, u32[]{:S(2)}) collective-permute-start(f32[8,1024]{1,0:T(8,128)} %get-tuple-element.20), channel_id=1, source_target_pairs={{0,1},{1,0},{2,3},{3,2},{4,5},{5,4},{6,7},{7,6},{8,9},{9,8},{10,11... | collective-permute-start | bytes 98312 | tf_op jit(solution)/shard_map/ppermute | solution.py:103
  46.4 2.7 %collective-permute-done.7.other_ref = f32[8,1024]{1,0:T(8,128)S(1)} collective-permute-done((f32[8,1024]{1,0:T(8,128)}, f32[8,1024]{1,0:T(8,128)S(1)}, u32[]{:S(2)}, u32[]{:S(2)}) %collective-permute-start.7) | collective-permute-done | bytes 32800 | tf_op jit(solution)/shard_map/ppermute | solution.py:103
  49.1 0.6 %copy-done.6 = f32[8,1024]{1,0:T(8,128)} copy-done((f32[8,1024]{1,0:T(8,128)}, f32[8,1024]{1,0:T(8,128)S(1)}, u32[]{:S(2)}) %copy-start.6) | copy-done | bytes 32792
  49.7 1.6 %shard_map.41 = f32[8,1000]{1,0:T(8,128)} custom-call(f32[8,1024]{1,0:T(8,128)} %get-tuple-element.19.mine_ref, f32[8,1024]{1,0:T(8,128)} %copy-done.6), custom_call_target="tpu_custom_call" | custom-call | tf_op jit(solution)/shard_map/pallas_call | solution.py:93
  (11 shorter events, 0.0 us)
Async XLA Ops:
  0.0 4.9 %collective-permute-start = (bf16[8,768]{1,0:T(8,128)(2,1)}, bf16[8,768]{1,0:T(8,128)(2,1)S(1)}, u32[]{:S(2)}, u32[]{:S(2)}) collective-permute-start(bf16[8,768]{1,0:T(8,128)(2,1)} %param.3), channel_id=1, source_target_pairs={{0,1},{1,0},{2,3},{3,2},{4,5},{5,4},{6,7},{7,6},{8,9},{9,8},{10,11... | collective-permute-start | bytes 36872 | tf_op jit(solution)/shard_map/ppermute | solution.py:103
  5.6 4.8 %collective-permute-start.1 = (bf16[16,768]{1,0:T(8,128)(2,1)S(1)}, bf16[16,768]{1,0:T(8,128)(2,1)S(1)}, u32[]{:S(2)}, u32[]{:S(2)}) collective-permute-start(bf16[16,768]{1,0:T(8,128)(2,1)S(1)} %pad_maximum_fusion.2), channel_id=1, source_target_pairs={{0,2},{1,3},{2,0},{3,1},{4,6},{5,7},{6,4},{7,5},{8,10},{9,11},{10,... | collective-permute-start | bytes 73736 | tf_op jit(solution)/shard_map/ppermute | solution.py:103
  11.2 4.1 %collective-permute-start.2 = (bf16[32,768]{1,0:T(8,128)(2,1)S(1)}, bf16[32,768]{1,0:T(8,128)(2,1)S(1)}, u32[]{:S(2)}, u32[]{:S(2)}) collective-permute-start(bf16[32,768]{1,0:T(8,128)(2,1)S(1)} %pad_maximum_fusion.1), channel_id=1, source_target_pairs={{0,8},{1,9},{2,10},{3,11},{4,12},{5,13},{6,14},{7,15},{8,0},{9,1},... | collective-permute-start | bytes 147464 | tf_op jit(solution)/shard_map/ppermute | solution.py:103
  16.0 1.3 %collective-permute-start.3 = (bf16[64,768]{1,0:T(8,128)(2,1)S(1)}, bf16[64,768]{1,0:T(8,128)(2,1)S(1)}, u32[]{:S(2)}, u32[]{:S(2)}) collective-permute-start(bf16[64,768]{1,0:T(8,128)(2,1)S(1)} %pad_maximum_fusion), channel_id=1, source_target_pairs={{0,4},{1,5},{2,6},{3,7},{4,0},{5,1},{6,2},{7,3},{8,12},{9,13},{10,... | collective-permute-start | bytes 294920 | tf_op jit(solution)/shard_map/ppermute | solution.py:103
  17.3 2.2 %copy-start = (bf16[2048,1000]{0,1:T(8,128)(2,1)S(1)}, bf16[2048,1000]{0,1:T(8,128)(2,1)}, u32[]{:S(2)}) copy-start(bf16[2048,1000]{0,1:T(8,128)(2,1)} %param.5) | copy-start | bytes 12288004
  19.5 1.9 %copy-start.1 = (bf16[2048,768]{1,0:T(8,128)(2,1)S(1)}, bf16[2048,768]{1,0:T(8,128)(2,1)}, u32[]{:S(2)}) copy-start(bf16[2048,768]{1,0:T(8,128)(2,1)} %k_ref.1) | copy-start | bytes 9437188
  24.0 0.7 %copy-start.2 = (f32[64,1024]{1,0:T(8,128)}, f32[64,1024]{1,0:T(8,128)S(1)}, u32[]{:S(2)}) copy-start(f32[64,1024]{1,0:T(8,128)S(1)} %get-tuple-element.13.mine_ref) | copy-start | bytes 786436
  24.7 1.5 %collective-permute-start.4 = (f32[64,1024]{1,0:T(8,128)S(1)}, f32[64,1024]{1,0:T(8,128)S(1)}, u32[]{:S(2)}, u32[]{:S(2)}) collective-permute-start(f32[64,1024]{1,0:T(8,128)S(1)} %get-tuple-element.14), channel_id=1, source_target_pairs={{0,4},{1,5},{2,6},{3,7},{4,0},{5,1},{6,2},{7,3},{8,12},{9,13},{10,... | collective-permute-start | bytes 786440 | tf_op jit(solution)/shard_map/ppermute | solution.py:103
  26.2 0.7 %copy-start.3 = (f32[64,1024]{1,0:T(8,128)}, f32[64,1024]{1,0:T(8,128)S(1)}, u32[]{:S(2)}) copy-start(f32[64,1024]{1,0:T(8,128)S(1)} %collective-permute-done.4.other_ref) | copy-start | bytes 786436
  28.7 5.8 %collective-permute-start.5 = (f32[32,1024]{1,0:T(8,128)}, f32[32,1024]{1,0:T(8,128)S(1)}, u32[]{:S(2)}, u32[]{:S(2)}) collective-permute-start(f32[32,1024]{1,0:T(8,128)} %get-tuple-element.16), channel_id=1, source_target_pairs={{0,8},{1,9},{2,10},{3,11},{4,12},{5,13},{6,14},{7,15},{8,0},{9,1},... | collective-permute-start | bytes 393224 | tf_op jit(solution)/shard_map/ppermute | solution.py:103
  34.6 0.7 %copy-start.4 = (f32[32,1024]{1,0:T(8,128)}, f32[32,1024]{1,0:T(8,128)S(1)}, u32[]{:S(2)}) copy-start(f32[32,1024]{1,0:T(8,128)S(1)} %collective-permute-done.5.other_ref) | copy-start | bytes 393220
  37.0 5.8 %collective-permute-start.6 = (f32[16,1024]{1,0:T(8,128)}, f32[16,1024]{1,0:T(8,128)S(1)}, u32[]{:S(2)}, u32[]{:S(2)}) collective-permute-start(f32[16,1024]{1,0:T(8,128)} %get-tuple-element.18), channel_id=1, source_target_pairs={{0,2},{1,3},{2,0},{3,1},{4,6},{5,7},{6,4},{7,5},{8,10},{9,11},{10,... | collective-permute-start | bytes 196616 | tf_op jit(solution)/shard_map/ppermute | solution.py:103
  42.8 0.6 %copy-start.5 = (f32[16,1024]{1,0:T(8,128)}, f32[16,1024]{1,0:T(8,128)S(1)}, u32[]{:S(2)}) copy-start(f32[16,1024]{1,0:T(8,128)S(1)} %collective-permute-done.6.other_ref) | copy-start | bytes 196612
  45.0 4.1 %collective-permute-start.7 = (f32[8,1024]{1,0:T(8,128)}, f32[8,1024]{1,0:T(8,128)S(1)}, u32[]{:S(2)}, u32[]{:S(2)}) collective-permute-start(f32[8,1024]{1,0:T(8,128)} %get-tuple-element.20), channel_id=1, source_target_pairs={{0,1},{1,0},{2,3},{3,2},{4,5},{5,4},{6,7},{7,6},{8,9},{9,8},{10,11... | collective-permute-start | bytes 98312 | tf_op jit(solution)/shard_map/ppermute | solution.py:103
  49.1 0.6 %copy-start.6 = (f32[8,1024]{1,0:T(8,128)}, f32[8,1024]{1,0:T(8,128)S(1)}, u32[]{:S(2)}) copy-start(f32[8,1024]{1,0:T(8,128)S(1)} %collective-permute-done.7.other_ref) | copy-start | bytes 98308

commit v2 on v1

--- a/solution.py
+++ b/solution.py
@@ -14,16 +14,42 @@
 VMEM = pl.BlockSpec(memory_space=pltpu.VMEM)
 
 
+MIB = 1 << 20
+
+
 def pad_lanes(width):
     return -(-(width + 2) // LANES) * LANES
 
 
-def stats_kernel(q_ref, k_ref, lt_ref, keep_ref, send_ref):
-    rows, width = q_ref.shape
+def grant(*arrays):
+    return pltpu.CompilerParams(
+        vmem_limit_bytes=sum(2 * math.prod(a.shape) * a.dtype.itemsize for a in arrays) + MIB
+    )
+
+
+def join_kernel(a_ref, b_ref, out_ref):
+    rows = a_ref.shape[0]
+    out_ref[:rows] = a_ref[...]
+    out_ref[rows:] = b_ref[...]
+
+
+def join(a, b):
+    out = jax.ShapeDtypeStruct((2 * a.shape[0], a.shape[1]), a.dtype)
+    return pl.pallas_call(
+        join_kernel,
+        out_shape=out,
+        in_specs=[VMEM] * 2,
+        out_specs=VMEM,
+        compiler_params=grant(out, out),
+    )(a, b)
+
+
+def stats_kernel(near_ref, far_ref, k_ref, lt_ref, keep_ref, send_ref):
+    half, width = near_ref.shape
     classes = lt_ref.shape[0]
-    half = rows // 2
+    queries = jnp.concatenate([near_ref[...], far_ref[...]], axis=0)
     scores = lax.dot_general(
-        q_ref[...], k_ref[...], (((1,), (1,)), ((), ())), preferred_element_type=jnp.float32
+        queries, k_ref[...], (((1,), (1,)), ((), ())), preferred_element_type=jnp.float32
     ) * (SCORE_GAIN / math.sqrt(width))
     peaks = jnp.max(scores, axis=1, keepdims=True)
     weights = jnp.exp(scores - peaks)
@@ -40,23 +66,24 @@
         ref[:, classes + 1 : classes + 2] = totals[lo : lo + half]
 
 
-def stats(queries, keys, labels_t):
-    rows, width = queries.shape
+def stats(near, far, keys, labels_t):
+    rows, width = 2 * near.shape[0], near.shape[1]
     bank = keys.shape[0]
     classes = labels_t.shape[0]
     out = jax.ShapeDtypeStruct((rows // 2, pad_lanes(classes)), jnp.float32)
+    scores = jax.ShapeDtypeStruct((rows, bank), jnp.float32)
     return pl.pallas_call(
         stats_kernel,
         out_shape=(out, out),
-        in_specs=[VMEM] * 3,
+        in_specs=[VMEM] * 4,
         out_specs=(VMEM, VMEM),
-        compiler_params=pltpu.CompilerParams(vmem_limit_bytes=32 * 1024 * 1024),
+        compiler_params=grant(near, far, keys, labels_t, out, out, scores),
         cost_estimate=pl.CostEstimate(
             flops=2 * rows * bank * (width + classes),
             bytes_accessed=2 * bank * (width + classes),
             transcendentals=rows * bank,
         ),
-    )(queries, keys, labels_t)
+    )(near, far, keys, labels_t)
 
 
 def combine(mine, other, classes):
@@ -81,6 +108,7 @@
         out_shape=(out, out),
         in_specs=[VMEM] * 2,
         out_specs=(VMEM, VMEM),
+        compiler_params=grant(mine, other, out, out),
     )(mine, other)
 
 
@@ -90,11 +118,13 @@
 
 
 def finish(mine, other, classes):
+    out = jax.ShapeDtypeStruct((mine.shape[0], classes), jnp.float32)
     return pl.pallas_call(
         functools.partial(finish_kernel, classes),
-        out_shape=jax.ShapeDtypeStruct((mine.shape[0], classes), jnp.float32),
+        out_shape=out,
         in_specs=[VMEM] * 2,
         out_specs=VMEM,
+        compiler_params=grant(mine, other, out),
     )(mine, other)
 
 
@@ -104,9 +134,9 @@
 
     classes = bank_labels.shape[1]
     rows = queries
-    for bit in bits:
-        rows = jnp.concatenate([rows, swap(rows, bit)], axis=0)
-    keep, send = stats(rows, bank_keys, bank_labels.T)
+    for bit in bits[:-1]:
+        rows = join(rows, swap(rows, bit))
+    keep, send = stats(rows, swap(rows, bits[-1]), bank_keys, bank_labels.T)
     for bit in bits[:0:-1]:
         keep, send = merge(keep, swap(send, bit), classes)
     return finish(keep, swap(send, bits[0]), classes)

time: 51.8 us -> 40.9 us (0.79)
  Pallas kernels: 9.3 us -> 3.71 us
  local copies, waits for them, and re-layouts: 8.12 us -> 4.76 us
  other arithmetic: 2.14 us -> 0 us
    pallas_call x3, Pallas kernels: 5.1 us -> 0.28 us  [merge(): pl.pallas_call(functools.partial(merge_kernel, classes), out_shape=(out,...]
    unnamed x18 -> x6, local copies, waits for them, and re-layouts: 8.11 us -> 4.76 us
    concatenate x3 -> x0, other arithmetic: 2.14 us -> none  [local(): rows = jnp.concatenate([rows, swap(rows, bit)], axis=0)]
    pallas_call x2 -> x5, Pallas kernels: 4.19 us -> 3.43 us  [the longest x1 2.64 us: stats(): pl.pallas_call(stats_kernel, out_shape=(out, out), in_specs=[VMEM] * 4, o...]
  transfers between devices with their start and end apart: 8 -> 8, of which waited for: 8 -> 8; matrix products, arithmetic and copies ran while one was open for 1% -> 0% of each run, Pallas kernels for 0% -> 0%
where the time goes in v2:
time: 40.9 us; the launch traced here: 40.6 us
  waiting for transfers between devices  17.7 us (43%)
  starting transfers between devices  14.4 us (35%)
  local copies, waits for them, and re-layouts  4.76 us (12%)
  Pallas kernels  3.71 us (9%)
    ppermute x8, waiting for transfers between devices, swap(): return lax.ppermute(block, AXES, [(i, i ^ bit) for i in range(size)])  17.7 us
    ppermute x8, starting transfers between devices, swap(): return lax.ppermute(block, AXES, [(i, i ^ bit) for i in range(size)])  14.4 us
    unnamed x6, local copies, waits for them, and re-layouts  4.76 us
    pallas_call x1, Pallas kernels, stats(): pl.pallas_call(stats_kernel, out_shape=(out, out), in_specs=[VMEM] * 4, o...  2.64 us
  transfers between devices with their start and end apart: 8, of which 8 were waited for; matrix products, arithmetic and copies ran while one was open for 0% of the time, Pallas kernels for 0%

profile of v2, /device:TPU:0, one launch (start us, length us, event | category | flops | bytes accessed | tf_op | source)
XLA Modules:
  0.0 40.6 jit_solution(3790586457168270480)
XLA Ops:
  0.0 3.0 %collective-permute-start = (bf16[8,768]{1,0:T(8,128)(2,1)}, bf16[8,768]{1,0:T(8,128)(2,1)S(1)}, u32[]{:S(2)}, u32[]{:S(2)}) collective-permute-start(bf16[8,768]{1,0:T(8,128)(2,1)} %a_ref.1), channel_id=1, source_target_pairs={{0,1},{1,0},{2,3},{3,2},{4,5},{5,4},{6,7},{7,6},{8,9},{9,8},{10,11... | collective-permute-start | bytes 36872 | tf_op jit(solution)/shard_map/ppermute | solution.py:133
  3.0 1.9 %collective-permute-done.b_ref = bf16[8,768]{1,0:T(8,128)(2,1)S(1)} collective-permute-done((bf16[8,768]{1,0:T(8,128)(2,1)}, bf16[8,768]{1,0:T(8,128)(2,1)S(1)}, u32[]{:S(2)}, u32[]{:S(2)}) %collective-permute-start) | collective-permute-done | bytes 12320 | tf_op jit(solution)/shard_map/ppermute | solution.py:133
  4.9 0.0 copy-start.2
  4.9 0.7 %copy-done.2 = bf16[8,768]{1,0:T(8,128)(2,1)S(1)} copy-done((bf16[8,768]{1,0:T(8,128)(2,1)S(1)}, bf16[8,768]{1,0:T(8,128)(2,1)}, u32[]{:S(2)}) %copy-start.2) | copy-done | bytes 12312
  5.6 3.0 %collective-permute-start.1 = (bf16[16,768]{1,0:T(8,128)(2,1)S(1)}, bf16[16,768]{1,0:T(8,128)(2,1)S(1)}, u32[]{:S(2)}, u32[]{:S(2)}) collective-permute-start(bf16[16,768]{1,0:T(8,128)(2,1)S(1)} %shard_map.37.a_ref), channel_id=1, source_target_pairs={{0,2},{1,3},{2,0},{3,1},{4,6},{5,7},{6,4},{7,5},{8,10},{9,11},{10,... | collective-permute-start | bytes 73736 | tf_op jit(solution)/shard_map/ppermute | solution.py:133
  8.7 1.8 %collective-permute-done.1.b_ref = bf16[16,768]{1,0:T(8,128)(2,1)S(1)} collective-permute-done((bf16[16,768]{1,0:T(8,128)(2,1)S(1)}, bf16[16,768]{1,0:T(8,128)(2,1)S(1)}, u32[]{:S(2)}, u32[]{:S(2)}) %collective-permute-start.1) | collective-permute-done | bytes 24608 | tf_op jit(solution)/shard_map/ppermute | solution.py:133
  10.5 1.8 %collective-permute-start.2 = (bf16[32,768]{1,0:T(8,128)(2,1)S(1)}, bf16[32,768]{1,0:T(8,128)(2,1)S(1)}, u32[]{:S(2)}, u32[]{:S(2)}) collective-permute-start(bf16[32,768]{1,0:T(8,128)(2,1)S(1)} %shard_map.38.a_ref), channel_id=1, source_target_pairs={{0,8},{1,9},{2,10},{3,11},{4,12},{5,13},{6,14},{7,15},{8,0},{9,1},... | collective-permute-start | bytes 147464 | tf_op jit(solution)/shard_map/ppermute | solution.py:133
  12.3 2.3 %collective-permute-done.2.b_ref = bf16[32,768]{1,0:T(8,128)(2,1)S(1)} collective-permute-done((bf16[32,768]{1,0:T(8,128)(2,1)S(1)}, bf16[32,768]{1,0:T(8,128)(2,1)S(1)}, u32[]{:S(2)}, u32[]{:S(2)}) %collective-permute-start.2) | collective-permute-done | bytes 49184 | tf_op jit(solution)/shard_map/ppermute | solution.py:133
  14.6 0.1 collective-permute-start.3
  14.6 1.3 %collective-permute-done.3.far_ref = bf16[64,768]{1,0:T(8,128)(2,1)S(1)} collective-permute-done((bf16[64,768]{1,0:T(8,128)(2,1)S(1)}, bf16[64,768]{1,0:T(8,128)(2,1)S(1)}, u32[]{:S(2)}, u32[]{:S(2)}) %collective-permute-start.3) | collective-permute-done | bytes 98336 | tf_op jit(solution)/shard_map/ppermute | solution.py:133
  15.9 0.0 copy-start
  15.9 2.2 %copy-done = bf16[2048,1000]{0,1:T(8,128)(2,1)S(1)} copy-done((bf16[2048,1000]{0,1:T(8,128)(2,1)S(1)}, bf16[2048,1000]{0,1:T(8,128)(2,1)}, u32[]{:S(2)}) %copy-start) | copy-done | bytes 4096024
  18.1 0.0 copy-start.1
  18.1 1.9 %copy-done.1 = bf16[2048,768]{1,0:T(8,128)(2,1)S(1)} copy-done((bf16[2048,768]{1,0:T(8,128)(2,1)S(1)}, bf16[2048,768]{1,0:T(8,128)(2,1)}, u32[]{:S(2)}) %copy-start.1) | copy-done | bytes 3145752
  20.0 2.6 %shard_map.40 = (f32[64,1024]{1,0:T(8,128)S(1)}, f32[64,1024]{1,0:T(8,128)S(1)}) custom-call(bf16[64,768]{1,0:T(8,128)(2,1)S(1)} %shard_map.39.near_ref, bf16[64,768]{1,0:T(8,128)(2,1)S(1)} %collective-permute-done.3.far_ref, bf16[2048,768]{1,0:T(8,128)(2,1)S(1)} %copy-done.1, bf16[1000,2048]{1,0:T(8,128)(2,1)S(1)} %bitcast.1), custom_call_target="tpu_custom_call" | custom-call | flops 926941184 | bytes 7241728 | tf_op jit(solution)/shard_map/pallas_call | solution.py:75
  22.6 0.2 collective-permute-start.4
  22.8 1.4 %collective-permute-done.4.other_ref = f32[64,1024]{1,0:T(8,128)S(1)} collective-permute-done((f32[64,1024]{1,0:T(8,128)S(1)}, f32[64,1024]{1,0:T(8,128)S(1)}, u32[]{:S(2)}, u32[]{:S(2)}) %collective-permute-start.4) | collective-permute-done | bytes 262176 | tf_op jit(solution)/shard_map/ppermute | solution.py:133
  24.2 0.1 shard_map.41
  24.3 1.9 %collective-permute-start.5 = (f32[32,1024]{1,0:T(8,128)S(1)}, f32[32,1024]{1,0:T(8,128)S(1)}, u32[]{:S(2)}, u32[]{:S(2)}) collective-permute-start(f32[32,1024]{1,0:T(8,128)S(1)} %get-tuple-element.16), channel_id=1, source_target_pairs={{0,8},{1,9},{2,10},{3,11},{4,12},{5,13},{6,14},{7,15},{8,0},{9,1},... | collective-permute-start | bytes 393224 | tf_op jit(solution)/shard_map/ppermute | solution.py:133
  26.2 3.8 %collective-permute-done.5.other_ref = f32[32,1024]{1,0:T(8,128)S(1)} collective-permute-done((f32[32,1024]{1,0:T(8,128)S(1)}, f32[32,1024]{1,0:T(8,128)S(1)}, u32[]{:S(2)}, u32[]{:S(2)}) %collective-permute-start.5) | collective-permute-done | bytes 131104 | tf_op jit(solution)/shard_map/ppermute | solution.py:133
  30.0 0.1 shard_map.42
  30.1 2.9 %collective-permute-start.6 = (f32[16,1024]{1,0:T(8,128)S(1)}, f32[16,1024]{1,0:T(8,128)S(1)}, u32[]{:S(2)}, u32[]{:S(2)}) collective-permute-start(f32[16,1024]{1,0:T(8,128)S(1)} %get-tuple-element.18), channel_id=1, source_target_pairs={{0,2},{1,3},{2,0},{3,1},{4,6},{5,7},{6,4},{7,5},{8,10},{9,11},{10,... | collective-permute-start | bytes 196616 | tf_op jit(solution)/shard_map/ppermute | solution.py:133
  33.1 2.7 %collective-permute-done.6.other_ref = f32[16,1024]{1,0:T(8,128)S(1)} collective-permute-done((f32[16,1024]{1,0:T(8,128)S(1)}, f32[16,1024]{1,0:T(8,128)S(1)}, u32[]{:S(2)}, u32[]{:S(2)}) %collective-permute-start.6) | collective-permute-done | bytes 65568 | tf_op jit(solution)/shard_map/ppermute | solution.py:133
  35.8 0.1 shard_map.43
  35.9 1.5 %collective-permute-start.7 = (f32[8,1024]{1,0:T(8,128)S(1)}, f32[8,1024]{1,0:T(8,128)S(1)}, u32[]{:S(2)}, u32[]{:S(2)}) collective-permute-start(f32[8,1024]{1,0:T(8,128)S(1)} %get-tuple-element.20), channel_id=1, source_target_pairs={{0,1},{1,0},{2,3},{3,2},{4,5},{5,4},{6,7},{7,6},{8,9},{9,8},{10,11... | collective-permute-start | bytes 98312 | tf_op jit(solution)/shard_map/ppermute | solution.py:133
  37.4 2.5 %collective-permute-done.7.other_ref = f32[8,1024]{1,0:T(8,128)S(1)} collective-permute-done((f32[8,1024]{1,0:T(8,128)S(1)}, f32[8,1024]{1,0:T(8,128)S(1)}, u32[]{:S(2)}, u32[]{:S(2)}) %collective-permute-start.7) | collective-permute-done | bytes 32800 | tf_op jit(solution)/shard_map/ppermute | solution.py:133
  39.9 0.8 %shard_map.44 = f32[8,1000]{1,0:T(8,128)} custom-call(f32[8,1024]{1,0:T(8,128)S(1)} %get-tuple-element.19.mine_ref, f32[8,1024]{1,0:T(8,128)S(1)} %collective-permute-done.7.other_ref), custom_call_target="tpu_custom_call" | custom-call | tf_op jit(solution)/shard_map/pallas_call | solution.py:122
  (3 shorter events, 0.0 us)
Async XLA Ops:
  0.0 4.9 %collective-permute-start = (bf16[8,768]{1,0:T(8,128)(2,1)}, bf16[8,768]{1,0:T(8,128)(2,1)S(1)}, u32[]{:S(2)}, u32[]{:S(2)}) collective-permute-start(bf16[8,768]{1,0:T(8,128)(2,1)} %a_ref.1), channel_id=1, source_target_pairs={{0,1},{1,0},{2,3},{3,2},{4,5},{5,4},{6,7},{7,6},{8,9},{9,8},{10,11... | collective-permute-start | bytes 36872 | tf_op jit(solution)/shard_map/ppermute | solution.py:133
  4.9 0.7 %copy-start.2 = (bf16[8,768]{1,0:T(8,128)(2,1)S(1)}, bf16[8,768]{1,0:T(8,128)(2,1)}, u32[]{:S(2)}) copy-start(bf16[8,768]{1,0:T(8,128)(2,1)} %a_ref.1) | copy-start | bytes 36868
  5.6 4.8 %collective-permute-start.1 = (bf16[16,768]{1,0:T(8,128)(2,1)S(1)}, bf16[16,768]{1,0:T(8,128)(2,1)S(1)}, u32[]{:S(2)}, u32[]{:S(2)}) collective-permute-start(bf16[16,768]{1,0:T(8,128)(2,1)S(1)} %shard_map.37.a_ref), channel_id=1, source_target_pairs={{0,2},{1,3},{2,0},{3,1},{4,6},{5,7},{6,4},{7,5},{8,10},{9,11},{10,... | collective-permute-start | bytes 73736 | tf_op jit(solution)/shard_map/ppermute | solution.py:133
  10.5 4.1 %collective-permute-start.2 = (bf16[32,768]{1,0:T(8,128)(2,1)S(1)}, bf16[32,768]{1,0:T(8,128)(2,1)S(1)}, u32[]{:S(2)}, u32[]{:S(2)}) collective-permute-start(bf16[32,768]{1,0:T(8,128)(2,1)S(1)} %shard_map.38.a_ref), channel_id=1, source_target_pairs={{0,8},{1,9},{2,10},{3,11},{4,12},{5,13},{6,14},{7,15},{8,0},{9,1},... | collective-permute-start | bytes 147464 | tf_op jit(solution)/shard_map/ppermute | solution.py:133
  14.6 1.4 %collective-permute-start.3 = (bf16[64,768]{1,0:T(8,128)(2,1)S(1)}, bf16[64,768]{1,0:T(8,128)(2,1)S(1)}, u32[]{:S(2)}, u32[]{:S(2)}) collective-permute-start(bf16[64,768]{1,0:T(8,128)(2,1)S(1)} %shard_map.39.near_ref), channel_id=1, source_target_pairs={{0,4},{1,5},{2,6},{3,7},{4,0},{5,1},{6,2},{7,3},{8,12},{9,13},{10,... | collective-permute-start | bytes 294920 | tf_op jit(solution)/shard_map/ppermute | solution.py:133
  15.9 2.2 %copy-start = (bf16[2048,1000]{0,1:T(8,128)(2,1)S(1)}, bf16[2048,1000]{0,1:T(8,128)(2,1)}, u32[]{:S(2)}) copy-start(bf16[2048,1000]{0,1:T(8,128)(2,1)} %param.5) | copy-start | bytes 12288004
  18.1 1.9 %copy-start.1 = (bf16[2048,768]{1,0:T(8,128)(2,1)S(1)}, bf16[2048,768]{1,0:T(8,128)(2,1)}, u32[]{:S(2)}) copy-start(bf16[2048,768]{1,0:T(8,128)(2,1)} %k_ref.1) | copy-start | bytes 9437188
  22.6 1.6 %collective-permute-start.4 = (f32[64,1024]{1,0:T(8,128)S(1)}, f32[64,1024]{1,0:T(8,128)S(1)}, u32[]{:S(2)}, u32[]{:S(2)}) collective-permute-start(f32[64,1024]{1,0:T(8,128)S(1)} %get-tuple-element.14), channel_id=1, source_target_pairs={{0,4},{1,5},{2,6},{3,7},{4,0},{5,1},{6,2},{7,3},{8,12},{9,13},{10,... | collective-permute-start | bytes 786440 | tf_op jit(solution)/shard_map/ppermute | solution.py:133
  24.3 5.7 %collective-permute-start.5 = (f32[32,1024]{1,0:T(8,128)S(1)}, f32[32,1024]{1,0:T(8,128)S(1)}, u32[]{:S(2)}, u32[]{:S(2)}) collective-permute-start(f32[32,1024]{1,0:T(8,128)S(1)} %get-tuple-element.16), channel_id=1, source_target_pairs={{0,8},{1,9},{2,10},{3,11},{4,12},{5,13},{6,14},{7,15},{8,0},{9,1},... | collective-permute-start | bytes 393224 | tf_op jit(solution)/shard_map/ppermute | solution.py:133
  30.1 5.6 %collective-permute-start.6 = (f32[16,1024]{1,0:T(8,128)S(1)}, f32[16,1024]{1,0:T(8,128)S(1)}, u32[]{:S(2)}, u32[]{:S(2)}) collective-permute-start(f32[16,1024]{1,0:T(8,128)S(1)} %get-tuple-element.18), channel_id=1, source_target_pairs={{0,2},{1,3},{2,0},{3,1},{4,6},{5,7},{6,4},{7,5},{8,10},{9,11},{10,... | collective-permute-start | bytes 196616 | tf_op jit(solution)/shard_map/ppermute | solution.py:133
  35.9 4.0 %collective-permute-start.7 = (f32[8,1024]{1,0:T(8,128)S(1)}, f32[8,1024]{1,0:T(8,128)S(1)}, u32[]{:S(2)}, u32[]{:S(2)}) collective-permute-start(f32[8,1024]{1,0:T(8,128)S(1)} %get-tuple-element.20), channel_id=1, source_target_pairs={{0,1},{1,0},{2,3},{3,2},{4,5},{5,4},{6,7},{7,6},{8,9},{9,8},{10,11... | collective-permute-start | bytes 98312 | tf_op jit(solution)/shard_map/ppermute | solution.py:133

commit v3 on v2

--- a/solution.py
+++ b/solution.py
@@ -27,6 +27,24 @@
     )
 
 
+BESIDE = pl.CostEstimate(flops=4_000_000_000, bytes_accessed=1 << 17, transcendentals=0)
+
+
+def fetch_kernel(a_ref, out_ref):
+    out_ref[...] = a_ref[...]
+
+
+def fetch(a):
+    return pl.pallas_call(
+        fetch_kernel,
+        out_shape=jax.ShapeDtypeStruct(a.shape, a.dtype),
+        in_specs=[VMEM],
+        out_specs=VMEM,
+        compiler_params=grant(a, a),
+        cost_estimate=BESIDE,
+    )(a)
+
+
 def join_kernel(a_ref, b_ref, out_ref):
     rows = a_ref.shape[0]
     out_ref[:rows] = a_ref[...]
@@ -41,6 +59,7 @@
         in_specs=[VMEM] * 2,
         out_specs=VMEM,
         compiler_params=grant(out, out),
+        cost_estimate=BESIDE,
     )(a, b)
 
 
@@ -133,8 +152,8 @@
         return lax.ppermute(block, AXES, [(i, i ^ bit) for i in range(size)])
 
     classes = bank_labels.shape[1]
-    rows = queries
-    for bit in bits[:-1]:
+    rows = join(fetch(queries), swap(queries, bits[0]))
+    for bit in bits[1:-1]:
         rows = join(rows, swap(rows, bit))
     keep, send = stats(rows, swap(rows, bits[-1]), bank_keys, bank_labels.T)
     for bit in bits[:0:-1]:
@@ -147,7 +166,7 @@
     size = mesh.shape["bank"] * mesh.shape["query"]
     query_bits = [1 << b for b in range(mesh.shape["query"].bit_length() - 1)]
     bank_bits = [mesh.shape["query"] << b for b in range(mesh.shape["bank"].bit_length() - 1)]
-    bits = query_bits + bank_bits[1:] + bank_bits[:1]
+    bits = query_bits[::-1] + bank_bits[1:] + bank_bits[:1]
     return jax.shard_map(
         functools.partial(local, bits, size),
         mesh=mesh,

time: 40.9 us -> 35.8 us (0.88)
  local copies, waits for them, and re-layouts: 4.76 us -> 0.75 us
  waiting for transfers between devices: 17.7 us -> 16.2 us
    unnamed x6, local copies, waits for them, and re-layouts: 4.76 us -> 0.75 us
    ppermute x8, waiting for transfers between devices: 17.7 us -> 16.2 us  [swap(): return lax.ppermute(block, AXES, [(i, i ^ bit) for i in range(size)])]
where the time goes in v3:
time: 35.8 us; the launch traced here: 35.6 us
  waiting for transfers between devices  16.2 us (45%)
  starting transfers between devices  14.8 us (41%)
  Pallas kernels  3.72 us (10%)
  local copies, waits for them, and re-layouts  0.75 us (2%)
    ppermute x8, waiting for transfers between devices, swap(): return lax.ppermute(block, AXES, [(i, i ^ bit) for i in range(size)])  16.2 us
    ppermute x8, starting transfers between devices, swap(): return lax.ppermute(block, AXES, [(i, i ^ bit) for i in range(size)])  14.8 us
    pallas_call x1, Pallas kernels, stats(): pl.pallas_call(stats_kernel, out_shape=(out, out), in_specs=[VMEM] * 4, o...  2.64 us
    pallas_call x1, Pallas kernels, finish(): pl.pallas_call(functools.partial(finish_kernel, classes), out_shape=out,...  0.78 us
    unnamed x6, local copies, waits for them, and re-layouts  0.75 us
  transfers between devices with their start and end apart: 8, of which 8 were waited for; matrix products, arithmetic and copies ran while one was open for 0% of the time, Pallas kernels for 0%

profile of v3, /device:TPU:0, one launch (start us, length us, event | category | flops | bytes accessed | tf_op | source)
XLA Modules:
  0.0 35.6 jit_solution(10512766589672748820)
XLA Ops:
  0.0 4.0 %collective-permute-start = (bf16[8,768]{1,0:T(8,128)(2,1)}, bf16[8,768]{1,0:T(8,128)(2,1)S(1)}, u32[]{:S(2)}, u32[]{:S(2)}) collective-permute-start(bf16[8,768]{1,0:T(8,128)(2,1)} %a_ref.1), channel_id=1, source_target_pairs={{0,2},{1,3},{2,0},{3,1},{4,6},{5,7},{6,4},{7,5},{8,10},{9,11},{10,... | collective-permute-start | bytes 36872 | tf_op jit(solution)/shard_map/ppermute | solution.py:152
  4.0 0.0 copy-start.2
  4.0 0.7 %copy-done.2 = bf16[8,768]{1,0:T(8,128)(2,1)S(1)} copy-done((bf16[8,768]{1,0:T(8,128)(2,1)S(1)}, bf16[8,768]{1,0:T(8,128)(2,1)}, u32[]{:S(2)}) %copy-start.2) | copy-done | bytes 12312
  4.8 1.1 %collective-permute-done.b_ref = bf16[8,768]{1,0:T(8,128)(2,1)S(1)} collective-permute-done((bf16[8,768]{1,0:T(8,128)(2,1)}, bf16[8,768]{1,0:T(8,128)(2,1)S(1)}, u32[]{:S(2)}, u32[]{:S(2)}) %collective-permute-start) | collective-permute-done | bytes 12320 | tf_op jit(solution)/shard_map/ppermute | solution.py:152
  5.9 1.9 %collective-permute-start.1 = (bf16[16,768]{1,0:T(8,128)(2,1)S(1)}, bf16[16,768]{1,0:T(8,128)(2,1)S(1)}, u32[]{:S(2)}, u32[]{:S(2)}) collective-permute-start(bf16[16,768]{1,0:T(8,128)(2,1)S(1)} %shard_map.38.a_ref), channel_id=1, source_target_pairs={{0,1},{1,0},{2,3},{3,2},{4,5},{5,4},{6,7},{7,6},{8,9},{9,8},{10,11... | collective-permute-start | bytes 73736 | tf_op jit(solution)/shard_map/ppermute | solution.py:152
  7.8 1.9 %collective-permute-done.1.b_ref = bf16[16,768]{1,0:T(8,128)(2,1)S(1)} collective-permute-done((bf16[16,768]{1,0:T(8,128)(2,1)S(1)}, bf16[16,768]{1,0:T(8,128)(2,1)S(1)}, u32[]{:S(2)}, u32[]{:S(2)}) %collective-permute-start.1) | collective-permute-done | bytes 24608 | tf_op jit(solution)/shard_map/ppermute | solution.py:152
  9.8 0.0 copy-start
  9.8 0.0 copy-start.1
  9.8 1.9 %collective-permute-start.2 = (bf16[32,768]{1,0:T(8,128)(2,1)S(1)}, bf16[32,768]{1,0:T(8,128)(2,1)S(1)}, u32[]{:S(2)}, u32[]{:S(2)}) collective-permute-start(bf16[32,768]{1,0:T(8,128)(2,1)S(1)} %shard_map.39.a_ref), channel_id=1, source_target_pairs={{0,8},{1,9},{2,10},{3,11},{4,12},{5,13},{6,14},{7,15},{8,0},{9,1},... | collective-permute-start | bytes 147464 | tf_op jit(solution)/shard_map/ppermute | solution.py:152
  11.7 2.3 %collective-permute-done.2.b_ref = bf16[32,768]{1,0:T(8,128)(2,1)S(1)} collective-permute-done((bf16[32,768]{1,0:T(8,128)(2,1)S(1)}, bf16[32,768]{1,0:T(8,128)(2,1)S(1)}, u32[]{:S(2)}, u32[]{:S(2)}) %collective-permute-start.2) | collective-permute-done | bytes 49184 | tf_op jit(solution)/shard_map/ppermute | solution.py:152
  13.9 0.1 collective-permute-start.3
  14.0 1.3 %collective-permute-done.3.far_ref = bf16[64,768]{1,0:T(8,128)(2,1)S(1)} collective-permute-done((bf16[64,768]{1,0:T(8,128)(2,1)S(1)}, bf16[64,768]{1,0:T(8,128)(2,1)S(1)}, u32[]{:S(2)}, u32[]{:S(2)}) %collective-permute-start.3) | collective-permute-done | bytes 98336 | tf_op jit(solution)/shard_map/ppermute | solution.py:152
  15.3 0.0 copy-done
  15.3 0.0 copy-done.1
  15.3 2.6 %shard_map.41 = (f32[64,1024]{1,0:T(8,128)S(1)}, f32[64,1024]{1,0:T(8,128)S(1)}) custom-call(bf16[64,768]{1,0:T(8,128)(2,1)S(1)} %shard_map.40.near_ref, bf16[64,768]{1,0:T(8,128)(2,1)S(1)} %collective-permute-done.3.far_ref, bf16[2048,768]{1,0:T(8,128)(2,1)S(1)} %copy-done.1, bf16[1000,2048]{1,0:T(8,128)(2,1)S(1)} %bitcast.1), custom_call_target="tpu_custom_call" | custom-call | flops 926941184 | bytes 7241728 | tf_op jit(solution)/shard_map/pallas_call | solution.py:94
  17.9 0.2 collective-permute-start.4
  18.2 1.4 %collective-permute-done.4.other_ref = f32[64,1024]{1,0:T(8,128)S(1)} collective-permute-done((f32[64,1024]{1,0:T(8,128)S(1)}, f32[64,1024]{1,0:T(8,128)S(1)}, u32[]{:S(2)}, u32[]{:S(2)}) %collective-permute-start.4) | collective-permute-done | bytes 262176 | tf_op jit(solution)/shard_map/ppermute | solution.py:152
  19.5 0.1 shard_map.42
  19.7 1.9 %collective-permute-start.5 = (f32[32,1024]{1,0:T(8,128)S(1)}, f32[32,1024]{1,0:T(8,128)S(1)}, u32[]{:S(2)}, u32[]{:S(2)}) collective-permute-start(f32[32,1024]{1,0:T(8,128)S(1)} %get-tuple-element.16), channel_id=1, source_target_pairs={{0,8},{1,9},{2,10},{3,11},{4,12},{5,13},{6,14},{7,15},{8,0},{9,1},... | collective-permute-start | bytes 393224 | tf_op jit(solution)/shard_map/ppermute | solution.py:152
  21.6 3.8 %collective-permute-done.5.other_ref = f32[32,1024]{1,0:T(8,128)S(1)} collective-permute-done((f32[32,1024]{1,0:T(8,128)S(1)}, f32[32,1024]{1,0:T(8,128)S(1)}, u32[]{:S(2)}, u32[]{:S(2)}) %collective-permute-start.5) | collective-permute-done | bytes 131104 | tf_op jit(solution)/shard_map/ppermute | solution.py:152
  25.4 0.1 shard_map.43
  25.5 1.9 %collective-permute-start.6 = (f32[16,1024]{1,0:T(8,128)S(1)}, f32[16,1024]{1,0:T(8,128)S(1)}, u32[]{:S(2)}, u32[]{:S(2)}) collective-permute-start(f32[16,1024]{1,0:T(8,128)S(1)} %get-tuple-element.18), channel_id=1, source_target_pairs={{0,1},{1,0},{2,3},{3,2},{4,5},{5,4},{6,7},{7,6},{8,9},{9,8},{10,11... | collective-permute-start | bytes 196616 | tf_op jit(solution)/shard_map/ppermute | solution.py:152
  27.4 2.4 %collective-permute-done.6.other_ref = f32[16,1024]{1,0:T(8,128)S(1)} collective-permute-done((f32[16,1024]{1,0:T(8,128)S(1)}, f32[16,1024]{1,0:T(8,128)S(1)}, u32[]{:S(2)}, u32[]{:S(2)}) %collective-permute-start.6) | collective-permute-done | bytes 65568 | tf_op jit(solution)/shard_map/ppermute | solution.py:152
  29.8 0.1 shard_map.44
  29.9 2.9 %collective-permute-start.7 = (f32[8,1024]{1,0:T(8,128)S(1)}, f32[8,1024]{1,0:T(8,128)S(1)}, u32[]{:S(2)}, u32[]{:S(2)}) collective-permute-start(f32[8,1024]{1,0:T(8,128)S(1)} %get-tuple-element.20), channel_id=1, source_target_pairs={{0,2},{1,3},{2,0},{3,1},{4,6},{5,7},{6,4},{7,5},{8,10},{9,11},{10,... | collective-permute-start | bytes 98312 | tf_op jit(solution)/shard_map/ppermute | solution.py:152
  32.8 2.0 %collective-permute-done.7.other_ref = f32[8,1024]{1,0:T(8,128)S(1)} collective-permute-done((f32[8,1024]{1,0:T(8,128)S(1)}, f32[8,1024]{1,0:T(8,128)S(1)}, u32[]{:S(2)}, u32[]{:S(2)}) %collective-permute-start.7) | collective-permute-done | bytes 32800 | tf_op jit(solution)/shard_map/ppermute | solution.py:152
  34.8 0.8 %shard_map.45 = f32[8,1000]{1,0:T(8,128)} custom-call(f32[8,1024]{1,0:T(8,128)S(1)} %get-tuple-element.19.mine_ref, f32[8,1024]{1,0:T(8,128)S(1)} %collective-permute-done.7.other_ref), custom_call_target="tpu_custom_call" | custom-call | tf_op jit(solution)/shard_map/pallas_call | solution.py:141
  (4 shorter events, 0.0 us)
Async XLA Ops:
  0.0 5.9 %collective-permute-start = (bf16[8,768]{1,0:T(8,128)(2,1)}, bf16[8,768]{1,0:T(8,128)(2,1)S(1)}, u32[]{:S(2)}, u32[]{:S(2)}) collective-permute-start(bf16[8,768]{1,0:T(8,128)(2,1)} %a_ref.1), channel_id=1, source_target_pairs={{0,2},{1,3},{2,0},{3,1},{4,6},{5,7},{6,4},{7,5},{8,10},{9,11},{10,... | collective-permute-start | bytes 36872 | tf_op jit(solution)/shard_map/ppermute | solution.py:152
  4.0 0.7 %copy-start.2 = (bf16[8,768]{1,0:T(8,128)(2,1)S(1)}, bf16[8,768]{1,0:T(8,128)(2,1)}, u32[]{:S(2)}) copy-start(bf16[8,768]{1,0:T(8,128)(2,1)} %a_ref.1) | copy-start | bytes 36868
  5.9 3.8 %collective-permute-start.1 = (bf16[16,768]{1,0:T(8,128)(2,1)S(1)}, bf16[16,768]{1,0:T(8,128)(2,1)S(1)}, u32[]{:S(2)}, u32[]{:S(2)}) collective-permute-start(bf16[16,768]{1,0:T(8,128)(2,1)S(1)} %shard_map.38.a_ref), channel_id=1, source_target_pairs={{0,1},{1,0},{2,3},{3,2},{4,5},{5,4},{6,7},{7,6},{8,9},{9,8},{10,11... | collective-permute-start | bytes 73736 | tf_op jit(solution)/shard_map/ppermute | solution.py:152
  9.8 5.5 %copy-start = (bf16[2048,1000]{0,1:T(8,128)(2,1)S(1)}, bf16[2048,1000]{0,1:T(8,128)(2,1)}, u32[]{:S(2)}) copy-start(bf16[2048,1000]{0,1:T(8,128)(2,1)} %param.5) | copy-start | bytes 12288004
  9.8 5.5 %copy-start.1 = (bf16[2048,768]{1,0:T(8,128)(2,1)S(1)}, bf16[2048,768]{1,0:T(8,128)(2,1)}, u32[]{:S(2)}) copy-start(bf16[2048,768]{1,0:T(8,128)(2,1)} %k_ref.1) | copy-start | bytes 9437188
  9.8 4.2 %collective-permute-start.2 = (bf16[32,768]{1,0:T(8,128)(2,1)S(1)}, bf16[32,768]{1,0:T(8,128)(2,1)S(1)}, u32[]{:S(2)}, u32[]{:S(2)}) collective-permute-start(bf16[32,768]{1,0:T(8,128)(2,1)S(1)} %shard_map.39.a_ref), channel_id=1, source_target_pairs={{0,8},{1,9},{2,10},{3,11},{4,12},{5,13},{6,14},{7,15},{8,0},{9,1},... | collective-permute-start | bytes 147464 | tf_op jit(solution)/shard_map/ppermute | solution.py:152
  13.9 1.4 %collective-permute-start.3 = (bf16[64,768]{1,0:T(8,128)(2,1)S(1)}, bf16[64,768]{1,0:T(8,128)(2,1)S(1)}, u32[]{:S(2)}, u32[]{:S(2)}) collective-permute-start(bf16[64,768]{1,0:T(8,128)(2,1)S(1)} %shard_map.40.near_ref), channel_id=1, source_target_pairs={{0,4},{1,5},{2,6},{3,7},{4,0},{5,1},{6,2},{7,3},{8,12},{9,13},{10,... | collective-permute-start | bytes 294920 | tf_op jit(solution)/shard_map/ppermute | solution.py:152
  17.9 1.6 %collective-permute-start.4 = (f32[64,1024]{1,0:T(8,128)S(1)}, f32[64,1024]{1,0:T(8,128)S(1)}, u32[]{:S(2)}, u32[]{:S(2)}) collective-permute-start(f32[64,1024]{1,0:T(8,128)S(1)} %get-tuple-element.14), channel_id=1, source_target_pairs={{0,4},{1,5},{2,6},{3,7},{4,0},{5,1},{6,2},{7,3},{8,12},{9,13},{10,... | collective-permute-start | bytes 786440 | tf_op jit(solution)/shard_map/ppermute | solution.py:152
  19.7 5.7 %collective-permute-start.5 = (f32[32,1024]{1,0:T(8,128)S(1)}, f32[32,1024]{1,0:T(8,128)S(1)}, u32[]{:S(2)}, u32[]{:S(2)}) collective-permute-start(f32[32,1024]{1,0:T(8,128)S(1)} %get-tuple-element.16), channel_id=1, source_target_pairs={{0,8},{1,9},{2,10},{3,11},{4,12},{5,13},{6,14},{7,15},{8,0},{9,1},... | collective-permute-start | bytes 393224 | tf_op jit(solution)/shard_map/ppermute | solution.py:152
  25.5 4.3 %collective-permute-start.6 = (f32[16,1024]{1,0:T(8,128)S(1)}, f32[16,1024]{1,0:T(8,128)S(1)}, u32[]{:S(2)}, u32[]{:S(2)}) collective-permute-start(f32[16,1024]{1,0:T(8,128)S(1)} %get-tuple-element.18), channel_id=1, source_target_pairs={{0,1},{1,0},{2,3},{3,2},{4,5},{5,4},{6,7},{7,6},{8,9},{9,8},{10,11... | collective-permute-start | bytes 196616 | tf_op jit(solution)/shard_map/ppermute | solution.py:152
  29.9 4.9 %collective-permute-start.7 = (f32[8,1024]{1,0:T(8,128)S(1)}, f32[8,1024]{1,0:T(8,128)S(1)}, u32[]{:S(2)}, u32[]{:S(2)}) collective-permute-start(f32[8,1024]{1,0:T(8,128)S(1)} %get-tuple-element.20), channel_id=1, source_target_pairs={{0,2},{1,3},{2,0},{3,1},{4,6},{5,7},{6,4},{7,5},{8,10},{9,11},{10,... | collective-permute-start | bytes 98312 | tf_op jit(solution)/shard_map/ppermute | solution.py:152

commit v4 on v0

v4 whole, which is shorter than its diff:
```python
import functools
import math

import jax
import jax.numpy as jnp
from jax import lax
from jax.experimental import pallas as pl
from jax.experimental.pallas import tpu as pltpu
from jax.sharding import PartitionSpec as P

SCORE_GAIN = 3.0
AXES = ("bank", "query")
LANES = 128
MIB = 1 << 20
VMEM = pl.BlockSpec(memory_space=pltpu.VMEM)
BESIDE = pl.CostEstimate(flops=4_000_000_000, bytes_accessed=1 << 17, transcendentals=0)


def grant(*arrays):
    return pltpu.CompilerParams(
        vmem_limit_bytes=sum(2 * math.prod(a.shape) * a.dtype.itemsize for a in arrays) + MIB
    )


def call(kernel, outs, *args, scratch=(), cost=None):
    return pl.pallas_call(
        kernel,
        out_shape=outs,
        in_specs=[VMEM] * len(args),
        out_specs=jax.tree.map(lambda _: VMEM, outs),
        compiler_params=grant(*args, *jax.tree.leaves(outs), *scratch),
        cost_estimate=cost,
    )(*args)


def fetch_kernel(a_ref, out_ref):
    out_ref[...] = a_ref[...]


def fetch(a):
    return call(fetch_kernel, jax.ShapeDtypeStruct(a.shape, a.dtype), a, cost=BESIDE)


def join_kernel(a_ref, b_ref, out_ref):
    rows = a_ref.shape[0]
    out_ref[:rows] = a_ref[...]
    out_ref[rows:] = b_ref[...]


def join(a, b):
    out = jax.ShapeDtypeStruct((2 * a.shape[0], a.shape[1]), a.dtype)
    return call(join_kernel, out, a, b, cost=BESIDE)


def record_shape(rows, classes):
    return jax.ShapeDtypeStruct((rows, -(-(classes + 2) // LANES) * LANES), jnp.float32)


def parts_of(record, classes):
    return (
        record[:, classes : classes + 1],
        record[:, classes + 1 : classes + 2],
        record[:, :classes],
    )


def combine(*parts):
    top = functools.reduce(jnp.maximum, [peak for peak, _, _ in parts])
    factors = [jnp.exp(peak - top) for peak, _, _ in parts]
    total = sum(f * t for f, (_, t, _) in zip(factors, parts))
    votes = sum(f * v for f, (_, _, v) in zip(factors, parts))
    return top, total, votes


def put(ref, row, parts):
    peak, total, votes = parts
    rows, classes = votes.shape
    at = slice(row, row + rows)
    ref[at, :classes] = votes
    spare = ref.shape[1] - classes
    column = lax.broadcasted_iota(jnp.int32, (rows, spare), 1)
    ref[at, classes:] = jnp.where(column == 0, peak, jnp.where(column == 1, total, 0.0))


def stats_kernel(own_ref, near_ref, far_ref, across_ref, k_ref, lt_ref, keep_ref, send_ref):
    count, width = own_ref.shape
    half = count // 2
    queries = jnp.concatenate(
        [own_ref[...], near_ref[...], far_ref[...], across_ref[...]], axis=0
    )
    scores = lax.dot_general(
        queries, k_ref[...], (((1,), (1,)), ((), ())), preferred_element_type=jnp.float32
    ) * (SCORE_GAIN / math.sqrt(width))
    peaks = jnp.max(scores, axis=1, keepdims=True)
    weights = jnp.exp(scores - peaks)
    totals = jnp.sum(weights, axis=1, keepdims=True)
    votes = lax.dot_general(
        weights.astype(jnp.bfloat16),
        lt_ref[...],
        (((1,), (1,)), ((), ())),
        preferred_element_type=jnp.float32,
    )

    def move(ref, row, start, rows):
        at = slice(start, start + rows)
        put(ref, row, (peaks[at], totals[at], votes[at]))

    move(keep_ref, 0, 0, half)
    move(send_ref, 0, half, half)
    move(keep_ref, half, count, half)
    move(send_ref, half, count + half, half)
    move(keep_ref, count, 2 * count, count)
    move(send_ref, count, 3 * count, count)


def stats(blocks, keys, labels_t):
    rows, width = 4 * blocks[0].shape[0], keys.shape[1]
    bank, classes = keys.shape[0], labels_t.shape[0]
    out = record_shape(rows // 2, classes)
    scores = jax.ShapeDtypeStruct((rows, bank), jnp.float32)
    cost = pl.CostEstimate(
        flops=2 * rows * bank * (width + classes),
        bytes_accessed=2 * bank * (width + classes),
        transcendentals=rows * bank,
    )
    return call(
        stats_kernel, (out, out), *blocks, keys, labels_t, scratch=(scores,), cost=cost
    )


def merge_kernel(classes, mine_ref, other_ref, keep_ref, send_ref):
    half = keep_ref.shape[0] // 4
    for quarter in range(4):
        for ref, lo in ((keep_ref, 0), (send_ref, half)):
            at = slice(2 * quarter * half + lo, 2 * quarter * half + lo + half)
            both = [parts_of(r[at], classes) for r in (mine_ref, other_ref)]
            put(ref, quarter * half, combine(*both))


def merge(mine, other, classes):
    out = record_shape(mine.shape[0] // 2, classes)
    return call(functools.partial(merge_kernel, classes), (out, out), mine, other)


def split_kernel(classes, mine_ref, other_ref, own_ref, near_ref, far_ref):
    rows = own_ref.shape[0]
    both = [parts_of(r[...], classes) for r in (mine_ref, other_ref)]
    peak, total, votes = combine(*both)
    for ref, lo, count in ((own_ref, 0, rows), (near_ref, rows, rows), (far_ref, 2 * rows, 2 * rows)):
        at = slice(lo, lo + count)
        put(ref, 0, (peak[at], total[at], votes[at]))


def split(mine, other, classes):
    rows = mine.shape[0] // 4
    outs = (
        record_shape(rows, classes),
        record_shape(rows, classes),
        record_shape(2 * rows, classes),
    )
    return call(functools.partial(split_kernel, classes), outs, mine, other)


def tail_kernel(a_ref, out_ref):
    out_ref[...] = a_ref[out_ref.shape[0] :]


def tail(a):
    out = jax.ShapeDtypeStruct((a.shape[0] // 2, a.shape[1]), a.dtype)
    return call(tail_kernel, out, a)


def finish_kernel(classes, own_ref, near_ref, far_ref, across_ref, out_ref):
    rows = out_ref.shape[0]
    refs = (own_ref, near_ref, far_ref, across_ref)
    _, total, votes = combine(*[parts_of(r[:rows], classes) for r in refs])
    out_ref[...] = jnp.log(votes / total)


def finish(own, near, far, across, classes):
    out = jax.ShapeDtypeStruct((own.shape[0], classes), jnp.float32)
    return call(functools.partial(finish_kernel, classes), out, own, near, far, across)


def local(size, core, lead, queries, bank_keys, bank_labels):
    def swap(block, bit):
        return lax.ppermute(block, AXES, [(i, i ^ bit) for i in range(size)])

    def swap_far(block):
        return lax.ppermute(block, AXES, [(i, i ^ (2 if i & core else 3)) for i in range(size)])

    classes = bank_labels.shape[1]
    first, *rest = [*lead, core]
    own = join(fetch(queries), swap(queries, first))
    for bit in rest:
        own = join(own, swap(own, bit))
    far = swap_far(own)
    near = swap(own, 1)
    across = swap(far, core)
    keep, send = stats((own, near, far, across), bank_keys, bank_labels.T)
    came = swap(send, core)
    for bit in lead[::-1]:
        keep, send = merge(keep, came, classes)
        came = swap(send, bit)
    own, near, far = split(keep, came, classes)
    far = swap_far(far)
    near = swap(near, 1)
    across = swap(tail(far), core)
    return finish(own, near, far, across, classes)


def solution(mesh):
    placed = P(("groups", "bank", "query"), None)
    query, bank = mesh.shape["query"], mesh.shape["bank"]
    lead = [1 << b for b in range(2, query.bit_length() - 1)]
    lead += [query << b for b in range(1, bank.bit_length() - 1)]
    return jax.shard_map(
        functools.partial(local, query * bank, query, lead),
        mesh=mesh,
        in_specs=(placed,) * 3,
        out_specs=placed,
        check_vma=False,
    )
```

time: 144 us -> 32.9 us (0.23)
  blocking collectives: 97.5 us -> 0 us
  between operations: 14.1 us -> 0.04 us
  starting transfers between devices: 0.01 us -> 11.9 us
  matrix products: 6.87 us -> 0 us
  waiting for transfers between devices: 21.7 us -> 16.2 us
  Pallas kernels: 0 us -> 3.85 us
  other arithmetic: 2.98 us -> 0 us
    all_gather x1 -> x0, blocking collectives: 35.9 us -> none  [local(): lax.all_gather(queries, ('bank', 'query'), axis=0, tiled=True)]
    unnamed x1 -> x0, blocking collectives: 32 us -> none
    pmax x1 -> x0, blocking collectives: 29.7 us -> none  [local(): row_top = lax.pmax(peaks, ('bank', 'query'))]
    reduce_scatter x1 -> x0, waiting for transfers between devices: 21.7 us -> none  [local(): lax.psum_scatter(votes * factor[:, None], ('bank', 'query'), scatter_dime...]
    ppermute x0 -> x10, waiting for transfers between devices: none -> 16.2 us  [the longest x8 10.6 us: swap(): return lax.ppermute(block, AXES, [(i, i ^ bit) for i in range(size)])]
    ppermute x0 -> x10, starting transfers between devices: none -> 11.9 us  [the longest x2 7.22 us: swap_far(): lax.ppermute(block, AXES, [(i, i ^ (2 if i & core else 3)) for i in range...]
    dot_general x2 -> x0, matrix products: 6.87 us -> none  [the longest x1 4.74 us: partial_stats(): jnp.dot(weights.astype(jnp.bfloat16), label_block, preferred_element_type...]
    pallas_call x0 -> x8, Pallas kernels: none -> 3.85 us  [call(): pl.pallas_call(kernel, out_shape=outs, in_specs=[VMEM] * len(args), out_s...]
  transfers between devices with their start and end apart: 1 -> 10, of which waited for: 1 -> 9; matrix products, arithmetic and copies ran while one was open for 0% -> 0% of each run, Pallas kernels for 0% -> 0%
where the time goes in v4:
time: 32.9 us; the launch traced here: 32.7 us
  waiting for transfers between devices  16.2 us (49%)
  starting transfers between devices  11.9 us (36%)
  Pallas kernels  3.85 us (12%)
  local copies, waits for them, and re-layouts  0.75 us (2%)
    ppermute x8, waiting for transfers between devices, swap(): return lax.ppermute(block, AXES, [(i, i ^ bit) for i in range(size)])  10.6 us
    ppermute x2, starting transfers between devices, swap_far(): lax.ppermute(block, AXES, [(i, i ^ (2 if i & core else 3)) for i in range...  7.22 us
    ppermute x2, waiting for transfers between devices, swap_far(): lax.ppermute(block, AXES, [(i, i ^ (2 if i & core else 3)) for i in range...  5.51 us
    ppermute x8, starting transfers between devices, swap(): return lax.ppermute(block, AXES, [(i, i ^ bit) for i in range(size)])  4.64 us
    pallas_call x8, Pallas kernels, call(): pl.pallas_call(kernel, out_shape=outs, in_specs=[VMEM] * len(args), out_s...  3.85 us
    unnamed x6, local copies, waits for them, and re-layouts  0.75 us
  transfers between devices with their start and end apart: 10, of which 9 were waited for; matrix products, arithmetic and copies ran while one was open for 0% of the time, Pallas kernels for 0%

profile of v4, /device:TPU:0, one launch (start us, length us, event | category | flops | bytes accessed | tf_op | source)
XLA Modules:
  0.0 32.7 jit_solution(14554417734286423686)
XLA Ops:
  0.0 2.9 %collective-permute-start = (bf16[8,768]{1,0:T(8,128)(2,1)}, bf16[8,768]{1,0:T(8,128)(2,1)S(1)}, u32[]{:S(2)}, u32[]{:S(2)}) collective-permute-start(bf16[8,768]{1,0:T(8,128)(2,1)} %a_ref.1), channel_id=1, source_target_pairs={{0,8},{1,9},{2,10},{3,11},{4,12},{5,13},{6,14},{7,15},{8,0},{9,1},... | collective-permute-start | bytes 36872 | tf_op jit(solution)/shard_map/ppermute | solution.py:187
  2.9 0.0 copy-start.2
  2.9 0.7 %copy-done.2 = bf16[8,768]{1,0:T(8,128)(2,1)S(1)} copy-done((bf16[8,768]{1,0:T(8,128)(2,1)S(1)}, bf16[8,768]{1,0:T(8,128)(2,1)}, u32[]{:S(2)}) %copy-start.2) | copy-done | bytes 12312
  3.7 1.1 %collective-permute-done.b_ref = bf16[8,768]{1,0:T(8,128)(2,1)S(1)} collective-permute-done((bf16[8,768]{1,0:T(8,128)(2,1)}, bf16[8,768]{1,0:T(8,128)(2,1)S(1)}, u32[]{:S(2)}, u32[]{:S(2)}) %collective-permute-start) | collective-permute-done | bytes 12320 | tf_op jit(solution)/shard_map/ppermute | solution.py:187
  4.8 0.0 copy-start
  4.8 0.0 copy-start.1
  4.8 0.1 collective-permute-start.1
  4.9 1.2 %collective-permute-done.1.b_ref = bf16[16,768]{1,0:T(8,128)(2,1)S(1)} collective-permute-done((bf16[16,768]{1,0:T(8,128)(2,1)S(1)}, bf16[16,768]{1,0:T(8,128)(2,1)S(1)}, u32[]{:S(2)}, u32[]{:S(2)}) %collective-permute-start.1) | collective-permute-done | bytes 24608 | tf_op jit(solution)/shard_map/ppermute | solution.py:187
  6.1 4.1 %collective-permute-start.3 = (bf16[32,768]{1,0:T(8,128)(2,1)S(1)}, bf16[32,768]{1,0:T(8,128)(2,1)S(1)}, u32[]{:S(2)}, u32[]{:S(2)}) collective-permute-start(bf16[32,768]{1,0:T(8,128)(2,1)S(1)} %shard_map.39.own_ref), channel_id=1, source_target_pairs={{0,3},{1,2},{2,1},{3,0},{4,6},{5,7},{6,4},{7,5},{8,11},{9,10},{10,... | collective-permute-start | bytes 147464 | tf_op jit(solution)/shard_map/ppermute | solution.py:190
  10.2 0.0 collective-permute-start.2
  10.2 2.5 %collective-permute-done.3.far_ref = bf16[32,768]{1,0:T(8,128)(2,1)S(1)} collective-permute-done((bf16[32,768]{1,0:T(8,128)(2,1)S(1)}, bf16[32,768]{1,0:T(8,128)(2,1)S(1)}, u32[]{:S(2)}, u32[]{:S(2)}) %collective-permute-start.3) | collective-permute-done | bytes 49184 | tf_op jit(solution)/shard_map/ppermute | solution.py:190
  12.7 0.0 collective-permute-start.4
  12.7 1.6 %collective-permute-done.2.near_ref = bf16[32,768]{1,0:T(8,128)(2,1)S(1)} collective-permute-done((bf16[32,768]{1,0:T(8,128)(2,1)S(1)}, bf16[32,768]{1,0:T(8,128)(2,1)S(1)}, u32[]{:S(2)}, u32[]{:S(2)}) %collective-permute-start.2) | collective-permute-done | bytes 49184 | tf_op jit(solution)/shard_map/ppermute | solution.py:187
  14.3 0.0 collective-permute-done.4.across_ref
  14.3 0.0 copy-done
  14.3 0.0 copy-done.1
  14.3 2.6 %shard_map.40 = (f32[64,1024]{1,0:T(8,128)S(1)}, f32[64,1024]{1,0:T(8,128)S(1)}) custom-call(bf16[32,768]{1,0:T(8,128)(2,1)S(1)} %shard_map.39.own_ref, bf16[32,768]{1,0:T(8,128)(2,1)S(1)} %collective-permute-done.2.near_ref, bf16[32,768]{1,0:T(8,128)(2,1)S(1)} %collective-permute-done.3.far_ref, bf16[32,768]{1,0:T(8,128)(2,1)S(1)} %collective-permute-done.4.across_ref, ...), custom_call_target="tpu_custom_call" | custom-call | flops 926941184 | bytes 7241728 | tf_op jit(solution)/shard_map/pallas_call | solution.py:26
  17.0 0.1 collective-permute-start.5
  17.0 1.5 %collective-permute-done.5.other_ref = f32[64,1024]{1,0:T(8,128)S(1)} collective-permute-done((f32[64,1024]{1,0:T(8,128)S(1)}, f32[64,1024]{1,0:T(8,128)S(1)}, u32[]{:S(2)}, u32[]{:S(2)}) %collective-permute-start.5) | collective-permute-done | bytes 262176 | tf_op jit(solution)/shard_map/ppermute | solution.py:187
  18.6 0.2 shard_map.41
  18.8 1.6 %collective-permute-start.6 = (f32[32,1024]{1,0:T(8,128)S(1)}, f32[32,1024]{1,0:T(8,128)S(1)}, u32[]{:S(2)}, u32[]{:S(2)}) collective-permute-start(f32[32,1024]{1,0:T(8,128)S(1)} %get-tuple-element.15), channel_id=1, source_target_pairs={{0,8},{1,9},{2,10},{3,11},{4,12},{5,13},{6,14},{7,15},{8,0},{9,1},... | collective-permute-start | bytes 393224 | tf_op jit(solution)/shard_map/ppermute | solution.py:187
  20.3 4.0 %collective-permute-done.6.other_ref = f32[32,1024]{1,0:T(8,128)S(1)} collective-permute-done((f32[32,1024]{1,0:T(8,128)S(1)}, f32[32,1024]{1,0:T(8,128)S(1)}, u32[]{:S(2)}, u32[]{:S(2)}) %collective-permute-start.6) | collective-permute-done | bytes 131104 | tf_op jit(solution)/shard_map/ppermute | solution.py:187
  24.4 0.2 shard_map.42
  24.6 3.1 %collective-permute-start.8 = (f32[16,1024]{1,0:T(8,128)S(1)}, f32[16,1024]{1,0:T(8,128)S(1)}, u32[]{:S(2)}, u32[]{:S(2)}) collective-permute-start(f32[16,1024]{1,0:T(8,128)S(1)} %get-tuple-element.18), channel_id=1, source_target_pairs={{0,3},{1,2},{2,1},{3,0},{4,6},{5,7},{6,4},{7,5},{8,11},{9,10},{10,... | collective-permute-start | bytes 196616 | tf_op jit(solution)/shard_map/ppermute | solution.py:190
  27.7 0.0 collective-permute-start.7
  27.7 3.0 %collective-permute-done.8.a_ref.far_ref = f32[16,1024]{1,0:T(8,128)S(1)} collective-permute-done((f32[16,1024]{1,0:T(8,128)S(1)}, f32[16,1024]{1,0:T(8,128)S(1)}, u32[]{:S(2)}, u32[]{:S(2)}) %collective-permute-start.8) | collective-permute-done | bytes 65568 | tf_op jit(solution)/shard_map/ppermute | solution.py:190
  30.7 0.0 collective-permute-start.9
  30.7 0.9 %collective-permute-done.7.near_ref = f32[8,1024]{1,0:T(8,128)S(1)} collective-permute-done((f32[8,1024]{1,0:T(8,128)S(1)}, f32[8,1024]{1,0:T(8,128)S(1)}, u32[]{:S(2)}, u32[]{:S(2)}) %collective-permute-start.7) | collective-permute-done | bytes 32800 | tf_op jit(solution)/shard_map/ppermute | solution.py:187
  31.6 0.3 collective-permute-done.9.across_ref
  31.9 0.8 %shard_map.44 = f32[8,1000]{1,0:T(8,128)} custom-call(f32[8,1024]{1,0:T(8,128)S(1)} %get-tuple-element.16.own_ref, f32[8,1024]{1,0:T(8,128)S(1)} %collective-permute-done.7.near_ref, f32[16,1024]{1,0:T(8,128)S(1)} %collective-permute-done.8.a_ref.far_ref, f32[8,1024]{1,0:T(8,128)S(1)} %collective-permute-done.9.across_ref), custom_call_target="tpu_custom_call" | custom-call | tf_op jit(solution)/shard_map/pallas_call | solution.py:26
  (4 shorter events, 0.0 us)
Async XLA Ops:
  0.0 4.8 %collective-permute-start = (bf16[8,768]{1,0:T(8,128)(2,1)}, bf16[8,768]{1,0:T(8,128)(2,1)S(1)}, u32[]{:S(2)}, u32[]{:S(2)}) collective-permute-start(bf16[8,768]{1,0:T(8,128)(2,1)} %a_ref.1), channel_id=1, source_target_pairs={{0,8},{1,9},{2,10},{3,11},{4,12},{5,13},{6,14},{7,15},{8,0},{9,1},... | collective-permute-start | bytes 36872 | tf_op jit(solution)/shard_map/ppermute | solution.py:187
  2.9 0.7 %copy-start.2 = (bf16[8,768]{1,0:T(8,128)(2,1)S(1)}, bf16[8,768]{1,0:T(8,128)(2,1)}, u32[]{:S(2)}) copy-start(bf16[8,768]{1,0:T(8,128)(2,1)} %a_ref.1) | copy-start | bytes 36868
  4.8 9.5 %copy-start = (bf16[2048,1000]{0,1:T(8,128)(2,1)S(1)}, bf16[2048,1000]{0,1:T(8,128)(2,1)}, u32[]{:S(2)}) copy-start(bf16[2048,1000]{0,1:T(8,128)(2,1)} %param.5) | copy-start | bytes 12288004
  4.8 9.5 %copy-start.1 = (bf16[2048,768]{1,0:T(8,128)(2,1)S(1)}, bf16[2048,768]{1,0:T(8,128)(2,1)}, u32[]{:S(2)}) copy-start(bf16[2048,768]{1,0:T(8,128)(2,1)} %k_ref.1) | copy-start | bytes 9437188
  4.8 1.3 %collective-permute-start.1 = (bf16[16,768]{1,0:T(8,128)(2,1)S(1)}, bf16[16,768]{1,0:T(8,128)(2,1)S(1)}, u32[]{:S(2)}, u32[]{:S(2)}) collective-permute-start(bf16[16,768]{1,0:T(8,128)(2,1)S(1)} %shard_map.38.a_ref), channel_id=1, source_target_pairs={{0,4},{1,5},{2,6},{3,7},{4,0},{5,1},{6,2},{7,3},{8,12},{9,13},{10,... | collective-permute-start | bytes 73736 | tf_op jit(solution)/shard_map/ppermute | solution.py:187
  6.1 6.7 %collective-permute-start.3 = (bf16[32,768]{1,0:T(8,128)(2,1)S(1)}, bf16[32,768]{1,0:T(8,128)(2,1)S(1)}, u32[]{:S(2)}, u32[]{:S(2)}) collective-permute-start(bf16[32,768]{1,0:T(8,128)(2,1)S(1)} %shard_map.39.own_ref), channel_id=1, source_target_pairs={{0,3},{1,2},{2,1},{3,0},{4,6},{5,7},{6,4},{7,5},{8,11},{9,10},{10,... | collective-permute-start | bytes 147464 | tf_op jit(solution)/shard_map/ppermute | solution.py:190
  10.2 4.1 %collective-permute-start.2 = (bf16[32,768]{1,0:T(8,128)(2,1)S(1)}, bf16[32,768]{1,0:T(8,128)(2,1)S(1)}, u32[]{:S(2)}, u32[]{:S(2)}) collective-permute-start(bf16[32,768]{1,0:T(8,128)(2,1)S(1)} %shard_map.39.own_ref), channel_id=1, source_target_pairs={{0,1},{1,0},{2,3},{3,2},{4,5},{5,4},{6,7},{7,6},{8,9},{9,8},{10,11... | collective-permute-start | bytes 147464 | tf_op jit(solution)/shard_map/ppermute | solution.py:187
  12.7 1.6 %collective-permute-start.4 = (bf16[32,768]{1,0:T(8,128)(2,1)S(1)}, bf16[32,768]{1,0:T(8,128)(2,1)S(1)}, u32[]{:S(2)}, u32[]{:S(2)}) collective-permute-start(bf16[32,768]{1,0:T(8,128)(2,1)S(1)} %collective-permute-done.3.far_ref), channel_id=1, source_target_pairs={{0,4},{1,5},{2,6},{3,7},{4,0},{5,1},{6,2},{7,3},{8,12},{9,13},{10,... | collective-permute-start | bytes 147464 | tf_op jit(solution)/shard_map/ppermute | solution.py:187
  17.0 1.6 %collective-permute-start.5 = (f32[64,1024]{1,0:T(8,128)S(1)}, f32[64,1024]{1,0:T(8,128)S(1)}, u32[]{:S(2)}, u32[]{:S(2)}) collective-permute-start(f32[64,1024]{1,0:T(8,128)S(1)} %get-tuple-element.13), channel_id=1, source_target_pairs={{0,4},{1,5},{2,6},{3,7},{4,0},{5,1},{6,2},{7,3},{8,12},{9,13},{10,... | collective-permute-start | bytes 786440 | tf_op jit(solution)/shard_map/ppermute | solution.py:187
  18.8 5.6 %collective-permute-start.6 = (f32[32,1024]{1,0:T(8,128)S(1)}, f32[32,1024]{1,0:T(8,128)S(1)}, u32[]{:S(2)}, u32[]{:S(2)}) collective-permute-start(f32[32,1024]{1,0:T(8,128)S(1)} %get-tuple-element.15), channel_id=1, source_target_pairs={{0,8},{1,9},{2,10},{3,11},{4,12},{5,13},{6,14},{7,15},{8,0},{9,1},... | collective-permute-start | bytes 393224 | tf_op jit(solution)/shard_map/ppermute | solution.py:187
  24.6 6.1 %collective-permute-start.8 = (f32[16,1024]{1,0:T(8,128)S(1)}, f32[16,1024]{1,0:T(8,128)S(1)}, u32[]{:S(2)}, u32[]{:S(2)}) collective-permute-start(f32[16,1024]{1,0:T(8,128)S(1)} %get-tuple-element.18), channel_id=1, source_target_pairs={{0,3},{1,2},{2,1},{3,0},{4,6},{5,7},{6,4},{7,5},{8,11},{9,10},{10,... | collective-permute-start | bytes 196616 | tf_op jit(solution)/shard_map/ppermute | solution.py:190
  27.7 3.9 %collective-permute-start.7 = (f32[8,1024]{1,0:T(8,128)S(1)}, f32[8,1024]{1,0:T(8,128)S(1)}, u32[]{:S(2)}, u32[]{:S(2)}) collective-permute-start(f32[8,1024]{1,0:T(8,128)S(1)} %get-tuple-element.17), channel_id=1, source_target_pairs={{0,1},{1,0},{2,3},{3,2},{4,5},{5,4},{6,7},{7,6},{8,9},{9,8},{10,11... | collective-permute-start | bytes 98312 | tf_op jit(solution)/shard_map/ppermute | solution.py:187
  30.7 1.2 %collective-permute-start.9 = (f32[8,1024]{1,0:T(8,128)S(1)}, f32[8,1024]{1,0:T(8,128)S(1)}, u32[]{:S(2)}, u32[]{:S(2)}) collective-permute-start(f32[8,1024]{1,0:T(8,128)S(1)} %shard_map.43), channel_id=1, source_target_pairs={{0,4},{1,5},{2,6},{3,7},{4,0},{5,1},{6,2},{7,3},{8,12},{9,13},{10,... | collective-permute-start | bytes 98312 | tf_op jit(solution)/shard_map/ppermute | solution.py:187

commit v5 on v4

--- a/solution.py
+++ b/solution.py
@@ -11,6 +11,7 @@
 SCORE_GAIN = 3.0
 AXES = ("bank", "query")
 LANES = 128
+POWER, CENTRE = 24.0, 5.0
 MIB = 1 << 20
 VMEM = pl.BlockSpec(memory_space=pltpu.VMEM)
 BESIDE = pl.CostEstimate(flops=4_000_000_000, bytes_accessed=1 << 17, transcendentals=0)
@@ -52,16 +53,47 @@
     return call(join_kernel, out, a, b, cost=BESIDE)
 
 
-def record_shape(rows, classes):
-    return jax.ShapeDtypeStruct((rows, -(-(classes + 2) // LANES) * LANES), jnp.float32)
+def record_shape(rows, classes, dtype=jnp.float32):
+    return jax.ShapeDtypeStruct((rows, -(-(classes + 6) // LANES) * LANES), dtype)
+
+
+def columns(block, start, count):
+    return [block[:, c : c + 1] for c in range(start, start + count)]
 
 
 def parts_of(record, classes):
-    return (
-        record[:, classes : classes + 1],
-        record[:, classes + 1 : classes + 2],
-        record[:, :classes],
-    )
+    peak, total = columns(record, classes, 2)
+    return peak, total, record[:, :classes]
+
+
+def write(ref, votes, extra):
+    rows, classes = votes.shape
+    spare = ref.shape[1] - classes
+    column = lax.broadcasted_iota(jnp.int32, (rows, spare), 1)
+    after = jnp.zeros((rows, spare), jnp.float32)
+    for c, values in enumerate(extra):
+        after = jnp.where(column == c, values, after)
+    ref[...] = jnp.concatenate([votes, after], axis=1).astype(ref.dtype)
+
+
+def pieces(x):
+    high = x.astype(jnp.bfloat16).astype(jnp.float32)
+    middle = (x - high).astype(jnp.bfloat16).astype(jnp.float32)
+    return [high, middle, x - high - middle]
+
+
+def encode(ref, parts):
+    peak, total, votes = parts
+    code = jnp.exp2(POWER * jnp.log2(votes) + POWER * (CENTRE - jnp.log2(total)))
+    write(ref, code, pieces(peak) + pieces(total))
+
+
+def decode(block, classes):
+    record = block.astype(jnp.float32)
+    p = columns(record, classes, 6)
+    peak, total = p[0] + p[1] + p[2], p[3] + p[4] + p[5]
+    log = jnp.log2(record[:, :classes]) * (1 / POWER)
+    return peak, total, jnp.exp2(log + (jnp.log2(total) - CENTRE))
 
 
 def combine(*parts):
@@ -72,14 +104,8 @@
     return top, total, votes
 
 
-def put(ref, row, parts):
-    peak, total, votes = parts
-    rows, classes = votes.shape
-    at = slice(row, row + rows)
-    ref[at, :classes] = votes
-    spare = ref.shape[1] - classes
-    column = lax.broadcasted_iota(jnp.int32, (rows, spare), 1)
-    ref[at, classes:] = jnp.where(column == 0, peak, jnp.where(column == 1, total, 0.0))
+def rows_of(parts, *ranges):
+    return tuple(jnp.concatenate([x[lo:hi] for lo, hi in ranges], axis=0) for x in parts)
 
 
 def stats_kernel(own_ref, near_ref, far_ref, across_ref, k_ref, lt_ref, keep_ref, send_ref):
@@ -101,22 +127,17 @@
         preferred_element_type=jnp.float32,
     )
 
-    def move(ref, row, start, rows):
-        at = slice(start, start + rows)
-        put(ref, row, (peaks[at], totals[at], votes[at]))
-
-    move(keep_ref, 0, 0, half)
-    move(send_ref, 0, half, half)
-    move(keep_ref, half, count, half)
-    move(send_ref, half, count + half, half)
-    move(keep_ref, count, 2 * count, count)
-    move(send_ref, count, 3 * count, count)
+    parts = (peaks, totals, votes)
+    keep = rows_of(parts, (0, half), (count, count + half), (2 * count, 3 * count))
+    send = rows_of(parts, (half, count), (count + half, 2 * count), (3 * count, 4 * count))
+    write(keep_ref, keep[2], keep[:2])
+    encode(send_ref, send)
 
 
 def stats(blocks, keys, labels_t):
     rows, width = 4 * blocks[0].shape[0], keys.shape[1]
     bank, classes = keys.shape[0], labels_t.shape[0]
-    out = record_shape(rows // 2, classes)
+    outs = (record_shape(rows // 2, classes), record_shape(rows // 2, classes, jnp.bfloat16))
     scores = jax.ShapeDtypeStruct((rows, bank), jnp.float32)
     cost = pl.CostEstimate(
         flops=2 * rows * bank * (width + classes),
@@ -124,45 +145,47 @@
         transcendentals=rows * bank,
     )
     return call(
-        stats_kernel, (out, out), *blocks, keys, labels_t, scratch=(scores,), cost=cost
+        stats_kernel, outs, *blocks, keys, labels_t, scratch=(scores,), cost=cost
     )
 
 
 def merge_kernel(classes, mine_ref, other_ref, keep_ref, send_ref):
     half = keep_ref.shape[0] // 4
-    for quarter in range(4):
-        for ref, lo in ((keep_ref, 0), (send_ref, half)):
-            at = slice(2 * quarter * half + lo, 2 * quarter * half + lo + half)
-            both = [parts_of(r[at], classes) for r in (mine_ref, other_ref)]
-            put(ref, quarter * half, combine(*both))
+    starts = range(0, 8 * half, 2 * half)
+    parts = combine(parts_of(mine_ref[...], classes), decode(other_ref[...], classes))
+    keep = rows_of(parts, *[(lo, lo + half) for lo in starts])
+    send = rows_of(parts, *[(lo + half, lo + 2 * half) for lo in starts])
+    write(keep_ref, keep[2], keep[:2])
+    encode(send_ref, send)
 
 
 def merge(mine, other, classes):
-    out = record_shape(mine.shape[0] // 2, classes)
-    return call(functools.partial(merge_kernel, classes), (out, out), mine, other)
+    rows = mine.shape[0] // 2
+    outs = (record_shape(rows, classes), record_shape(rows, classes, jnp.bfloat16))
+    return call(functools.partial(merge_kernel, classes), outs, mine, other)
 
 
 def split_kernel(classes, mine_ref, other_ref, own_ref, near_ref, far_ref):
     rows = own_ref.shape[0]
-    both = [parts_of(r[...], classes) for r in (mine_ref, other_ref)]
-    peak, total, votes = combine(*both)
-    for ref, lo, count in ((own_ref, 0, rows), (near_ref, rows, rows), (far_ref, 2 * rows, 2 * rows)):
-        at = slice(lo, lo + count)
-        put(ref, 0, (peak[at], total[at], votes[at]))
+    parts = combine(parts_of(mine_ref[...], classes), decode(other_ref[...], classes))
+    own = rows_of(parts, (0, rows))
+    write(own_ref, own[2], own[:2])
+    encode(near_ref, rows_of(parts, (rows, 2 * rows)))
+    encode(far_ref, rows_of(parts, (2 * rows, 4 * rows)))
 
 
 def split(mine, other, classes):
     rows = mine.shape[0] // 4
     outs = (
         record_shape(rows, classes),
-        record_shape(rows, classes),
-        record_shape(2 * rows, classes),
+        record_shape(rows, classes, jnp.bfloat16),
+        record_shape(2 * rows, classes, jnp.bfloat16),
     )
     return call(functools.partial(split_kernel, classes), outs, mine, other)
 
 
 def tail_kernel(a_ref, out_ref):
-    out_ref[...] = a_ref[out_ref.shape[0] :]
+    out_ref[...] = a_ref[...].astype(jnp.float32)[out_ref.shape[0] :].astype(out_ref.dtype)
 
 
 def tail(a):
@@ -172,8 +195,9 @@
 
 def finish_kernel(classes, own_ref, near_ref, far_ref, across_ref, out_ref):
     rows = out_ref.shape[0]
-    refs = (own_ref, near_ref, far_ref, across_ref)
-    _, total, votes = combine(*[parts_of(r[:rows], classes) for r in refs])
+    came = [decode(r[...], classes) for r in (near_ref, far_ref, across_ref)]
+    came[1] = rows_of(came[1], (0, rows))
+    _, total, votes = combine(parts_of(own_ref[...], classes), *came)
     out_ref[...] = jnp.log(votes / total)
 
 

time: 32.9 us -> 31.3 us (0.951)
  waiting for transfers between devices: 16.2 us -> 14.4 us
    ppermute x8, waiting for transfers between devices: 10.6 us -> 9.16 us  [swap(): return lax.ppermute(block, AXES, [(i, i ^ bit) for i in range(size)])]
where the time goes in v5:
time: 31.3 us; the launch traced here: 31.1 us
  waiting for transfers between devices  14.4 us (46%)
  starting transfers between devices  11.9 us (38%)
  Pallas kernels  4.06 us (13%)
  local copies, waits for them, and re-layouts  0.75 us (2%)
    ppermute x8, waiting for transfers between devices, swap(): return lax.ppermute(block, AXES, [(i, i ^ bit) for i in range(size)])  9.16 us
    ppermute x2, starting transfers between devices, swap_far(): lax.ppermute(block, AXES, [(i, i ^ (2 if i & core else 3)) for i in range...  7.22 us
    ppermute x2, waiting for transfers between devices, swap_far(): lax.ppermute(block, AXES, [(i, i ^ (2 if i & core else 3)) for i in range...  5.19 us
    ppermute x8, starting transfers between devices, swap(): return lax.ppermute(block, AXES, [(i, i ^ bit) for i in range(size)])  4.66 us
    pallas_call x8, Pallas kernels, call(): pl.pallas_call(kernel, out_shape=outs, in_specs=[VMEM] * len(args), out_s...  4.06 us
    unnamed x6, local copies, waits for them, and re-layouts  0.75 us
  transfers between devices with their start and end apart: 10, of which 9 were waited for; matrix products, arithmetic and copies ran while one was open for 0% of the time, Pallas kernels for 0%

profile of v5, /device:TPU:0, one launch (start us, length us, event | category | flops | bytes accessed | tf_op | source)
XLA Modules:
  0.0 31.1 jit_solution(5837153632399929454)
XLA Ops:
  0.0 2.9 %collective-permute-start = (bf16[8,768]{1,0:T(8,128)(2,1)}, bf16[8,768]{1,0:T(8,128)(2,1)S(1)}, u32[]{:S(2)}, u32[]{:S(2)}) collective-permute-start(bf16[8,768]{1,0:T(8,128)(2,1)} %a_ref.1), channel_id=1, source_target_pairs={{0,8},{1,9},{2,10},{3,11},{4,12},{5,13},{6,14},{7,15},{8,0},{9,1},... | collective-permute-start | bytes 36872 | tf_op jit(solution)/shard_map/ppermute | solution.py:211
  2.9 0.0 copy-start.2
  2.9 0.7 %copy-done.2 = bf16[8,768]{1,0:T(8,128)(2,1)S(1)} copy-done((bf16[8,768]{1,0:T(8,128)(2,1)S(1)}, bf16[8,768]{1,0:T(8,128)(2,1)}, u32[]{:S(2)}) %copy-start.2) | copy-done | bytes 12312
  3.7 1.1 %collective-permute-done.b_ref = bf16[8,768]{1,0:T(8,128)(2,1)S(1)} collective-permute-done((bf16[8,768]{1,0:T(8,128)(2,1)}, bf16[8,768]{1,0:T(8,128)(2,1)S(1)}, u32[]{:S(2)}, u32[]{:S(2)}) %collective-permute-start) | collective-permute-done | bytes 12320 | tf_op jit(solution)/shard_map/ppermute | solution.py:211
  4.8 0.0 copy-start
  4.8 0.0 copy-start.1
  4.8 0.1 collective-permute-start.1
  4.9 1.2 %collective-permute-done.1.b_ref = bf16[16,768]{1,0:T(8,128)(2,1)S(1)} collective-permute-done((bf16[16,768]{1,0:T(8,128)(2,1)S(1)}, bf16[16,768]{1,0:T(8,128)(2,1)S(1)}, u32[]{:S(2)}, u32[]{:S(2)}) %collective-permute-start.1) | collective-permute-done | bytes 24608 | tf_op jit(solution)/shard_map/ppermute | solution.py:211
  6.1 4.1 %collective-permute-start.3 = (bf16[32,768]{1,0:T(8,128)(2,1)S(1)}, bf16[32,768]{1,0:T(8,128)(2,1)S(1)}, u32[]{:S(2)}, u32[]{:S(2)}) collective-permute-start(bf16[32,768]{1,0:T(8,128)(2,1)S(1)} %shard_map.39.own_ref), channel_id=1, source_target_pairs={{0,3},{1,2},{2,1},{3,0},{4,6},{5,7},{6,4},{7,5},{8,11},{9,10},{10,... | collective-permute-start | bytes 147464 | tf_op jit(solution)/shard_map/ppermute | solution.py:214
  10.2 0.0 collective-permute-start.2
  10.2 2.5 %collective-permute-done.3.far_ref = bf16[32,768]{1,0:T(8,128)(2,1)S(1)} collective-permute-done((bf16[32,768]{1,0:T(8,128)(2,1)S(1)}, bf16[32,768]{1,0:T(8,128)(2,1)S(1)}, u32[]{:S(2)}, u32[]{:S(2)}) %collective-permute-start.3) | collective-permute-done | bytes 49184 | tf_op jit(solution)/shard_map/ppermute | solution.py:214
  12.7 0.0 collective-permute-start.4
  12.7 1.6 %collective-permute-done.2.near_ref = bf16[32,768]{1,0:T(8,128)(2,1)S(1)} collective-permute-done((bf16[32,768]{1,0:T(8,128)(2,1)S(1)}, bf16[32,768]{1,0:T(8,128)(2,1)S(1)}, u32[]{:S(2)}, u32[]{:S(2)}) %collective-permute-start.2) | collective-permute-done | bytes 49184 | tf_op jit(solution)/shard_map/ppermute | solution.py:211
  14.3 0.0 collective-permute-done.4.across_ref
  14.3 0.0 copy-done
  14.3 0.0 copy-done.1
  14.3 2.6 %shard_map.40 = (f32[64,1024]{1,0:T(8,128)S(1)}, bf16[64,1024]{1,0:T(8,128)(2,1)S(1)}) custom-call(bf16[32,768]{1,0:T(8,128)(2,1)S(1)} %shard_map.39.own_ref, bf16[32,768]{1,0:T(8,128)(2,1)S(1)} %collective-permute-done.2.near_ref, bf16[32,768]{1,0:T(8,128)(2,1)S(1)} %collective-permute-done.3.far_ref, ...), custom_call_target="tpu_custom_call" | custom-call | flops 926941184 | bytes 7241728 | tf_op jit(solution)/shard_map/pallas_call | solution.py:27
  17.0 0.1 collective-permute-start.5
  17.0 1.3 %collective-permute-done.5.other_ref = bf16[64,1024]{1,0:T(8,128)(2,1)S(1)} collective-permute-done((bf16[64,1024]{1,0:T(8,128)(2,1)S(1)}, bf16[64,1024]{1,0:T(8,128)(2,1)S(1)}, u32[]{:S(2)}, u32[]{:S(2)}) %collective-permute-start.5) | collective-permute-done | bytes 131104 | tf_op jit(solution)/shard_map/ppermute | solution.py:211
  18.4 0.3 shard_map.41
  18.7 1.6 %collective-permute-start.6 = (bf16[32,1024]{1,0:T(8,128)(2,1)S(1)}, bf16[32,1024]{1,0:T(8,128)(2,1)S(1)}, u32[]{:S(2)}, u32[]{:S(2)}) collective-permute-start(bf16[32,1024]{1,0:T(8,128)(2,1)S(1)} %get-tuple-element.15), channel_id=1, source_target_pairs={{0,8},{1,9},{2,10},{3,11},{4,12},{5,13},{6,14},{7,15},{8,0},{9,1},... | collective-permute-start | bytes 196616 | tf_op jit(solution)/shard_map/ppermute | solution.py:211
  20.2 2.8 %collective-permute-done.6.other_ref = bf16[32,1024]{1,0:T(8,128)(2,1)S(1)} collective-permute-done((bf16[32,1024]{1,0:T(8,128)(2,1)S(1)}, bf16[32,1024]{1,0:T(8,128)(2,1)S(1)}, u32[]{:S(2)}, u32[]{:S(2)}) %collective-permute-start.6) | collective-permute-done | bytes 65568 | tf_op jit(solution)/shard_map/ppermute | solution.py:211
  23.0 0.3 shard_map.42
  23.3 3.1 %collective-permute-start.8 = (bf16[16,1024]{1,0:T(8,128)(2,1)S(1)}, bf16[16,1024]{1,0:T(8,128)(2,1)S(1)}, u32[]{:S(2)}, u32[]{:S(2)}) collective-permute-start(bf16[16,1024]{1,0:T(8,128)(2,1)S(1)} %get-tuple-element.18), channel_id=1, source_target_pairs={{0,3},{1,2},{2,1},{3,0},{4,6},{5,7},{6,4},{7,5},{8,11},{9,10},{10,... | collective-permute-start | bytes 98312 | tf_op jit(solution)/shard_map/ppermute | solution.py:214
  26.4 0.0 collective-permute-start.7
  26.4 2.7 %collective-permute-done.8.a_ref.far_ref = bf16[16,1024]{1,0:T(8,128)(2,1)S(1)} collective-permute-done((bf16[16,1024]{1,0:T(8,128)(2,1)S(1)}, bf16[16,1024]{1,0:T(8,128)(2,1)S(1)}, u32[]{:S(2)}, u32[]{:S(2)}) %collective-permute-start.8) | collective-permute-done | bytes 32800 | tf_op jit(solution)/shard_map/ppermute | solution.py:214
  29.1 0.0 collective-permute-start.9
  29.1 1.1 %collective-permute-done.7.near_ref = bf16[8,1024]{1,0:T(8,128)(2,1)S(1)} collective-permute-done((bf16[8,1024]{1,0:T(8,128)(2,1)S(1)}, bf16[8,1024]{1,0:T(8,128)(2,1)S(1)}, u32[]{:S(2)}, u32[]{:S(2)}) %collective-permute-start.7) | collective-permute-done | bytes 16416 | tf_op jit(solution)/shard_map/ppermute | solution.py:211
  30.1 0.1 collective-permute-done.9.across_ref
  30.2 0.8 %shard_map.44 = f32[8,1000]{1,0:T(8,128)} custom-call(f32[8,1024]{1,0:T(8,128)S(1)} %get-tuple-element.16.own_ref, bf16[8,1024]{1,0:T(8,128)(2,1)S(1)} %collective-permute-done.7.near_ref, bf16[16,1024]{1,0:T(8,128)(2,1)S(1)} %collective-permute-done.8.a_ref.far_ref, bf16[8,1024]{1,0:T(8,128)(2,1)S(1)} %collective-permute-done.9.across_ref), custom_call_target="tpu_custom_call" | custom-call | tf_op jit(solution)/shard_map/pallas_call | solution.py:27
  (4 shorter events, 0.0 us)
Async XLA Ops:
  0.0 4.8 %collective-permute-start = (bf16[8,768]{1,0:T(8,128)(2,1)}, bf16[8,768]{1,0:T(8,128)(2,1)S(1)}, u32[]{:S(2)}, u32[]{:S(2)}) collective-permute-start(bf16[8,768]{1,0:T(8,128)(2,1)} %a_ref.1), channel_id=1, source_target_pairs={{0,8},{1,9},{2,10},{3,11},{4,12},{5,13},{6,14},{7,15},{8,0},{9,1},... | collective-permute-start | bytes 36872 | tf_op jit(solution)/shard_map/ppermute | solution.py:211
  2.9 0.7 %copy-start.2 = (bf16[8,768]{1,0:T(8,128)(2,1)S(1)}, bf16[8,768]{1,0:T(8,128)(2,1)}, u32[]{:S(2)}) copy-start(bf16[8,768]{1,0:T(8,128)(2,1)} %a_ref.1) | copy-start | bytes 36868
  4.8 9.5 %copy-start = (bf16[2048,1000]{0,1:T(8,128)(2,1)S(1)}, bf16[2048,1000]{0,1:T(8,128)(2,1)}, u32[]{:S(2)}) copy-start(bf16[2048,1000]{0,1:T(8,128)(2,1)} %param.5) | copy-start | bytes 12288004
  4.8 9.5 %copy-start.1 = (bf16[2048,768]{1,0:T(8,128)(2,1)S(1)}, bf16[2048,768]{1,0:T(8,128)(2,1)}, u32[]{:S(2)}) copy-start(bf16[2048,768]{1,0:T(8,128)(2,1)} %k_ref.1) | copy-start | bytes 9437188
  4.8 1.3 %collective-permute-start.1 = (bf16[16,768]{1,0:T(8,128)(2,1)S(1)}, bf16[16,768]{1,0:T(8,128)(2,1)S(1)}, u32[]{:S(2)}, u32[]{:S(2)}) collective-permute-start(bf16[16,768]{1,0:T(8,128)(2,1)S(1)} %shard_map.38.a_ref), channel_id=1, source_target_pairs={{0,4},{1,5},{2,6},{3,7},{4,0},{5,1},{6,2},{7,3},{8,12},{9,13},{10,... | collective-permute-start | bytes 73736 | tf_op jit(solution)/shard_map/ppermute | solution.py:211
  6.1 6.7 %collective-permute-start.3 = (bf16[32,768]{1,0:T(8,128)(2,1)S(1)}, bf16[32,768]{1,0:T(8,128)(2,1)S(1)}, u32[]{:S(2)}, u32[]{:S(2)}) collective-permute-start(bf16[32,768]{1,0:T(8,128)(2,1)S(1)} %shard_map.39.own_ref), channel_id=1, source_target_pairs={{0,3},{1,2},{2,1},{3,0},{4,6},{5,7},{6,4},{7,5},{8,11},{9,10},{10,... | collective-permute-start | bytes 147464 | tf_op jit(solution)/shard_map/ppermute | solution.py:214
  10.2 4.1 %collective-permute-start.2 = (bf16[32,768]{1,0:T(8,128)(2,1)S(1)}, bf16[32,768]{1,0:T(8,128)(2,1)S(1)}, u32[]{:S(2)}, u32[]{:S(2)}) collective-permute-start(bf16[32,768]{1,0:T(8,128)(2,1)S(1)} %shard_map.39.own_ref), channel_id=1, source_target_pairs={{0,1},{1,0},{2,3},{3,2},{4,5},{5,4},{6,7},{7,6},{8,9},{9,8},{10,11... | collective-permute-start | bytes 147464 | tf_op jit(solution)/shard_map/ppermute | solution.py:211
  12.7 1.6 %collective-permute-start.4 = (bf16[32,768]{1,0:T(8,128)(2,1)S(1)}, bf16[32,768]{1,0:T(8,128)(2,1)S(1)}, u32[]{:S(2)}, u32[]{:S(2)}) collective-permute-start(bf16[32,768]{1,0:T(8,128)(2,1)S(1)} %collective-permute-done.3.far_ref), channel_id=1, source_target_pairs={{0,4},{1,5},{2,6},{3,7},{4,0},{5,1},{6,2},{7,3},{8,12},{9,13},{10,... | collective-permute-start | bytes 147464 | tf_op jit(solution)/shard_map/ppermute | solution.py:211
  17.0 1.4 %collective-permute-start.5 = (bf16[64,1024]{1,0:T(8,128)(2,1)S(1)}, bf16[64,1024]{1,0:T(8,128)(2,1)S(1)}, u32[]{:S(2)}, u32[]{:S(2)}) collective-permute-start(bf16[64,1024]{1,0:T(8,128)(2,1)S(1)} %get-tuple-element.13), channel_id=1, source_target_pairs={{0,4},{1,5},{2,6},{3,7},{4,0},{5,1},{6,2},{7,3},{8,12},{9,13},{10,... | collective-permute-start | bytes 393224 | tf_op jit(solution)/shard_map/ppermute | solution.py:211
  18.7 4.3 %collective-permute-start.6 = (bf16[32,1024]{1,0:T(8,128)(2,1)S(1)}, bf16[32,1024]{1,0:T(8,128)(2,1)S(1)}, u32[]{:S(2)}, u32[]{:S(2)}) collective-permute-start(bf16[32,1024]{1,0:T(8,128)(2,1)S(1)} %get-tuple-element.15), channel_id=1, source_target_pairs={{0,8},{1,9},{2,10},{3,11},{4,12},{5,13},{6,14},{7,15},{8,0},{9,1},... | collective-permute-start | bytes 196616 | tf_op jit(solution)/shard_map/ppermute | solution.py:211
  23.3 5.8 %collective-permute-start.8 = (bf16[16,1024]{1,0:T(8,128)(2,1)S(1)}, bf16[16,1024]{1,0:T(8,128)(2,1)S(1)}, u32[]{:S(2)}, u32[]{:S(2)}) collective-permute-start(bf16[16,1024]{1,0:T(8,128)(2,1)S(1)} %get-tuple-element.18), channel_id=1, source_target_pairs={{0,3},{1,2},{2,1},{3,0},{4,6},{5,7},{6,4},{7,5},{8,11},{9,10},{10,... | collective-permute-start | bytes 98312 | tf_op jit(solution)/shard_map/ppermute | solution.py:214
  26.4 3.7 %collective-permute-start.7 = (bf16[8,1024]{1,0:T(8,128)(2,1)S(1)}, bf16[8,1024]{1,0:T(8,128)(2,1)S(1)}, u32[]{:S(2)}, u32[]{:S(2)}) collective-permute-start(bf16[8,1024]{1,0:T(8,128)(2,1)S(1)} %get-tuple-element.17), channel_id=1, source_target_pairs={{0,1},{1,0},{2,3},{3,2},{4,5},{5,4},{6,7},{7,6},{8,9},{9,8},{10,11... | collective-permute-start | bytes 49160 | tf_op jit(solution)/shard_map/ppermute | solution.py:211
  29.1 1.2 %collective-permute-start.9 = (bf16[8,1024]{1,0:T(8,128)(2,1)S(1)}, bf16[8,1024]{1,0:T(8,128)(2,1)S(1)}, u32[]{:S(2)}, u32[]{:S(2)}) collective-permute-start(bf16[8,1024]{1,0:T(8,128)(2,1)S(1)} %shard_map.43), channel_id=1, source_target_pairs={{0,4},{1,5},{2,6},{3,7},{4,0},{5,1},{6,2},{7,3},{8,12},{9,13},{10,... | collective-permute-start | bytes 49160 | tf_op jit(solution)/shard_map/ppermute | solution.py:211

commit v6 on v5

--- a/solution.py
+++ b/solution.py
@@ -108,7 +108,7 @@
     return tuple(jnp.concatenate([x[lo:hi] for lo, hi in ranges], axis=0) for x in parts)
 
 
-def stats_kernel(own_ref, near_ref, far_ref, across_ref, k_ref, lt_ref, keep_ref, send_ref):
+def stats_kernel(unit, own_ref, near_ref, far_ref, across_ref, k_ref, lt_ref, keep_ref, send_ref):
     count, width = own_ref.shape
     half = count // 2
     queries = jnp.concatenate(
@@ -127,14 +127,21 @@
         preferred_element_type=jnp.float32,
     )
 
+    slots = half // unit
+    keep, send = [], []
+    for block in range(4):
+        odd = [n.bit_count() % 2 for n in range(slots)]
+        same = [block * count + (n + slots * o) * unit for n, o in enumerate(odd)]
+        other = [block * count + (n + slots * (1 - o)) * unit for n, o in enumerate(odd)]
+        (send if block == 3 else keep).extend(same)
+        (keep if block == 2 else send).extend(other)
     parts = (peaks, totals, votes)
-    keep = rows_of(parts, (0, half), (count, count + half), (2 * count, 3 * count))
-    send = rows_of(parts, (half, count), (count + half, 2 * count), (3 * count, 4 * count))
+    keep, send = (rows_of(parts, *[(lo, lo + unit) for lo in los]) for los in (keep, send))
     write(keep_ref, keep[2], keep[:2])
     encode(send_ref, send)
 
 
-def stats(blocks, keys, labels_t):
+def stats(blocks, keys, labels_t, unit):
     rows, width = 4 * blocks[0].shape[0], keys.shape[1]
     bank, classes = keys.shape[0], labels_t.shape[0]
     outs = (record_shape(rows // 2, classes), record_shape(rows // 2, classes, jnp.bfloat16))
@@ -145,7 +152,7 @@
         transcendentals=rows * bank,
     )
     return call(
-        stats_kernel, outs, *blocks, keys, labels_t, scratch=(scores,), cost=cost
+        functools.partial(stats_kernel, unit), outs, *blocks, keys, labels_t, scratch=(scores,), cost=cost
     )
 
 
@@ -211,24 +218,24 @@
         return lax.ppermute(block, AXES, [(i, i ^ bit) for i in range(size)])
 
     def swap_far(block):
-        return lax.ppermute(block, AXES, [(i, i ^ (2 if i & core else 3)) for i in range(size)])
+        return lax.ppermute(block, AXES, [(i, i ^ (3 if i & core else 2)) for i in range(size)])
 
     classes = bank_labels.shape[1]
-    first, *rest = [*lead, core]
+    first, *rest = [bit ^ core for bit in lead] + [core]
     own = join(fetch(queries), swap(queries, first))
     for bit in rest:
         own = join(own, swap(own, bit))
     far = swap_far(own)
-    near = swap(own, 1)
+    near = swap(own, 1 ^ core)
     across = swap(far, core)
-    keep, send = stats((own, near, far, across), bank_keys, bank_labels.T)
+    keep, send = stats((own, near, far, across), bank_keys, bank_labels.T, queries.shape[0])
     came = swap(send, core)
     for bit in lead[::-1]:
         keep, send = merge(keep, came, classes)
         came = swap(send, bit)
     own, near, far = split(keep, came, classes)
     far = swap_far(far)
-    near = swap(near, 1)
+    near = swap(near, 1 ^ core)
     across = swap(tail(far), core)
     return finish(own, near, far, across, classes)
 

time: 31.3 us -> 28.9 us (0.923)
  waiting for transfers between devices: 14.4 us -> 12.8 us
  starting transfers between devices: 11.9 us -> 11.1 us
    ppermute x2, starting transfers between devices: 7.22 us -> 5.7 us  [swap_far(): lax.ppermute(block, AXES, [(i, i ^ (3 if i & core else 2)) for i in range...]
    ppermute x8, waiting for transfers between devices: 9.16 us -> 7.8 us  [swap(): return lax.ppermute(block, AXES, [(i, i ^ bit) for i in range(size)])]
    ppermute x8, starting transfers between devices: 4.66 us -> 5.37 us  [swap(): return lax.ppermute(block, AXES, [(i, i ^ bit) for i in range(size)])]
  transfers between devices with their start and end apart: 10 -> 10, of which waited for: 9 -> 10; matrix products, arithmetic and copies ran while one was open for 0% -> 0% of each run, Pallas kernels for 0% -> 0%
where the time goes in v6:
time: 28.9 us; the launch traced here: 28.7 us
  waiting for transfers between devices  12.8 us (44%)
  starting transfers between devices  11.1 us (38%)
  Pallas kernels  4.05 us (14%)
  local copies, waits for them, and re-layouts  0.75 us (3%)
    ppermute x8, waiting for transfers between devices, swap(): return lax.ppermute(block, AXES, [(i, i ^ bit) for i in range(size)])  7.8 us
    ppermute x2, starting transfers between devices, swap_far(): lax.ppermute(block, AXES, [(i, i ^ (3 if i & core else 2)) for i in range...  5.7 us
    ppermute x8, starting transfers between devices, swap(): return lax.ppermute(block, AXES, [(i, i ^ bit) for i in range(size)])  5.37 us
    ppermute x2, waiting for transfers between devices, swap_far(): lax.ppermute(block, AXES, [(i, i ^ (3 if i & core else 2)) for i in range...  5.03 us
    pallas_call x8, Pallas kernels, call(): pl.pallas_call(kernel, out_shape=outs, in_specs=[VMEM] * len(args), out_s...  4.05 us
    unnamed x6, local copies, waits for them, and re-layouts  0.75 us
  transfers between devices with their start and end apart: 10, of which 10 were waited for; matrix products, arithmetic and copies ran while one was open for 0% of the time, Pallas kernels for 0%

profile of v6, /device:TPU:0, one launch (start us, length us, event | category | flops | bytes accessed | tf_op | source)
XLA Modules:
  0.0 28.7 jit_solution(814169351561745970)
XLA Ops:
  0.0 2.4 %collective-permute-start = (bf16[8,768]{1,0:T(8,128)(2,1)}, bf16[8,768]{1,0:T(8,128)(2,1)S(1)}, u32[]{:S(2)}, u32[]{:S(2)}) collective-permute-start(bf16[8,768]{1,0:T(8,128)(2,1)} %a_ref.1), channel_id=1, source_target_pairs={{0,12},{1,13},{2,14},{3,15},{4,8},{5,9},{6,10},{7,11},{8,4},{9,5},... | collective-permute-start | bytes 36872 | tf_op jit(solution)/shard_map/ppermute | solution.py:218
  2.4 0.0 copy-start.2
  2.4 0.7 %copy-done.2 = bf16[8,768]{1,0:T(8,128)(2,1)S(1)} copy-done((bf16[8,768]{1,0:T(8,128)(2,1)S(1)}, bf16[8,768]{1,0:T(8,128)(2,1)}, u32[]{:S(2)}) %copy-start.2) | copy-done | bytes 12312
  3.1 0.9 %collective-permute-done.b_ref = bf16[8,768]{1,0:T(8,128)(2,1)S(1)} collective-permute-done((bf16[8,768]{1,0:T(8,128)(2,1)}, bf16[8,768]{1,0:T(8,128)(2,1)S(1)}, u32[]{:S(2)}, u32[]{:S(2)}) %collective-permute-start) | collective-permute-done | bytes 12320 | tf_op jit(solution)/shard_map/ppermute | solution.py:218
  4.0 0.0 copy-start
  4.0 0.0 copy-start.1
  4.0 0.7 %collective-permute-start.1 = (bf16[16,768]{1,0:T(8,128)(2,1)S(1)}, bf16[16,768]{1,0:T(8,128)(2,1)S(1)}, u32[]{:S(2)}, u32[]{:S(2)}) collective-permute-start(bf16[16,768]{1,0:T(8,128)(2,1)S(1)} %shard_map.38.a_ref), channel_id=1, source_target_pairs={{0,4},{1,5},{2,6},{3,7},{4,0},{5,1},{6,2},{7,3},{8,12},{9,13},{10,... | collective-permute-start | bytes 73736 | tf_op jit(solution)/shard_map/ppermute | solution.py:218
  4.7 0.8 %collective-permute-done.1.b_ref = bf16[16,768]{1,0:T(8,128)(2,1)S(1)} collective-permute-done((bf16[16,768]{1,0:T(8,128)(2,1)S(1)}, bf16[16,768]{1,0:T(8,128)(2,1)S(1)}, u32[]{:S(2)}, u32[]{:S(2)}) %collective-permute-start.1) | collective-permute-done | bytes 24608 | tf_op jit(solution)/shard_map/ppermute | solution.py:218
  5.6 3.2 %collective-permute-start.3 = (bf16[32,768]{1,0:T(8,128)(2,1)S(1)}, bf16[32,768]{1,0:T(8,128)(2,1)S(1)}, u32[]{:S(2)}, u32[]{:S(2)}) collective-permute-start(bf16[32,768]{1,0:T(8,128)(2,1)S(1)} %shard_map.39.own_ref), channel_id=1, source_target_pairs={{0,2},{1,3},{2,0},{3,1},{4,7},{5,6},{6,5},{7,4},{8,10},{9,11},{10,... | collective-permute-start | bytes 147464 | tf_op jit(solution)/shard_map/ppermute | solution.py:221
  8.7 0.1 collective-permute-start.2
  8.8 2.7 %collective-permute-done.3.far_ref = bf16[32,768]{1,0:T(8,128)(2,1)S(1)} collective-permute-done((bf16[32,768]{1,0:T(8,128)(2,1)S(1)}, bf16[32,768]{1,0:T(8,128)(2,1)S(1)}, u32[]{:S(2)}, u32[]{:S(2)}) %collective-permute-start.3) | collective-permute-done | bytes 49184 | tf_op jit(solution)/shard_map/ppermute | solution.py:221
  11.5 0.0 collective-permute-start.4
  11.5 0.8 %collective-permute-done.2.near_ref = bf16[32,768]{1,0:T(8,128)(2,1)S(1)} collective-permute-done((bf16[32,768]{1,0:T(8,128)(2,1)S(1)}, bf16[32,768]{1,0:T(8,128)(2,1)S(1)}, u32[]{:S(2)}, u32[]{:S(2)}) %collective-permute-start.2) | collective-permute-done | bytes 49184 | tf_op jit(solution)/shard_map/ppermute | solution.py:218
  12.2 0.5 %collective-permute-done.4.across_ref = bf16[32,768]{1,0:T(8,128)(2,1)S(1)} collective-permute-done((bf16[32,768]{1,0:T(8,128)(2,1)S(1)}, bf16[32,768]{1,0:T(8,128)(2,1)S(1)}, u32[]{:S(2)}, u32[]{:S(2)}) %collective-permute-start.4) | collective-permute-done | bytes 49184 | tf_op jit(solution)/shard_map/ppermute | solution.py:218
  12.7 0.0 copy-done
  12.7 0.0 copy-done.1
  12.7 2.6 %shard_map.40 = (f32[64,1024]{1,0:T(8,128)S(1)}, bf16[64,1024]{1,0:T(8,128)(2,1)S(1)}) custom-call(bf16[32,768]{1,0:T(8,128)(2,1)S(1)} %shard_map.39.own_ref, bf16[32,768]{1,0:T(8,128)(2,1)S(1)} %collective-permute-done.2.near_ref, bf16[32,768]{1,0:T(8,128)(2,1)S(1)} %collective-permute-done.3.far_ref, ...), custom_call_target="tpu_custom_call" | custom-call | flops 926941184 | bytes 7241728 | tf_op jit(solution)/shard_map/pallas_call | solution.py:27
  15.3 0.5 %collective-permute-start.5 = (bf16[64,1024]{1,0:T(8,128)(2,1)S(1)}, bf16[64,1024]{1,0:T(8,128)(2,1)S(1)}, u32[]{:S(2)}, u32[]{:S(2)}) collective-permute-start(bf16[64,1024]{1,0:T(8,128)(2,1)S(1)} %get-tuple-element.13), channel_id=1, source_target_pairs={{0,4},{1,5},{2,6},{3,7},{4,0},{5,1},{6,2},{7,3},{8,12},{9,13},{10,... | collective-permute-start | bytes 393224 | tf_op jit(solution)/shard_map/ppermute | solution.py:218
  15.8 1.0 %collective-permute-done.5.other_ref = bf16[64,1024]{1,0:T(8,128)(2,1)S(1)} collective-permute-done((bf16[64,1024]{1,0:T(8,128)(2,1)S(1)}, bf16[64,1024]{1,0:T(8,128)(2,1)S(1)}, u32[]{:S(2)}, u32[]{:S(2)}) %collective-permute-start.5) | collective-permute-done | bytes 131104 | tf_op jit(solution)/shard_map/ppermute | solution.py:218
  16.8 0.3 %shard_map.41 = (f32[32,1024]{1,0:T(8,128)S(1)}, bf16[32,1024]{1,0:T(8,128)(2,1)S(1)}) custom-call(f32[64,1024]{1,0:T(8,128)S(1)} %get-tuple-element.12.mine_ref, bf16[64,1024]{1,0:T(8,128)(2,1)S(1)} %collective-permute-done.5.other_ref), custom_call_target="tpu_custom_call" | custom-call | tf_op jit(solution)/shard_map/pallas_call | solution.py:27
  17.1 1.7 %collective-permute-start.6 = (bf16[32,1024]{1,0:T(8,128)(2,1)S(1)}, bf16[32,1024]{1,0:T(8,128)(2,1)S(1)}, u32[]{:S(2)}, u32[]{:S(2)}) collective-permute-start(bf16[32,1024]{1,0:T(8,128)(2,1)S(1)} %get-tuple-element.15), channel_id=1, source_target_pairs={{0,8},{1,9},{2,10},{3,11},{4,12},{5,13},{6,14},{7,15},{8,0},{9,1},... | collective-permute-start | bytes 196616 | tf_op jit(solution)/shard_map/ppermute | solution.py:218
  18.9 2.7 %collective-permute-done.6.other_ref = bf16[32,1024]{1,0:T(8,128)(2,1)S(1)} collective-permute-done((bf16[32,1024]{1,0:T(8,128)(2,1)S(1)}, bf16[32,1024]{1,0:T(8,128)(2,1)S(1)}, u32[]{:S(2)}, u32[]{:S(2)}) %collective-permute-start.6) | collective-permute-done | bytes 65568 | tf_op jit(solution)/shard_map/ppermute | solution.py:218
  21.5 0.3 %shard_map.42 = (f32[8,1024]{1,0:T(8,128)S(1)}, bf16[8,1024]{1,0:T(8,128)(2,1)S(1)}, bf16[16,1024]{1,0:T(8,128)(2,1)S(1)}) custom-call(f32[32,1024]{1,0:T(8,128)S(1)} %get-tuple-element.14.mine_ref, bf16[32,1024]{1,0:T(8,128)(2,1)S(1)} %collective-permute-done.6.other_ref), custom_call_target="tpu_custom_call" | custom-call | tf_op jit(solution)/shard_map/pallas_call | solution.py:27
  21.8 2.5 %collective-permute-start.8 = (bf16[16,1024]{1,0:T(8,128)(2,1)S(1)}, bf16[16,1024]{1,0:T(8,128)(2,1)S(1)}, u32[]{:S(2)}, u32[]{:S(2)}) collective-permute-start(bf16[16,1024]{1,0:T(8,128)(2,1)S(1)} %get-tuple-element.18), channel_id=1, source_target_pairs={{0,2},{1,3},{2,0},{3,1},{4,7},{5,6},{6,5},{7,4},{8,10},{9,11},{10,... | collective-permute-start | bytes 98312 | tf_op jit(solution)/shard_map/ppermute | solution.py:221
  24.4 0.0 collective-permute-start.7
  24.4 2.3 %collective-permute-done.8.a_ref.far_ref = bf16[16,1024]{1,0:T(8,128)(2,1)S(1)} collective-permute-done((bf16[16,1024]{1,0:T(8,128)(2,1)S(1)}, bf16[16,1024]{1,0:T(8,128)(2,1)S(1)}, u32[]{:S(2)}, u32[]{:S(2)}) %collective-permute-start.8) | collective-permute-done | bytes 32800 | tf_op jit(solution)/shard_map/ppermute | solution.py:221
  26.7 0.0 collective-permute-start.9
  26.7 0.8 %collective-permute-done.7.near_ref = bf16[8,1024]{1,0:T(8,128)(2,1)S(1)} collective-permute-done((bf16[8,1024]{1,0:T(8,128)(2,1)S(1)}, bf16[8,1024]{1,0:T(8,128)(2,1)S(1)}, u32[]{:S(2)}, u32[]{:S(2)}) %collective-permute-start.7) | collective-permute-done | bytes 16416 | tf_op jit(solution)/shard_map/ppermute | solution.py:218
  27.5 0.4 %collective-permute-done.9.across_ref = bf16[8,1024]{1,0:T(8,128)(2,1)S(1)} collective-permute-done((bf16[8,1024]{1,0:T(8,128)(2,1)S(1)}, bf16[8,1024]{1,0:T(8,128)(2,1)S(1)}, u32[]{:S(2)}, u32[]{:S(2)}) %collective-permute-start.9) | collective-permute-done | bytes 16416 | tf_op jit(solution)/shard_map/ppermute | solution.py:218
  27.9 0.8 %shard_map.44 = f32[8,1000]{1,0:T(8,128)} custom-call(f32[8,1024]{1,0:T(8,128)S(1)} %get-tuple-element.16.own_ref, bf16[8,1024]{1,0:T(8,128)(2,1)S(1)} %collective-permute-done.7.near_ref, bf16[16,1024]{1,0:T(8,128)(2,1)S(1)} %collective-permute-done.8.a_ref.far_ref, bf16[8,1024]{1,0:T(8,128)(2,1)S(1)} %collective-permute-done.9.across_ref), custom_call_target="tpu_custom_call" | custom-call | tf_op jit(solution)/shard_map/pallas_call | solution.py:27
  (4 shorter events, 0.0 us)
Async XLA Ops:
  0.0 4.0 %collective-permute-start = (bf16[8,768]{1,0:T(8,128)(2,1)}, bf16[8,768]{1,0:T(8,128)(2,1)S(1)}, u32[]{:S(2)}, u32[]{:S(2)}) collective-permute-start(bf16[8,768]{1,0:T(8,128)(2,1)} %a_ref.1), channel_id=1, source_target_pairs={{0,12},{1,13},{2,14},{3,15},{4,8},{5,9},{6,10},{7,11},{8,4},{9,5},... | collective-permute-start | bytes 36872 | tf_op jit(solution)/shard_map/ppermute | solution.py:218
  2.4 0.7 %copy-start.2 = (bf16[8,768]{1,0:T(8,128)(2,1)S(1)}, bf16[8,768]{1,0:T(8,128)(2,1)}, u32[]{:S(2)}) copy-start(bf16[8,768]{1,0:T(8,128)(2,1)} %a_ref.1) | copy-start | bytes 36868
  4.0 8.7 %copy-start = (bf16[2048,1000]{0,1:T(8,128)(2,1)S(1)}, bf16[2048,1000]{0,1:T(8,128)(2,1)}, u32[]{:S(2)}) copy-start(bf16[2048,1000]{0,1:T(8,128)(2,1)} %param.5) | copy-start | bytes 12288004
  4.0 8.7 %copy-start.1 = (bf16[2048,768]{1,0:T(8,128)(2,1)S(1)}, bf16[2048,768]{1,0:T(8,128)(2,1)}, u32[]{:S(2)}) copy-start(bf16[2048,768]{1,0:T(8,128)(2,1)} %k_ref.1) | copy-start | bytes 9437188
  4.0 1.6 %collective-permute-start.1 = (bf16[16,768]{1,0:T(8,128)(2,1)S(1)}, bf16[16,768]{1,0:T(8,128)(2,1)S(1)}, u32[]{:S(2)}, u32[]{:S(2)}) collective-permute-start(bf16[16,768]{1,0:T(8,128)(2,1)S(1)} %shard_map.38.a_ref), channel_id=1, source_target_pairs={{0,4},{1,5},{2,6},{3,7},{4,0},{5,1},{6,2},{7,3},{8,12},{9,13},{10,... | collective-permute-start | bytes 73736 | tf_op jit(solution)/shard_map/ppermute | solution.py:218
  5.6 5.9 %collective-permute-start.3 = (bf16[32,768]{1,0:T(8,128)(2,1)S(1)}, bf16[32,768]{1,0:T(8,128)(2,1)S(1)}, u32[]{:S(2)}, u32[]{:S(2)}) collective-permute-start(bf16[32,768]{1,0:T(8,128)(2,1)S(1)} %shard_map.39.own_ref), channel_id=1, source_target_pairs={{0,2},{1,3},{2,0},{3,1},{4,7},{5,6},{6,5},{7,4},{8,10},{9,11},{10,... | collective-permute-start | bytes 147464 | tf_op jit(solution)/shard_map/ppermute | solution.py:221
  8.7 3.5 %collective-permute-start.2 = (bf16[32,768]{1,0:T(8,128)(2,1)S(1)}, bf16[32,768]{1,0:T(8,128)(2,1)S(1)}, u32[]{:S(2)}, u32[]{:S(2)}) collective-permute-start(bf16[32,768]{1,0:T(8,128)(2,1)S(1)} %shard_map.39.own_ref), channel_id=1, source_target_pairs={{0,5},{1,4},{2,7},{3,6},{4,1},{5,0},{6,3},{7,2},{8,13},{9,12},{10,... | collective-permute-start | bytes 147464 | tf_op jit(solution)/shard_map/ppermute | solution.py:218
  11.5 1.2 %collective-permute-start.4 = (bf16[32,768]{1,0:T(8,128)(2,1)S(1)}, bf16[32,768]{1,0:T(8,128)(2,1)S(1)}, u32[]{:S(2)}, u32[]{:S(2)}) collective-permute-start(bf16[32,768]{1,0:T(8,128)(2,1)S(1)} %collective-permute-done.3.far_ref), channel_id=1, source_target_pairs={{0,4},{1,5},{2,6},{3,7},{4,0},{5,1},{6,2},{7,3},{8,12},{9,13},{10,... | collective-permute-start | bytes 147464 | tf_op jit(solution)/shard_map/ppermute | solution.py:218
  15.3 1.5 %collective-permute-start.5 = (bf16[64,1024]{1,0:T(8,128)(2,1)S(1)}, bf16[64,1024]{1,0:T(8,128)(2,1)S(1)}, u32[]{:S(2)}, u32[]{:S(2)}) collective-permute-start(bf16[64,1024]{1,0:T(8,128)(2,1)S(1)} %get-tuple-element.13), channel_id=1, source_target_pairs={{0,4},{1,5},{2,6},{3,7},{4,0},{5,1},{6,2},{7,3},{8,12},{9,13},{10,... | collective-permute-start | bytes 393224 | tf_op jit(solution)/shard_map/ppermute | solution.py:218
  17.1 4.4 %collective-permute-start.6 = (bf16[32,1024]{1,0:T(8,128)(2,1)S(1)}, bf16[32,1024]{1,0:T(8,128)(2,1)S(1)}, u32[]{:S(2)}, u32[]{:S(2)}) collective-permute-start(bf16[32,1024]{1,0:T(8,128)(2,1)S(1)} %get-tuple-element.15), channel_id=1, source_target_pairs={{0,8},{1,9},{2,10},{3,11},{4,12},{5,13},{6,14},{7,15},{8,0},{9,1},... | collective-permute-start | bytes 196616 | tf_op jit(solution)/shard_map/ppermute | solution.py:218
  21.8 4.9 %collective-permute-start.8 = (bf16[16,1024]{1,0:T(8,128)(2,1)S(1)}, bf16[16,1024]{1,0:T(8,128)(2,1)S(1)}, u32[]{:S(2)}, u32[]{:S(2)}) collective-permute-start(bf16[16,1024]{1,0:T(8,128)(2,1)S(1)} %get-tuple-element.18), channel_id=1, source_target_pairs={{0,2},{1,3},{2,0},{3,1},{4,7},{5,6},{6,5},{7,4},{8,10},{9,11},{10,... | collective-permute-start | bytes 98312 | tf_op jit(solution)/shard_map/ppermute | solution.py:221
  24.4 3.2 %collective-permute-start.7 = (bf16[8,1024]{1,0:T(8,128)(2,1)S(1)}, bf16[8,1024]{1,0:T(8,128)(2,1)S(1)}, u32[]{:S(2)}, u32[]{:S(2)}) collective-permute-start(bf16[8,1024]{1,0:T(8,128)(2,1)S(1)} %get-tuple-element.17), channel_id=1, source_target_pairs={{0,5},{1,4},{2,7},{3,6},{4,1},{5,0},{6,3},{7,2},{8,13},{9,12},{10,... | collective-permute-start | bytes 49160 | tf_op jit(solution)/shard_map/ppermute | solution.py:218
  26.7 1.2 %collective-permute-start.9 = (bf16[8,1024]{1,0:T(8,128)(2,1)S(1)}, bf16[8,1024]{1,0:T(8,128)(2,1)S(1)}, u32[]{:S(2)}, u32[]{:S(2)}) collective-permute-start(bf16[8,1024]{1,0:T(8,128)(2,1)S(1)} %shard_map.43), channel_id=1, source_target_pairs={{0,4},{1,5},{2,6},{3,7},{4,0},{5,1},{6,2},{7,3},{8,12},{9,13},{10,... | collective-permute-start | bytes 49160 | tf_op jit(solution)/shard_map/ppermute | solution.py:218

commit v7 on v6

--- a/solution.py
+++ b/solution.py
@@ -128,13 +128,16 @@
     )
 
     slots = half // unit
-    keep, send = [], []
-    for block in range(4):
-        odd = [n.bit_count() % 2 for n in range(slots)]
-        same = [block * count + (n + slots * o) * unit for n, o in enumerate(odd)]
-        other = [block * count + (n + slots * (1 - o)) * unit for n, o in enumerate(odd)]
-        (send if block == 3 else keep).extend(same)
-        (keep if block == 2 else send).extend(other)
+    odd = [n.bit_count() % 2 for n in range(slots)]
+
+    def rows(block, n, other_core):
+        return block * count + (n + slots * (other_core ^ odd[n])) * unit
+
+    keep = [rows(block, n, odd[n]) for block in (0, 1) for n in range(slots)]
+    send = [rows(block, n, 1 ^ odd[n]) for block in (0, 1) for n in range(slots)]
+    for other_core in (0, 1):
+        keep += [rows(2 + odd[n], n, other_core) for n in range(slots)]
+        send += [rows(3 - odd[n], n, other_core) for n in range(slots)]
     parts = (peaks, totals, votes)
     keep, send = (rows_of(parts, *[(lo, lo + unit) for lo in los]) for los in (keep, send))
     write(keep_ref, keep[2], keep[:2])
@@ -232,7 +235,7 @@
     came = swap(send, core)
     for bit in lead[::-1]:
         keep, send = merge(keep, came, classes)
-        came = swap(send, bit)
+        came = swap(send, bit ^ core)
     own, near, far = split(keep, came, classes)
     far = swap_far(far)
     near = swap(near, 1 ^ core)

time: 28.9 us -> 29.4 us (1.017)
  the two profiles are of different devices: /device:TPU:0 before, /device:TPU:1 now
where the time goes in v7:
time: 29.4 us; the launch traced here: 29.2 us
  starting transfers between devices  14.3 us (49%)
  waiting for transfers between devices  10 us (34%)
  Pallas kernels  4.05 us (14%)
  local copies, waits for them, and re-layouts  0.75 us (3%)
    ppermute x8, waiting for transfers between devices, swap(): return lax.ppermute(block, AXES, [(i, i ^ bit) for i in range(size)])  8.72 us
    ppermute x2, starting transfers between devices, swap_far(): lax.ppermute(block, AXES, [(i, i ^ (3 if i & core else 2)) for i in range...  7.6 us
    ppermute x8, starting transfers between devices, swap(): return lax.ppermute(block, AXES, [(i, i ^ bit) for i in range(size)])  6.7 us
    pallas_call x8, Pallas kernels, call(): pl.pallas_call(kernel, out_shape=outs, in_specs=[VMEM] * len(args), out_s...  4.05 us
    ppermute x2, waiting for transfers between devices, swap_far(): lax.ppermute(block, AXES, [(i, i ^ (3 if i & core else 2)) for i in range...  1.3 us
    unnamed x6, local copies, waits for them, and re-layouts  0.75 us
  transfers between devices with their start and end apart: 10, of which 8 were waited for; matrix products, arithmetic and copies ran while one was open for 0% of the time, Pallas kernels for 0%

profile of v7, /device:TPU:1, one launch (start us, length us, event | category | flops | bytes accessed | tf_op | source)
XLA Modules:
  0.0 29.2 jit_solution(17087028549052025736)
XLA Ops:
  0.0 2.6 %collective-permute-start = (bf16[8,768]{1,0:T(8,128)(2,1)}, bf16[8,768]{1,0:T(8,128)(2,1)S(1)}, u32[]{:S(2)}, u32[]{:S(2)}) collective-permute-start(bf16[8,768]{1,0:T(8,128)(2,1)} %a_ref.1), channel_id=1, source_target_pairs={{0,12},{1,13},{2,14},{3,15},{4,8},{5,9},{6,10},{7,11},{8,4},{9,5},... | collective-permute-start | bytes 36872 | tf_op jit(solution)/shard_map/ppermute | solution.py:221
  2.6 0.0 copy-start.2
  2.6 0.7 %copy-done.2 = bf16[8,768]{1,0:T(8,128)(2,1)S(1)} copy-done((bf16[8,768]{1,0:T(8,128)(2,1)S(1)}, bf16[8,768]{1,0:T(8,128)(2,1)}, u32[]{:S(2)}) %copy-start.2) | copy-done | bytes 12312
  3.3 0.8 %collective-permute-done.b_ref = bf16[8,768]{1,0:T(8,128)(2,1)S(1)} collective-permute-done((bf16[8,768]{1,0:T(8,128)(2,1)}, bf16[8,768]{1,0:T(8,128)(2,1)S(1)}, u32[]{:S(2)}, u32[]{:S(2)}) %collective-permute-start) | collective-permute-done | bytes 12320 | tf_op jit(solution)/shard_map/ppermute | solution.py:221
  4.2 0.0 copy-start
  4.2 0.0 copy-start.1
  4.2 0.1 collective-permute-start.1
  4.3 1.2 %collective-permute-done.1.b_ref = bf16[16,768]{1,0:T(8,128)(2,1)S(1)} collective-permute-done((bf16[16,768]{1,0:T(8,128)(2,1)S(1)}, bf16[16,768]{1,0:T(8,128)(2,1)S(1)}, u32[]{:S(2)}, u32[]{:S(2)}) %collective-permute-start.1) | collective-permute-done | bytes 24608 | tf_op jit(solution)/shard_map/ppermute | solution.py:221
  5.5 3.7 %collective-permute-start.3 = (bf16[32,768]{1,0:T(8,128)(2,1)S(1)}, bf16[32,768]{1,0:T(8,128)(2,1)S(1)}, u32[]{:S(2)}, u32[]{:S(2)}) collective-permute-start(bf16[32,768]{1,0:T(8,128)(2,1)S(1)} %shard_map.39.own_ref), channel_id=1, source_target_pairs={{0,2},{1,3},{2,0},{3,1},{4,7},{5,6},{6,5},{7,4},{8,10},{9,11},{10,... | collective-permute-start | bytes 147464 | tf_op jit(solution)/shard_map/ppermute | solution.py:224
  9.2 0.8 %collective-permute-start.2 = (bf16[32,768]{1,0:T(8,128)(2,1)S(1)}, bf16[32,768]{1,0:T(8,128)(2,1)S(1)}, u32[]{:S(2)}, u32[]{:S(2)}) collective-permute-start(bf16[32,768]{1,0:T(8,128)(2,1)S(1)} %shard_map.39.own_ref), channel_id=1, source_target_pairs={{0,5},{1,4},{2,7},{3,6},{4,1},{5,0},{6,3},{7,2},{8,13},{9,12},{10,... | collective-permute-start | bytes 147464 | tf_op jit(solution)/shard_map/ppermute | solution.py:221
  10.0 0.8 %collective-permute-done.3.far_ref = bf16[32,768]{1,0:T(8,128)(2,1)S(1)} collective-permute-done((bf16[32,768]{1,0:T(8,128)(2,1)S(1)}, bf16[32,768]{1,0:T(8,128)(2,1)S(1)}, u32[]{:S(2)}, u32[]{:S(2)}) %collective-permute-start.3) | collective-permute-done | bytes 49184 | tf_op jit(solution)/shard_map/ppermute | solution.py:224
  10.8 0.8 %collective-permute-start.4 = (bf16[32,768]{1,0:T(8,128)(2,1)S(1)}, bf16[32,768]{1,0:T(8,128)(2,1)S(1)}, u32[]{:S(2)}, u32[]{:S(2)}) collective-permute-start(bf16[32,768]{1,0:T(8,128)(2,1)S(1)} %collective-permute-done.3.far_ref), channel_id=1, source_target_pairs={{0,4},{1,5},{2,6},{3,7},{4,0},{5,1},{6,2},{7,3},{8,12},{9,13},{10,... | collective-permute-start | bytes 147464 | tf_op jit(solution)/shard_map/ppermute | solution.py:221
  11.5 1.1 %collective-permute-done.2.near_ref = bf16[32,768]{1,0:T(8,128)(2,1)S(1)} collective-permute-done((bf16[32,768]{1,0:T(8,128)(2,1)S(1)}, bf16[32,768]{1,0:T(8,128)(2,1)S(1)}, u32[]{:S(2)}, u32[]{:S(2)}) %collective-permute-start.2) | collective-permute-done | bytes 49184 | tf_op jit(solution)/shard_map/ppermute | solution.py:221
  12.7 0.0 collective-permute-done.4.across_ref
  12.7 0.0 copy-done
  12.7 0.0 copy-done.1
  12.7 2.6 %shard_map.40 = (f32[64,1024]{1,0:T(8,128)S(1)}, bf16[64,1024]{1,0:T(8,128)(2,1)S(1)}) custom-call(bf16[32,768]{1,0:T(8,128)(2,1)S(1)} %shard_map.39.own_ref, bf16[32,768]{1,0:T(8,128)(2,1)S(1)} %collective-permute-done.2.near_ref, bf16[32,768]{1,0:T(8,128)(2,1)S(1)} %collective-permute-done.3.far_ref, ...), custom_call_target="tpu_custom_call" | custom-call | flops 926941184 | bytes 7241728 | tf_op jit(solution)/shard_map/pallas_call | solution.py:27
  15.3 0.2 collective-permute-start.5
  15.5 1.3 %collective-permute-done.5.other_ref = bf16[64,1024]{1,0:T(8,128)(2,1)S(1)} collective-permute-done((bf16[64,1024]{1,0:T(8,128)(2,1)S(1)}, bf16[64,1024]{1,0:T(8,128)(2,1)S(1)}, u32[]{:S(2)}, u32[]{:S(2)}) %collective-permute-start.5) | collective-permute-done | bytes 131104 | tf_op jit(solution)/shard_map/ppermute | solution.py:221
  16.7 0.3 %shard_map.41 = (f32[32,1024]{1,0:T(8,128)S(1)}, bf16[32,1024]{1,0:T(8,128)(2,1)S(1)}) custom-call(f32[64,1024]{1,0:T(8,128)S(1)} %get-tuple-element.12.mine_ref, bf16[64,1024]{1,0:T(8,128)(2,1)S(1)} %collective-permute-done.5.other_ref), custom_call_target="tpu_custom_call" | custom-call | tf_op jit(solution)/shard_map/pallas_call | solution.py:27
  17.0 1.5 %collective-permute-start.6 = (bf16[32,1024]{1,0:T(8,128)(2,1)S(1)}, bf16[32,1024]{1,0:T(8,128)(2,1)S(1)}, u32[]{:S(2)}, u32[]{:S(2)}) collective-permute-start(bf16[32,1024]{1,0:T(8,128)(2,1)S(1)} %get-tuple-element.15), channel_id=1, source_target_pairs={{0,12},{1,13},{2,14},{3,15},{4,8},{5,9},{6,10},{7,11},{8,4},{9,5},... | collective-permute-start | bytes 196616 | tf_op jit(solution)/shard_map/ppermute | solution.py:221
  18.5 2.4 %collective-permute-done.6.other_ref = bf16[32,1024]{1,0:T(8,128)(2,1)S(1)} collective-permute-done((bf16[32,1024]{1,0:T(8,128)(2,1)S(1)}, bf16[32,1024]{1,0:T(8,128)(2,1)S(1)}, u32[]{:S(2)}, u32[]{:S(2)}) %collective-permute-start.6) | collective-permute-done | bytes 65568 | tf_op jit(solution)/shard_map/ppermute | solution.py:221
  21.0 0.3 shard_map.42
  21.2 3.9 %collective-permute-start.8 = (bf16[16,1024]{1,0:T(8,128)(2,1)S(1)}, bf16[16,1024]{1,0:T(8,128)(2,1)S(1)}, u32[]{:S(2)}, u32[]{:S(2)}) collective-permute-start(bf16[16,1024]{1,0:T(8,128)(2,1)S(1)} %get-tuple-element.18), channel_id=1, source_target_pairs={{0,2},{1,3},{2,0},{3,1},{4,7},{5,6},{6,5},{7,4},{8,10},{9,11},{10,... | collective-permute-start | bytes 98312 | tf_op jit(solution)/shard_map/ppermute | solution.py:224
  25.1 0.8 %collective-permute-start.7 = (bf16[8,1024]{1,0:T(8,128)(2,1)S(1)}, bf16[8,1024]{1,0:T(8,128)(2,1)S(1)}, u32[]{:S(2)}, u32[]{:S(2)}) collective-permute-start(bf16[8,1024]{1,0:T(8,128)(2,1)S(1)} %get-tuple-element.17), channel_id=1, source_target_pairs={{0,5},{1,4},{2,7},{3,6},{4,1},{5,0},{6,3},{7,2},{8,13},{9,12},{10,... | collective-permute-start | bytes 49160 | tf_op jit(solution)/shard_map/ppermute | solution.py:221
  25.9 0.5 %collective-permute-done.8.a_ref.far_ref = bf16[16,1024]{1,0:T(8,128)(2,1)S(1)} collective-permute-done((bf16[16,1024]{1,0:T(8,128)(2,1)S(1)}, bf16[16,1024]{1,0:T(8,128)(2,1)S(1)}, u32[]{:S(2)}, u32[]{:S(2)}) %collective-permute-start.8) | collective-permute-done | bytes 32800 | tf_op jit(solution)/shard_map/ppermute | solution.py:224
  26.4 0.0 collective-permute-start.9
  26.4 1.9 %collective-permute-done.7.near_ref = bf16[8,1024]{1,0:T(8,128)(2,1)S(1)} collective-permute-done((bf16[8,1024]{1,0:T(8,128)(2,1)S(1)}, bf16[8,1024]{1,0:T(8,128)(2,1)S(1)}, u32[]{:S(2)}, u32[]{:S(2)}) %collective-permute-start.7) | collective-permute-done | bytes 16416 | tf_op jit(solution)/shard_map/ppermute | solution.py:221
  28.3 0.0 collective-permute-done.9.across_ref
  28.3 0.8 %shard_map.44 = f32[8,1000]{1,0:T(8,128)} custom-call(f32[8,1024]{1,0:T(8,128)S(1)} %get-tuple-element.16.own_ref, bf16[8,1024]{1,0:T(8,128)(2,1)S(1)} %collective-permute-done.7.near_ref, bf16[16,1024]{1,0:T(8,128)(2,1)S(1)} %collective-permute-done.8.a_ref.far_ref, bf16[8,1024]{1,0:T(8,128)(2,1)S(1)} %collective-permute-done.9.across_ref), custom_call_target="tpu_custom_call" | custom-call | tf_op jit(solution)/shard_map/pallas_call | solution.py:27
  (4 shorter events, 0.0 us)
Async XLA Ops:
  0.0 4.2 %collective-permute-start = (bf16[8,768]{1,0:T(8,128)(2,1)}, bf16[8,768]{1,0:T(8,128)(2,1)S(1)}, u32[]{:S(2)}, u32[]{:S(2)}) collective-permute-start(bf16[8,768]{1,0:T(8,128)(2,1)} %a_ref.1), channel_id=1, source_target_pairs={{0,12},{1,13},{2,14},{3,15},{4,8},{5,9},{6,10},{7,11},{8,4},{9,5},... | collective-permute-start | bytes 36872 | tf_op jit(solution)/shard_map/ppermute | solution.py:221
  2.6 0.7 %copy-start.2 = (bf16[8,768]{1,0:T(8,128)(2,1)S(1)}, bf16[8,768]{1,0:T(8,128)(2,1)}, u32[]{:S(2)}) copy-start(bf16[8,768]{1,0:T(8,128)(2,1)} %a_ref.1) | copy-start | bytes 36868
  4.2 8.5 %copy-start = (bf16[2048,1000]{0,1:T(8,128)(2,1)S(1)}, bf16[2048,1000]{0,1:T(8,128)(2,1)}, u32[]{:S(2)}) copy-start(bf16[2048,1000]{0,1:T(8,128)(2,1)} %param.5) | copy-start | bytes 12288004
  4.2 8.5 %copy-start.1 = (bf16[2048,768]{1,0:T(8,128)(2,1)S(1)}, bf16[2048,768]{1,0:T(8,128)(2,1)}, u32[]{:S(2)}) copy-start(bf16[2048,768]{1,0:T(8,128)(2,1)} %k_ref.1) | copy-start | bytes 9437188
  4.2 1.3 %collective-permute-start.1 = (bf16[16,768]{1,0:T(8,128)(2,1)S(1)}, bf16[16,768]{1,0:T(8,128)(2,1)S(1)}, u32[]{:S(2)}, u32[]{:S(2)}) collective-permute-start(bf16[16,768]{1,0:T(8,128)(2,1)S(1)} %shard_map.38.a_ref), channel_id=1, source_target_pairs={{0,4},{1,5},{2,6},{3,7},{4,0},{5,1},{6,2},{7,3},{8,12},{9,13},{10,... | collective-permute-start | bytes 73736 | tf_op jit(solution)/shard_map/ppermute | solution.py:221
  5.5 5.3 %collective-permute-start.3 = (bf16[32,768]{1,0:T(8,128)(2,1)S(1)}, bf16[32,768]{1,0:T(8,128)(2,1)S(1)}, u32[]{:S(2)}, u32[]{:S(2)}) collective-permute-start(bf16[32,768]{1,0:T(8,128)(2,1)S(1)} %shard_map.39.own_ref), channel_id=1, source_target_pairs={{0,2},{1,3},{2,0},{3,1},{4,7},{5,6},{6,5},{7,4},{8,10},{9,11},{10,... | collective-permute-start | bytes 147464 | tf_op jit(solution)/shard_map/ppermute | solution.py:224
  9.2 3.5 %collective-permute-start.2 = (bf16[32,768]{1,0:T(8,128)(2,1)S(1)}, bf16[32,768]{1,0:T(8,128)(2,1)S(1)}, u32[]{:S(2)}, u32[]{:S(2)}) collective-permute-start(bf16[32,768]{1,0:T(8,128)(2,1)S(1)} %shard_map.39.own_ref), channel_id=1, source_target_pairs={{0,5},{1,4},{2,7},{3,6},{4,1},{5,0},{6,3},{7,2},{8,13},{9,12},{10,... | collective-permute-start | bytes 147464 | tf_op jit(solution)/shard_map/ppermute | solution.py:221
  10.8 1.9 %collective-permute-start.4 = (bf16[32,768]{1,0:T(8,128)(2,1)S(1)}, bf16[32,768]{1,0:T(8,128)(2,1)S(1)}, u32[]{:S(2)}, u32[]{:S(2)}) collective-permute-start(bf16[32,768]{1,0:T(8,128)(2,1)S(1)} %collective-permute-done.3.far_ref), channel_id=1, source_target_pairs={{0,4},{1,5},{2,6},{3,7},{4,0},{5,1},{6,2},{7,3},{8,12},{9,13},{10,... | collective-permute-start | bytes 147464 | tf_op jit(solution)/shard_map/ppermute | solution.py:221
  15.3 1.4 %collective-permute-start.5 = (bf16[64,1024]{1,0:T(8,128)(2,1)S(1)}, bf16[64,1024]{1,0:T(8,128)(2,1)S(1)}, u32[]{:S(2)}, u32[]{:S(2)}) collective-permute-start(bf16[64,1024]{1,0:T(8,128)(2,1)S(1)} %get-tuple-element.13), channel_id=1, source_target_pairs={{0,4},{1,5},{2,6},{3,7},{4,0},{5,1},{6,2},{7,3},{8,12},{9,13},{10,... | collective-permute-start | bytes 393224 | tf_op jit(solution)/shard_map/ppermute | solution.py:221
  17.0 3.9 %collective-permute-start.6 = (bf16[32,1024]{1,0:T(8,128)(2,1)S(1)}, bf16[32,1024]{1,0:T(8,128)(2,1)S(1)}, u32[]{:S(2)}, u32[]{:S(2)}) collective-permute-start(bf16[32,1024]{1,0:T(8,128)(2,1)S(1)} %get-tuple-element.15), channel_id=1, source_target_pairs={{0,12},{1,13},{2,14},{3,15},{4,8},{5,9},{6,10},{7,11},{8,4},{9,5},... | collective-permute-start | bytes 196616 | tf_op jit(solution)/shard_map/ppermute | solution.py:221
  21.2 5.2 %collective-permute-start.8 = (bf16[16,1024]{1,0:T(8,128)(2,1)S(1)}, bf16[16,1024]{1,0:T(8,128)(2,1)S(1)}, u32[]{:S(2)}, u32[]{:S(2)}) collective-permute-start(bf16[16,1024]{1,0:T(8,128)(2,1)S(1)} %get-tuple-element.18), channel_id=1, source_target_pairs={{0,2},{1,3},{2,0},{3,1},{4,7},{5,6},{6,5},{7,4},{8,10},{9,11},{10,... | collective-permute-start | bytes 98312 | tf_op jit(solution)/shard_map/ppermute | solution.py:224
  25.1 3.2 %collective-permute-start.7 = (bf16[8,1024]{1,0:T(8,128)(2,1)S(1)}, bf16[8,1024]{1,0:T(8,128)(2,1)S(1)}, u32[]{:S(2)}, u32[]{:S(2)}) collective-permute-start(bf16[8,1024]{1,0:T(8,128)(2,1)S(1)} %get-tuple-element.17), channel_id=1, source_target_pairs={{0,5},{1,4},{2,7},{3,6},{4,1},{5,0},{6,3},{7,2},{8,13},{9,12},{10,... | collective-permute-start | bytes 49160 | tf_op jit(solution)/shard_map/ppermute | solution.py:221
  26.4 1.9 %collective-permute-start.9 = (bf16[8,1024]{1,0:T(8,128)(2,1)S(1)}, bf16[8,1024]{1,0:T(8,128)(2,1)S(1)}, u32[]{:S(2)}, u32[]{:S(2)}) collective-permute-start(bf16[8,1024]{1,0:T(8,128)(2,1)S(1)} %shard_map.43), channel_id=1, source_target_pairs={{0,4},{1,5},{2,6},{3,7},{4,0},{5,1},{6,2},{7,3},{8,12},{9,13},{10,... | collective-permute-start | bytes 49160 | tf_op jit(solution)/shard_map/ppermute | solution.py:221

commit v8 on v7

v8 whole, which is shorter than its diff:
```python
import functools
import math

import jax
import jax.numpy as jnp
from jax import lax
from jax.experimental import pallas as pl
from jax.experimental.pallas import tpu as pltpu
from jax.sharding import PartitionSpec as P

SCORE_GAIN = 3.0
AXES = ("bank", "query")
LANES = 128
POWER, CENTRE = 24.0, 5.0
MIB = 1 << 20
VMEM = pl.BlockSpec(memory_space=pltpu.VMEM)
BESIDE = pl.CostEstimate(flops=4_000_000_000, bytes_accessed=1 << 17, transcendentals=0)


def grant(*arrays):
    return pltpu.CompilerParams(
        vmem_limit_bytes=sum(2 * math.prod(a.shape) * a.dtype.itemsize for a in arrays) + MIB
    )


def call(kernel, outs, *args, scratch=(), cost=None):
    return pl.pallas_call(
        kernel,
        out_shape=outs,
        in_specs=[VMEM] * len(args),
        out_specs=jax.tree.map(lambda _: VMEM, outs),
        compiler_params=grant(*args, *jax.tree.leaves(outs), *scratch),
        cost_estimate=cost,
    )(*args)


def fetch_kernel(a_ref, out_ref):
    out_ref[...] = a_ref[...]


def fetch(a):
    return call(fetch_kernel, jax.ShapeDtypeStruct(a.shape, a.dtype), a, cost=BESIDE)


def join_kernel(a_ref, b_ref, out_ref):
    rows = a_ref.shape[0]
    out_ref[:rows] = a_ref[...]
    out_ref[rows:] = b_ref[...]


def join(a, b):
    out = jax.ShapeDtypeStruct((2 * a.shape[0], a.shape[1]), a.dtype)
    return call(join_kernel, out, a, b, cost=BESIDE)


def record_shape(rows, classes, dtype=jnp.float32):
    return jax.ShapeDtypeStruct((rows, -(-(classes + 3) // LANES) * LANES), dtype)


def extra_columns(shape, classes, count):
    column = lax.broadcasted_iota(jnp.int32, (shape[0], LANES), 1) + (shape[1] - LANES)
    return [column == classes + c for c in range(count)]


def tiles(record):
    return [record[:, lo : lo + LANES] for lo in range(0, record.shape[1], LANES)]


def log_weight(last, shape, classes, count):
    held = functools.reduce(jnp.logical_or, extra_columns(shape, classes, count))
    return jnp.sum(jnp.where(held, last, 0.0), axis=1, keepdims=True)


def kept(record, classes):
    averages = tiles(record)
    return log_weight(averages[-1], record.shape, classes, 1), averages


def decoded(record, classes):
    codes = tiles(record)
    averages = [jnp.exp2(jnp.log2(c) * (1 / POWER) - CENTRE) for c in codes]
    return log_weight(codes[-1], record.shape, classes, 3), averages


def store(ref, at, averages, classes, extra):
    width = ref.shape[1]
    rows = averages[0].shape[0]
    for lo, values in zip(range(0, width, LANES), averages):
        if lo + LANES == width:
            for held, value in zip(extra_columns((rows, width), classes, len(extra)), extra):
                values = jnp.where(held, value, values)
        ref[at : at + rows, lo : lo + LANES] = values.astype(ref.dtype)


def keep(ref, at, parts, classes):
    store(ref, at, parts[1], classes, [parts[0]])


def encode(ref, at, parts, classes):
    log, averages = parts
    high = log.astype(jnp.bfloat16).astype(jnp.float32)
    middle = (log - high).astype(jnp.bfloat16).astype(jnp.float32)
    codes = [jnp.exp2(POWER * jnp.log2(x) + POWER * CENTRE) for x in averages]
    store(ref, at, codes, classes, [high, middle, log - high - middle])


def combine(*parts):
    top = functools.reduce(jnp.maximum, [log for log, _ in parts])
    weights = [jnp.exp(log - top) for log, _ in parts]
    total = functools.reduce(jnp.add, weights)
    factors = [w / total for w in weights]
    columns = zip(*[averages for _, averages in parts])
    return top + jnp.log(total), [sum(f * x for f, x in zip(factors, c)) for c in columns]


def rows_of(parts, *ranges):
    take = lambda x: jnp.concatenate([x[lo:hi] for lo, hi in ranges], axis=0)
    return take(parts[0]), [take(x) for x in parts[1]]


def stats_kernel(unit, own_ref, near_ref, far_ref, across_ref, k_ref, lt_ref, *out_refs):
    count, width = own_ref.shape
    classes = lt_ref.shape[0]
    half = count // 2
    queries = jnp.concatenate(
        [own_ref[...], near_ref[...], far_ref[...], across_ref[...]], axis=0
    )
    scores = lax.dot_general(
        queries, k_ref[...], (((1,), (1,)), ((), ())), preferred_element_type=jnp.float32
    ) * (SCORE_GAIN / math.sqrt(width))
    peaks = jnp.max(scores, axis=1, keepdims=True)
    weights = jnp.exp(scores - peaks)
    totals = jnp.sum(weights, axis=1, keepdims=True)
    votes = lax.dot_general(
        weights.astype(jnp.bfloat16),
        lt_ref[...],
        (((1,), (1,)), ((), ())),
        preferred_element_type=jnp.float32,
    )

    slots = half // unit
    odd = [n.bit_count() % 2 for n in range(slots)]

    def rows(block, other_core):
        starts = [block * count + (n + slots * (other_core ^ o)) * unit for n, o in enumerate(odd)]
        return [(lo, lo + unit) for lo in starts]

    votes = votes * (1 / totals)
    spare = out_refs[0].shape[1] - classes
    votes = jnp.concatenate([votes, jnp.ones((4 * count, spare), jnp.float32)], axis=1)
    parts = (peaks + jnp.log(totals), tiles(votes))
    far_send, near_send, far_keep, near_keep = out_refs
    encode(far_send, 0, rows_of(parts, *rows(3, 0), *rows(3, 1)), classes)
    encode(near_send, 0, rows_of(parts, *rows(0, 1), *rows(1, 1)), classes)
    keep(far_keep, 0, rows_of(parts, *rows(2, 0), *rows(2, 1)), classes)
    keep(near_keep, 0, rows_of(parts, *rows(0, 0), *rows(1, 0)), classes)


def stats(blocks, keys, labels_t, unit):
    rows, width = 4 * blocks[0].shape[0], keys.shape[1]
    bank, classes = keys.shape[0], labels_t.shape[0]
    outs = [record_shape(rows // 4, classes, d) for d in (jnp.bfloat16, jnp.float32) for _ in range(2)]
    scores = jax.ShapeDtypeStruct((rows, bank), jnp.float32)
    cost = pl.CostEstimate(
        flops=2 * rows * bank * (width + classes),
        bytes_accessed=2 * bank * (width + classes),
        transcendentals=rows * bank,
    )
    return call(
        functools.partial(stats_kernel, unit), outs, *blocks, keys, labels_t, scratch=(scores,), cost=cost
    )


def merge_kernel(put, classes, first, last, mine_ref, other_ref, *out_refs):
    half = mine_ref.shape[0] // 2
    ranges = [(at + first * half // 2, at + last * half // 2) for at in (0, half)]
    mine, other = mine_ref[...], other_ref[...].astype(jnp.float32)

    def merged(ranges):
        a, b = (jnp.concatenate([x[lo:hi] for lo, hi in ranges], axis=0) for x in (mine, other))
        return combine(kept(a, classes), decoded(b, classes))

    for p, ref, chosen in zip(put, out_refs, [[r] for r in ranges] if len(put) > 1 else [ranges]):
        p(ref, 0, merged(chosen), classes)


def merge(mine, other, classes, first, last, *put):
    rows = mine.shape[0] * (last - first) // 2 // len(put)
    outs = [record_shape(rows, classes, jnp.float32 if p is keep else jnp.bfloat16) for p in put]
    kernel = functools.partial(merge_kernel, put, classes, first, last)
    return call(kernel, outs, mine, other)


def tail_kernel(a_ref, out_ref):
    out_ref[...] = a_ref[...].astype(jnp.float32)[out_ref.shape[0] :].astype(out_ref.dtype)


def tail(a):
    out = jax.ShapeDtypeStruct((a.shape[0] // 2, a.shape[1]), a.dtype)
    return call(tail_kernel, out, a)


def finish_kernel(classes, own_ref, near_ref, far_ref, across_ref, out_ref):
    rows = out_ref.shape[0]
    came = [r[...].astype(jnp.float32)[:rows] for r in (near_ref, far_ref, across_ref)]
    _, averages = combine(kept(own_ref[...], classes), *[decoded(r, classes) for r in came])
    out_ref[...] = jnp.concatenate([jnp.log(x) for x in averages], axis=1)[:, :classes]


def finish(own, near, far, across, classes):
    out = jax.ShapeDtypeStruct((own.shape[0], classes), jnp.float32)
    return call(functools.partial(finish_kernel, classes), out, own, near, far, across)


def local(size, core, lead, queries, bank_keys, bank_labels):
    def swap(block, bit):
        return lax.ppermute(block, AXES, [(i, i ^ bit) for i in range(size)])

    def swap_far(block):
        return lax.ppermute(block, AXES, [(i, i ^ (3 if i & core else 2)) for i in range(size)])

    classes = bank_labels.shape[1]
    first, *rest = [bit ^ core for bit in lead] + [core]
    own = join(fetch(queries), swap(queries, first))
    for bit in rest:
        own = join(own, swap(own, bit))
    far = swap_far(own)
    near = swap(own, 1 ^ core)
    across = swap(far, core)
    *sends, far, near = stats((own, near, far, across), bank_keys, bank_labels.T, queries.shape[0])
    far_came, near_came = (swap(send, core) for send in sends)
    for bit in lead[::-1]:
        (send,) = merge(far, far_came, classes, 1, 2, encode)
        (far,) = merge(far, far_came, classes, 0, 1, keep)
        far_came = swap(send, bit)
        (send,) = merge(near, near_came, classes, 1, 2, encode)
        (near,) = merge(near, near_came, classes, 0, 1, keep)
        near_came = swap(send, bit)
    (far,) = merge(far, far_came, classes, 0, 2, encode)
    own, near = merge(near, near_came, classes, 0, 2, keep, encode)
    far = swap_far(far)
    near = swap(near, 1 ^ core)
    across = swap(tail(far), core)
    return finish(own, near, far, across, classes)


def solution(mesh):
    placed = P(("groups", "bank", "query"), None)
    query, bank = mesh.shape["query"], mesh.shape["bank"]
    lead = [1 << b for b in range(2, query.bit_length() - 1)]
    lead += [query << b for b in range(1, bank.bit_length() - 1)]
    return jax.shard_map(
        functools.partial(local, query * bank, query, lead),
        mesh=mesh,
        in_specs=(placed,) * 3,
        out_specs=placed,
        check_vma=False,
    )
```

time: 29.4 us -> 28.1 us (0.956)
  the two profiles are of different devices: /device:TPU:1 before, /device:TPU:0 now
where the time goes in v8:
time: 28.1 us; the launch traced here: 27.9 us
  starting transfers between devices  12 us (43%)
  waiting for transfers between devices  10.9 us (39%)
  Pallas kernels  4.14 us (15%)
  local copies, waits for them, and re-layouts  0.75 us (3%)
    ppermute x10, waiting for transfers between devices, swap(): return lax.ppermute(block, AXES, [(i, i ^ bit) for i in range(size)])  6.27 us
    ppermute x10, starting transfers between devices, swap(): return lax.ppermute(block, AXES, [(i, i ^ bit) for i in range(size)])  6.24 us
    ppermute x2, starting transfers between devices, swap_far(): lax.ppermute(block, AXES, [(i, i ^ (3 if i & core else 2)) for i in range...  5.78 us
    ppermute x2, waiting for transfers between devices, swap_far(): lax.ppermute(block, AXES, [(i, i ^ (3 if i & core else 2)) for i in range...  4.64 us
    pallas_call x12, Pallas kernels, call(): pl.pallas_call(kernel, out_shape=outs, in_specs=[VMEM] * len(args), out_s...  4.14 us
    unnamed x6, local copies, waits for them, and re-layouts  0.75 us
  transfers between devices with their start and end apart: 12, of which 9 were waited for; matrix products, arithmetic and copies ran while one was open for 0% of the time, Pallas kernels for 3%

profile of v8, /device:TPU:0, one launch (start us, length us, event | category | flops | bytes accessed | tf_op | source)
XLA Modules:
  0.0 27.9 jit_solution(11922883623586667035)
XLA Ops:
  0.0 2.4 %collective-permute-start = (bf16[8,768]{1,0:T(8,128)(2,1)}, bf16[8,768]{1,0:T(8,128)(2,1)S(1)}, u32[]{:S(2)}, u32[]{:S(2)}) collective-permute-start(bf16[8,768]{1,0:T(8,128)(2,1)} %a_ref.1), channel_id=1, source_target_pairs={{0,12},{1,13},{2,14},{3,15},{4,8},{5,9},{6,10},{7,11},{8,4},{9,5},... | collective-permute-start | bytes 36872 | tf_op jit(solution)/shard_map/ppermute | solution.py:217
  2.4 0.7 %copy-done.2 = bf16[8,768]{1,0:T(8,128)(2,1)S(1)} copy-done((bf16[8,768]{1,0:T(8,128)(2,1)S(1)}, bf16[8,768]{1,0:T(8,128)(2,1)}, u32[]{:S(2)}) %copy-start.2) | copy-done | bytes 12312
  3.1 0.9 %collective-permute-done.b_ref = bf16[8,768]{1,0:T(8,128)(2,1)S(1)} collective-permute-done((bf16[8,768]{1,0:T(8,128)(2,1)}, bf16[8,768]{1,0:T(8,128)(2,1)S(1)}, u32[]{:S(2)}, u32[]{:S(2)}) %collective-permute-start) | collective-permute-done | bytes 12320 | tf_op jit(solution)/shard_map/ppermute | solution.py:217
  4.0 0.7 %collective-permute-start.1 = (bf16[16,768]{1,0:T(8,128)(2,1)S(1)}, bf16[16,768]{1,0:T(8,128)(2,1)S(1)}, u32[]{:S(2)}, u32[]{:S(2)}) collective-permute-start(bf16[16,768]{1,0:T(8,128)(2,1)S(1)} %shard_map.38.a_ref), channel_id=1, source_target_pairs={{0,4},{1,5},{2,6},{3,7},{4,0},{5,1},{6,2},{7,3},{8,12},{9,13},{10,... | collective-permute-start | bytes 73736 | tf_op jit(solution)/shard_map/ppermute | solution.py:217
  4.7 0.8 %collective-permute-done.1.b_ref = bf16[16,768]{1,0:T(8,128)(2,1)S(1)} collective-permute-done((bf16[16,768]{1,0:T(8,128)(2,1)S(1)}, bf16[16,768]{1,0:T(8,128)(2,1)S(1)}, u32[]{:S(2)}, u32[]{:S(2)}) %collective-permute-start.1) | collective-permute-done | bytes 24608 | tf_op jit(solution)/shard_map/ppermute | solution.py:217
  5.6 3.2 %collective-permute-start.3 = (bf16[32,768]{1,0:T(8,128)(2,1)S(1)}, bf16[32,768]{1,0:T(8,128)(2,1)S(1)}, u32[]{:S(2)}, u32[]{:S(2)}) collective-permute-start(bf16[32,768]{1,0:T(8,128)(2,1)S(1)} %shard_map.39.own_ref), channel_id=1, source_target_pairs={{0,2},{1,3},{2,0},{3,1},{4,7},{5,6},{6,5},{7,4},{8,10},{9,11},{10,... | collective-permute-start | bytes 147464 | tf_op jit(solution)/shard_map/ppermute | solution.py:220
  8.7 0.1 collective-permute-start.2
  8.8 2.7 %collective-permute-done.3.far_ref = bf16[32,768]{1,0:T(8,128)(2,1)S(1)} collective-permute-done((bf16[32,768]{1,0:T(8,128)(2,1)S(1)}, bf16[32,768]{1,0:T(8,128)(2,1)S(1)}, u32[]{:S(2)}, u32[]{:S(2)}) %collective-permute-start.3) | collective-permute-done | bytes 49184 | tf_op jit(solution)/shard_map/ppermute | solution.py:220
  11.5 0.0 collective-permute-start.4
  11.5 0.8 %collective-permute-done.2.near_ref = bf16[32,768]{1,0:T(8,128)(2,1)S(1)} collective-permute-done((bf16[32,768]{1,0:T(8,128)(2,1)S(1)}, bf16[32,768]{1,0:T(8,128)(2,1)S(1)}, u32[]{:S(2)}, u32[]{:S(2)}) %collective-permute-start.2) | collective-permute-done | bytes 49184 | tf_op jit(solution)/shard_map/ppermute | solution.py:217
  12.2 0.5 %collective-permute-done.4.across_ref = bf16[32,768]{1,0:T(8,128)(2,1)S(1)} collective-permute-done((bf16[32,768]{1,0:T(8,128)(2,1)S(1)}, bf16[32,768]{1,0:T(8,128)(2,1)S(1)}, u32[]{:S(2)}, u32[]{:S(2)}) %collective-permute-start.4) | collective-permute-done | bytes 49184 | tf_op jit(solution)/shard_map/ppermute | solution.py:217
  12.7 2.7 %shard_map.40 = (bf16[32,1024]{1,0:T(8,128)(2,1)S(1)}, bf16[32,1024]{1,0:T(8,128)(2,1)S(1)}, f32[32,1024]{1,0:T(8,128)S(1)}, f32[32,1024]{1,0:T(8,128)S(1)}) custom-call(bf16[32,768]{1,0:T(8,128)(2,1)S(1)} %shard_map.39.own_ref, bf16[32,768]{1,0:T(8,128)(2,1)S(1)} %collective-permute-done.2.near_ref, bf16[32,768]{1,0:T(8,128)(2,1)S(1)} %collective-permute-done.3.far_ref, ...), custom_call_target="tpu_custom_call" | custom-call | flops 926941184 | bytes 7241728 | tf_op jit(solution)/shard_map/pallas_call | solution.py:27
  15.4 0.5 %collective-permute-start.8 = (bf16[32,1024]{1,0:T(8,128)(2,1)S(1)}, bf16[32,1024]{1,0:T(8,128)(2,1)S(1)}, u32[]{:S(2)}, u32[]{:S(2)}) collective-permute-start(bf16[32,1024]{1,0:T(8,128)(2,1)S(1)} %get-tuple-element.16), channel_id=1, source_target_pairs={{0,4},{1,5},{2,6},{3,7},{4,0},{5,1},{6,2},{7,3},{8,12},{9,13},{10,... | collective-permute-start | bytes 196616 | tf_op jit(solution)/shard_map/ppermute | solution.py:217
  15.9 0.1 collective-permute-start.5
  16.0 0.8 %collective-permute-done.8.other_ref = bf16[32,1024]{1,0:T(8,128)(2,1)S(1)} collective-permute-done((bf16[32,1024]{1,0:T(8,128)(2,1)S(1)}, bf16[32,1024]{1,0:T(8,128)(2,1)S(1)}, u32[]{:S(2)}, u32[]{:S(2)}) %collective-permute-start.8) | collective-permute-done | bytes 65568 | tf_op jit(solution)/shard_map/ppermute | solution.py:217
  16.8 0.1 shard_map.45
  16.9 1.7 %collective-permute-start.9 = (bf16[16,1024]{1,0:T(8,128)(2,1)S(1)}, bf16[16,1024]{1,0:T(8,128)(2,1)S(1)}, u32[]{:S(2)}, u32[]{:S(2)}) collective-permute-start(bf16[16,1024]{1,0:T(8,128)(2,1)S(1)} %shard_map.45), channel_id=1, source_target_pairs={{0,8},{1,9},{2,10},{3,11},{4,12},{5,13},{6,14},{7,15},{8,0},{9,1},... | collective-permute-start | bytes 98312 | tf_op jit(solution)/shard_map/ppermute | solution.py:217
  18.6 0.0 collective-permute-done.5.other_ref
  18.7 0.1 shard_map.42
  18.8 0.4 %collective-permute-start.6 = (bf16[16,1024]{1,0:T(8,128)(2,1)S(1)}, bf16[16,1024]{1,0:T(8,128)(2,1)S(1)}, u32[]{:S(2)}, u32[]{:S(2)}) collective-permute-start(bf16[16,1024]{1,0:T(8,128)(2,1)S(1)} %shard_map.42), channel_id=1, source_target_pairs={{0,8},{1,9},{2,10},{3,11},{4,12},{5,13},{6,14},{7,15},{8,0},{9,1},... | collective-permute-start | bytes 98312 | tf_op jit(solution)/shard_map/ppermute | solution.py:217
  19.2 0.1 shard_map.44.mine_ref
  19.3 1.6 %collective-permute-done.9.other_ref = bf16[16,1024]{1,0:T(8,128)(2,1)S(1)} collective-permute-done((bf16[16,1024]{1,0:T(8,128)(2,1)S(1)}, bf16[16,1024]{1,0:T(8,128)(2,1)S(1)}, u32[]{:S(2)}, u32[]{:S(2)}) %collective-permute-start.9) | collective-permute-done | bytes 32800 | tf_op jit(solution)/shard_map/ppermute | solution.py:217
  20.9 0.1 shard_map.46
  21.0 2.6 %collective-permute-start.10 = (bf16[16,1024]{1,0:T(8,128)(2,1)S(1)}, bf16[16,1024]{1,0:T(8,128)(2,1)S(1)}, u32[]{:S(2)}, u32[]{:S(2)}) collective-permute-start(bf16[16,1024]{1,0:T(8,128)(2,1)S(1)} %shard_map.46), channel_id=1, source_target_pairs={{0,2},{1,3},{2,0},{3,1},{4,7},{5,6},{6,5},{7,4},{8,10},{9,11},{10,... | collective-permute-start | bytes 98312 | tf_op jit(solution)/shard_map/ppermute | solution.py:220
  23.7 0.1 shard_map.41.mine_ref
  23.8 0.0 collective-permute-done.6.other_ref
  23.8 0.1 shard_map.43
  23.9 0.1 collective-permute-start.7
  24.0 1.9 %collective-permute-done.10.a_ref.far_ref = bf16[16,1024]{1,0:T(8,128)(2,1)S(1)} collective-permute-done((bf16[16,1024]{1,0:T(8,128)(2,1)S(1)}, bf16[16,1024]{1,0:T(8,128)(2,1)S(1)}, u32[]{:S(2)}, u32[]{:S(2)}) %collective-permute-start.10) | collective-permute-done | bytes 32800 | tf_op jit(solution)/shard_map/ppermute | solution.py:220
  25.9 0.3 %collective-permute-start.11 = (bf16[8,1024]{1,0:T(8,128)(2,1)S(1)}, bf16[8,1024]{1,0:T(8,128)(2,1)S(1)}, u32[]{:S(2)}, u32[]{:S(2)}) collective-permute-start(bf16[8,1024]{1,0:T(8,128)(2,1)S(1)} %shard_map.47), channel_id=1, source_target_pairs={{0,4},{1,5},{2,6},{3,7},{4,0},{5,1},{6,2},{7,3},{8,12},{9,13},{10,... | collective-permute-start | bytes 49160 | tf_op jit(solution)/shard_map/ppermute | solution.py:217
  26.2 0.9 %collective-permute-done.7.near_ref = bf16[8,1024]{1,0:T(8,128)(2,1)S(1)} collective-permute-done((bf16[8,1024]{1,0:T(8,128)(2,1)S(1)}, bf16[8,1024]{1,0:T(8,128)(2,1)S(1)}, u32[]{:S(2)}, u32[]{:S(2)}) %collective-permute-start.7) | collective-permute-done | bytes 16416 | tf_op jit(solution)/shard_map/ppermute | solution.py:217
  27.1 0.7 %shard_map.48 = f32[8,1000]{1,0:T(8,128)} custom-call(f32[8,1024]{1,0:T(8,128)S(1)} %get-tuple-element.13.own_ref, bf16[8,1024]{1,0:T(8,128)(2,1)S(1)} %collective-permute-done.7.near_ref, bf16[16,1024]{1,0:T(8,128)(2,1)S(1)} %collective-permute-done.10.a_ref.far_ref, bf16[8,1024]{1,0:T(8,128)(2,1)S(1)} %collective-permute-done.11.across_ref), custom_call_target="tpu_custom_call" | custom-call | tf_op jit(solution)/shard_map/pallas_call | solution.py:27
  (10 shorter events, 0.0 us)
Async XLA Ops:
  0.0 4.0 %collective-permute-start = (bf16[8,768]{1,0:T(8,128)(2,1)}, bf16[8,768]{1,0:T(8,128)(2,1)S(1)}, u32[]{:S(2)}, u32[]{:S(2)}) collective-permute-start(bf16[8,768]{1,0:T(8,128)(2,1)} %a_ref.1), channel_id=1, source_target_pairs={{0,12},{1,13},{2,14},{3,15},{4,8},{5,9},{6,10},{7,11},{8,4},{9,5},... | collective-permute-start | bytes 36872 | tf_op jit(solution)/shard_map/ppermute | solution.py:217
  2.4 0.7 %copy-start.2 = (bf16[8,768]{1,0:T(8,128)(2,1)S(1)}, bf16[8,768]{1,0:T(8,128)(2,1)}, u32[]{:S(2)}) copy-start(bf16[8,768]{1,0:T(8,128)(2,1)} %a_ref.1) | copy-start | bytes 36868
  4.0 8.7 %copy-start = (bf16[2048,1000]{0,1:T(8,128)(2,1)S(1)}, bf16[2048,1000]{0,1:T(8,128)(2,1)}, u32[]{:S(2)}) copy-start(bf16[2048,1000]{0,1:T(8,128)(2,1)} %param.5) | copy-start | bytes 12288004
  4.0 8.7 %copy-start.1 = (bf16[2048,768]{1,0:T(8,128)(2,1)S(1)}, bf16[2048,768]{1,0:T(8,128)(2,1)}, u32[]{:S(2)}) copy-start(bf16[2048,768]{1,0:T(8,128)(2,1)} %k_ref.1) | copy-start | bytes 9437188
  4.0 1.6 %collective-permute-start.1 = (bf16[16,768]{1,0:T(8,128)(2,1)S(1)}, bf16[16,768]{1,0:T(8,128)(2,1)S(1)}, u32[]{:S(2)}, u32[]{:S(2)}) collective-permute-start(bf16[16,768]{1,0:T(8,128)(2,1)S(1)} %shard_map.38.a_ref), channel_id=1, source_target_pairs={{0,4},{1,5},{2,6},{3,7},{4,0},{5,1},{6,2},{7,3},{8,12},{9,13},{10,... | collective-permute-start | bytes 73736 | tf_op jit(solution)/shard_map/ppermute | solution.py:217
  5.6 5.9 %collective-permute-start.3 = (bf16[32,768]{1,0:T(8,128)(2,1)S(1)}, bf16[32,768]{1,0:T(8,128)(2,1)S(1)}, u32[]{:S(2)}, u32[]{:S(2)}) collective-permute-start(bf16[32,768]{1,0:T(8,128)(2,1)S(1)} %shard_map.39.own_ref), channel_id=1, source_target_pairs={{0,2},{1,3},{2,0},{3,1},{4,7},{5,6},{6,5},{7,4},{8,10},{9,11},{10,... | collective-permute-start | bytes 147464 | tf_op jit(solution)/shard_map/ppermute | solution.py:220
  8.7 3.5 %collective-permute-start.2 = (bf16[32,768]{1,0:T(8,128)(2,1)S(1)}, bf16[32,768]{1,0:T(8,128)(2,1)S(1)}, u32[]{:S(2)}, u32[]{:S(2)}) collective-permute-start(bf16[32,768]{1,0:T(8,128)(2,1)S(1)} %shard_map.39.own_ref), channel_id=1, source_target_pairs={{0,5},{1,4},{2,7},{3,6},{4,1},{5,0},{6,3},{7,2},{8,13},{9,12},{10,... | collective-permute-start | bytes 147464 | tf_op jit(solution)/shard_map/ppermute | solution.py:217
  11.5 1.2 %collective-permute-start.4 = (bf16[32,768]{1,0:T(8,128)(2,1)S(1)}, bf16[32,768]{1,0:T(8,128)(2,1)S(1)}, u32[]{:S(2)}, u32[]{:S(2)}) collective-permute-start(bf16[32,768]{1,0:T(8,128)(2,1)S(1)} %collective-permute-done.3.far_ref), channel_id=1, source_target_pairs={{0,4},{1,5},{2,6},{3,7},{4,0},{5,1},{6,2},{7,3},{8,12},{9,13},{10,... | collective-permute-start | bytes 147464 | tf_op jit(solution)/shard_map/ppermute | solution.py:217
  15.4 1.4 %collective-permute-start.8 = (bf16[32,1024]{1,0:T(8,128)(2,1)S(1)}, bf16[32,1024]{1,0:T(8,128)(2,1)S(1)}, u32[]{:S(2)}, u32[]{:S(2)}) collective-permute-start(bf16[32,1024]{1,0:T(8,128)(2,1)S(1)} %get-tuple-element.16), channel_id=1, source_target_pairs={{0,4},{1,5},{2,6},{3,7},{4,0},{5,1},{6,2},{7,3},{8,12},{9,13},{10,... | collective-permute-start | bytes 196616 | tf_op jit(solution)/shard_map/ppermute | solution.py:217
  15.9 2.8 %collective-permute-start.5 = (bf16[32,1024]{1,0:T(8,128)(2,1)S(1)}, bf16[32,1024]{1,0:T(8,128)(2,1)S(1)}, u32[]{:S(2)}, u32[]{:S(2)}) collective-permute-start(bf16[32,1024]{1,0:T(8,128)(2,1)S(1)} %get-tuple-element.12), channel_id=1, source_target_pairs={{0,4},{1,5},{2,6},{3,7},{4,0},{5,1},{6,2},{7,3},{8,12},{9,13},{10,... | collective-permute-start | bytes 196616 | tf_op jit(solution)/shard_map/ppermute | solution.py:217
  16.9 4.0 %collective-permute-start.9 = (bf16[16,1024]{1,0:T(8,128)(2,1)S(1)}, bf16[16,1024]{1,0:T(8,128)(2,1)S(1)}, u32[]{:S(2)}, u32[]{:S(2)}) collective-permute-start(bf16[16,1024]{1,0:T(8,128)(2,1)S(1)} %shard_map.45), channel_id=1, source_target_pairs={{0,8},{1,9},{2,10},{3,11},{4,12},{5,13},{6,14},{7,15},{8,0},{9,1},... | collective-permute-start | bytes 98312 | tf_op jit(solution)/shard_map/ppermute | solution.py:217
  18.8 5.0 %collective-permute-start.6 = (bf16[16,1024]{1,0:T(8,128)(2,1)S(1)}, bf16[16,1024]{1,0:T(8,128)(2,1)S(1)}, u32[]{:S(2)}, u32[]{:S(2)}) collective-permute-start(bf16[16,1024]{1,0:T(8,128)(2,1)S(1)} %shard_map.42), channel_id=1, source_target_pairs={{0,8},{1,9},{2,10},{3,11},{4,12},{5,13},{6,14},{7,15},{8,0},{9,1},... | collective-permute-start | bytes 98312 | tf_op jit(solution)/shard_map/ppermute | solution.py:217
  21.0 4.9 %collective-permute-start.10 = (bf16[16,1024]{1,0:T(8,128)(2,1)S(1)}, bf16[16,1024]{1,0:T(8,128)(2,1)S(1)}, u32[]{:S(2)}, u32[]{:S(2)}) collective-permute-start(bf16[16,1024]{1,0:T(8,128)(2,1)S(1)} %shard_map.46), channel_id=1, source_target_pairs={{0,2},{1,3},{2,0},{3,1},{4,7},{5,6},{6,5},{7,4},{8,10},{9,11},{10,... | collective-permute-start | bytes 98312 | tf_op jit(solution)/shard_map/ppermute | solution.py:220
  23.9 3.2 %collective-permute-start.7 = (bf16[8,1024]{1,0:T(8,128)(2,1)S(1)}, bf16[8,1024]{1,0:T(8,128)(2,1)S(1)}, u32[]{:S(2)}, u32[]{:S(2)}) collective-permute-start(bf16[8,1024]{1,0:T(8,128)(2,1)S(1)} %get-tuple-element.14), channel_id=1, source_target_pairs={{0,5},{1,4},{2,7},{3,6},{4,1},{5,0},{6,3},{7,2},{8,13},{9,12},{10,... | collective-permute-start | bytes 49160 | tf_op jit(solution)/shard_map/ppermute | solution.py:217
  25.9 1.2 %collective-permute-start.11 = (bf16[8,1024]{1,0:T(8,128)(2,1)S(1)}, bf16[8,1024]{1,0:T(8,128)(2,1)S(1)}, u32[]{:S(2)}, u32[]{:S(2)}) collective-permute-start(bf16[8,1024]{1,0:T(8,128)(2,1)S(1)} %shard_map.47), channel_id=1, source_target_pairs={{0,4},{1,5},{2,6},{3,7},{4,0},{5,1},{6,2},{7,3},{8,12},{9,13},{10,... | collective-permute-start | bytes 49160 | tf_op jit(solution)/shard_map/ppermute | solution.py:217

commit v9 on v8

--- a/solution.py
+++ b/solution.py
@@ -151,9 +151,9 @@
     parts = (peaks + jnp.log(totals), tiles(votes))
     far_send, near_send, far_keep, near_keep = out_refs
     encode(far_send, 0, rows_of(parts, *rows(3, 0), *rows(3, 1)), classes)
-    encode(near_send, 0, rows_of(parts, *rows(0, 1), *rows(1, 1)), classes)
+    encode(near_send, 0, rows_of(parts, *rows(0, 1), *rows(1, 0)), classes)
     keep(far_keep, 0, rows_of(parts, *rows(2, 0), *rows(2, 1)), classes)
-    keep(near_keep, 0, rows_of(parts, *rows(0, 0), *rows(1, 0)), classes)
+    keep(near_keep, 0, rows_of(parts, *rows(0, 0), *rows(1, 1)), classes)
 
 
 def stats(blocks, keys, labels_t, unit):
@@ -217,7 +217,11 @@
         return lax.ppermute(block, AXES, [(i, i ^ bit) for i in range(size)])
 
     def swap_far(block):
-        return lax.ppermute(block, AXES, [(i, i ^ (3 if i & core else 2)) for i in range(size)])
+        def partner(i):
+            inner = (i ^ i >> 1) & 1
+            return i ^ 3 if bool(i & core) != bool(inner) else i ^ 2 ^ core
+
+        return lax.ppermute(block, AXES, [(i, partner(i)) for i in range(size)])
 
     classes = bank_labels.shape[1]
     first, *rest = [bit ^ core for bit in lead] + [core]
@@ -239,7 +243,7 @@
     (far,) = merge(far, far_came, classes, 0, 2, encode)
     own, near = merge(near, near_came, classes, 0, 2, keep, encode)
     far = swap_far(far)
-    near = swap(near, 1 ^ core)
+    near = swap(near, 1)
     across = swap(tail(far), core)
     return finish(own, near, far, across, classes)
 

time: 28.1 us -> 27.5 us (0.979)
  waiting for transfers between devices: 10.9 us -> 8.53 us
  starting transfers between devices: 12 us -> 13.9 us
    ppermute x10, starting transfers between devices: 6.24 us -> 10.4 us  [swap(): return lax.ppermute(block, AXES, [(i, i ^ bit) for i in range(size)])]
    ppermute x2, waiting for transfers between devices: 4.64 us -> 1.54 us  [swap_far(): return lax.ppermute(block, AXES, [(i, partner(i)) for i in range(size)])]
    ppermute x2, starting transfers between devices: 5.78 us -> 3.46 us  [swap_far(): return lax.ppermute(block, AXES, [(i, partner(i)) for i in range(size)])]
    ppermute x10, waiting for transfers between devices: 6.27 us -> 7 us  [swap(): return lax.ppermute(block, AXES, [(i, i ^ bit) for i in range(size)])]
  transfers between devices with their start and end apart: 12 -> 12, of which waited for: 9 -> 10; matrix products, arithmetic and copies ran while one was open for 0% -> 0% of each run, Pallas kernels for 3% -> 3%
where the time goes in v9:
time: 27.5 us; the launch traced here: 27.3 us
  starting transfers between devices  13.9 us (51%)
  waiting for transfers between devices  8.53 us (31%)
  Pallas kernels  4.14 us (15%)
  local copies, waits for them, and re-layouts  0.75 us (3%)
    ppermute x10, starting transfers between devices, swap(): return lax.ppermute(block, AXES, [(i, i ^ bit) for i in range(size)])  10.4 us
    ppermute x10, waiting for transfers between devices, swap(): return lax.ppermute(block, AXES, [(i, i ^ bit) for i in range(size)])  7 us
    pallas_call x12, Pallas kernels, call(): pl.pallas_call(kernel, out_shape=outs, in_specs=[VMEM] * len(args), out_s...  4.14 us
    ppermute x2, starting transfers between devices, swap_far(): return lax.ppermute(block, AXES, [(i, partner(i)) for i in range(size)])  3.46 us
    ppermute x2, waiting for transfers between devices, swap_far(): return lax.ppermute(block, AXES, [(i, partner(i)) for i in range(size)])  1.54 us
    unnamed x6, local copies, waits for them, and re-layouts  0.75 us
  transfers between devices with their start and end apart: 12, of which 10 were waited for; matrix products, arithmetic and copies ran while one was open for 0% of the time, Pallas kernels for 3%

profile of v9, /device:TPU:0, one launch (start us, length us, event | category | flops | bytes accessed | tf_op | source)
XLA Modules:
  0.0 27.3 jit_solution(6393141481840817658)
XLA Ops:
  0.0 2.4 %collective-permute-start = (bf16[8,768]{1,0:T(8,128)(2,1)}, bf16[8,768]{1,0:T(8,128)(2,1)S(1)}, u32[]{:S(2)}, u32[]{:S(2)}) collective-permute-start(bf16[8,768]{1,0:T(8,128)(2,1)} %a_ref.1), channel_id=1, source_target_pairs={{0,12},{1,13},{2,14},{3,15},{4,8},{5,9},{6,10},{7,11},{8,4},{9,5},... | collective-permute-start | bytes 36872 | tf_op jit(solution)/shard_map/ppermute | solution.py:217
  2.4 0.7 %copy-done.2 = bf16[8,768]{1,0:T(8,128)(2,1)S(1)} copy-done((bf16[8,768]{1,0:T(8,128)(2,1)S(1)}, bf16[8,768]{1,0:T(8,128)(2,1)}, u32[]{:S(2)}) %copy-start.2) | copy-done | bytes 12312
  3.1 0.9 %collective-permute-done.b_ref = bf16[8,768]{1,0:T(8,128)(2,1)S(1)} collective-permute-done((bf16[8,768]{1,0:T(8,128)(2,1)}, bf16[8,768]{1,0:T(8,128)(2,1)S(1)}, u32[]{:S(2)}, u32[]{:S(2)}) %collective-permute-start) | collective-permute-done | bytes 12320 | tf_op jit(solution)/shard_map/ppermute | solution.py:217
  4.0 0.7 %collective-permute-start.1 = (bf16[16,768]{1,0:T(8,128)(2,1)S(1)}, bf16[16,768]{1,0:T(8,128)(2,1)S(1)}, u32[]{:S(2)}, u32[]{:S(2)}) collective-permute-start(bf16[16,768]{1,0:T(8,128)(2,1)S(1)} %shard_map.38.a_ref), channel_id=1, source_target_pairs={{0,4},{1,5},{2,6},{3,7},{4,0},{5,1},{6,2},{7,3},{8,12},{9,13},{10,... | collective-permute-start | bytes 73736 | tf_op jit(solution)/shard_map/ppermute | solution.py:217
  4.7 0.8 %collective-permute-done.1.b_ref = bf16[16,768]{1,0:T(8,128)(2,1)S(1)} collective-permute-done((bf16[16,768]{1,0:T(8,128)(2,1)S(1)}, bf16[16,768]{1,0:T(8,128)(2,1)S(1)}, u32[]{:S(2)}, u32[]{:S(2)}) %collective-permute-start.1) | collective-permute-done | bytes 24608 | tf_op jit(solution)/shard_map/ppermute | solution.py:217
  5.6 2.9 %collective-permute-start.3 = (bf16[32,768]{1,0:T(8,128)(2,1)S(1)}, bf16[32,768]{1,0:T(8,128)(2,1)S(1)}, u32[]{:S(2)}, u32[]{:S(2)}) collective-permute-start(bf16[32,768]{1,0:T(8,128)(2,1)S(1)} %shard_map.39.own_ref), channel_id=1, source_target_pairs={{0,6},{1,2},{2,1},{3,5},{4,7},{5,3},{6,0},{7,4},{8,14},{9,10},{10,... | collective-permute-start | bytes 147464 | tf_op jit(solution)/shard_map/ppermute | solution.py:224
  8.5 1.5 %collective-permute-start.2 = (bf16[32,768]{1,0:T(8,128)(2,1)S(1)}, bf16[32,768]{1,0:T(8,128)(2,1)S(1)}, u32[]{:S(2)}, u32[]{:S(2)}) collective-permute-start(bf16[32,768]{1,0:T(8,128)(2,1)S(1)} %shard_map.39.own_ref), channel_id=1, source_target_pairs={{0,5},{1,4},{2,7},{3,6},{4,1},{5,0},{6,3},{7,2},{8,13},{9,12},{10,... | collective-permute-start | bytes 147464 | tf_op jit(solution)/shard_map/ppermute | solution.py:217
  10.0 0.3 collective-permute-done.3.far_ref
  10.3 0.9 %collective-permute-start.4 = (bf16[32,768]{1,0:T(8,128)(2,1)S(1)}, bf16[32,768]{1,0:T(8,128)(2,1)S(1)}, u32[]{:S(2)}, u32[]{:S(2)}) collective-permute-start(bf16[32,768]{1,0:T(8,128)(2,1)S(1)} %collective-permute-done.3.far_ref), channel_id=1, source_target_pairs={{0,4},{1,5},{2,6},{3,7},{4,0},{5,1},{6,2},{7,3},{8,12},{9,13},{10,... | collective-permute-start | bytes 147464 | tf_op jit(solution)/shard_map/ppermute | solution.py:217
  11.2 0.8 %collective-permute-done.2.near_ref = bf16[32,768]{1,0:T(8,128)(2,1)S(1)} collective-permute-done((bf16[32,768]{1,0:T(8,128)(2,1)S(1)}, bf16[32,768]{1,0:T(8,128)(2,1)S(1)}, u32[]{:S(2)}, u32[]{:S(2)}) %collective-permute-start.2) | collective-permute-done | bytes 49184 | tf_op jit(solution)/shard_map/ppermute | solution.py:217
  12.0 0.1 collective-permute-done.4.across_ref
  12.1 2.7 %shard_map.40 = (bf16[32,1024]{1,0:T(8,128)(2,1)S(1)}, bf16[32,1024]{1,0:T(8,128)(2,1)S(1)}, f32[32,1024]{1,0:T(8,128)S(1)}, f32[32,1024]{1,0:T(8,128)S(1)}) custom-call(bf16[32,768]{1,0:T(8,128)(2,1)S(1)} %shard_map.39.own_ref, bf16[32,768]{1,0:T(8,128)(2,1)S(1)} %collective-permute-done.2.near_ref, bf16[32,768]{1,0:T(8,128)(2,1)S(1)} %collective-permute-done.3.far_ref, ...), custom_call_target="tpu_custom_call" | custom-call | flops 926941184 | bytes 7241728 | tf_op jit(solution)/shard_map/pallas_call | solution.py:27
  14.8 1.1 %collective-permute-start.8 = (bf16[32,1024]{1,0:T(8,128)(2,1)S(1)}, bf16[32,1024]{1,0:T(8,128)(2,1)S(1)}, u32[]{:S(2)}, u32[]{:S(2)}) collective-permute-start(bf16[32,1024]{1,0:T(8,128)(2,1)S(1)} %get-tuple-element.16), channel_id=1, source_target_pairs={{0,4},{1,5},{2,6},{3,7},{4,0},{5,1},{6,2},{7,3},{8,12},{9,13},{10,... | collective-permute-start | bytes 196616 | tf_op jit(solution)/shard_map/ppermute | solution.py:217
  15.9 0.1 collective-permute-start.5
  16.0 0.8 %collective-permute-done.8.other_ref = bf16[32,1024]{1,0:T(8,128)(2,1)S(1)} collective-permute-done((bf16[32,1024]{1,0:T(8,128)(2,1)S(1)}, bf16[32,1024]{1,0:T(8,128)(2,1)S(1)}, u32[]{:S(2)}, u32[]{:S(2)}) %collective-permute-start.8) | collective-permute-done | bytes 65568 | tf_op jit(solution)/shard_map/ppermute | solution.py:217
  16.8 0.1 shard_map.45
  16.9 1.6 %collective-permute-start.9 = (bf16[16,1024]{1,0:T(8,128)(2,1)S(1)}, bf16[16,1024]{1,0:T(8,128)(2,1)S(1)}, u32[]{:S(2)}, u32[]{:S(2)}) collective-permute-start(bf16[16,1024]{1,0:T(8,128)(2,1)S(1)} %shard_map.45), channel_id=1, source_target_pairs={{0,8},{1,9},{2,10},{3,11},{4,12},{5,13},{6,14},{7,15},{8,0},{9,1},... | collective-permute-start | bytes 98312 | tf_op jit(solution)/shard_map/ppermute | solution.py:217
  18.5 0.1 shard_map.42
  18.7 0.6 %collective-permute-start.6 = (bf16[16,1024]{1,0:T(8,128)(2,1)S(1)}, bf16[16,1024]{1,0:T(8,128)(2,1)S(1)}, u32[]{:S(2)}, u32[]{:S(2)}) collective-permute-start(bf16[16,1024]{1,0:T(8,128)(2,1)S(1)} %shard_map.42), channel_id=1, source_target_pairs={{0,8},{1,9},{2,10},{3,11},{4,12},{5,13},{6,14},{7,15},{8,0},{9,1},... | collective-permute-start | bytes 98312 | tf_op jit(solution)/shard_map/ppermute | solution.py:217
  19.2 0.1 shard_map.44.mine_ref
  19.3 1.6 %collective-permute-done.9.other_ref = bf16[16,1024]{1,0:T(8,128)(2,1)S(1)} collective-permute-done((bf16[16,1024]{1,0:T(8,128)(2,1)S(1)}, bf16[16,1024]{1,0:T(8,128)(2,1)S(1)}, u32[]{:S(2)}, u32[]{:S(2)}) %collective-permute-start.9) | collective-permute-done | bytes 32800 | tf_op jit(solution)/shard_map/ppermute | solution.py:217
  20.9 0.1 shard_map.46
  21.0 0.5 %collective-permute-start.10 = (bf16[16,1024]{1,0:T(8,128)(2,1)S(1)}, bf16[16,1024]{1,0:T(8,128)(2,1)S(1)}, u32[]{:S(2)}, u32[]{:S(2)}) collective-permute-start(bf16[16,1024]{1,0:T(8,128)(2,1)S(1)} %shard_map.46), channel_id=1, source_target_pairs={{0,6},{1,2},{2,1},{3,5},{4,7},{5,3},{6,0},{7,4},{8,14},{9,10},{10,... | collective-permute-start | bytes 98312 | tf_op jit(solution)/shard_map/ppermute | solution.py:224
  21.6 0.1 shard_map.41.mine_ref
  21.7 1.0 %collective-permute-done.6.other_ref = bf16[16,1024]{1,0:T(8,128)(2,1)S(1)} collective-permute-done((bf16[16,1024]{1,0:T(8,128)(2,1)S(1)}, bf16[16,1024]{1,0:T(8,128)(2,1)S(1)}, u32[]{:S(2)}, u32[]{:S(2)}) %collective-permute-start.6) | collective-permute-done | bytes 32800 | tf_op jit(solution)/shard_map/ppermute | solution.py:217
  22.6 0.1 shard_map.43
  22.8 1.4 %collective-permute-start.7 = (bf16[8,1024]{1,0:T(8,128)(2,1)S(1)}, bf16[8,1024]{1,0:T(8,128)(2,1)S(1)}, u32[]{:S(2)}, u32[]{:S(2)}) collective-permute-start(bf16[8,1024]{1,0:T(8,128)(2,1)S(1)} %get-tuple-element.14), channel_id=1, source_target_pairs={{0,1},{1,0},{2,3},{3,2},{4,5},{5,4},{6,7},{7,6},{8,9},{9,8},{10,11... | collective-permute-start | bytes 49160 | tf_op jit(solution)/shard_map/ppermute | solution.py:217
  24.1 1.3 %collective-permute-done.10.a_ref.far_ref = bf16[16,1024]{1,0:T(8,128)(2,1)S(1)} collective-permute-done((bf16[16,1024]{1,0:T(8,128)(2,1)S(1)}, bf16[16,1024]{1,0:T(8,128)(2,1)S(1)}, u32[]{:S(2)}, u32[]{:S(2)}) %collective-permute-start.10) | collective-permute-done | bytes 32800 | tf_op jit(solution)/shard_map/ppermute | solution.py:224
  25.4 0.1 collective-permute-start.11
  25.6 1.0 %collective-permute-done.7.near_ref = bf16[8,1024]{1,0:T(8,128)(2,1)S(1)} collective-permute-done((bf16[8,1024]{1,0:T(8,128)(2,1)S(1)}, bf16[8,1024]{1,0:T(8,128)(2,1)S(1)}, u32[]{:S(2)}, u32[]{:S(2)}) %collective-permute-start.7) | collective-permute-done | bytes 16416 | tf_op jit(solution)/shard_map/ppermute | solution.py:217
  26.6 0.0 collective-permute-done.11.across_ref
  26.6 0.7 %shard_map.48 = f32[8,1000]{1,0:T(8,128)} custom-call(f32[8,1024]{1,0:T(8,128)S(1)} %get-tuple-element.13.own_ref, bf16[8,1024]{1,0:T(8,128)(2,1)S(1)} %collective-permute-done.7.near_ref, bf16[16,1024]{1,0:T(8,128)(2,1)S(1)} %collective-permute-done.10.a_ref.far_ref, bf16[8,1024]{1,0:T(8,128)(2,1)S(1)} %collective-permute-done.11.across_ref), custom_call_target="tpu_custom_call" | custom-call | tf_op jit(solution)/shard_map/pallas_call | solution.py:27
  (10 shorter events, 0.0 us)
Async XLA Ops:
  0.0 4.0 %collective-permute-start = (bf16[8,768]{1,0:T(8,128)(2,1)}, bf16[8,768]{1,0:T(8,128)(2,1)S(1)}, u32[]{:S(2)}, u32[]{:S(2)}) collective-permute-start(bf16[8,768]{1,0:T(8,128)(2,1)} %a_ref.1), channel_id=1, source_target_pairs={{0,12},{1,13},{2,14},{3,15},{4,8},{5,9},{6,10},{7,11},{8,4},{9,5},... | collective-permute-start | bytes 36872 | tf_op jit(solution)/shard_map/ppermute | solution.py:217
  2.4 0.7 %copy-start.2 = (bf16[8,768]{1,0:T(8,128)(2,1)S(1)}, bf16[8,768]{1,0:T(8,128)(2,1)}, u32[]{:S(2)}) copy-start(bf16[8,768]{1,0:T(8,128)(2,1)} %a_ref.1) | copy-start | bytes 36868
  4.0 8.1 %copy-start = (bf16[2048,1000]{0,1:T(8,128)(2,1)S(1)}, bf16[2048,1000]{0,1:T(8,128)(2,1)}, u32[]{:S(2)}) copy-start(bf16[2048,1000]{0,1:T(8,128)(2,1)} %param.5) | copy-start | bytes 12288004
  4.0 8.1 %copy-start.1 = (bf16[2048,768]{1,0:T(8,128)(2,1)S(1)}, bf16[2048,768]{1,0:T(8,128)(2,1)}, u32[]{:S(2)}) copy-start(bf16[2048,768]{1,0:T(8,128)(2,1)} %k_ref.1) | copy-start | bytes 9437188
  4.0 1.6 %collective-permute-start.1 = (bf16[16,768]{1,0:T(8,128)(2,1)S(1)}, bf16[16,768]{1,0:T(8,128)(2,1)S(1)}, u32[]{:S(2)}, u32[]{:S(2)}) collective-permute-start(bf16[16,768]{1,0:T(8,128)(2,1)S(1)} %shard_map.38.a_ref), channel_id=1, source_target_pairs={{0,4},{1,5},{2,6},{3,7},{4,0},{5,1},{6,2},{7,3},{8,12},{9,13},{10,... | collective-permute-start | bytes 73736 | tf_op jit(solution)/shard_map/ppermute | solution.py:217
  5.6 4.7 %collective-permute-start.3 = (bf16[32,768]{1,0:T(8,128)(2,1)S(1)}, bf16[32,768]{1,0:T(8,128)(2,1)S(1)}, u32[]{:S(2)}, u32[]{:S(2)}) collective-permute-start(bf16[32,768]{1,0:T(8,128)(2,1)S(1)} %shard_map.39.own_ref), channel_id=1, source_target_pairs={{0,6},{1,2},{2,1},{3,5},{4,7},{5,3},{6,0},{7,4},{8,14},{9,10},{10,... | collective-permute-start | bytes 147464 | tf_op jit(solution)/shard_map/ppermute | solution.py:224
  8.5 3.5 %collective-permute-start.2 = (bf16[32,768]{1,0:T(8,128)(2,1)S(1)}, bf16[32,768]{1,0:T(8,128)(2,1)S(1)}, u32[]{:S(2)}, u32[]{:S(2)}) collective-permute-start(bf16[32,768]{1,0:T(8,128)(2,1)S(1)} %shard_map.39.own_ref), channel_id=1, source_target_pairs={{0,5},{1,4},{2,7},{3,6},{4,1},{5,0},{6,3},{7,2},{8,13},{9,12},{10,... | collective-permute-start | bytes 147464 | tf_op jit(solution)/shard_map/ppermute | solution.py:217
  10.3 1.8 %collective-permute-start.4 = (bf16[32,768]{1,0:T(8,128)(2,1)S(1)}, bf16[32,768]{1,0:T(8,128)(2,1)S(1)}, u32[]{:S(2)}, u32[]{:S(2)}) collective-permute-start(bf16[32,768]{1,0:T(8,128)(2,1)S(1)} %collective-permute-done.3.far_ref), channel_id=1, source_target_pairs={{0,4},{1,5},{2,6},{3,7},{4,0},{5,1},{6,2},{7,3},{8,12},{9,13},{10,... | collective-permute-start | bytes 147464 | tf_op jit(solution)/shard_map/ppermute | solution.py:217
  14.8 2.0 %collective-permute-start.8 = (bf16[32,1024]{1,0:T(8,128)(2,1)S(1)}, bf16[32,1024]{1,0:T(8,128)(2,1)S(1)}, u32[]{:S(2)}, u32[]{:S(2)}) collective-permute-start(bf16[32,1024]{1,0:T(8,128)(2,1)S(1)} %get-tuple-element.16), channel_id=1, source_target_pairs={{0,4},{1,5},{2,6},{3,7},{4,0},{5,1},{6,2},{7,3},{8,12},{9,13},{10,... | collective-permute-start | bytes 196616 | tf_op jit(solution)/shard_map/ppermute | solution.py:217
  15.9 2.6 %collective-permute-start.5 = (bf16[32,1024]{1,0:T(8,128)(2,1)S(1)}, bf16[32,1024]{1,0:T(8,128)(2,1)S(1)}, u32[]{:S(2)}, u32[]{:S(2)}) collective-permute-start(bf16[32,1024]{1,0:T(8,128)(2,1)S(1)} %get-tuple-element.12), channel_id=1, source_target_pairs={{0,4},{1,5},{2,6},{3,7},{4,0},{5,1},{6,2},{7,3},{8,12},{9,13},{10,... | collective-permute-start | bytes 196616 | tf_op jit(solution)/shard_map/ppermute | solution.py:217
  16.9 4.0 %collective-permute-start.9 = (bf16[16,1024]{1,0:T(8,128)(2,1)S(1)}, bf16[16,1024]{1,0:T(8,128)(2,1)S(1)}, u32[]{:S(2)}, u32[]{:S(2)}) collective-permute-start(bf16[16,1024]{1,0:T(8,128)(2,1)S(1)} %shard_map.45), channel_id=1, source_target_pairs={{0,8},{1,9},{2,10},{3,11},{4,12},{5,13},{6,14},{7,15},{8,0},{9,1},... | collective-permute-start | bytes 98312 | tf_op jit(solution)/shard_map/ppermute | solution.py:217
  18.7 4.0 %collective-permute-start.6 = (bf16[16,1024]{1,0:T(8,128)(2,1)S(1)}, bf16[16,1024]{1,0:T(8,128)(2,1)S(1)}, u32[]{:S(2)}, u32[]{:S(2)}) collective-permute-start(bf16[16,1024]{1,0:T(8,128)(2,1)S(1)} %shard_map.42), channel_id=1, source_target_pairs={{0,8},{1,9},{2,10},{3,11},{4,12},{5,13},{6,14},{7,15},{8,0},{9,1},... | collective-permute-start | bytes 98312 | tf_op jit(solution)/shard_map/ppermute | solution.py:217
  21.0 4.4 %collective-permute-start.10 = (bf16[16,1024]{1,0:T(8,128)(2,1)S(1)}, bf16[16,1024]{1,0:T(8,128)(2,1)S(1)}, u32[]{:S(2)}, u32[]{:S(2)}) collective-permute-start(bf16[16,1024]{1,0:T(8,128)(2,1)S(1)} %shard_map.46), channel_id=1, source_target_pairs={{0,6},{1,2},{2,1},{3,5},{4,7},{5,3},{6,0},{7,4},{8,14},{9,10},{10,... | collective-permute-start | bytes 98312 | tf_op jit(solution)/shard_map/ppermute | solution.py:224
  22.8 3.8 %collective-permute-start.7 = (bf16[8,1024]{1,0:T(8,128)(2,1)S(1)}, bf16[8,1024]{1,0:T(8,128)(2,1)S(1)}, u32[]{:S(2)}, u32[]{:S(2)}) collective-permute-start(bf16[8,1024]{1,0:T(8,128)(2,1)S(1)} %get-tuple-element.14), channel_id=1, source_target_pairs={{0,1},{1,0},{2,3},{3,2},{4,5},{5,4},{6,7},{7,6},{8,9},{9,8},{10,11... | collective-permute-start | bytes 49160 | tf_op jit(solution)/shard_map/ppermute | solution.py:217
  25.4 1.2 %collective-permute-start.11 = (bf16[8,1024]{1,0:T(8,128)(2,1)S(1)}, bf16[8,1024]{1,0:T(8,128)(2,1)S(1)}, u32[]{:S(2)}, u32[]{:S(2)}) collective-permute-start(bf16[8,1024]{1,0:T(8,128)(2,1)S(1)} %shard_map.47), channel_id=1, source_target_pairs={{0,4},{1,5},{2,6},{3,7},{4,0},{5,1},{6,2},{7,3},{8,12},{9,13},{10,... | collective-permute-start | bytes 49160 | tf_op jit(solution)/shard_map/ppermute | solution.py:217

commit v10 on v9

--- a/solution.py
+++ b/solution.py
@@ -125,18 +125,15 @@
     queries = jnp.concatenate(
         [own_ref[...], near_ref[...], far_ref[...], across_ref[...]], axis=0
     )
-    scores = lax.dot_general(
-        queries, k_ref[...], (((1,), (1,)), ((), ())), preferred_element_type=jnp.float32
-    ) * (SCORE_GAIN / math.sqrt(width))
-    peaks = jnp.max(scores, axis=1, keepdims=True)
-    weights = jnp.exp(scores - peaks)
-    totals = jnp.sum(weights, axis=1, keepdims=True)
-    votes = lax.dot_general(
-        weights.astype(jnp.bfloat16),
-        lt_ref[...],
-        (((1,), (1,)), ((), ())),
-        preferred_element_type=jnp.float32,
-    )
+    gain = SCORE_GAIN / math.sqrt(width)
+    dot = functools.partial(lax.dot_general, preferred_element_type=jnp.float32)
+    by_rows, by_columns = (((1,), (1,)), ((), ())), (((1,), (0,)), ((), ()))
+    chunks = [slice(lo, lo + 256) for lo in range(0, k_ref.shape[0], 256)]
+    scores = [dot(k_ref[at], queries, by_rows) * gain for at in chunks]
+    peaks = jnp.max(functools.reduce(jnp.maximum, scores), axis=0, keepdims=True)
+    weights = [jnp.exp(s - peaks) for s in scores]
+    totals = jnp.sum(sum(weights), axis=0, keepdims=True)
+    weights = jnp.concatenate([w.astype(jnp.bfloat16) for w in weights], axis=0)
 
     slots = half // unit
     odd = [n.bit_count() % 2 for n in range(slots)]
@@ -145,10 +142,11 @@
         starts = [block * count + (n + slots * (other_core ^ o)) * unit for n, o in enumerate(odd)]
         return [(lo, lo + unit) for lo in starts]
 
-    votes = votes * (1 / totals)
-    spare = out_refs[0].shape[1] - classes
-    votes = jnp.concatenate([votes, jnp.ones((4 * count, spare), jnp.float32)], axis=1)
-    parts = (peaks + jnp.log(totals), tiles(votes))
+    share = 1 / totals
+    votes = dot(lt_ref[...], weights, by_columns) * share
+    spare = jnp.ones((out_refs[0].shape[1] - classes, 4 * count), jnp.float32)
+    averages = tiles(jnp.concatenate([votes, spare], axis=0).T)
+    parts = ((peaks + jnp.log(totals)).T, averages)
     far_send, near_send, far_keep, near_keep = out_refs
     encode(far_send, 0, rows_of(parts, *rows(3, 0), *rows(3, 1)), classes)
     encode(near_send, 0, rows_of(parts, *rows(0, 1), *rows(1, 0)), classes)

time: 27.5 us -> 27.4 us (level)
  no operation moved by 1% of the time
where the time goes in v10:
time: 27.4 us; the launch traced here: 27.1 us
  starting transfers between devices  13.9 us (51%)
  waiting for transfers between devices  8.52 us (31%)
  Pallas kernels  3.96 us (14%)
  local copies, waits for them, and re-layouts  0.75 us (3%)
    ppermute x10, starting transfers between devices, swap(): return lax.ppermute(block, AXES, [(i, i ^ bit) for i in range(size)])  10.4 us
    ppermute x10, waiting for transfers between devices, swap(): return lax.ppermute(block, AXES, [(i, i ^ bit) for i in range(size)])  6.97 us
    pallas_call x12, Pallas kernels, call(): pl.pallas_call(kernel, out_shape=outs, in_specs=[VMEM] * len(args), out_s...  3.96 us
    ppermute x2, starting transfers between devices, swap_far(): return lax.ppermute(block, AXES, [(i, partner(i)) for i in range(size)])  3.46 us
    ppermute x2, waiting for transfers between devices, swap_far(): return lax.ppermute(block, AXES, [(i, partner(i)) for i in range(size)])  1.55 us
    unnamed x6, local copies, waits for them, and re-layouts  0.75 us
  transfers between devices with their start and end apart: 12, of which 10 were waited for; matrix products, arithmetic and copies ran while one was open for 0% of the time, Pallas kernels for 3%

profile of v10, /device:TPU:0, one launch (start us, length us, event | category | flops | bytes accessed | tf_op | source)
XLA Modules:
  0.0 27.1 jit_solution(13819297051765386282)
XLA Ops:
  0.0 2.4 %collective-permute-start = (bf16[8,768]{1,0:T(8,128)(2,1)}, bf16[8,768]{1,0:T(8,128)(2,1)S(1)}, u32[]{:S(2)}, u32[]{:S(2)}) collective-permute-start(bf16[8,768]{1,0:T(8,128)(2,1)} %a_ref.1), channel_id=1, source_target_pairs={{0,12},{1,13},{2,14},{3,15},{4,8},{5,9},{6,10},{7,11},{8,4},{9,5},... | collective-permute-start | bytes 36872 | tf_op jit(solution)/shard_map/ppermute | solution.py:215
  2.4 0.7 %copy-done.2 = bf16[8,768]{1,0:T(8,128)(2,1)S(1)} copy-done((bf16[8,768]{1,0:T(8,128)(2,1)S(1)}, bf16[8,768]{1,0:T(8,128)(2,1)}, u32[]{:S(2)}) %copy-start.2) | copy-done | bytes 12312
  3.1 0.9 %collective-permute-done.b_ref = bf16[8,768]{1,0:T(8,128)(2,1)S(1)} collective-permute-done((bf16[8,768]{1,0:T(8,128)(2,1)}, bf16[8,768]{1,0:T(8,128)(2,1)S(1)}, u32[]{:S(2)}, u32[]{:S(2)}) %collective-permute-start) | collective-permute-done | bytes 12320 | tf_op jit(solution)/shard_map/ppermute | solution.py:215
  4.0 0.7 %collective-permute-start.1 = (bf16[16,768]{1,0:T(8,128)(2,1)S(1)}, bf16[16,768]{1,0:T(8,128)(2,1)S(1)}, u32[]{:S(2)}, u32[]{:S(2)}) collective-permute-start(bf16[16,768]{1,0:T(8,128)(2,1)S(1)} %shard_map.38.a_ref), channel_id=1, source_target_pairs={{0,4},{1,5},{2,6},{3,7},{4,0},{5,1},{6,2},{7,3},{8,12},{9,13},{10,... | collective-permute-start | bytes 73736 | tf_op jit(solution)/shard_map/ppermute | solution.py:215
  4.7 0.8 %collective-permute-done.1.b_ref = bf16[16,768]{1,0:T(8,128)(2,1)S(1)} collective-permute-done((bf16[16,768]{1,0:T(8,128)(2,1)S(1)}, bf16[16,768]{1,0:T(8,128)(2,1)S(1)}, u32[]{:S(2)}, u32[]{:S(2)}) %collective-permute-start.1) | collective-permute-done | bytes 24608 | tf_op jit(solution)/shard_map/ppermute | solution.py:215
  5.6 2.9 %collective-permute-start.3 = (bf16[32,768]{1,0:T(8,128)(2,1)S(1)}, bf16[32,768]{1,0:T(8,128)(2,1)S(1)}, u32[]{:S(2)}, u32[]{:S(2)}) collective-permute-start(bf16[32,768]{1,0:T(8,128)(2,1)S(1)} %shard_map.39.own_ref), channel_id=1, source_target_pairs={{0,6},{1,2},{2,1},{3,5},{4,7},{5,3},{6,0},{7,4},{8,14},{9,10},{10,... | collective-permute-start | bytes 147464 | tf_op jit(solution)/shard_map/ppermute | solution.py:222
  8.5 1.5 %collective-permute-start.2 = (bf16[32,768]{1,0:T(8,128)(2,1)S(1)}, bf16[32,768]{1,0:T(8,128)(2,1)S(1)}, u32[]{:S(2)}, u32[]{:S(2)}) collective-permute-start(bf16[32,768]{1,0:T(8,128)(2,1)S(1)} %shard_map.39.own_ref), channel_id=1, source_target_pairs={{0,5},{1,4},{2,7},{3,6},{4,1},{5,0},{6,3},{7,2},{8,13},{9,12},{10,... | collective-permute-start | bytes 147464 | tf_op jit(solution)/shard_map/ppermute | solution.py:215
  10.0 0.3 collective-permute-done.3.far_ref
  10.3 0.9 %collective-permute-start.4 = (bf16[32,768]{1,0:T(8,128)(2,1)S(1)}, bf16[32,768]{1,0:T(8,128)(2,1)S(1)}, u32[]{:S(2)}, u32[]{:S(2)}) collective-permute-start(bf16[32,768]{1,0:T(8,128)(2,1)S(1)} %collective-permute-done.3.far_ref), channel_id=1, source_target_pairs={{0,4},{1,5},{2,6},{3,7},{4,0},{5,1},{6,2},{7,3},{8,12},{9,13},{10,... | collective-permute-start | bytes 147464 | tf_op jit(solution)/shard_map/ppermute | solution.py:215
  11.2 0.8 %collective-permute-done.2.near_ref = bf16[32,768]{1,0:T(8,128)(2,1)S(1)} collective-permute-done((bf16[32,768]{1,0:T(8,128)(2,1)S(1)}, bf16[32,768]{1,0:T(8,128)(2,1)S(1)}, u32[]{:S(2)}, u32[]{:S(2)}) %collective-permute-start.2) | collective-permute-done | bytes 49184 | tf_op jit(solution)/shard_map/ppermute | solution.py:215
  12.0 0.1 collective-permute-done.4.across_ref
  12.1 2.5 %shard_map.40 = (bf16[32,1024]{1,0:T(8,128)(2,1)S(1)}, bf16[32,1024]{1,0:T(8,128)(2,1)S(1)}, f32[32,1024]{1,0:T(8,128)S(1)}, f32[32,1024]{1,0:T(8,128)S(1)}) custom-call(bf16[32,768]{1,0:T(8,128)(2,1)S(1)} %shard_map.39.own_ref, bf16[32,768]{1,0:T(8,128)(2,1)S(1)} %collective-permute-done.2.near_ref, bf16[32,768]{1,0:T(8,128)(2,1)S(1)} %collective-permute-done.3.far_ref, ...), custom_call_target="tpu_custom_call" | custom-call | flops 926941184 | bytes 7241728 | tf_op jit(solution)/shard_map/pallas_call | solution.py:27
  14.6 1.1 %collective-permute-start.8 = (bf16[32,1024]{1,0:T(8,128)(2,1)S(1)}, bf16[32,1024]{1,0:T(8,128)(2,1)S(1)}, u32[]{:S(2)}, u32[]{:S(2)}) collective-permute-start(bf16[32,1024]{1,0:T(8,128)(2,1)S(1)} %get-tuple-element.16), channel_id=1, source_target_pairs={{0,4},{1,5},{2,6},{3,7},{4,0},{5,1},{6,2},{7,3},{8,12},{9,13},{10,... | collective-permute-start | bytes 196616 | tf_op jit(solution)/shard_map/ppermute | solution.py:215
  15.7 0.1 collective-permute-start.5
  15.8 0.8 %collective-permute-done.8.other_ref = bf16[32,1024]{1,0:T(8,128)(2,1)S(1)} collective-permute-done((bf16[32,1024]{1,0:T(8,128)(2,1)S(1)}, bf16[32,1024]{1,0:T(8,128)(2,1)S(1)}, u32[]{:S(2)}, u32[]{:S(2)}) %collective-permute-start.8) | collective-permute-done | bytes 65568 | tf_op jit(solution)/shard_map/ppermute | solution.py:215
  16.6 0.1 shard_map.45
  16.7 1.6 %collective-permute-start.9 = (bf16[16,1024]{1,0:T(8,128)(2,1)S(1)}, bf16[16,1024]{1,0:T(8,128)(2,1)S(1)}, u32[]{:S(2)}, u32[]{:S(2)}) collective-permute-start(bf16[16,1024]{1,0:T(8,128)(2,1)S(1)} %shard_map.45), channel_id=1, source_target_pairs={{0,8},{1,9},{2,10},{3,11},{4,12},{5,13},{6,14},{7,15},{8,0},{9,1},... | collective-permute-start | bytes 98312 | tf_op jit(solution)/shard_map/ppermute | solution.py:215
  18.3 0.1 shard_map.42
  18.5 0.6 %collective-permute-start.6 = (bf16[16,1024]{1,0:T(8,128)(2,1)S(1)}, bf16[16,1024]{1,0:T(8,128)(2,1)S(1)}, u32[]{:S(2)}, u32[]{:S(2)}) collective-permute-start(bf16[16,1024]{1,0:T(8,128)(2,1)S(1)} %shard_map.42), channel_id=1, source_target_pairs={{0,8},{1,9},{2,10},{3,11},{4,12},{5,13},{6,14},{7,15},{8,0},{9,1},... | collective-permute-start | bytes 98312 | tf_op jit(solution)/shard_map/ppermute | solution.py:215
  19.0 0.1 shard_map.44.mine_ref
  19.2 1.6 %collective-permute-done.9.other_ref = bf16[16,1024]{1,0:T(8,128)(2,1)S(1)} collective-permute-done((bf16[16,1024]{1,0:T(8,128)(2,1)S(1)}, bf16[16,1024]{1,0:T(8,128)(2,1)S(1)}, u32[]{:S(2)}, u32[]{:S(2)}) %collective-permute-start.9) | collective-permute-done | bytes 32800 | tf_op jit(solution)/shard_map/ppermute | solution.py:215
  20.7 0.1 shard_map.46
  20.9 0.5 %collective-permute-start.10 = (bf16[16,1024]{1,0:T(8,128)(2,1)S(1)}, bf16[16,1024]{1,0:T(8,128)(2,1)S(1)}, u32[]{:S(2)}, u32[]{:S(2)}) collective-permute-start(bf16[16,1024]{1,0:T(8,128)(2,1)S(1)} %shard_map.46), channel_id=1, source_target_pairs={{0,6},{1,2},{2,1},{3,5},{4,7},{5,3},{6,0},{7,4},{8,14},{9,10},{10,... | collective-permute-start | bytes 98312 | tf_op jit(solution)/shard_map/ppermute | solution.py:222
  21.4 0.1 shard_map.41.mine_ref
  21.5 0.9 %collective-permute-done.6.other_ref = bf16[16,1024]{1,0:T(8,128)(2,1)S(1)} collective-permute-done((bf16[16,1024]{1,0:T(8,128)(2,1)S(1)}, bf16[16,1024]{1,0:T(8,128)(2,1)S(1)}, u32[]{:S(2)}, u32[]{:S(2)}) %collective-permute-start.6) | collective-permute-done | bytes 32800 | tf_op jit(solution)/shard_map/ppermute | solution.py:215
  22.4 0.1 shard_map.43
  22.6 1.4 %collective-permute-start.7 = (bf16[8,1024]{1,0:T(8,128)(2,1)S(1)}, bf16[8,1024]{1,0:T(8,128)(2,1)S(1)}, u32[]{:S(2)}, u32[]{:S(2)}) collective-permute-start(bf16[8,1024]{1,0:T(8,128)(2,1)S(1)} %get-tuple-element.14), channel_id=1, source_target_pairs={{0,1},{1,0},{2,3},{3,2},{4,5},{5,4},{6,7},{7,6},{8,9},{9,8},{10,11... | collective-permute-start | bytes 49160 | tf_op jit(solution)/shard_map/ppermute | solution.py:215
  23.9 1.3 %collective-permute-done.10.a_ref.far_ref = bf16[16,1024]{1,0:T(8,128)(2,1)S(1)} collective-permute-done((bf16[16,1024]{1,0:T(8,128)(2,1)S(1)}, bf16[16,1024]{1,0:T(8,128)(2,1)S(1)}, u32[]{:S(2)}, u32[]{:S(2)}) %collective-permute-start.10) | collective-permute-done | bytes 32800 | tf_op jit(solution)/shard_map/ppermute | solution.py:222
  25.2 0.2 collective-permute-start.11
  25.4 1.0 %collective-permute-done.7.near_ref = bf16[8,1024]{1,0:T(8,128)(2,1)S(1)} collective-permute-done((bf16[8,1024]{1,0:T(8,128)(2,1)S(1)}, bf16[8,1024]{1,0:T(8,128)(2,1)S(1)}, u32[]{:S(2)}, u32[]{:S(2)}) %collective-permute-start.7) | collective-permute-done | bytes 16416 | tf_op jit(solution)/shard_map/ppermute | solution.py:215
  26.4 0.0 collective-permute-done.11.across_ref
  26.4 0.7 %shard_map.48 = f32[8,1000]{1,0:T(8,128)} custom-call(f32[8,1024]{1,0:T(8,128)S(1)} %get-tuple-element.13.own_ref, bf16[8,1024]{1,0:T(8,128)(2,1)S(1)} %collective-permute-done.7.near_ref, bf16[16,1024]{1,0:T(8,128)(2,1)S(1)} %collective-permute-done.10.a_ref.far_ref, bf16[8,1024]{1,0:T(8,128)(2,1)S(1)} %collective-permute-done.11.across_ref), custom_call_target="tpu_custom_call" | custom-call | tf_op jit(solution)/shard_map/pallas_call | solution.py:27
  (10 shorter events, 0.0 us)
Async XLA Ops:
  0.0 4.0 %collective-permute-start = (bf16[8,768]{1,0:T(8,128)(2,1)}, bf16[8,768]{1,0:T(8,128)(2,1)S(1)}, u32[]{:S(2)}, u32[]{:S(2)}) collective-permute-start(bf16[8,768]{1,0:T(8,128)(2,1)} %a_ref.1), channel_id=1, source_target_pairs={{0,12},{1,13},{2,14},{3,15},{4,8},{5,9},{6,10},{7,11},{8,4},{9,5},... | collective-permute-start | bytes 36872 | tf_op jit(solution)/shard_map/ppermute | solution.py:215
  2.4 0.7 %copy-start.2 = (bf16[8,768]{1,0:T(8,128)(2,1)S(1)}, bf16[8,768]{1,0:T(8,128)(2,1)}, u32[]{:S(2)}) copy-start(bf16[8,768]{1,0:T(8,128)(2,1)} %a_ref.1) | copy-start | bytes 36868
  4.0 8.1 %copy-start = (bf16[2048,1000]{0,1:T(8,128)(2,1)S(1)}, bf16[2048,1000]{0,1:T(8,128)(2,1)}, u32[]{:S(2)}) copy-start(bf16[2048,1000]{0,1:T(8,128)(2,1)} %param.5) | copy-start | bytes 12288004
  4.0 8.1 %copy-start.1 = (bf16[2048,768]{1,0:T(8,128)(2,1)S(1)}, bf16[2048,768]{1,0:T(8,128)(2,1)}, u32[]{:S(2)}) copy-start(bf16[2048,768]{1,0:T(8,128)(2,1)} %k_ref.1) | copy-start | bytes 9437188
  4.0 1.6 %collective-permute-start.1 = (bf16[16,768]{1,0:T(8,128)(2,1)S(1)}, bf16[16,768]{1,0:T(8,128)(2,1)S(1)}, u32[]{:S(2)}, u32[]{:S(2)}) collective-permute-start(bf16[16,768]{1,0:T(8,128)(2,1)S(1)} %shard_map.38.a_ref), channel_id=1, source_target_pairs={{0,4},{1,5},{2,6},{3,7},{4,0},{5,1},{6,2},{7,3},{8,12},{9,13},{10,... | collective-permute-start | bytes 73736 | tf_op jit(solution)/shard_map/ppermute | solution.py:215
  5.6 4.7 %collective-permute-start.3 = (bf16[32,768]{1,0:T(8,128)(2,1)S(1)}, bf16[32,768]{1,0:T(8,128)(2,1)S(1)}, u32[]{:S(2)}, u32[]{:S(2)}) collective-permute-start(bf16[32,768]{1,0:T(8,128)(2,1)S(1)} %shard_map.39.own_ref), channel_id=1, source_target_pairs={{0,6},{1,2},{2,1},{3,5},{4,7},{5,3},{6,0},{7,4},{8,14},{9,10},{10,... | collective-permute-start | bytes 147464 | tf_op jit(solution)/shard_map/ppermute | solution.py:222
  8.5 3.5 %collective-permute-start.2 = (bf16[32,768]{1,0:T(8,128)(2,1)S(1)}, bf16[32,768]{1,0:T(8,128)(2,1)S(1)}, u32[]{:S(2)}, u32[]{:S(2)}) collective-permute-start(bf16[32,768]{1,0:T(8,128)(2,1)S(1)} %shard_map.39.own_ref), channel_id=1, source_target_pairs={{0,5},{1,4},{2,7},{3,6},{4,1},{5,0},{6,3},{7,2},{8,13},{9,12},{10,... | collective-permute-start | bytes 147464 | tf_op jit(solution)/shard_map/ppermute | solution.py:215
  10.3 1.8 %collective-permute-start.4 = (bf16[32,768]{1,0:T(8,128)(2,1)S(1)}, bf16[32,768]{1,0:T(8,128)(2,1)S(1)}, u32[]{:S(2)}, u32[]{:S(2)}) collective-permute-start(bf16[32,768]{1,0:T(8,128)(2,1)S(1)} %collective-permute-done.3.far_ref), channel_id=1, source_target_pairs={{0,4},{1,5},{2,6},{3,7},{4,0},{5,1},{6,2},{7,3},{8,12},{9,13},{10,... | collective-permute-start | bytes 147464 | tf_op jit(solution)/shard_map/ppermute | solution.py:215
  14.6 2.0 %collective-permute-start.8 = (bf16[32,1024]{1,0:T(8,128)(2,1)S(1)}, bf16[32,1024]{1,0:T(8,128)(2,1)S(1)}, u32[]{:S(2)}, u32[]{:S(2)}) collective-permute-start(bf16[32,1024]{1,0:T(8,128)(2,1)S(1)} %get-tuple-element.16), channel_id=1, source_target_pairs={{0,4},{1,5},{2,6},{3,7},{4,0},{5,1},{6,2},{7,3},{8,12},{9,13},{10,... | collective-permute-start | bytes 196616 | tf_op jit(solution)/shard_map/ppermute | solution.py:215
  15.7 2.6 %collective-permute-start.5 = (bf16[32,1024]{1,0:T(8,128)(2,1)S(1)}, bf16[32,1024]{1,0:T(8,128)(2,1)S(1)}, u32[]{:S(2)}, u32[]{:S(2)}) collective-permute-start(bf16[32,1024]{1,0:T(8,128)(2,1)S(1)} %get-tuple-element.12), channel_id=1, source_target_pairs={{0,4},{1,5},{2,6},{3,7},{4,0},{5,1},{6,2},{7,3},{8,12},{9,13},{10,... | collective-permute-start | bytes 196616 | tf_op jit(solution)/shard_map/ppermute | solution.py:215
  16.7 4.0 %collective-permute-start.9 = (bf16[16,1024]{1,0:T(8,128)(2,1)S(1)}, bf16[16,1024]{1,0:T(8,128)(2,1)S(1)}, u32[]{:S(2)}, u32[]{:S(2)}) collective-permute-start(bf16[16,1024]{1,0:T(8,128)(2,1)S(1)} %shard_map.45), channel_id=1, source_target_pairs={{0,8},{1,9},{2,10},{3,11},{4,12},{5,13},{6,14},{7,15},{8,0},{9,1},... | collective-permute-start | bytes 98312 | tf_op jit(solution)/shard_map/ppermute | solution.py:215
  18.5 4.0 %collective-permute-start.6 = (bf16[16,1024]{1,0:T(8,128)(2,1)S(1)}, bf16[16,1024]{1,0:T(8,128)(2,1)S(1)}, u32[]{:S(2)}, u32[]{:S(2)}) collective-permute-start(bf16[16,1024]{1,0:T(8,128)(2,1)S(1)} %shard_map.42), channel_id=1, source_target_pairs={{0,8},{1,9},{2,10},{3,11},{4,12},{5,13},{6,14},{7,15},{8,0},{9,1},... | collective-permute-start | bytes 98312 | tf_op jit(solution)/shard_map/ppermute | solution.py:215
  20.9 4.4 %collective-permute-start.10 = (bf16[16,1024]{1,0:T(8,128)(2,1)S(1)}, bf16[16,1024]{1,0:T(8,128)(2,1)S(1)}, u32[]{:S(2)}, u32[]{:S(2)}) collective-permute-start(bf16[16,1024]{1,0:T(8,128)(2,1)S(1)} %shard_map.46), channel_id=1, source_target_pairs={{0,6},{1,2},{2,1},{3,5},{4,7},{5,3},{6,0},{7,4},{8,14},{9,10},{10,... | collective-permute-start | bytes 98312 | tf_op jit(solution)/shard_map/ppermute | solution.py:222
  22.6 3.8 %collective-permute-start.7 = (bf16[8,1024]{1,0:T(8,128)(2,1)S(1)}, bf16[8,1024]{1,0:T(8,128)(2,1)S(1)}, u32[]{:S(2)}, u32[]{:S(2)}) collective-permute-start(bf16[8,1024]{1,0:T(8,128)(2,1)S(1)} %get-tuple-element.14), channel_id=1, source_target_pairs={{0,1},{1,0},{2,3},{3,2},{4,5},{5,4},{6,7},{7,6},{8,9},{9,8},{10,11... | collective-permute-start | bytes 49160 | tf_op jit(solution)/shard_map/ppermute | solution.py:215
  25.2 1.2 %collective-permute-start.11 = (bf16[8,1024]{1,0:T(8,128)(2,1)S(1)}, bf16[8,1024]{1,0:T(8,128)(2,1)S(1)}, u32[]{:S(2)}, u32[]{:S(2)}) collective-permute-start(bf16[8,1024]{1,0:T(8,128)(2,1)S(1)} %shard_map.47), channel_id=1, source_target_pairs={{0,4},{1,5},{2,6},{3,7},{4,0},{5,1},{6,2},{7,3},{8,12},{9,13},{10,... | collective-permute-start | bytes 49160 | tf_op jit(solution)/shard_map/ppermute | solution.py:215

commit v11 on v10

--- a/solution.py
+++ b/solution.py
@@ -43,9 +43,8 @@
 
 
 def join_kernel(a_ref, b_ref, out_ref):
-    rows = a_ref.shape[0]
-    out_ref[:rows] = a_ref[...]
-    out_ref[rows:] = b_ref[...]
+    both = jnp.concatenate([r[...].astype(jnp.float32) for r in (a_ref, b_ref)], axis=0)
+    out_ref[...] = both.astype(out_ref.dtype)
 
 
 def join(a, b):
@@ -118,13 +117,11 @@
     return take(parts[0]), [take(x) for x in parts[1]]
 
 
-def stats_kernel(unit, own_ref, near_ref, far_ref, across_ref, k_ref, lt_ref, *out_refs):
-    count, width = own_ref.shape
-    classes = lt_ref.shape[0]
-    half = count // 2
-    queries = jnp.concatenate(
-        [own_ref[...], near_ref[...], far_ref[...], across_ref[...]], axis=0
-    )
+def stats_kernel(places, unit, *refs):
+    *block_refs, k_ref, lt_ref = refs[:-4]
+    out_refs = refs[-4:]
+    width, classes = k_ref.shape[1], lt_ref.shape[0]
+    queries = jnp.concatenate([r[...] for r in block_refs], axis=0)
     gain = SCORE_GAIN / math.sqrt(width)
     dot = functools.partial(lax.dot_general, preferred_element_type=jnp.float32)
     by_rows, by_columns = (((1,), (1,)), ((), ())), (((1,), (0,)), ((), ()))
@@ -135,27 +132,17 @@
     totals = jnp.sum(sum(weights), axis=0, keepdims=True)
     weights = jnp.concatenate([w.astype(jnp.bfloat16) for w in weights], axis=0)
 
-    slots = half // unit
-    odd = [n.bit_count() % 2 for n in range(slots)]
-
-    def rows(block, other_core):
-        starts = [block * count + (n + slots * (other_core ^ o)) * unit for n, o in enumerate(odd)]
-        return [(lo, lo + unit) for lo in starts]
-
     share = 1 / totals
     votes = dot(lt_ref[...], weights, by_columns) * share
-    spare = jnp.ones((out_refs[0].shape[1] - classes, 4 * count), jnp.float32)
+    spare = jnp.ones((out_refs[0].shape[1] - classes, queries.shape[0]), jnp.float32)
     averages = tiles(jnp.concatenate([votes, spare], axis=0).T)
     parts = ((peaks + jnp.log(totals)).T, averages)
-    far_send, near_send, far_keep, near_keep = out_refs
-    encode(far_send, 0, rows_of(parts, *rows(3, 0), *rows(3, 1)), classes)
-    encode(near_send, 0, rows_of(parts, *rows(0, 1), *rows(1, 0)), classes)
-    keep(far_keep, 0, rows_of(parts, *rows(2, 0), *rows(2, 1)), classes)
-    keep(near_keep, 0, rows_of(parts, *rows(0, 0), *rows(1, 1)), classes)
-
-
-def stats(blocks, keys, labels_t, unit):
-    rows, width = 4 * blocks[0].shape[0], keys.shape[1]
+    for put, ref, chosen in zip((encode, encode, keep, keep), out_refs, places):
+        put(ref, 0, rows_of(parts, *[(lo * unit, (lo + 1) * unit) for lo in chosen]), classes)
+
+
+def stats(blocks, keys, labels_t, places, unit):
+    rows, width = sum(b.shape[0] for b in blocks), keys.shape[1]
     bank, classes = keys.shape[0], labels_t.shape[0]
     outs = [record_shape(rows // 4, classes, d) for d in (jnp.bfloat16, jnp.float32) for _ in range(2)]
     scores = jax.ShapeDtypeStruct((rows, bank), jnp.float32)
@@ -165,7 +152,7 @@
         transcendentals=rows * bank,
     )
     return call(
-        functools.partial(stats_kernel, unit), outs, *blocks, keys, labels_t, scratch=(scores,), cost=cost
+        functools.partial(stats_kernel, places, unit), outs, *blocks, keys, labels_t, scratch=(scores,), cost=cost
     )
 
 
@@ -222,22 +209,45 @@
         return lax.ppermute(block, AXES, [(i, partner(i)) for i in range(size)])
 
     classes = bank_labels.shape[1]
-    first, *rest = [bit ^ core for bit in lead] + [core]
-    own = join(fetch(queries), swap(queries, first))
-    for bit in rest:
-        own = join(own, swap(own, bit))
+    last, *others = lead
+    masks, own, mine = [0], queries, fetch(queries)
+    for bit in [bit ^ core for bit in others] + [core]:
+        own = mine = join(mine, swap(own, bit))
+        masks += [m ^ bit for m in masks]
     far = swap_far(own)
-    near = swap(own, 1 ^ core)
+    near = swap(own, 1)
     across = swap(far, core)
-    *sends, far, near = stats((own, near, far, across), bank_keys, bank_labels.T, queries.shape[0])
+    one = swap(join(own, far), last ^ core)
+    two = swap(join(near, across), last ^ core)
+
+    def place(first, second, flip):
+        at = {m: first * len(masks) + k for k, m in enumerate(masks)}
+        at |= {m ^ last ^ flip: second * len(masks) + k for k, m in enumerate(masks)}
+        offsets = [0]
+        for bit in lead:
+            offsets += [m ^ bit for m in offsets]
+        return [[at[m ^ f] for m in offsets] for f in (0, core)]
+
+    own_rows, near_rows = place(0, 4, core), place(1, 6, core)
+    far_rows, across_rows = place(2, 7, 0), place(3, 5, 0)
+    odd = [n.bit_count() % 2 for n in range(1 << len(lead))]
+    far_block, across_block = (far_rows, across_rows), (across_rows, far_rows)
+    places = (
+        [across_block[o][f][n] for f in (0, 1) for n, o in enumerate(odd)],
+        [block[1 - o][n] for block in (own_rows, near_rows) for n, o in enumerate(odd)],
+        [far_block[o][f][n] for f in (0, 1) for n, o in enumerate(odd)],
+        [block[o][n] for block in (own_rows, near_rows) for n, o in enumerate(odd)],
+    )
+    blocks = (own, near, far, across, one, two)
+    *sends, far, near = stats(blocks, bank_keys, bank_labels.T, places, queries.shape[0])
     far_came, near_came = (swap(send, core) for send in sends)
     for bit in lead[::-1]:
         (send,) = merge(far, far_came, classes, 1, 2, encode)
         (far,) = merge(far, far_came, classes, 0, 1, keep)
-        far_came = swap(send, bit)
+        far_came = swap(send, bit ^ core)
         (send,) = merge(near, near_came, classes, 1, 2, encode)
         (near,) = merge(near, near_came, classes, 0, 1, keep)
-        near_came = swap(send, bit)
+        near_came = swap(send, bit ^ core)
     (far,) = merge(far, far_came, classes, 0, 2, encode)
     own, near = merge(near, near_came, classes, 0, 2, keep, encode)
     far = swap_far(far)

time: 27.4 us -> 27.3 us (level)
    ppermute x10 -> x11, starting transfers between devices: 10.4 us -> 8.19 us  [swap(): return lax.ppermute(block, AXES, [(i, i ^ bit) for i in range(size)])]
    ppermute x2, starting transfers between devices: 3.46 us -> 5.46 us  [swap_far(): return lax.ppermute(block, AXES, [(i, partner(i)) for i in range(size)])]
    ppermute x2, waiting for transfers between devices: 1.55 us -> 2.66 us  [swap_far(): return lax.ppermute(block, AXES, [(i, partner(i)) for i in range(size)])]
    ppermute x10 -> x11, waiting for transfers between devices: 6.97 us -> 6.03 us  [swap(): return lax.ppermute(block, AXES, [(i, i ^ bit) for i in range(size)])]
    pallas_call x12 -> x13, Pallas kernels: 3.96 us -> 3.96 us  [call(): pl.pallas_call(kernel, out_shape=outs, in_specs=[VMEM] * len(args), out_s...]
  transfers between devices with their start and end apart: 12 -> 13, of which waited for: 10 -> 10; matrix products, arithmetic and copies ran while one was open for 0% -> 0% of each run, Pallas kernels for 3% -> 3%
where the time goes in v11:
time: 27.3 us; the launch traced here: 27.1 us
  starting transfers between devices  13.7 us (50%)
  waiting for transfers between devices  8.68 us (32%)
  Pallas kernels  3.96 us (15%)
  local copies, waits for them, and re-layouts  0.71 us (3%)
    ppermute x11, starting transfers between devices, swap(): return lax.ppermute(block, AXES, [(i, i ^ bit) for i in range(size)])  8.19 us
    ppermute x11, waiting for transfers between devices, swap(): return lax.ppermute(block, AXES, [(i, i ^ bit) for i in range(size)])  6.03 us
    ppermute x2, starting transfers between devices, swap_far(): return lax.ppermute(block, AXES, [(i, partner(i)) for i in range(size)])  5.46 us
    pallas_call x13, Pallas kernels, call(): pl.pallas_call(kernel, out_shape=outs, in_specs=[VMEM] * len(args), out_s...  3.96 us
    ppermute x2, waiting for transfers between devices, swap_far(): return lax.ppermute(block, AXES, [(i, partner(i)) for i in range(size)])  2.66 us
    unnamed x6, local copies, waits for them, and re-layouts  0.71 us
  transfers between devices with their start and end apart: 13, of which 10 were waited for; matrix products, arithmetic and copies ran while one was open for 0% of the time, Pallas kernels for 3%

profile of v11, /device:TPU:0, one launch (start us, length us, event | category | flops | bytes accessed | tf_op | source)
XLA Modules:
  0.0 27.1 jit_solution(4759202404592372847)
XLA Ops:
  0.0 0.5 %collective-permute-start = (bf16[8,768]{1,0:T(8,128)(2,1)}, bf16[8,768]{1,0:T(8,128)(2,1)S(1)}, u32[]{:S(2)}, u32[]{:S(2)}) collective-permute-start(bf16[8,768]{1,0:T(8,128)(2,1)} %a_ref.1), channel_id=1, source_target_pairs={{0,4},{1,5},{2,6},{3,7},{4,0},{5,1},{6,2},{7,3},{8,12},{9,13},{10,... | collective-permute-start | bytes 36872 | tf_op jit(solution)/shard_map/ppermute | solution.py:202
  0.5 0.7 %copy-done.2 = bf16[8,768]{1,0:T(8,128)(2,1)S(1)} copy-done((bf16[8,768]{1,0:T(8,128)(2,1)S(1)}, bf16[8,768]{1,0:T(8,128)(2,1)}, u32[]{:S(2)}) %copy-start.2) | copy-done | bytes 12312
  1.2 0.3 %collective-permute-done.b_ref = bf16[8,768]{1,0:T(8,128)(2,1)S(1)} collective-permute-done((bf16[8,768]{1,0:T(8,128)(2,1)}, bf16[8,768]{1,0:T(8,128)(2,1)S(1)}, u32[]{:S(2)}, u32[]{:S(2)}) %collective-permute-start) | collective-permute-done | bytes 12320 | tf_op jit(solution)/shard_map/ppermute | solution.py:202
  1.5 3.7 %collective-permute-start.2 = (bf16[16,768]{1,0:T(8,128)(2,1)S(1)}, bf16[16,768]{1,0:T(8,128)(2,1)S(1)}, u32[]{:S(2)}, u32[]{:S(2)}) collective-permute-start(bf16[16,768]{1,0:T(8,128)(2,1)S(1)} %shard_map.38.a_ref.refs_0_), channel_id=1, source_target_pairs={{0,6},{1,2},{2,1},{3,5},{4,7},{5,3},{6,0},{7,4},{8,14},{9,10},{10,... | collective-permute-start | bytes 73736 | tf_op jit(solution)/shard_map/ppermute | solution.py:209
  5.2 0.8 %collective-permute-start.1 = (bf16[16,768]{1,0:T(8,128)(2,1)S(1)}, bf16[16,768]{1,0:T(8,128)(2,1)S(1)}, u32[]{:S(2)}, u32[]{:S(2)}) collective-permute-start(bf16[16,768]{1,0:T(8,128)(2,1)S(1)} %shard_map.38.a_ref.refs_0_), channel_id=1, source_target_pairs={{0,1},{1,0},{2,3},{3,2},{4,5},{5,4},{6,7},{7,6},{8,9},{9,8},{10,11... | collective-permute-start | bytes 73736 | tf_op jit(solution)/shard_map/ppermute | solution.py:202
  6.0 0.7 %collective-permute-done.2.b_ref.refs_2_ = bf16[16,768]{1,0:T(8,128)(2,1)S(1)} collective-permute-done((bf16[16,768]{1,0:T(8,128)(2,1)S(1)}, bf16[16,768]{1,0:T(8,128)(2,1)S(1)}, u32[]{:S(2)}, u32[]{:S(2)}) %collective-permute-start.2) | collective-permute-done | bytes 24608 | tf_op jit(solution)/shard_map/ppermute | solution.py:209
  6.7 0.9 %collective-permute-start.3 = (bf16[16,768]{1,0:T(8,128)(2,1)S(1)}, bf16[16,768]{1,0:T(8,128)(2,1)S(1)}, u32[]{:S(2)}, u32[]{:S(2)}) collective-permute-start(bf16[16,768]{1,0:T(8,128)(2,1)S(1)} %collective-permute-done.2.b_ref.refs_2_), channel_id=1, source_target_pairs={{0,4},{1,5},{2,6},{3,7},{4,0},{5,1},{6,2},{7,3},{8,12},{9,13},{10,... | collective-permute-start | bytes 73736 | tf_op jit(solution)/shard_map/ppermute | solution.py:202
  7.7 1.2 %collective-permute-start.4 = (bf16[32,768]{1,0:T(8,128)(2,1)S(1)}, bf16[32,768]{1,0:T(8,128)(2,1)S(1)}, u32[]{:S(2)}, u32[]{:S(2)}) collective-permute-start(bf16[32,768]{1,0:T(8,128)(2,1)S(1)} %shard_map.39), channel_id=1, source_target_pairs={{0,12},{1,13},{2,14},{3,15},{4,8},{5,9},{6,10},{7,11},{8,4},{9,5},... | collective-permute-start | bytes 147464 | tf_op jit(solution)/shard_map/ppermute | solution.py:202
  8.8 0.3 %collective-permute-done.1.a_ref.refs_1_ = bf16[16,768]{1,0:T(8,128)(2,1)S(1)} collective-permute-done((bf16[16,768]{1,0:T(8,128)(2,1)S(1)}, bf16[16,768]{1,0:T(8,128)(2,1)S(1)}, u32[]{:S(2)}, u32[]{:S(2)}) %collective-permute-start.1) | collective-permute-done | bytes 24608 | tf_op jit(solution)/shard_map/ppermute | solution.py:202
  9.1 1.3 %collective-permute-start.5 = (bf16[32,768]{1,0:T(8,128)(2,1)S(1)}, bf16[32,768]{1,0:T(8,128)(2,1)S(1)}, u32[]{:S(2)}, u32[]{:S(2)}) collective-permute-start(bf16[32,768]{1,0:T(8,128)(2,1)S(1)} %shard_map.40), channel_id=1, source_target_pairs={{0,12},{1,13},{2,14},{3,15},{4,8},{5,9},{6,10},{7,11},{8,4},{9,5},... | collective-permute-start | bytes 147464 | tf_op jit(solution)/shard_map/ppermute | solution.py:202
  10.4 1.1 %collective-permute-done.4.refs_4_ = bf16[32,768]{1,0:T(8,128)(2,1)S(1)} collective-permute-done((bf16[32,768]{1,0:T(8,128)(2,1)S(1)}, bf16[32,768]{1,0:T(8,128)(2,1)S(1)}, u32[]{:S(2)}, u32[]{:S(2)}) %collective-permute-start.4) | collective-permute-done | bytes 49184 | tf_op jit(solution)/shard_map/ppermute | solution.py:202
  11.6 1.4 %collective-permute-done.5.refs_5_ = bf16[32,768]{1,0:T(8,128)(2,1)S(1)} collective-permute-done((bf16[32,768]{1,0:T(8,128)(2,1)S(1)}, bf16[32,768]{1,0:T(8,128)(2,1)S(1)}, u32[]{:S(2)}, u32[]{:S(2)}) %collective-permute-start.5) | collective-permute-done | bytes 49184 | tf_op jit(solution)/shard_map/ppermute | solution.py:202
  13.0 2.5 %shard_map.41 = (bf16[32,1024]{1,0:T(8,128)(2,1)S(1)}, bf16[32,1024]{1,0:T(8,128)(2,1)S(1)}, f32[32,1024]{1,0:T(8,128)S(1)}, f32[32,1024]{1,0:T(8,128)S(1)}) custom-call(bf16[16,768]{1,0:T(8,128)(2,1)S(1)} %shard_map.38.a_ref.refs_0_, bf16[16,768]{1,0:T(8,128)(2,1)S(1)} %collective-permute-done.1.a_ref.refs_1_, ...), custom_call_target="tpu_custom_call" | custom-call | flops 926941184 | bytes 7241728 | tf_op jit(solution)/shard_map/pallas_call | solution.py:27
  15.4 0.2 collective-permute-start.9
  15.6 0.4 %collective-permute-start.6 = (bf16[32,1024]{1,0:T(8,128)(2,1)S(1)}, bf16[32,1024]{1,0:T(8,128)(2,1)S(1)}, u32[]{:S(2)}, u32[]{:S(2)}) collective-permute-start(bf16[32,1024]{1,0:T(8,128)(2,1)S(1)} %get-tuple-element.12), channel_id=1, source_target_pairs={{0,4},{1,5},{2,6},{3,7},{4,0},{5,1},{6,2},{7,3},{8,12},{9,13},{10,... | collective-permute-start | bytes 196616 | tf_op jit(solution)/shard_map/ppermute | solution.py:202
  16.0 0.7 %collective-permute-done.9.other_ref = bf16[32,1024]{1,0:T(8,128)(2,1)S(1)} collective-permute-done((bf16[32,1024]{1,0:T(8,128)(2,1)S(1)}, bf16[32,1024]{1,0:T(8,128)(2,1)S(1)}, u32[]{:S(2)}, u32[]{:S(2)}) %collective-permute-start.9) | collective-permute-done | bytes 65568 | tf_op jit(solution)/shard_map/ppermute | solution.py:202
  16.8 0.1 shard_map.46
  16.9 1.3 %collective-permute-start.10 = (bf16[16,1024]{1,0:T(8,128)(2,1)S(1)}, bf16[16,1024]{1,0:T(8,128)(2,1)S(1)}, u32[]{:S(2)}, u32[]{:S(2)}) collective-permute-start(bf16[16,1024]{1,0:T(8,128)(2,1)S(1)} %shard_map.46), channel_id=1, source_target_pairs={{0,12},{1,13},{2,14},{3,15},{4,8},{5,9},{6,10},{7,11},{8,4},{9,5},... | collective-permute-start | bytes 98312 | tf_op jit(solution)/shard_map/ppermute | solution.py:202
  18.2 0.1 shard_map.43
  18.4 0.6 %collective-permute-start.7 = (bf16[16,1024]{1,0:T(8,128)(2,1)S(1)}, bf16[16,1024]{1,0:T(8,128)(2,1)S(1)}, u32[]{:S(2)}, u32[]{:S(2)}) collective-permute-start(bf16[16,1024]{1,0:T(8,128)(2,1)S(1)} %shard_map.43), channel_id=1, source_target_pairs={{0,12},{1,13},{2,14},{3,15},{4,8},{5,9},{6,10},{7,11},{8,4},{9,5},... | collective-permute-start | bytes 98312 | tf_op jit(solution)/shard_map/ppermute | solution.py:202
  18.9 0.1 shard_map.45.mine_ref
  19.0 1.3 %collective-permute-done.10.other_ref = bf16[16,1024]{1,0:T(8,128)(2,1)S(1)} collective-permute-done((bf16[16,1024]{1,0:T(8,128)(2,1)S(1)}, bf16[16,1024]{1,0:T(8,128)(2,1)S(1)}, u32[]{:S(2)}, u32[]{:S(2)}) %collective-permute-start.10) | collective-permute-done | bytes 32800 | tf_op jit(solution)/shard_map/ppermute | solution.py:202
  20.3 0.1 shard_map.47
  20.4 1.8 %collective-permute-start.11 = (bf16[16,1024]{1,0:T(8,128)(2,1)S(1)}, bf16[16,1024]{1,0:T(8,128)(2,1)S(1)}, u32[]{:S(2)}, u32[]{:S(2)}) collective-permute-start(bf16[16,1024]{1,0:T(8,128)(2,1)S(1)} %shard_map.47), channel_id=1, source_target_pairs={{0,6},{1,2},{2,1},{3,5},{4,7},{5,3},{6,0},{7,4},{8,14},{9,10},{10,... | collective-permute-start | bytes 98312 | tf_op jit(solution)/shard_map/ppermute | solution.py:209
  22.2 0.1 shard_map.42.mine_ref
  22.3 0.1 shard_map.44
  22.5 0.7 %collective-permute-start.8 = (bf16[8,1024]{1,0:T(8,128)(2,1)S(1)}, bf16[8,1024]{1,0:T(8,128)(2,1)S(1)}, u32[]{:S(2)}, u32[]{:S(2)}) collective-permute-start(bf16[8,1024]{1,0:T(8,128)(2,1)S(1)} %get-tuple-element.14), channel_id=1, source_target_pairs={{0,1},{1,0},{2,3},{3,2},{4,5},{5,4},{6,7},{7,6},{8,9},{9,8},{10,11... | collective-permute-start | bytes 49160 | tf_op jit(solution)/shard_map/ppermute | solution.py:202
  23.1 1.9 %collective-permute-done.11.a_ref.far_ref = bf16[16,1024]{1,0:T(8,128)(2,1)S(1)} collective-permute-done((bf16[16,1024]{1,0:T(8,128)(2,1)S(1)}, bf16[16,1024]{1,0:T(8,128)(2,1)S(1)}, u32[]{:S(2)}, u32[]{:S(2)}) %collective-permute-start.11) | collective-permute-done | bytes 32800 | tf_op jit(solution)/shard_map/ppermute | solution.py:209
  25.1 0.4 %collective-permute-start.12 = (bf16[8,1024]{1,0:T(8,128)(2,1)S(1)}, bf16[8,1024]{1,0:T(8,128)(2,1)S(1)}, u32[]{:S(2)}, u32[]{:S(2)}) collective-permute-start(bf16[8,1024]{1,0:T(8,128)(2,1)S(1)} %shard_map.48), channel_id=1, source_target_pairs={{0,4},{1,5},{2,6},{3,7},{4,0},{5,1},{6,2},{7,3},{8,12},{9,13},{10,... | collective-permute-start | bytes 49160 | tf_op jit(solution)/shard_map/ppermute | solution.py:202
  25.5 0.8 %collective-permute-done.8.near_ref = bf16[8,1024]{1,0:T(8,128)(2,1)S(1)} collective-permute-done((bf16[8,1024]{1,0:T(8,128)(2,1)S(1)}, bf16[8,1024]{1,0:T(8,128)(2,1)S(1)}, u32[]{:S(2)}, u32[]{:S(2)}) %collective-permute-start.8) | collective-permute-done | bytes 16416 | tf_op jit(solution)/shard_map/ppermute | solution.py:202
  26.3 0.1 collective-permute-done.12.across_ref
  26.3 0.7 %shard_map.49 = f32[8,1000]{1,0:T(8,128)} custom-call(f32[8,1024]{1,0:T(8,128)S(1)} %get-tuple-element.13.own_ref, bf16[8,1024]{1,0:T(8,128)(2,1)S(1)} %collective-permute-done.8.near_ref, bf16[16,1024]{1,0:T(8,128)(2,1)S(1)} %collective-permute-done.11.a_ref.far_ref, bf16[8,1024]{1,0:T(8,128)(2,1)S(1)} %collective-permute-done.12.across_ref), custom_call_target="tpu_custom_call" | custom-call | tf_op jit(solution)/shard_map/pallas_call | solution.py:27
  (13 shorter events, 0.0 us)
Async XLA Ops:
  0.0 1.5 %collective-permute-start = (bf16[8,768]{1,0:T(8,128)(2,1)}, bf16[8,768]{1,0:T(8,128)(2,1)S(1)}, u32[]{:S(2)}, u32[]{:S(2)}) collective-permute-start(bf16[8,768]{1,0:T(8,128)(2,1)} %a_ref.1), channel_id=1, source_target_pairs={{0,4},{1,5},{2,6},{3,7},{4,0},{5,1},{6,2},{7,3},{8,12},{9,13},{10,... | collective-permute-start | bytes 36872 | tf_op jit(solution)/shard_map/ppermute | solution.py:202
  0.5 0.7 %copy-start.2 = (bf16[8,768]{1,0:T(8,128)(2,1)S(1)}, bf16[8,768]{1,0:T(8,128)(2,1)}, u32[]{:S(2)}) copy-start(bf16[8,768]{1,0:T(8,128)(2,1)} %a_ref.1) | copy-start | bytes 36868
  1.5 5.2 %collective-permute-start.2 = (bf16[16,768]{1,0:T(8,128)(2,1)S(1)}, bf16[16,768]{1,0:T(8,128)(2,1)S(1)}, u32[]{:S(2)}, u32[]{:S(2)}) collective-permute-start(bf16[16,768]{1,0:T(8,128)(2,1)S(1)} %shard_map.38.a_ref.refs_0_), channel_id=1, source_target_pairs={{0,6},{1,2},{2,1},{3,5},{4,7},{5,3},{6,0},{7,4},{8,14},{9,10},{10,... | collective-permute-start | bytes 73736 | tf_op jit(solution)/shard_map/ppermute | solution.py:209
  5.2 3.9 %collective-permute-start.1 = (bf16[16,768]{1,0:T(8,128)(2,1)S(1)}, bf16[16,768]{1,0:T(8,128)(2,1)S(1)}, u32[]{:S(2)}, u32[]{:S(2)}) collective-permute-start(bf16[16,768]{1,0:T(8,128)(2,1)S(1)} %shard_map.38.a_ref.refs_0_), channel_id=1, source_target_pairs={{0,1},{1,0},{2,3},{3,2},{4,5},{5,4},{6,7},{7,6},{8,9},{9,8},{10,11... | collective-permute-start | bytes 73736 | tf_op jit(solution)/shard_map/ppermute | solution.py:202
  6.7 2.4 %collective-permute-start.3 = (bf16[16,768]{1,0:T(8,128)(2,1)S(1)}, bf16[16,768]{1,0:T(8,128)(2,1)S(1)}, u32[]{:S(2)}, u32[]{:S(2)}) collective-permute-start(bf16[16,768]{1,0:T(8,128)(2,1)S(1)} %collective-permute-done.2.b_ref.refs_2_), channel_id=1, source_target_pairs={{0,4},{1,5},{2,6},{3,7},{4,0},{5,1},{6,2},{7,3},{8,12},{9,13},{10,... | collective-permute-start | bytes 73736 | tf_op jit(solution)/shard_map/ppermute | solution.py:202
  7.7 5.3 %copy-start = (bf16[2048,1000]{0,1:T(8,128)(2,1)S(1)}, bf16[2048,1000]{0,1:T(8,128)(2,1)}, u32[]{:S(2)}) copy-start(bf16[2048,1000]{0,1:T(8,128)(2,1)} %param.5) | copy-start | bytes 12288004
  7.7 5.3 %copy-start.1 = (bf16[2048,768]{1,0:T(8,128)(2,1)S(1)}, bf16[2048,768]{1,0:T(8,128)(2,1)}, u32[]{:S(2)}) copy-start(bf16[2048,768]{1,0:T(8,128)(2,1)} %refs_6_.1) | copy-start | bytes 9437188
  7.7 3.9 %collective-permute-start.4 = (bf16[32,768]{1,0:T(8,128)(2,1)S(1)}, bf16[32,768]{1,0:T(8,128)(2,1)S(1)}, u32[]{:S(2)}, u32[]{:S(2)}) collective-permute-start(bf16[32,768]{1,0:T(8,128)(2,1)S(1)} %shard_map.39), channel_id=1, source_target_pairs={{0,12},{1,13},{2,14},{3,15},{4,8},{5,9},{6,10},{7,11},{8,4},{9,5},... | collective-permute-start | bytes 147464 | tf_op jit(solution)/shard_map/ppermute | solution.py:202
  9.1 3.8 %collective-permute-start.5 = (bf16[32,768]{1,0:T(8,128)(2,1)S(1)}, bf16[32,768]{1,0:T(8,128)(2,1)S(1)}, u32[]{:S(2)}, u32[]{:S(2)}) collective-permute-start(bf16[32,768]{1,0:T(8,128)(2,1)S(1)} %shard_map.40), channel_id=1, source_target_pairs={{0,12},{1,13},{2,14},{3,15},{4,8},{5,9},{6,10},{7,11},{8,4},{9,5},... | collective-permute-start | bytes 147464 | tf_op jit(solution)/shard_map/ppermute | solution.py:202
  15.4 1.3 %collective-permute-start.9 = (bf16[32,1024]{1,0:T(8,128)(2,1)S(1)}, bf16[32,1024]{1,0:T(8,128)(2,1)S(1)}, u32[]{:S(2)}, u32[]{:S(2)}) collective-permute-start(bf16[32,1024]{1,0:T(8,128)(2,1)S(1)} %get-tuple-element.16), channel_id=1, source_target_pairs={{0,4},{1,5},{2,6},{3,7},{4,0},{5,1},{6,2},{7,3},{8,12},{9,13},{10,... | collective-permute-start | bytes 196616 | tf_op jit(solution)/shard_map/ppermute | solution.py:202
  15.6 2.6 %collective-permute-start.6 = (bf16[32,1024]{1,0:T(8,128)(2,1)S(1)}, bf16[32,1024]{1,0:T(8,128)(2,1)S(1)}, u32[]{:S(2)}, u32[]{:S(2)}) collective-permute-start(bf16[32,1024]{1,0:T(8,128)(2,1)S(1)} %get-tuple-element.12), channel_id=1, source_target_pairs={{0,4},{1,5},{2,6},{3,7},{4,0},{5,1},{6,2},{7,3},{8,12},{9,13},{10,... | collective-permute-start | bytes 196616 | tf_op jit(solution)/shard_map/ppermute | solution.py:202
  16.9 3.4 %collective-permute-start.10 = (bf16[16,1024]{1,0:T(8,128)(2,1)S(1)}, bf16[16,1024]{1,0:T(8,128)(2,1)S(1)}, u32[]{:S(2)}, u32[]{:S(2)}) collective-permute-start(bf16[16,1024]{1,0:T(8,128)(2,1)S(1)} %shard_map.46), channel_id=1, source_target_pairs={{0,12},{1,13},{2,14},{3,15},{4,8},{5,9},{6,10},{7,11},{8,4},{9,5},... | collective-permute-start | bytes 98312 | tf_op jit(solution)/shard_map/ppermute | solution.py:202
  18.4 4.0 %collective-permute-start.7 = (bf16[16,1024]{1,0:T(8,128)(2,1)S(1)}, bf16[16,1024]{1,0:T(8,128)(2,1)S(1)}, u32[]{:S(2)}, u32[]{:S(2)}) collective-permute-start(bf16[16,1024]{1,0:T(8,128)(2,1)S(1)} %shard_map.43), channel_id=1, source_target_pairs={{0,12},{1,13},{2,14},{3,15},{4,8},{5,9},{6,10},{7,11},{8,4},{9,5},... | collective-permute-start | bytes 98312 | tf_op jit(solution)/shard_map/ppermute | solution.py:202
  20.4 4.6 %collective-permute-start.11 = (bf16[16,1024]{1,0:T(8,128)(2,1)S(1)}, bf16[16,1024]{1,0:T(8,128)(2,1)S(1)}, u32[]{:S(2)}, u32[]{:S(2)}) collective-permute-start(bf16[16,1024]{1,0:T(8,128)(2,1)S(1)} %shard_map.47), channel_id=1, source_target_pairs={{0,6},{1,2},{2,1},{3,5},{4,7},{5,3},{6,0},{7,4},{8,14},{9,10},{10,... | collective-permute-start | bytes 98312 | tf_op jit(solution)/shard_map/ppermute | solution.py:209
  22.5 3.8 %collective-permute-start.8 = (bf16[8,1024]{1,0:T(8,128)(2,1)S(1)}, bf16[8,1024]{1,0:T(8,128)(2,1)S(1)}, u32[]{:S(2)}, u32[]{:S(2)}) collective-permute-start(bf16[8,1024]{1,0:T(8,128)(2,1)S(1)} %get-tuple-element.14), channel_id=1, source_target_pairs={{0,1},{1,0},{2,3},{3,2},{4,5},{5,4},{6,7},{7,6},{8,9},{9,8},{10,11... | collective-permute-start | bytes 49160 | tf_op jit(solution)/shard_map/ppermute | solution.py:202
  25.1 1.3 %collective-permute-start.12 = (bf16[8,1024]{1,0:T(8,128)(2,1)S(1)}, bf16[8,1024]{1,0:T(8,128)(2,1)S(1)}, u32[]{:S(2)}, u32[]{:S(2)}) collective-permute-start(bf16[8,1024]{1,0:T(8,128)(2,1)S(1)} %shard_map.48), channel_id=1, source_target_pairs={{0,4},{1,5},{2,6},{3,7},{4,0},{5,1},{6,2},{7,3},{8,12},{9,13},{10,... | collective-permute-start | bytes 49160 | tf_op jit(solution)/shard_map/ppermute | solution.py:202

commit v12 on v11

--- a/solution.py
+++ b/solution.py
@@ -105,11 +105,12 @@
 
 def combine(*parts):
     top = functools.reduce(jnp.maximum, [log for log, _ in parts])
-    weights = [jnp.exp(log - top) for log, _ in parts]
+    weights = [jnp.exp2(log - top) for log, _ in parts]
     total = functools.reduce(jnp.add, weights)
-    factors = [w / total for w in weights]
+    share = 1 / total
+    factors = [w * share for w in weights]
     columns = zip(*[averages for _, averages in parts])
-    return top + jnp.log(total), [sum(f * x for f, x in zip(factors, c)) for c in columns]
+    return top + jnp.log2(total), [sum(f * x for f, x in zip(factors, c)) for c in columns]
 
 
 def rows_of(parts, *ranges):
@@ -122,13 +123,13 @@
     out_refs = refs[-4:]
     width, classes = k_ref.shape[1], lt_ref.shape[0]
     queries = jnp.concatenate([r[...] for r in block_refs], axis=0)
-    gain = SCORE_GAIN / math.sqrt(width)
+    gain = SCORE_GAIN * math.log2(math.e) / math.sqrt(width)
     dot = functools.partial(lax.dot_general, preferred_element_type=jnp.float32)
     by_rows, by_columns = (((1,), (1,)), ((), ())), (((1,), (0,)), ((), ()))
     chunks = [slice(lo, lo + 256) for lo in range(0, k_ref.shape[0], 256)]
     scores = [dot(k_ref[at], queries, by_rows) * gain for at in chunks]
     peaks = jnp.max(functools.reduce(jnp.maximum, scores), axis=0, keepdims=True)
-    weights = [jnp.exp(s - peaks) for s in scores]
+    weights = [jnp.exp2(s - peaks) for s in scores]
     totals = jnp.sum(sum(weights), axis=0, keepdims=True)
     weights = jnp.concatenate([w.astype(jnp.bfloat16) for w in weights], axis=0)
 
@@ -136,7 +137,7 @@
     votes = dot(lt_ref[...], weights, by_columns) * share
     spare = jnp.ones((out_refs[0].shape[1] - classes, queries.shape[0]), jnp.float32)
     averages = tiles(jnp.concatenate([votes, spare], axis=0).T)
-    parts = ((peaks + jnp.log(totals)).T, averages)
+    parts = ((peaks + jnp.log2(totals)).T, averages)
     for put, ref, chosen in zip((encode, encode, keep, keep), out_refs, places):
         put(ref, 0, rows_of(parts, *[(lo * unit, (lo + 1) * unit) for lo in chosen]), classes)
 

time: 27.3 us -> 27.2 us (level)
  no operation moved by 1% of the time
where the time goes in v12:
time: 27.2 us; the launch traced here: 27 us
  starting transfers between devices  13.7 us (50%)
  waiting for transfers between devices  8.69 us (32%)
  Pallas kernels  3.91 us (14%)
  local copies, waits for them, and re-layouts  0.71 us (3%)
    ppermute x11, starting transfers between devices, swap(): return lax.ppermute(block, AXES, [(i, i ^ bit) for i in range(size)])  8.19 us
    ppermute x11, waiting for transfers between devices, swap(): return lax.ppermute(block, AXES, [(i, i ^ bit) for i in range(size)])  6.03 us
    ppermute x2, starting transfers between devices, swap_far(): return lax.ppermute(block, AXES, [(i, partner(i)) for i in range(size)])  5.46 us
    pallas_call x13, Pallas kernels, call(): pl.pallas_call(kernel, out_shape=outs, in_specs=[VMEM] * len(args), out_s...  3.91 us
    ppermute x2, waiting for transfers between devices, swap_far(): return lax.ppermute(block, AXES, [(i, partner(i)) for i in range(size)])  2.66 us
    unnamed x6, local copies, waits for them, and re-layouts  0.71 us
  transfers between devices with their start and end apart: 13, of which 10 were waited for; matrix products, arithmetic and copies ran while one was open for 0% of the time, Pallas kernels for 3%

profile of v12, /device:TPU:0, one launch (start us, length us, event | category | flops | bytes accessed | tf_op | source)
XLA Modules:
  0.0 27.0 jit_solution(7339128035201979954)
XLA Ops:
  0.0 0.5 %collective-permute-start = (bf16[8,768]{1,0:T(8,128)(2,1)}, bf16[8,768]{1,0:T(8,128)(2,1)S(1)}, u32[]{:S(2)}, u32[]{:S(2)}) collective-permute-start(bf16[8,768]{1,0:T(8,128)(2,1)} %a_ref.1), channel_id=1, source_target_pairs={{0,4},{1,5},{2,6},{3,7},{4,0},{5,1},{6,2},{7,3},{8,12},{9,13},{10,... | collective-permute-start | bytes 36872 | tf_op jit(solution)/shard_map/ppermute | solution.py:203
  0.5 0.7 %copy-done.2 = bf16[8,768]{1,0:T(8,128)(2,1)S(1)} copy-done((bf16[8,768]{1,0:T(8,128)(2,1)S(1)}, bf16[8,768]{1,0:T(8,128)(2,1)}, u32[]{:S(2)}) %copy-start.2) | copy-done | bytes 12312
  1.2 0.3 %collective-permute-done.b_ref = bf16[8,768]{1,0:T(8,128)(2,1)S(1)} collective-permute-done((bf16[8,768]{1,0:T(8,128)(2,1)}, bf16[8,768]{1,0:T(8,128)(2,1)S(1)}, u32[]{:S(2)}, u32[]{:S(2)}) %collective-permute-start) | collective-permute-done | bytes 12320 | tf_op jit(solution)/shard_map/ppermute | solution.py:203
  1.5 3.7 %collective-permute-start.2 = (bf16[16,768]{1,0:T(8,128)(2,1)S(1)}, bf16[16,768]{1,0:T(8,128)(2,1)S(1)}, u32[]{:S(2)}, u32[]{:S(2)}) collective-permute-start(bf16[16,768]{1,0:T(8,128)(2,1)S(1)} %shard_map.38.a_ref.refs_0_), channel_id=1, source_target_pairs={{0,6},{1,2},{2,1},{3,5},{4,7},{5,3},{6,0},{7,4},{8,14},{9,10},{10,... | collective-permute-start | bytes 73736 | tf_op jit(solution)/shard_map/ppermute | solution.py:210
  5.2 0.8 %collective-permute-start.1 = (bf16[16,768]{1,0:T(8,128)(2,1)S(1)}, bf16[16,768]{1,0:T(8,128)(2,1)S(1)}, u32[]{:S(2)}, u32[]{:S(2)}) collective-permute-start(bf16[16,768]{1,0:T(8,128)(2,1)S(1)} %shard_map.38.a_ref.refs_0_), channel_id=1, source_target_pairs={{0,1},{1,0},{2,3},{3,2},{4,5},{5,4},{6,7},{7,6},{8,9},{9,8},{10,11... | collective-permute-start | bytes 73736 | tf_op jit(solution)/shard_map/ppermute | solution.py:203
  6.0 0.7 %collective-permute-done.2.b_ref.refs_2_ = bf16[16,768]{1,0:T(8,128)(2,1)S(1)} collective-permute-done((bf16[16,768]{1,0:T(8,128)(2,1)S(1)}, bf16[16,768]{1,0:T(8,128)(2,1)S(1)}, u32[]{:S(2)}, u32[]{:S(2)}) %collective-permute-start.2) | collective-permute-done | bytes 24608 | tf_op jit(solution)/shard_map/ppermute | solution.py:210
  6.7 0.9 %collective-permute-start.3 = (bf16[16,768]{1,0:T(8,128)(2,1)S(1)}, bf16[16,768]{1,0:T(8,128)(2,1)S(1)}, u32[]{:S(2)}, u32[]{:S(2)}) collective-permute-start(bf16[16,768]{1,0:T(8,128)(2,1)S(1)} %collective-permute-done.2.b_ref.refs_2_), channel_id=1, source_target_pairs={{0,4},{1,5},{2,6},{3,7},{4,0},{5,1},{6,2},{7,3},{8,12},{9,13},{10,... | collective-permute-start | bytes 73736 | tf_op jit(solution)/shard_map/ppermute | solution.py:203
  7.7 1.2 %collective-permute-start.4 = (bf16[32,768]{1,0:T(8,128)(2,1)S(1)}, bf16[32,768]{1,0:T(8,128)(2,1)S(1)}, u32[]{:S(2)}, u32[]{:S(2)}) collective-permute-start(bf16[32,768]{1,0:T(8,128)(2,1)S(1)} %shard_map.39), channel_id=1, source_target_pairs={{0,12},{1,13},{2,14},{3,15},{4,8},{5,9},{6,10},{7,11},{8,4},{9,5},... | collective-permute-start | bytes 147464 | tf_op jit(solution)/shard_map/ppermute | solution.py:203
  8.8 0.3 %collective-permute-done.1.a_ref.refs_1_ = bf16[16,768]{1,0:T(8,128)(2,1)S(1)} collective-permute-done((bf16[16,768]{1,0:T(8,128)(2,1)S(1)}, bf16[16,768]{1,0:T(8,128)(2,1)S(1)}, u32[]{:S(2)}, u32[]{:S(2)}) %collective-permute-start.1) | collective-permute-done | bytes 24608 | tf_op jit(solution)/shard_map/ppermute | solution.py:203
  9.1 1.3 %collective-permute-start.5 = (bf16[32,768]{1,0:T(8,128)(2,1)S(1)}, bf16[32,768]{1,0:T(8,128)(2,1)S(1)}, u32[]{:S(2)}, u32[]{:S(2)}) collective-permute-start(bf16[32,768]{1,0:T(8,128)(2,1)S(1)} %shard_map.40), channel_id=1, source_target_pairs={{0,12},{1,13},{2,14},{3,15},{4,8},{5,9},{6,10},{7,11},{8,4},{9,5},... | collective-permute-start | bytes 147464 | tf_op jit(solution)/shard_map/ppermute | solution.py:203
  10.4 1.1 %collective-permute-done.4.refs_4_ = bf16[32,768]{1,0:T(8,128)(2,1)S(1)} collective-permute-done((bf16[32,768]{1,0:T(8,128)(2,1)S(1)}, bf16[32,768]{1,0:T(8,128)(2,1)S(1)}, u32[]{:S(2)}, u32[]{:S(2)}) %collective-permute-start.4) | collective-permute-done | bytes 49184 | tf_op jit(solution)/shard_map/ppermute | solution.py:203
  11.6 1.4 %collective-permute-done.5.refs_5_ = bf16[32,768]{1,0:T(8,128)(2,1)S(1)} collective-permute-done((bf16[32,768]{1,0:T(8,128)(2,1)S(1)}, bf16[32,768]{1,0:T(8,128)(2,1)S(1)}, u32[]{:S(2)}, u32[]{:S(2)}) %collective-permute-start.5) | collective-permute-done | bytes 49184 | tf_op jit(solution)/shard_map/ppermute | solution.py:203
  13.0 2.4 %shard_map.41 = (bf16[32,1024]{1,0:T(8,128)(2,1)S(1)}, bf16[32,1024]{1,0:T(8,128)(2,1)S(1)}, f32[32,1024]{1,0:T(8,128)S(1)}, f32[32,1024]{1,0:T(8,128)S(1)}) custom-call(bf16[16,768]{1,0:T(8,128)(2,1)S(1)} %shard_map.38.a_ref.refs_0_, bf16[16,768]{1,0:T(8,128)(2,1)S(1)} %collective-permute-done.1.a_ref.refs_1_, ...), custom_call_target="tpu_custom_call" | custom-call | flops 926941184 | bytes 7241728 | tf_op jit(solution)/shard_map/pallas_call | solution.py:27
  15.4 0.2 collective-permute-start.9
  15.6 0.4 %collective-permute-start.6 = (bf16[32,1024]{1,0:T(8,128)(2,1)S(1)}, bf16[32,1024]{1,0:T(8,128)(2,1)S(1)}, u32[]{:S(2)}, u32[]{:S(2)}) collective-permute-start(bf16[32,1024]{1,0:T(8,128)(2,1)S(1)} %get-tuple-element.12), channel_id=1, source_target_pairs={{0,4},{1,5},{2,6},{3,7},{4,0},{5,1},{6,2},{7,3},{8,12},{9,13},{10,... | collective-permute-start | bytes 196616 | tf_op jit(solution)/shard_map/ppermute | solution.py:203
  16.0 0.7 %collective-permute-done.9.other_ref = bf16[32,1024]{1,0:T(8,128)(2,1)S(1)} collective-permute-done((bf16[32,1024]{1,0:T(8,128)(2,1)S(1)}, bf16[32,1024]{1,0:T(8,128)(2,1)S(1)}, u32[]{:S(2)}, u32[]{:S(2)}) %collective-permute-start.9) | collective-permute-done | bytes 65568 | tf_op jit(solution)/shard_map/ppermute | solution.py:203
  16.7 0.1 shard_map.46
  16.9 1.3 %collective-permute-start.10 = (bf16[16,1024]{1,0:T(8,128)(2,1)S(1)}, bf16[16,1024]{1,0:T(8,128)(2,1)S(1)}, u32[]{:S(2)}, u32[]{:S(2)}) collective-permute-start(bf16[16,1024]{1,0:T(8,128)(2,1)S(1)} %shard_map.46), channel_id=1, source_target_pairs={{0,12},{1,13},{2,14},{3,15},{4,8},{5,9},{6,10},{7,11},{8,4},{9,5},... | collective-permute-start | bytes 98312 | tf_op jit(solution)/shard_map/ppermute | solution.py:203
  18.2 0.1 shard_map.43
  18.3 0.6 %collective-permute-start.7 = (bf16[16,1024]{1,0:T(8,128)(2,1)S(1)}, bf16[16,1024]{1,0:T(8,128)(2,1)S(1)}, u32[]{:S(2)}, u32[]{:S(2)}) collective-permute-start(bf16[16,1024]{1,0:T(8,128)(2,1)S(1)} %shard_map.43), channel_id=1, source_target_pairs={{0,12},{1,13},{2,14},{3,15},{4,8},{5,9},{6,10},{7,11},{8,4},{9,5},... | collective-permute-start | bytes 98312 | tf_op jit(solution)/shard_map/ppermute | solution.py:203
  18.9 0.1 shard_map.45.mine_ref
  19.0 1.3 %collective-permute-done.10.other_ref = bf16[16,1024]{1,0:T(8,128)(2,1)S(1)} collective-permute-done((bf16[16,1024]{1,0:T(8,128)(2,1)S(1)}, bf16[16,1024]{1,0:T(8,128)(2,1)S(1)}, u32[]{:S(2)}, u32[]{:S(2)}) %collective-permute-start.10) | collective-permute-done | bytes 32800 | tf_op jit(solution)/shard_map/ppermute | solution.py:203
  20.3 0.1 shard_map.47
  20.4 1.8 %collective-permute-start.11 = (bf16[16,1024]{1,0:T(8,128)(2,1)S(1)}, bf16[16,1024]{1,0:T(8,128)(2,1)S(1)}, u32[]{:S(2)}, u32[]{:S(2)}) collective-permute-start(bf16[16,1024]{1,0:T(8,128)(2,1)S(1)} %shard_map.47), channel_id=1, source_target_pairs={{0,6},{1,2},{2,1},{3,5},{4,7},{5,3},{6,0},{7,4},{8,14},{9,10},{10,... | collective-permute-start | bytes 98312 | tf_op jit(solution)/shard_map/ppermute | solution.py:210
  22.2 0.1 shard_map.42.mine_ref
  22.3 0.1 shard_map.44
  22.4 0.7 %collective-permute-start.8 = (bf16[8,1024]{1,0:T(8,128)(2,1)S(1)}, bf16[8,1024]{1,0:T(8,128)(2,1)S(1)}, u32[]{:S(2)}, u32[]{:S(2)}) collective-permute-start(bf16[8,1024]{1,0:T(8,128)(2,1)S(1)} %get-tuple-element.14), channel_id=1, source_target_pairs={{0,1},{1,0},{2,3},{3,2},{4,5},{5,4},{6,7},{7,6},{8,9},{9,8},{10,11... | collective-permute-start | bytes 49160 | tf_op jit(solution)/shard_map/ppermute | solution.py:203
  23.1 1.9 %collective-permute-done.11.a_ref.far_ref = bf16[16,1024]{1,0:T(8,128)(2,1)S(1)} collective-permute-done((bf16[16,1024]{1,0:T(8,128)(2,1)S(1)}, bf16[16,1024]{1,0:T(8,128)(2,1)S(1)}, u32[]{:S(2)}, u32[]{:S(2)}) %collective-permute-start.11) | collective-permute-done | bytes 32800 | tf_op jit(solution)/shard_map/ppermute | solution.py:210
  25.0 0.4 %collective-permute-start.12 = (bf16[8,1024]{1,0:T(8,128)(2,1)S(1)}, bf16[8,1024]{1,0:T(8,128)(2,1)S(1)}, u32[]{:S(2)}, u32[]{:S(2)}) collective-permute-start(bf16[8,1024]{1,0:T(8,128)(2,1)S(1)} %shard_map.48), channel_id=1, source_target_pairs={{0,4},{1,5},{2,6},{3,7},{4,0},{5,1},{6,2},{7,3},{8,12},{9,13},{10,... | collective-permute-start | bytes 49160 | tf_op jit(solution)/shard_map/ppermute | solution.py:203
  25.5 0.8 %collective-permute-done.8.near_ref = bf16[8,1024]{1,0:T(8,128)(2,1)S(1)} collective-permute-done((bf16[8,1024]{1,0:T(8,128)(2,1)S(1)}, bf16[8,1024]{1,0:T(8,128)(2,1)S(1)}, u32[]{:S(2)}, u32[]{:S(2)}) %collective-permute-start.8) | collective-permute-done | bytes 16416 | tf_op jit(solution)/shard_map/ppermute | solution.py:203
  26.2 0.1 collective-permute-done.12.across_ref
  26.3 0.7 %shard_map.49 = f32[8,1000]{1,0:T(8,128)} custom-call(f32[8,1024]{1,0:T(8,128)S(1)} %get-tuple-element.13.own_ref, bf16[8,1024]{1,0:T(8,128)(2,1)S(1)} %collective-permute-done.8.near_ref, bf16[16,1024]{1,0:T(8,128)(2,1)S(1)} %collective-permute-done.11.a_ref.far_ref, bf16[8,1024]{1,0:T(8,128)(2,1)S(1)} %collective-permute-done.12.across_ref), custom_call_target="tpu_custom_call" | custom-call | tf_op jit(solution)/shard_map/pallas_call | solution.py:27
  (13 shorter events, 0.0 us)
Async XLA Ops:
  0.0 1.5 %collective-permute-start = (bf16[8,768]{1,0:T(8,128)(2,1)}, bf16[8,768]{1,0:T(8,128)(2,1)S(1)}, u32[]{:S(2)}, u32[]{:S(2)}) collective-permute-start(bf16[8,768]{1,0:T(8,128)(2,1)} %a_ref.1), channel_id=1, source_target_pairs={{0,4},{1,5},{2,6},{3,7},{4,0},{5,1},{6,2},{7,3},{8,12},{9,13},{10,... | collective-permute-start | bytes 36872 | tf_op jit(solution)/shard_map/ppermute | solution.py:203
  0.5 0.7 %copy-start.2 = (bf16[8,768]{1,0:T(8,128)(2,1)S(1)}, bf16[8,768]{1,0:T(8,128)(2,1)}, u32[]{:S(2)}) copy-start(bf16[8,768]{1,0:T(8,128)(2,1)} %a_ref.1) | copy-start | bytes 36868
  1.5 5.2 %collective-permute-start.2 = (bf16[16,768]{1,0:T(8,128)(2,1)S(1)}, bf16[16,768]{1,0:T(8,128)(2,1)S(1)}, u32[]{:S(2)}, u32[]{:S(2)}) collective-permute-start(bf16[16,768]{1,0:T(8,128)(2,1)S(1)} %shard_map.38.a_ref.refs_0_), channel_id=1, source_target_pairs={{0,6},{1,2},{2,1},{3,5},{4,7},{5,3},{6,0},{7,4},{8,14},{9,10},{10,... | collective-permute-start | bytes 73736 | tf_op jit(solution)/shard_map/ppermute | solution.py:210
  5.2 3.9 %collective-permute-start.1 = (bf16[16,768]{1,0:T(8,128)(2,1)S(1)}, bf16[16,768]{1,0:T(8,128)(2,1)S(1)}, u32[]{:S(2)}, u32[]{:S(2)}) collective-permute-start(bf16[16,768]{1,0:T(8,128)(2,1)S(1)} %shard_map.38.a_ref.refs_0_), channel_id=1, source_target_pairs={{0,1},{1,0},{2,3},{3,2},{4,5},{5,4},{6,7},{7,6},{8,9},{9,8},{10,11... | collective-permute-start | bytes 73736 | tf_op jit(solution)/shard_map/ppermute | solution.py:203
  6.7 2.4 %collective-permute-start.3 = (bf16[16,768]{1,0:T(8,128)(2,1)S(1)}, bf16[16,768]{1,0:T(8,128)(2,1)S(1)}, u32[]{:S(2)}, u32[]{:S(2)}) collective-permute-start(bf16[16,768]{1,0:T(8,128)(2,1)S(1)} %collective-permute-done.2.b_ref.refs_2_), channel_id=1, source_target_pairs={{0,4},{1,5},{2,6},{3,7},{4,0},{5,1},{6,2},{7,3},{8,12},{9,13},{10,... | collective-permute-start | bytes 73736 | tf_op jit(solution)/shard_map/ppermute | solution.py:203
  7.7 5.3 %copy-start = (bf16[2048,1000]{0,1:T(8,128)(2,1)S(1)}, bf16[2048,1000]{0,1:T(8,128)(2,1)}, u32[]{:S(2)}) copy-start(bf16[2048,1000]{0,1:T(8,128)(2,1)} %param.5) | copy-start | bytes 12288004
  7.7 5.3 %copy-start.1 = (bf16[2048,768]{1,0:T(8,128)(2,1)S(1)}, bf16[2048,768]{1,0:T(8,128)(2,1)}, u32[]{:S(2)}) copy-start(bf16[2048,768]{1,0:T(8,128)(2,1)} %refs_6_.1) | copy-start | bytes 9437188
  7.7 3.9 %collective-permute-start.4 = (bf16[32,768]{1,0:T(8,128)(2,1)S(1)}, bf16[32,768]{1,0:T(8,128)(2,1)S(1)}, u32[]{:S(2)}, u32[]{:S(2)}) collective-permute-start(bf16[32,768]{1,0:T(8,128)(2,1)S(1)} %shard_map.39), channel_id=1, source_target_pairs={{0,12},{1,13},{2,14},{3,15},{4,8},{5,9},{6,10},{7,11},{8,4},{9,5},... | collective-permute-start | bytes 147464 | tf_op jit(solution)/shard_map/ppermute | solution.py:203
  9.1 3.8 %collective-permute-start.5 = (bf16[32,768]{1,0:T(8,128)(2,1)S(1)}, bf16[32,768]{1,0:T(8,128)(2,1)S(1)}, u32[]{:S(2)}, u32[]{:S(2)}) collective-permute-start(bf16[32,768]{1,0:T(8,128)(2,1)S(1)} %shard_map.40), channel_id=1, source_target_pairs={{0,12},{1,13},{2,14},{3,15},{4,8},{5,9},{6,10},{7,11},{8,4},{9,5},... | collective-permute-start | bytes 147464 | tf_op jit(solution)/shard_map/ppermute | solution.py:203
  15.4 1.3 %collective-permute-start.9 = (bf16[32,1024]{1,0:T(8,128)(2,1)S(1)}, bf16[32,1024]{1,0:T(8,128)(2,1)S(1)}, u32[]{:S(2)}, u32[]{:S(2)}) collective-permute-start(bf16[32,1024]{1,0:T(8,128)(2,1)S(1)} %get-tuple-element.16), channel_id=1, source_target_pairs={{0,4},{1,5},{2,6},{3,7},{4,0},{5,1},{6,2},{7,3},{8,12},{9,13},{10,... | collective-permute-start | bytes 196616 | tf_op jit(solution)/shard_map/ppermute | solution.py:203
  15.6 2.6 %collective-permute-start.6 = (bf16[32,1024]{1,0:T(8,128)(2,1)S(1)}, bf16[32,1024]{1,0:T(8,128)(2,1)S(1)}, u32[]{:S(2)}, u32[]{:S(2)}) collective-permute-start(bf16[32,1024]{1,0:T(8,128)(2,1)S(1)} %get-tuple-element.12), channel_id=1, source_target_pairs={{0,4},{1,5},{2,6},{3,7},{4,0},{5,1},{6,2},{7,3},{8,12},{9,13},{10,... | collective-permute-start | bytes 196616 | tf_op jit(solution)/shard_map/ppermute | solution.py:203
  16.9 3.4 %collective-permute-start.10 = (bf16[16,1024]{1,0:T(8,128)(2,1)S(1)}, bf16[16,1024]{1,0:T(8,128)(2,1)S(1)}, u32[]{:S(2)}, u32[]{:S(2)}) collective-permute-start(bf16[16,1024]{1,0:T(8,128)(2,1)S(1)} %shard_map.46), channel_id=1, source_target_pairs={{0,12},{1,13},{2,14},{3,15},{4,8},{5,9},{6,10},{7,11},{8,4},{9,5},... | collective-permute-start | bytes 98312 | tf_op jit(solution)/shard_map/ppermute | solution.py:203
  18.3 4.0 %collective-permute-start.7 = (bf16[16,1024]{1,0:T(8,128)(2,1)S(1)}, bf16[16,1024]{1,0:T(8,128)(2,1)S(1)}, u32[]{:S(2)}, u32[]{:S(2)}) collective-permute-start(bf16[16,1024]{1,0:T(8,128)(2,1)S(1)} %shard_map.43), channel_id=1, source_target_pairs={{0,12},{1,13},{2,14},{3,15},{4,8},{5,9},{6,10},{7,11},{8,4},{9,5},... | collective-permute-start | bytes 98312 | tf_op jit(solution)/shard_map/ppermute | solution.py:203
  20.4 4.6 %collective-permute-start.11 = (bf16[16,1024]{1,0:T(8,128)(2,1)S(1)}, bf16[16,1024]{1,0:T(8,128)(2,1)S(1)}, u32[]{:S(2)}, u32[]{:S(2)}) collective-permute-start(bf16[16,1024]{1,0:T(8,128)(2,1)S(1)} %shard_map.47), channel_id=1, source_target_pairs={{0,6},{1,2},{2,1},{3,5},{4,7},{5,3},{6,0},{7,4},{8,14},{9,10},{10,... | collective-permute-start | bytes 98312 | tf_op jit(solution)/shard_map/ppermute | solution.py:210
  22.4 3.8 %collective-permute-start.8 = (bf16[8,1024]{1,0:T(8,128)(2,1)S(1)}, bf16[8,1024]{1,0:T(8,128)(2,1)S(1)}, u32[]{:S(2)}, u32[]{:S(2)}) collective-permute-start(bf16[8,1024]{1,0:T(8,128)(2,1)S(1)} %get-tuple-element.14), channel_id=1, source_target_pairs={{0,1},{1,0},{2,3},{3,2},{4,5},{5,4},{6,7},{7,6},{8,9},{9,8},{10,11... | collective-permute-start | bytes 49160 | tf_op jit(solution)/shard_map/ppermute | solution.py:203
  25.0 1.3 %collective-permute-start.12 = (bf16[8,1024]{1,0:T(8,128)(2,1)S(1)}, bf16[8,1024]{1,0:T(8,128)(2,1)S(1)}, u32[]{:S(2)}, u32[]{:S(2)}) collective-permute-start(bf16[8,1024]{1,0:T(8,128)(2,1)S(1)} %shard_map.48), channel_id=1, source_target_pairs={{0,4},{1,5},{2,6},{3,7},{4,0},{5,1},{6,2},{7,3},{8,12},{9,13},{10,... | collective-permute-start | bytes 49160 | tf_op jit(solution)/shard_map/ppermute | solution.py:203

commit v13 on v12

--- a/solution.py
+++ b/solution.py
@@ -186,16 +186,25 @@
     return call(tail_kernel, out, a)
 
 
-def finish_kernel(classes, own_ref, near_ref, far_ref, across_ref, out_ref):
-    rows = out_ref.shape[0]
-    came = [r[...].astype(jnp.float32)[:rows] for r in (near_ref, far_ref, across_ref)]
-    _, averages = combine(kept(own_ref[...], classes), *[decoded(r, classes) for r in came])
+def add_kernel(classes, own_ref, far_ref, out_ref):
+    far = far_ref[...].astype(jnp.float32)[: own_ref.shape[0]]
+    keep(out_ref, 0, combine(kept(own_ref[...], classes), decoded(far, classes)), classes)
+
+
+def add(own, far, classes):
+    out = record_shape(own.shape[0], classes)
+    return call(functools.partial(add_kernel, classes), out, own, far)
+
+
+def finish_kernel(classes, own_ref, near_ref, across_ref, out_ref):
+    came = [decoded(r[...].astype(jnp.float32), classes) for r in (near_ref, across_ref)]
+    _, averages = combine(kept(own_ref[...], classes), *came)
     out_ref[...] = jnp.concatenate([jnp.log(x) for x in averages], axis=1)[:, :classes]
 
 
-def finish(own, near, far, across, classes):
+def finish(own, near, across, classes):
     out = jax.ShapeDtypeStruct((own.shape[0], classes), jnp.float32)
-    return call(functools.partial(finish_kernel, classes), out, own, near, far, across)
+    return call(functools.partial(finish_kernel, classes), out, own, near, across)
 
 
 def local(size, core, lead, queries, bank_keys, bank_labels):
@@ -254,7 +263,7 @@
     far = swap_far(far)
     near = swap(near, 1)
     across = swap(tail(far), core)
-    return finish(own, near, far, across, classes)
+    return finish(add(own, far, classes), near, across, classes)
 
 
 def solution(mesh):

time: 27.2 us -> 27.2 us (level)
    pallas_call x13 -> x14, Pallas kernels: 3.91 us -> 4 us  [call(): pl.pallas_call(kernel, out_shape=outs, in_specs=[VMEM] * len(args), out_s...]
where the time goes in v13:
time: 27.2 us; the launch traced here: 27 us
  starting transfers between devices  13.7 us (50%)
  waiting for transfers between devices  8.58 us (32%)
  Pallas kernels  4 us (15%)
  local copies, waits for them, and re-layouts  0.71 us (3%)
    ppermute x11, starting transfers between devices, swap(): return lax.ppermute(block, AXES, [(i, i ^ bit) for i in range(size)])  8.19 us
    ppermute x11, waiting for transfers between devices, swap(): return lax.ppermute(block, AXES, [(i, i ^ bit) for i in range(size)])  5.93 us
    ppermute x2, starting transfers between devices, swap_far(): return lax.ppermute(block, AXES, [(i, partner(i)) for i in range(size)])  5.46 us
    pallas_call x14, Pallas kernels, call(): pl.pallas_call(kernel, out_shape=outs, in_specs=[VMEM] * len(args), out_s...  4 us
    ppermute x2, waiting for transfers between devices, swap_far(): return lax.ppermute(block, AXES, [(i, partner(i)) for i in range(size)])  2.66 us
    unnamed x6, local copies, waits for them, and re-layouts  0.71 us
  transfers between devices with their start and end apart: 13, of which 10 were waited for; matrix products, arithmetic and copies ran while one was open for 0% of the time, Pallas kernels for 3%

profile of v13, /device:TPU:0, one launch (start us, length us, event | category | flops | bytes accessed | tf_op | source)
XLA Modules:
  0.0 27.0 jit_solution(3480432676855347276)
XLA Ops:
  0.0 0.5 %collective-permute-start = (bf16[8,768]{1,0:T(8,128)(2,1)}, bf16[8,768]{1,0:T(8,128)(2,1)S(1)}, u32[]{:S(2)}, u32[]{:S(2)}) collective-permute-start(bf16[8,768]{1,0:T(8,128)(2,1)} %a_ref.1), channel_id=1, source_target_pairs={{0,4},{1,5},{2,6},{3,7},{4,0},{5,1},{6,2},{7,3},{8,12},{9,13},{10,... | collective-permute-start | bytes 36872 | tf_op jit(solution)/shard_map/ppermute | solution.py:212
  0.5 0.7 %copy-done.2 = bf16[8,768]{1,0:T(8,128)(2,1)S(1)} copy-done((bf16[8,768]{1,0:T(8,128)(2,1)S(1)}, bf16[8,768]{1,0:T(8,128)(2,1)}, u32[]{:S(2)}) %copy-start.2) | copy-done | bytes 12312
  1.2 0.3 %collective-permute-done.b_ref = bf16[8,768]{1,0:T(8,128)(2,1)S(1)} collective-permute-done((bf16[8,768]{1,0:T(8,128)(2,1)}, bf16[8,768]{1,0:T(8,128)(2,1)S(1)}, u32[]{:S(2)}, u32[]{:S(2)}) %collective-permute-start) | collective-permute-done | bytes 12320 | tf_op jit(solution)/shard_map/ppermute | solution.py:212
  1.5 3.7 %collective-permute-start.2 = (bf16[16,768]{1,0:T(8,128)(2,1)S(1)}, bf16[16,768]{1,0:T(8,128)(2,1)S(1)}, u32[]{:S(2)}, u32[]{:S(2)}) collective-permute-start(bf16[16,768]{1,0:T(8,128)(2,1)S(1)} %shard_map.38.a_ref.refs_0_), channel_id=1, source_target_pairs={{0,6},{1,2},{2,1},{3,5},{4,7},{5,3},{6,0},{7,4},{8,14},{9,10},{10,... | collective-permute-start | bytes 73736 | tf_op jit(solution)/shard_map/ppermute | solution.py:219
  5.2 0.8 %collective-permute-start.1 = (bf16[16,768]{1,0:T(8,128)(2,1)S(1)}, bf16[16,768]{1,0:T(8,128)(2,1)S(1)}, u32[]{:S(2)}, u32[]{:S(2)}) collective-permute-start(bf16[16,768]{1,0:T(8,128)(2,1)S(1)} %shard_map.38.a_ref.refs_0_), channel_id=1, source_target_pairs={{0,1},{1,0},{2,3},{3,2},{4,5},{5,4},{6,7},{7,6},{8,9},{9,8},{10,11... | collective-permute-start | bytes 73736 | tf_op jit(solution)/shard_map/ppermute | solution.py:212
  6.0 0.7 %collective-permute-done.2.b_ref.refs_2_ = bf16[16,768]{1,0:T(8,128)(2,1)S(1)} collective-permute-done((bf16[16,768]{1,0:T(8,128)(2,1)S(1)}, bf16[16,768]{1,0:T(8,128)(2,1)S(1)}, u32[]{:S(2)}, u32[]{:S(2)}) %collective-permute-start.2) | collective-permute-done | bytes 24608 | tf_op jit(solution)/shard_map/ppermute | solution.py:219
  6.7 0.9 %collective-permute-start.3 = (bf16[16,768]{1,0:T(8,128)(2,1)S(1)}, bf16[16,768]{1,0:T(8,128)(2,1)S(1)}, u32[]{:S(2)}, u32[]{:S(2)}) collective-permute-start(bf16[16,768]{1,0:T(8,128)(2,1)S(1)} %collective-permute-done.2.b_ref.refs_2_), channel_id=1, source_target_pairs={{0,4},{1,5},{2,6},{3,7},{4,0},{5,1},{6,2},{7,3},{8,12},{9,13},{10,... | collective-permute-start | bytes 73736 | tf_op jit(solution)/shard_map/ppermute | solution.py:212
  7.7 1.2 %collective-permute-start.4 = (bf16[32,768]{1,0:T(8,128)(2,1)S(1)}, bf16[32,768]{1,0:T(8,128)(2,1)S(1)}, u32[]{:S(2)}, u32[]{:S(2)}) collective-permute-start(bf16[32,768]{1,0:T(8,128)(2,1)S(1)} %shard_map.39), channel_id=1, source_target_pairs={{0,12},{1,13},{2,14},{3,15},{4,8},{5,9},{6,10},{7,11},{8,4},{9,5},... | collective-permute-start | bytes 147464 | tf_op jit(solution)/shard_map/ppermute | solution.py:212
  8.8 0.3 %collective-permute-done.1.a_ref.refs_1_ = bf16[16,768]{1,0:T(8,128)(2,1)S(1)} collective-permute-done((bf16[16,768]{1,0:T(8,128)(2,1)S(1)}, bf16[16,768]{1,0:T(8,128)(2,1)S(1)}, u32[]{:S(2)}, u32[]{:S(2)}) %collective-permute-start.1) | collective-permute-done | bytes 24608 | tf_op jit(solution)/shard_map/ppermute | solution.py:212
  9.1 1.3 %collective-permute-start.5 = (bf16[32,768]{1,0:T(8,128)(2,1)S(1)}, bf16[32,768]{1,0:T(8,128)(2,1)S(1)}, u32[]{:S(2)}, u32[]{:S(2)}) collective-permute-start(bf16[32,768]{1,0:T(8,128)(2,1)S(1)} %shard_map.40), channel_id=1, source_target_pairs={{0,12},{1,13},{2,14},{3,15},{4,8},{5,9},{6,10},{7,11},{8,4},{9,5},... | collective-permute-start | bytes 147464 | tf_op jit(solution)/shard_map/ppermute | solution.py:212
  10.4 1.1 %collective-permute-done.4.refs_4_ = bf16[32,768]{1,0:T(8,128)(2,1)S(1)} collective-permute-done((bf16[32,768]{1,0:T(8,128)(2,1)S(1)}, bf16[32,768]{1,0:T(8,128)(2,1)S(1)}, u32[]{:S(2)}, u32[]{:S(2)}) %collective-permute-start.4) | collective-permute-done | bytes 49184 | tf_op jit(solution)/shard_map/ppermute | solution.py:212
  11.6 1.4 %collective-permute-done.5.refs_5_ = bf16[32,768]{1,0:T(8,128)(2,1)S(1)} collective-permute-done((bf16[32,768]{1,0:T(8,128)(2,1)S(1)}, bf16[32,768]{1,0:T(8,128)(2,1)S(1)}, u32[]{:S(2)}, u32[]{:S(2)}) %collective-permute-start.5) | collective-permute-done | bytes 49184 | tf_op jit(solution)/shard_map/ppermute | solution.py:212
  13.0 2.4 %shard_map.41 = (bf16[32,1024]{1,0:T(8,128)(2,1)S(1)}, bf16[32,1024]{1,0:T(8,128)(2,1)S(1)}, f32[32,1024]{1,0:T(8,128)S(1)}, f32[32,1024]{1,0:T(8,128)S(1)}) custom-call(bf16[16,768]{1,0:T(8,128)(2,1)S(1)} %shard_map.38.a_ref.refs_0_, bf16[16,768]{1,0:T(8,128)(2,1)S(1)} %collective-permute-done.1.a_ref.refs_1_, ...), custom_call_target="tpu_custom_call" | custom-call | flops 926941184 | bytes 7241728 | tf_op jit(solution)/shard_map/pallas_call | solution.py:27
  15.4 0.2 collective-permute-start.8
  15.6 0.4 %collective-permute-start.6 = (bf16[32,1024]{1,0:T(8,128)(2,1)S(1)}, bf16[32,1024]{1,0:T(8,128)(2,1)S(1)}, u32[]{:S(2)}, u32[]{:S(2)}) collective-permute-start(bf16[32,1024]{1,0:T(8,128)(2,1)S(1)} %get-tuple-element.12), channel_id=1, source_target_pairs={{0,4},{1,5},{2,6},{3,7},{4,0},{5,1},{6,2},{7,3},{8,12},{9,13},{10,... | collective-permute-start | bytes 196616 | tf_op jit(solution)/shard_map/ppermute | solution.py:212
  16.0 0.7 %collective-permute-done.8.other_ref = bf16[32,1024]{1,0:T(8,128)(2,1)S(1)} collective-permute-done((bf16[32,1024]{1,0:T(8,128)(2,1)S(1)}, bf16[32,1024]{1,0:T(8,128)(2,1)S(1)}, u32[]{:S(2)}, u32[]{:S(2)}) %collective-permute-start.8) | collective-permute-done | bytes 65568 | tf_op jit(solution)/shard_map/ppermute | solution.py:212
  16.7 0.1 shard_map.46
  16.9 1.3 %collective-permute-start.9 = (bf16[16,1024]{1,0:T(8,128)(2,1)S(1)}, bf16[16,1024]{1,0:T(8,128)(2,1)S(1)}, u32[]{:S(2)}, u32[]{:S(2)}) collective-permute-start(bf16[16,1024]{1,0:T(8,128)(2,1)S(1)} %shard_map.46), channel_id=1, source_target_pairs={{0,12},{1,13},{2,14},{3,15},{4,8},{5,9},{6,10},{7,11},{8,4},{9,5},... | collective-permute-start | bytes 98312 | tf_op jit(solution)/shard_map/ppermute | solution.py:212
  18.2 0.1 shard_map.43
  18.3 0.6 %collective-permute-start.7 = (bf16[16,1024]{1,0:T(8,128)(2,1)S(1)}, bf16[16,1024]{1,0:T(8,128)(2,1)S(1)}, u32[]{:S(2)}, u32[]{:S(2)}) collective-permute-start(bf16[16,1024]{1,0:T(8,128)(2,1)S(1)} %shard_map.43), channel_id=1, source_target_pairs={{0,12},{1,13},{2,14},{3,15},{4,8},{5,9},{6,10},{7,11},{8,4},{9,5},... | collective-permute-start | bytes 98312 | tf_op jit(solution)/shard_map/ppermute | solution.py:212
  18.9 0.1 shard_map.45.mine_ref
  19.0 1.3 %collective-permute-done.9.other_ref = bf16[16,1024]{1,0:T(8,128)(2,1)S(1)} collective-permute-done((bf16[16,1024]{1,0:T(8,128)(2,1)S(1)}, bf16[16,1024]{1,0:T(8,128)(2,1)S(1)}, u32[]{:S(2)}, u32[]{:S(2)}) %collective-permute-start.9) | collective-permute-done | bytes 32800 | tf_op jit(solution)/shard_map/ppermute | solution.py:212
  20.3 0.1 shard_map.47
  20.4 1.8 %collective-permute-start.10 = (bf16[16,1024]{1,0:T(8,128)(2,1)S(1)}, bf16[16,1024]{1,0:T(8,128)(2,1)S(1)}, u32[]{:S(2)}, u32[]{:S(2)}) collective-permute-start(bf16[16,1024]{1,0:T(8,128)(2,1)S(1)} %shard_map.47), channel_id=1, source_target_pairs={{0,6},{1,2},{2,1},{3,5},{4,7},{5,3},{6,0},{7,4},{8,14},{9,10},{10,... | collective-permute-start | bytes 98312 | tf_op jit(solution)/shard_map/ppermute | solution.py:219
  22.2 0.1 shard_map.42.mine_ref
  22.3 0.1 shard_map.44
  22.4 0.7 %collective-permute-start.11 = (bf16[8,1024]{1,0:T(8,128)(2,1)S(1)}, bf16[8,1024]{1,0:T(8,128)(2,1)S(1)}, u32[]{:S(2)}, u32[]{:S(2)}) collective-permute-start(bf16[8,1024]{1,0:T(8,128)(2,1)S(1)} %get-tuple-element.16), channel_id=1, source_target_pairs={{0,1},{1,0},{2,3},{3,2},{4,5},{5,4},{6,7},{7,6},{8,9},{9,8},{10,11... | collective-permute-start | bytes 49160 | tf_op jit(solution)/shard_map/ppermute | solution.py:212
  23.1 1.9 %collective-permute-done.10.far_ref.a_ref = bf16[16,1024]{1,0:T(8,128)(2,1)S(1)} collective-permute-done((bf16[16,1024]{1,0:T(8,128)(2,1)S(1)}, bf16[16,1024]{1,0:T(8,128)(2,1)S(1)}, u32[]{:S(2)}, u32[]{:S(2)}) %collective-permute-start.10) | collective-permute-done | bytes 32800 | tf_op jit(solution)/shard_map/ppermute | solution.py:219
  25.0 0.4 %collective-permute-start.12 = (bf16[8,1024]{1,0:T(8,128)(2,1)S(1)}, bf16[8,1024]{1,0:T(8,128)(2,1)S(1)}, u32[]{:S(2)}, u32[]{:S(2)}) collective-permute-start(bf16[8,1024]{1,0:T(8,128)(2,1)S(1)} %shard_map.49), channel_id=1, source_target_pairs={{0,4},{1,5},{2,6},{3,7},{4,0},{5,1},{6,2},{7,3},{8,12},{9,13},{10,... | collective-permute-start | bytes 49160 | tf_op jit(solution)/shard_map/ppermute | solution.py:212
  25.5 0.1 shard_map.48.own_ref
  25.6 0.7 %collective-permute-done.11.near_ref = bf16[8,1024]{1,0:T(8,128)(2,1)S(1)} collective-permute-done((bf16[8,1024]{1,0:T(8,128)(2,1)S(1)}, bf16[8,1024]{1,0:T(8,128)(2,1)S(1)}, u32[]{:S(2)}, u32[]{:S(2)}) %collective-permute-start.11) | collective-permute-done | bytes 16416 | tf_op jit(solution)/shard_map/ppermute | solution.py:212
  26.3 0.7 %shard_map.50 = f32[8,1000]{1,0:T(8,128)} custom-call(f32[8,1024]{1,0:T(8,128)S(1)} %shard_map.48.own_ref, bf16[8,1024]{1,0:T(8,128)(2,1)S(1)} %collective-permute-done.11.near_ref, bf16[8,1024]{1,0:T(8,128)(2,1)S(1)} %collective-permute-done.12.across_ref), custom_call_target="tpu_custom_call" | custom-call | tf_op jit(solution)/shard_map/pallas_call | solution.py:27
  (14 shorter events, 0.1 us)
Async XLA Ops:
  0.0 1.5 %collective-permute-start = (bf16[8,768]{1,0:T(8,128)(2,1)}, bf16[8,768]{1,0:T(8,128)(2,1)S(1)}, u32[]{:S(2)}, u32[]{:S(2)}) collective-permute-start(bf16[8,768]{1,0:T(8,128)(2,1)} %a_ref.1), channel_id=1, source_target_pairs={{0,4},{1,5},{2,6},{3,7},{4,0},{5,1},{6,2},{7,3},{8,12},{9,13},{10,... | collective-permute-start | bytes 36872 | tf_op jit(solution)/shard_map/ppermute | solution.py:212
  0.5 0.7 %copy-start.2 = (bf16[8,768]{1,0:T(8,128)(2,1)S(1)}, bf16[8,768]{1,0:T(8,128)(2,1)}, u32[]{:S(2)}) copy-start(bf16[8,768]{1,0:T(8,128)(2,1)} %a_ref.1) | copy-start | bytes 36868
  1.5 5.2 %collective-permute-start.2 = (bf16[16,768]{1,0:T(8,128)(2,1)S(1)}, bf16[16,768]{1,0:T(8,128)(2,1)S(1)}, u32[]{:S(2)}, u32[]{:S(2)}) collective-permute-start(bf16[16,768]{1,0:T(8,128)(2,1)S(1)} %shard_map.38.a_ref.refs_0_), channel_id=1, source_target_pairs={{0,6},{1,2},{2,1},{3,5},{4,7},{5,3},{6,0},{7,4},{8,14},{9,10},{10,... | collective-permute-start | bytes 73736 | tf_op jit(solution)/shard_map/ppermute | solution.py:219
  5.2 3.9 %collective-permute-start.1 = (bf16[16,768]{1,0:T(8,128)(2,1)S(1)}, bf16[16,768]{1,0:T(8,128)(2,1)S(1)}, u32[]{:S(2)}, u32[]{:S(2)}) collective-permute-start(bf16[16,768]{1,0:T(8,128)(2,1)S(1)} %shard_map.38.a_ref.refs_0_), channel_id=1, source_target_pairs={{0,1},{1,0},{2,3},{3,2},{4,5},{5,4},{6,7},{7,6},{8,9},{9,8},{10,11... | collective-permute-start | bytes 73736 | tf_op jit(solution)/shard_map/ppermute | solution.py:212
  6.7 2.4 %collective-permute-start.3 = (bf16[16,768]{1,0:T(8,128)(2,1)S(1)}, bf16[16,768]{1,0:T(8,128)(2,1)S(1)}, u32[]{:S(2)}, u32[]{:S(2)}) collective-permute-start(bf16[16,768]{1,0:T(8,128)(2,1)S(1)} %collective-permute-done.2.b_ref.refs_2_), channel_id=1, source_target_pairs={{0,4},{1,5},{2,6},{3,7},{4,0},{5,1},{6,2},{7,3},{8,12},{9,13},{10,... | collective-permute-start | bytes 73736 | tf_op jit(solution)/shard_map/ppermute | solution.py:212
  7.7 5.3 %copy-start = (bf16[2048,1000]{0,1:T(8,128)(2,1)S(1)}, bf16[2048,1000]{0,1:T(8,128)(2,1)}, u32[]{:S(2)}) copy-start(bf16[2048,1000]{0,1:T(8,128)(2,1)} %param.5) | copy-start | bytes 12288004
  7.7 5.3 %copy-start.1 = (bf16[2048,768]{1,0:T(8,128)(2,1)S(1)}, bf16[2048,768]{1,0:T(8,128)(2,1)}, u32[]{:S(2)}) copy-start(bf16[2048,768]{1,0:T(8,128)(2,1)} %refs_6_.1) | copy-start | bytes 9437188
  7.7 3.9 %collective-permute-start.4 = (bf16[32,768]{1,0:T(8,128)(2,1)S(1)}, bf16[32,768]{1,0:T(8,128)(2,1)S(1)}, u32[]{:S(2)}, u32[]{:S(2)}) collective-permute-start(bf16[32,768]{1,0:T(8,128)(2,1)S(1)} %shard_map.39), channel_id=1, source_target_pairs={{0,12},{1,13},{2,14},{3,15},{4,8},{5,9},{6,10},{7,11},{8,4},{9,5},... | collective-permute-start | bytes 147464 | tf_op jit(solution)/shard_map/ppermute | solution.py:212
  9.1 3.8 %collective-permute-start.5 = (bf16[32,768]{1,0:T(8,128)(2,1)S(1)}, bf16[32,768]{1,0:T(8,128)(2,1)S(1)}, u32[]{:S(2)}, u32[]{:S(2)}) collective-permute-start(bf16[32,768]{1,0:T(8,128)(2,1)S(1)} %shard_map.40), channel_id=1, source_target_pairs={{0,12},{1,13},{2,14},{3,15},{4,8},{5,9},{6,10},{7,11},{8,4},{9,5},... | collective-permute-start | bytes 147464 | tf_op jit(solution)/shard_map/ppermute | solution.py:212
  15.4 1.3 %collective-permute-start.8 = (bf16[32,1024]{1,0:T(8,128)(2,1)S(1)}, bf16[32,1024]{1,0:T(8,128)(2,1)S(1)}, u32[]{:S(2)}, u32[]{:S(2)}) collective-permute-start(bf16[32,1024]{1,0:T(8,128)(2,1)S(1)} %get-tuple-element.15), channel_id=1, source_target_pairs={{0,4},{1,5},{2,6},{3,7},{4,0},{5,1},{6,2},{7,3},{8,12},{9,13},{10,... | collective-permute-start | bytes 196616 | tf_op jit(solution)/shard_map/ppermute | solution.py:212
  15.6 2.6 %collective-permute-start.6 = (bf16[32,1024]{1,0:T(8,128)(2,1)S(1)}, bf16[32,1024]{1,0:T(8,128)(2,1)S(1)}, u32[]{:S(2)}, u32[]{:S(2)}) collective-permute-start(bf16[32,1024]{1,0:T(8,128)(2,1)S(1)} %get-tuple-element.12), channel_id=1, source_target_pairs={{0,4},{1,5},{2,6},{3,7},{4,0},{5,1},{6,2},{7,3},{8,12},{9,13},{10,... | collective-permute-start | bytes 196616 | tf_op jit(solution)/shard_map/ppermute | solution.py:212
  16.9 3.4 %collective-permute-start.9 = (bf16[16,1024]{1,0:T(8,128)(2,1)S(1)}, bf16[16,1024]{1,0:T(8,128)(2,1)S(1)}, u32[]{:S(2)}, u32[]{:S(2)}) collective-permute-start(bf16[16,1024]{1,0:T(8,128)(2,1)S(1)} %shard_map.46), channel_id=1, source_target_pairs={{0,12},{1,13},{2,14},{3,15},{4,8},{5,9},{6,10},{7,11},{8,4},{9,5},... | collective-permute-start | bytes 98312 | tf_op jit(solution)/shard_map/ppermute | solution.py:212
  18.3 4.0 %collective-permute-start.7 = (bf16[16,1024]{1,0:T(8,128)(2,1)S(1)}, bf16[16,1024]{1,0:T(8,128)(2,1)S(1)}, u32[]{:S(2)}, u32[]{:S(2)}) collective-permute-start(bf16[16,1024]{1,0:T(8,128)(2,1)S(1)} %shard_map.43), channel_id=1, source_target_pairs={{0,12},{1,13},{2,14},{3,15},{4,8},{5,9},{6,10},{7,11},{8,4},{9,5},... | collective-permute-start | bytes 98312 | tf_op jit(solution)/shard_map/ppermute | solution.py:212
  20.4 4.6 %collective-permute-start.10 = (bf16[16,1024]{1,0:T(8,128)(2,1)S(1)}, bf16[16,1024]{1,0:T(8,128)(2,1)S(1)}, u32[]{:S(2)}, u32[]{:S(2)}) collective-permute-start(bf16[16,1024]{1,0:T(8,128)(2,1)S(1)} %shard_map.47), channel_id=1, source_target_pairs={{0,6},{1,2},{2,1},{3,5},{4,7},{5,3},{6,0},{7,4},{8,14},{9,10},{10,... | collective-permute-start | bytes 98312 | tf_op jit(solution)/shard_map/ppermute | solution.py:219
  22.4 3.8 %collective-permute-start.11 = (bf16[8,1024]{1,0:T(8,128)(2,1)S(1)}, bf16[8,1024]{1,0:T(8,128)(2,1)S(1)}, u32[]{:S(2)}, u32[]{:S(2)}) collective-permute-start(bf16[8,1024]{1,0:T(8,128)(2,1)S(1)} %get-tuple-element.16), channel_id=1, source_target_pairs={{0,1},{1,0},{2,3},{3,2},{4,5},{5,4},{6,7},{7,6},{8,9},{9,8},{10,11... | collective-permute-start | bytes 49160 | tf_op jit(solution)/shard_map/ppermute | solution.py:212
  25.0 1.3 %collective-permute-start.12 = (bf16[8,1024]{1,0:T(8,128)(2,1)S(1)}, bf16[8,1024]{1,0:T(8,128)(2,1)S(1)}, u32[]{:S(2)}, u32[]{:S(2)}) collective-permute-start(bf16[8,1024]{1,0:T(8,128)(2,1)S(1)} %shard_map.49), channel_id=1, source_target_pairs={{0,4},{1,5},{2,6},{3,7},{4,0},{5,1},{6,2},{7,3},{8,12},{9,13},{10,... | collective-permute-start | bytes 49160 | tf_op jit(solution)/shard_map/ppermute | solution.py:212

commit v14 on v13

--- a/solution.py
+++ b/solution.py
@@ -166,13 +166,15 @@
         a, b = (jnp.concatenate([x[lo:hi] for lo, hi in ranges], axis=0) for x in (mine, other))
         return combine(kept(a, classes), decoded(b, classes))
 
-    for p, ref, chosen in zip(put, out_refs, [[r] for r in ranges] if len(put) > 1 else [ranges]):
+    wanted = zip(put, [[r] for r in ranges] if len(put) > 1 else [ranges])
+    for (p, chosen), ref in zip([w for w in wanted if w[0] is not None], out_refs):
         p(ref, 0, merged(chosen), classes)
 
 
 def merge(mine, other, classes, first, last, *put):
     rows = mine.shape[0] * (last - first) // 2 // len(put)
-    outs = [record_shape(rows, classes, jnp.float32 if p is keep else jnp.bfloat16) for p in put]
+    forms = [p for p in put if p is not None]
+    outs = [record_shape(rows, classes, jnp.float32 if p is keep else jnp.bfloat16) for p in forms]
     kernel = functools.partial(merge_kernel, put, classes, first, last)
     return call(kernel, outs, mine, other)
 
@@ -259,7 +261,8 @@
         (near,) = merge(near, near_came, classes, 0, 1, keep)
         near_came = swap(send, bit ^ core)
     (far,) = merge(far, far_came, classes, 0, 2, encode)
-    own, near = merge(near, near_came, classes, 0, 2, keep, encode)
+    (own,) = merge(near, near_came, classes, 0, 2, keep, None)
+    (near,) = merge(near, near_came, classes, 0, 2, None, encode)
     far = swap_far(far)
     near = swap(near, 1)
     across = swap(tail(far), core)

time: 27.2 us -> 27.2 us (level)
    pallas_call x14 -> x15, Pallas kernels: 4 us -> 4.1 us  [call(): pl.pallas_call(kernel, out_shape=outs, in_specs=[VMEM] * len(args), out_s...]
where the time goes in v14:
time: 27.2 us; the launch traced here: 27 us
  starting transfers between devices  13.7 us (50%)
  waiting for transfers between devices  8.48 us (31%)
  Pallas kernels  4.1 us (15%)
  local copies, waits for them, and re-layouts  0.71 us (3%)
    ppermute x11, starting transfers between devices, swap(): return lax.ppermute(block, AXES, [(i, i ^ bit) for i in range(size)])  8.19 us
    ppermute x11, waiting for transfers between devices, swap(): return lax.ppermute(block, AXES, [(i, i ^ bit) for i in range(size)])  5.82 us
    ppermute x2, starting transfers between devices, swap_far(): return lax.ppermute(block, AXES, [(i, partner(i)) for i in range(size)])  5.46 us
    pallas_call x15, Pallas kernels, call(): pl.pallas_call(kernel, out_shape=outs, in_specs=[VMEM] * len(args), out_s...  4.1 us
    ppermute x2, waiting for transfers between devices, swap_far(): return lax.ppermute(block, AXES, [(i, partner(i)) for i in range(size)])  2.66 us
    unnamed x6, local copies, waits for them, and re-layouts  0.71 us
  transfers between devices with their start and end apart: 13, of which 10 were waited for; matrix products, arithmetic and copies ran while one was open for 0% of the time, Pallas kernels for 3%

profile of v14, /device:TPU:0, one launch (start us, length us, event | category | flops | bytes accessed | tf_op | source)
XLA Modules:
  0.0 27.0 jit_solution(10057883155216774127)
XLA Ops:
  0.0 0.5 %collective-permute-start = (bf16[8,768]{1,0:T(8,128)(2,1)}, bf16[8,768]{1,0:T(8,128)(2,1)S(1)}, u32[]{:S(2)}, u32[]{:S(2)}) collective-permute-start(bf16[8,768]{1,0:T(8,128)(2,1)} %a_ref.1), channel_id=1, source_target_pairs={{0,4},{1,5},{2,6},{3,7},{4,0},{5,1},{6,2},{7,3},{8,12},{9,13},{10,... | collective-permute-start | bytes 36872 | tf_op jit(solution)/shard_map/ppermute | solution.py:214
  0.5 0.7 %copy-done.2 = bf16[8,768]{1,0:T(8,128)(2,1)S(1)} copy-done((bf16[8,768]{1,0:T(8,128)(2,1)S(1)}, bf16[8,768]{1,0:T(8,128)(2,1)}, u32[]{:S(2)}) %copy-start.2) | copy-done | bytes 12312
  1.2 0.3 %collective-permute-done.b_ref = bf16[8,768]{1,0:T(8,128)(2,1)S(1)} collective-permute-done((bf16[8,768]{1,0:T(8,128)(2,1)}, bf16[8,768]{1,0:T(8,128)(2,1)S(1)}, u32[]{:S(2)}, u32[]{:S(2)}) %collective-permute-start) | collective-permute-done | bytes 12320 | tf_op jit(solution)/shard_map/ppermute | solution.py:214
  1.5 3.7 %collective-permute-start.2 = (bf16[16,768]{1,0:T(8,128)(2,1)S(1)}, bf16[16,768]{1,0:T(8,128)(2,1)S(1)}, u32[]{:S(2)}, u32[]{:S(2)}) collective-permute-start(bf16[16,768]{1,0:T(8,128)(2,1)S(1)} %shard_map.38.a_ref.refs_0_), channel_id=1, source_target_pairs={{0,6},{1,2},{2,1},{3,5},{4,7},{5,3},{6,0},{7,4},{8,14},{9,10},{10,... | collective-permute-start | bytes 73736 | tf_op jit(solution)/shard_map/ppermute | solution.py:221
  5.2 0.8 %collective-permute-start.1 = (bf16[16,768]{1,0:T(8,128)(2,1)S(1)}, bf16[16,768]{1,0:T(8,128)(2,1)S(1)}, u32[]{:S(2)}, u32[]{:S(2)}) collective-permute-start(bf16[16,768]{1,0:T(8,128)(2,1)S(1)} %shard_map.38.a_ref.refs_0_), channel_id=1, source_target_pairs={{0,1},{1,0},{2,3},{3,2},{4,5},{5,4},{6,7},{7,6},{8,9},{9,8},{10,11... | collective-permute-start | bytes 73736 | tf_op jit(solution)/shard_map/ppermute | solution.py:214
  6.0 0.7 %collective-permute-done.2.b_ref.refs_2_ = bf16[16,768]{1,0:T(8,128)(2,1)S(1)} collective-permute-done((bf16[16,768]{1,0:T(8,128)(2,1)S(1)}, bf16[16,768]{1,0:T(8,128)(2,1)S(1)}, u32[]{:S(2)}, u32[]{:S(2)}) %collective-permute-start.2) | collective-permute-done | bytes 24608 | tf_op jit(solution)/shard_map/ppermute | solution.py:221
  6.7 0.9 %collective-permute-start.3 = (bf16[16,768]{1,0:T(8,128)(2,1)S(1)}, bf16[16,768]{1,0:T(8,128)(2,1)S(1)}, u32[]{:S(2)}, u32[]{:S(2)}) collective-permute-start(bf16[16,768]{1,0:T(8,128)(2,1)S(1)} %collective-permute-done.2.b_ref.refs_2_), channel_id=1, source_target_pairs={{0,4},{1,5},{2,6},{3,7},{4,0},{5,1},{6,2},{7,3},{8,12},{9,13},{10,... | collective-permute-start | bytes 73736 | tf_op jit(solution)/shard_map/ppermute | solution.py:214
  7.7 1.2 %collective-permute-start.4 = (bf16[32,768]{1,0:T(8,128)(2,1)S(1)}, bf16[32,768]{1,0:T(8,128)(2,1)S(1)}, u32[]{:S(2)}, u32[]{:S(2)}) collective-permute-start(bf16[32,768]{1,0:T(8,128)(2,1)S(1)} %shard_map.39), channel_id=1, source_target_pairs={{0,12},{1,13},{2,14},{3,15},{4,8},{5,9},{6,10},{7,11},{8,4},{9,5},... | collective-permute-start | bytes 147464 | tf_op jit(solution)/shard_map/ppermute | solution.py:214
  8.8 0.3 %collective-permute-done.1.a_ref.refs_1_ = bf16[16,768]{1,0:T(8,128)(2,1)S(1)} collective-permute-done((bf16[16,768]{1,0:T(8,128)(2,1)S(1)}, bf16[16,768]{1,0:T(8,128)(2,1)S(1)}, u32[]{:S(2)}, u32[]{:S(2)}) %collective-permute-start.1) | collective-permute-done | bytes 24608 | tf_op jit(solution)/shard_map/ppermute | solution.py:214
  9.1 1.3 %collective-permute-start.5 = (bf16[32,768]{1,0:T(8,128)(2,1)S(1)}, bf16[32,768]{1,0:T(8,128)(2,1)S(1)}, u32[]{:S(2)}, u32[]{:S(2)}) collective-permute-start(bf16[32,768]{1,0:T(8,128)(2,1)S(1)} %shard_map.40), channel_id=1, source_target_pairs={{0,12},{1,13},{2,14},{3,15},{4,8},{5,9},{6,10},{7,11},{8,4},{9,5},... | collective-permute-start | bytes 147464 | tf_op jit(solution)/shard_map/ppermute | solution.py:214
  10.4 1.1 %collective-permute-done.4.refs_4_ = bf16[32,768]{1,0:T(8,128)(2,1)S(1)} collective-permute-done((bf16[32,768]{1,0:T(8,128)(2,1)S(1)}, bf16[32,768]{1,0:T(8,128)(2,1)S(1)}, u32[]{:S(2)}, u32[]{:S(2)}) %collective-permute-start.4) | collective-permute-done | bytes 49184 | tf_op jit(solution)/shard_map/ppermute | solution.py:214
  11.6 1.4 %collective-permute-done.5.refs_5_ = bf16[32,768]{1,0:T(8,128)(2,1)S(1)} collective-permute-done((bf16[32,768]{1,0:T(8,128)(2,1)S(1)}, bf16[32,768]{1,0:T(8,128)(2,1)S(1)}, u32[]{:S(2)}, u32[]{:S(2)}) %collective-permute-start.5) | collective-permute-done | bytes 49184 | tf_op jit(solution)/shard_map/ppermute | solution.py:214
  13.0 2.4 %shard_map.41 = (bf16[32,1024]{1,0:T(8,128)(2,1)S(1)}, bf16[32,1024]{1,0:T(8,128)(2,1)S(1)}, f32[32,1024]{1,0:T(8,128)S(1)}, f32[32,1024]{1,0:T(8,128)S(1)}) custom-call(bf16[16,768]{1,0:T(8,128)(2,1)S(1)} %shard_map.38.a_ref.refs_0_, bf16[16,768]{1,0:T(8,128)(2,1)S(1)} %collective-permute-done.1.a_ref.refs_1_, ...), custom_call_target="tpu_custom_call" | custom-call | flops 926941184 | bytes 7241728 | tf_op jit(solution)/shard_map/pallas_call | solution.py:27
  15.4 0.2 collective-permute-start.8
  15.6 0.4 %collective-permute-start.6 = (bf16[32,1024]{1,0:T(8,128)(2,1)S(1)}, bf16[32,1024]{1,0:T(8,128)(2,1)S(1)}, u32[]{:S(2)}, u32[]{:S(2)}) collective-permute-start(bf16[32,1024]{1,0:T(8,128)(2,1)S(1)} %get-tuple-element.10), channel_id=1, source_target_pairs={{0,4},{1,5},{2,6},{3,7},{4,0},{5,1},{6,2},{7,3},{8,12},{9,13},{10,... | collective-permute-start | bytes 196616 | tf_op jit(solution)/shard_map/ppermute | solution.py:214
  16.0 0.7 %collective-permute-done.8.other_ref = bf16[32,1024]{1,0:T(8,128)(2,1)S(1)} collective-permute-done((bf16[32,1024]{1,0:T(8,128)(2,1)S(1)}, bf16[32,1024]{1,0:T(8,128)(2,1)S(1)}, u32[]{:S(2)}, u32[]{:S(2)}) %collective-permute-start.8) | collective-permute-done | bytes 65568 | tf_op jit(solution)/shard_map/ppermute | solution.py:214
  16.7 0.1 shard_map.46
  16.9 1.3 %collective-permute-start.9 = (bf16[16,1024]{1,0:T(8,128)(2,1)S(1)}, bf16[16,1024]{1,0:T(8,128)(2,1)S(1)}, u32[]{:S(2)}, u32[]{:S(2)}) collective-permute-start(bf16[16,1024]{1,0:T(8,128)(2,1)S(1)} %shard_map.46), channel_id=1, source_target_pairs={{0,12},{1,13},{2,14},{3,15},{4,8},{5,9},{6,10},{7,11},{8,4},{9,5},... | collective-permute-start | bytes 98312 | tf_op jit(solution)/shard_map/ppermute | solution.py:214
  18.2 0.1 shard_map.43
  18.3 0.6 %collective-permute-start.7 = (bf16[16,1024]{1,0:T(8,128)(2,1)S(1)}, bf16[16,1024]{1,0:T(8,128)(2,1)S(1)}, u32[]{:S(2)}, u32[]{:S(2)}) collective-permute-start(bf16[16,1024]{1,0:T(8,128)(2,1)S(1)} %shard_map.43), channel_id=1, source_target_pairs={{0,12},{1,13},{2,14},{3,15},{4,8},{5,9},{6,10},{7,11},{8,4},{9,5},... | collective-permute-start | bytes 98312 | tf_op jit(solution)/shard_map/ppermute | solution.py:214
  18.9 0.1 shard_map.45.mine_ref
  19.0 1.3 %collective-permute-done.9.other_ref = bf16[16,1024]{1,0:T(8,128)(2,1)S(1)} collective-permute-done((bf16[16,1024]{1,0:T(8,128)(2,1)S(1)}, bf16[16,1024]{1,0:T(8,128)(2,1)S(1)}, u32[]{:S(2)}, u32[]{:S(2)}) %collective-permute-start.9) | collective-permute-done | bytes 32800 | tf_op jit(solution)/shard_map/ppermute | solution.py:214
  20.3 0.1 shard_map.47
  20.4 1.8 %collective-permute-start.10 = (bf16[16,1024]{1,0:T(8,128)(2,1)S(1)}, bf16[16,1024]{1,0:T(8,128)(2,1)S(1)}, u32[]{:S(2)}, u32[]{:S(2)}) collective-permute-start(bf16[16,1024]{1,0:T(8,128)(2,1)S(1)} %shard_map.47), channel_id=1, source_target_pairs={{0,6},{1,2},{2,1},{3,5},{4,7},{5,3},{6,0},{7,4},{8,14},{9,10},{10,... | collective-permute-start | bytes 98312 | tf_op jit(solution)/shard_map/ppermute | solution.py:221
  22.2 0.1 shard_map.42.mine_ref
  22.3 0.1 shard_map.49
  22.4 0.7 %collective-permute-start.11 = (bf16[8,1024]{1,0:T(8,128)(2,1)S(1)}, bf16[8,1024]{1,0:T(8,128)(2,1)S(1)}, u32[]{:S(2)}, u32[]{:S(2)}) collective-permute-start(bf16[8,1024]{1,0:T(8,128)(2,1)S(1)} %shard_map.49), channel_id=1, source_target_pairs={{0,1},{1,0},{2,3},{3,2},{4,5},{5,4},{6,7},{7,6},{8,9},{9,8},{10,11... | collective-permute-start | bytes 49160 | tf_op jit(solution)/shard_map/ppermute | solution.py:214
  23.1 1.9 %collective-permute-done.10.far_ref.a_ref = bf16[16,1024]{1,0:T(8,128)(2,1)S(1)} collective-permute-done((bf16[16,1024]{1,0:T(8,128)(2,1)S(1)}, bf16[16,1024]{1,0:T(8,128)(2,1)S(1)}, u32[]{:S(2)}, u32[]{:S(2)}) %collective-permute-start.10) | collective-permute-done | bytes 32800 | tf_op jit(solution)/shard_map/ppermute | solution.py:221
  25.0 0.4 %collective-permute-start.12 = (bf16[8,1024]{1,0:T(8,128)(2,1)S(1)}, bf16[8,1024]{1,0:T(8,128)(2,1)S(1)}, u32[]{:S(2)}, u32[]{:S(2)}) collective-permute-start(bf16[8,1024]{1,0:T(8,128)(2,1)S(1)} %shard_map.50), channel_id=1, source_target_pairs={{0,4},{1,5},{2,6},{3,7},{4,0},{5,1},{6,2},{7,3},{8,12},{9,13},{10,... | collective-permute-start | bytes 49160 | tf_op jit(solution)/shard_map/ppermute | solution.py:214
  25.6 0.1 shard_map.48.own_ref
  25.7 0.5 %collective-permute-done.11.near_ref = bf16[8,1024]{1,0:T(8,128)(2,1)S(1)} collective-permute-done((bf16[8,1024]{1,0:T(8,128)(2,1)S(1)}, bf16[8,1024]{1,0:T(8,128)(2,1)S(1)}, u32[]{:S(2)}, u32[]{:S(2)}) %collective-permute-start.11) | collective-permute-done | bytes 16416 | tf_op jit(solution)/shard_map/ppermute | solution.py:214
  26.3 0.7 %shard_map.51 = f32[8,1000]{1,0:T(8,128)} custom-call(f32[8,1024]{1,0:T(8,128)S(1)} %shard_map.48.own_ref, bf16[8,1024]{1,0:T(8,128)(2,1)S(1)} %collective-permute-done.11.near_ref, bf16[8,1024]{1,0:T(8,128)(2,1)S(1)} %collective-permute-done.12.across_ref), custom_call_target="tpu_custom_call" | custom-call | tf_op jit(solution)/shard_map/pallas_call | solution.py:27
  (15 shorter events, 0.2 us)
Async XLA Ops:
  0.0 1.5 %collective-permute-start = (bf16[8,768]{1,0:T(8,128)(2,1)}, bf16[8,768]{1,0:T(8,128)(2,1)S(1)}, u32[]{:S(2)}, u32[]{:S(2)}) collective-permute-start(bf16[8,768]{1,0:T(8,128)(2,1)} %a_ref.1), channel_id=1, source_target_pairs={{0,4},{1,5},{2,6},{3,7},{4,0},{5,1},{6,2},{7,3},{8,12},{9,13},{10,... | collective-permute-start | bytes 36872 | tf_op jit(solution)/shard_map/ppermute | solution.py:214
  0.5 0.7 %copy-start.2 = (bf16[8,768]{1,0:T(8,128)(2,1)S(1)}, bf16[8,768]{1,0:T(8,128)(2,1)}, u32[]{:S(2)}) copy-start(bf16[8,768]{1,0:T(8,128)(2,1)} %a_ref.1) | copy-start | bytes 36868
  1.5 5.2 %collective-permute-start.2 = (bf16[16,768]{1,0:T(8,128)(2,1)S(1)}, bf16[16,768]{1,0:T(8,128)(2,1)S(1)}, u32[]{:S(2)}, u32[]{:S(2)}) collective-permute-start(bf16[16,768]{1,0:T(8,128)(2,1)S(1)} %shard_map.38.a_ref.refs_0_), channel_id=1, source_target_pairs={{0,6},{1,2},{2,1},{3,5},{4,7},{5,3},{6,0},{7,4},{8,14},{9,10},{10,... | collective-permute-start | bytes 73736 | tf_op jit(solution)/shard_map/ppermute | solution.py:221
  5.2 3.9 %collective-permute-start.1 = (bf16[16,768]{1,0:T(8,128)(2,1)S(1)}, bf16[16,768]{1,0:T(8,128)(2,1)S(1)}, u32[]{:S(2)}, u32[]{:S(2)}) collective-permute-start(bf16[16,768]{1,0:T(8,128)(2,1)S(1)} %shard_map.38.a_ref.refs_0_), channel_id=1, source_target_pairs={{0,1},{1,0},{2,3},{3,2},{4,5},{5,4},{6,7},{7,6},{8,9},{9,8},{10,11... | collective-permute-start | bytes 73736 | tf_op jit(solution)/shard_map/ppermute | solution.py:214
  6.7 2.4 %collective-permute-start.3 = (bf16[16,768]{1,0:T(8,128)(2,1)S(1)}, bf16[16,768]{1,0:T(8,128)(2,1)S(1)}, u32[]{:S(2)}, u32[]{:S(2)}) collective-permute-start(bf16[16,768]{1,0:T(8,128)(2,1)S(1)} %collective-permute-done.2.b_ref.refs_2_), channel_id=1, source_target_pairs={{0,4},{1,5},{2,6},{3,7},{4,0},{5,1},{6,2},{7,3},{8,12},{9,13},{10,... | collective-permute-start | bytes 73736 | tf_op jit(solution)/shard_map/ppermute | solution.py:214
  7.7 5.3 %copy-start = (bf16[2048,1000]{0,1:T(8,128)(2,1)S(1)}, bf16[2048,1000]{0,1:T(8,128)(2,1)}, u32[]{:S(2)}) copy-start(bf16[2048,1000]{0,1:T(8,128)(2,1)} %param.5) | copy-start | bytes 12288004
  7.7 5.3 %copy-start.1 = (bf16[2048,768]{1,0:T(8,128)(2,1)S(1)}, bf16[2048,768]{1,0:T(8,128)(2,1)}, u32[]{:S(2)}) copy-start(bf16[2048,768]{1,0:T(8,128)(2,1)} %refs_6_.1) | copy-start | bytes 9437188
  7.7 3.9 %collective-permute-start.4 = (bf16[32,768]{1,0:T(8,128)(2,1)S(1)}, bf16[32,768]{1,0:T(8,128)(2,1)S(1)}, u32[]{:S(2)}, u32[]{:S(2)}) collective-permute-start(bf16[32,768]{1,0:T(8,128)(2,1)S(1)} %shard_map.39), channel_id=1, source_target_pairs={{0,12},{1,13},{2,14},{3,15},{4,8},{5,9},{6,10},{7,11},{8,4},{9,5},... | collective-permute-start | bytes 147464 | tf_op jit(solution)/shard_map/ppermute | solution.py:214
  9.1 3.8 %collective-permute-start.5 = (bf16[32,768]{1,0:T(8,128)(2,1)S(1)}, bf16[32,768]{1,0:T(8,128)(2,1)S(1)}, u32[]{:S(2)}, u32[]{:S(2)}) collective-permute-start(bf16[32,768]{1,0:T(8,128)(2,1)S(1)} %shard_map.40), channel_id=1, source_target_pairs={{0,12},{1,13},{2,14},{3,15},{4,8},{5,9},{6,10},{7,11},{8,4},{9,5},... | collective-permute-start | bytes 147464 | tf_op jit(solution)/shard_map/ppermute | solution.py:214
  15.4 1.3 %collective-permute-start.8 = (bf16[32,1024]{1,0:T(8,128)(2,1)S(1)}, bf16[32,1024]{1,0:T(8,128)(2,1)S(1)}, u32[]{:S(2)}, u32[]{:S(2)}) collective-permute-start(bf16[32,1024]{1,0:T(8,128)(2,1)S(1)} %get-tuple-element.12), channel_id=1, source_target_pairs={{0,4},{1,5},{2,6},{3,7},{4,0},{5,1},{6,2},{7,3},{8,12},{9,13},{10,... | collective-permute-start | bytes 196616 | tf_op jit(solution)/shard_map/ppermute | solution.py:214
  15.6 2.6 %collective-permute-start.6 = (bf16[32,1024]{1,0:T(8,128)(2,1)S(1)}, bf16[32,1024]{1,0:T(8,128)(2,1)S(1)}, u32[]{:S(2)}, u32[]{:S(2)}) collective-permute-start(bf16[32,1024]{1,0:T(8,128)(2,1)S(1)} %get-tuple-element.10), channel_id=1, source_target_pairs={{0,4},{1,5},{2,6},{3,7},{4,0},{5,1},{6,2},{7,3},{8,12},{9,13},{10,... | collective-permute-start | bytes 196616 | tf_op jit(solution)/shard_map/ppermute | solution.py:214
  16.9 3.4 %collective-permute-start.9 = (bf16[16,1024]{1,0:T(8,128)(2,1)S(1)}, bf16[16,1024]{1,0:T(8,128)(2,1)S(1)}, u32[]{:S(2)}, u32[]{:S(2)}) collective-permute-start(bf16[16,1024]{1,0:T(8,128)(2,1)S(1)} %shard_map.46), channel_id=1, source_target_pairs={{0,12},{1,13},{2,14},{3,15},{4,8},{5,9},{6,10},{7,11},{8,4},{9,5},... | collective-permute-start | bytes 98312 | tf_op jit(solution)/shard_map/ppermute | solution.py:214
  18.3 4.0 %collective-permute-start.7 = (bf16[16,1024]{1,0:T(8,128)(2,1)S(1)}, bf16[16,1024]{1,0:T(8,128)(2,1)S(1)}, u32[]{:S(2)}, u32[]{:S(2)}) collective-permute-start(bf16[16,1024]{1,0:T(8,128)(2,1)S(1)} %shard_map.43), channel_id=1, source_target_pairs={{0,12},{1,13},{2,14},{3,15},{4,8},{5,9},{6,10},{7,11},{8,4},{9,5},... | collective-permute-start | bytes 98312 | tf_op jit(solution)/shard_map/ppermute | solution.py:214
  20.4 4.6 %collective-permute-start.10 = (bf16[16,1024]{1,0:T(8,128)(2,1)S(1)}, bf16[16,1024]{1,0:T(8,128)(2,1)S(1)}, u32[]{:S(2)}, u32[]{:S(2)}) collective-permute-start(bf16[16,1024]{1,0:T(8,128)(2,1)S(1)} %shard_map.47), channel_id=1, source_target_pairs={{0,6},{1,2},{2,1},{3,5},{4,7},{5,3},{6,0},{7,4},{8,14},{9,10},{10,... | collective-permute-start | bytes 98312 | tf_op jit(solution)/shard_map/ppermute | solution.py:221
  22.4 3.8 %collective-permute-start.11 = (bf16[8,1024]{1,0:T(8,128)(2,1)S(1)}, bf16[8,1024]{1,0:T(8,128)(2,1)S(1)}, u32[]{:S(2)}, u32[]{:S(2)}) collective-permute-start(bf16[8,1024]{1,0:T(8,128)(2,1)S(1)} %shard_map.49), channel_id=1, source_target_pairs={{0,1},{1,0},{2,3},{3,2},{4,5},{5,4},{6,7},{7,6},{8,9},{9,8},{10,11... | collective-permute-start | bytes 49160 | tf_op jit(solution)/shard_map/ppermute | solution.py:214
  25.0 1.3 %collective-permute-start.12 = (bf16[8,1024]{1,0:T(8,128)(2,1)S(1)}, bf16[8,1024]{1,0:T(8,128)(2,1)S(1)}, u32[]{:S(2)}, u32[]{:S(2)}) collective-permute-start(bf16[8,1024]{1,0:T(8,128)(2,1)S(1)} %shard_map.50), channel_id=1, source_target_pairs={{0,4},{1,5},{2,6},{3,7},{4,0},{5,1},{6,2},{7,3},{8,12},{9,13},{10,... | collective-permute-start | bytes 49160 | tf_op jit(solution)/shard_map/ppermute | solution.py:214

commit v15 on v13

--- a/solution.py
+++ b/solution.py
@@ -126,7 +126,7 @@
     gain = SCORE_GAIN * math.log2(math.e) / math.sqrt(width)
     dot = functools.partial(lax.dot_general, preferred_element_type=jnp.float32)
     by_rows, by_columns = (((1,), (1,)), ((), ())), (((1,), (0,)), ((), ()))
-    chunks = [slice(lo, lo + 256) for lo in range(0, k_ref.shape[0], 256)]
+    chunks = [slice(lo, lo + 512) for lo in range(0, k_ref.shape[0], 512)]
     scores = [dot(k_ref[at], queries, by_rows) * gain for at in chunks]
     peaks = jnp.max(functools.reduce(jnp.maximum, scores), axis=0, keepdims=True)
     weights = [jnp.exp2(s - peaks) for s in scores]

time: 27.2 us -> 27.2 us (level)
  no operation moved by 1% of the time
where the time goes in v15:
time: 27.2 us; the launch traced here: 27 us
  starting transfers between devices  13.7 us (50%)
  waiting for transfers between devices  8.58 us (32%)
  Pallas kernels  4 us (15%)
  local copies, waits for them, and re-layouts  0.71 us (3%)
    ppermute x11, starting transfers between devices, swap(): return lax.ppermute(block, AXES, [(i, i ^ bit) for i in range(size)])  8.19 us
    ppermute x11, waiting for transfers between devices, swap(): return lax.ppermute(block, AXES, [(i, i ^ bit) for i in range(size)])  5.93 us
    ppermute x2, starting transfers between devices, swap_far(): return lax.ppermute(block, AXES, [(i, partner(i)) for i in range(size)])  5.47 us
    pallas_call x14, Pallas kernels, call(): pl.pallas_call(kernel, out_shape=outs, in_specs=[VMEM] * len(args), out_s...  4 us
    ppermute x2, waiting for transfers between devices, swap_far(): return lax.ppermute(block, AXES, [(i, partner(i)) for i in range(size)])  2.65 us
    unnamed x6, local copies, waits for them, and re-layouts  0.71 us
  transfers between devices with their start and end apart: 13, of which 10 were waited for; matrix products, arithmetic and copies ran while one was open for 0% of the time, Pallas kernels for 3%

profile of v15, /device:TPU:0, one launch (start us, length us, event | category | flops | bytes accessed | tf_op | source)
XLA Modules:
  0.0 27.0 jit_solution(3347618094084859872)
XLA Ops:
  0.0 0.5 %collective-permute-start = (bf16[8,768]{1,0:T(8,128)(2,1)}, bf16[8,768]{1,0:T(8,128)(2,1)S(1)}, u32[]{:S(2)}, u32[]{:S(2)}) collective-permute-start(bf16[8,768]{1,0:T(8,128)(2,1)} %a_ref.1), channel_id=1, source_target_pairs={{0,4},{1,5},{2,6},{3,7},{4,0},{5,1},{6,2},{7,3},{8,12},{9,13},{10,... | collective-permute-start | bytes 36872 | tf_op jit(solution)/shard_map/ppermute | solution.py:212
  0.5 0.7 %copy-done.2 = bf16[8,768]{1,0:T(8,128)(2,1)S(1)} copy-done((bf16[8,768]{1,0:T(8,128)(2,1)S(1)}, bf16[8,768]{1,0:T(8,128)(2,1)}, u32[]{:S(2)}) %copy-start.2) | copy-done | bytes 12312
  1.2 0.3 %collective-permute-done.b_ref = bf16[8,768]{1,0:T(8,128)(2,1)S(1)} collective-permute-done((bf16[8,768]{1,0:T(8,128)(2,1)}, bf16[8,768]{1,0:T(8,128)(2,1)S(1)}, u32[]{:S(2)}, u32[]{:S(2)}) %collective-permute-start) | collective-permute-done | bytes 12320 | tf_op jit(solution)/shard_map/ppermute | solution.py:212
  1.5 3.7 %collective-permute-start.2 = (bf16[16,768]{1,0:T(8,128)(2,1)S(1)}, bf16[16,768]{1,0:T(8,128)(2,1)S(1)}, u32[]{:S(2)}, u32[]{:S(2)}) collective-permute-start(bf16[16,768]{1,0:T(8,128)(2,1)S(1)} %shard_map.38.a_ref.refs_0_), channel_id=1, source_target_pairs={{0,6},{1,2},{2,1},{3,5},{4,7},{5,3},{6,0},{7,4},{8,14},{9,10},{10,... | collective-permute-start | bytes 73736 | tf_op jit(solution)/shard_map/ppermute | solution.py:219
  5.2 0.8 %collective-permute-start.1 = (bf16[16,768]{1,0:T(8,128)(2,1)S(1)}, bf16[16,768]{1,0:T(8,128)(2,1)S(1)}, u32[]{:S(2)}, u32[]{:S(2)}) collective-permute-start(bf16[16,768]{1,0:T(8,128)(2,1)S(1)} %shard_map.38.a_ref.refs_0_), channel_id=1, source_target_pairs={{0,1},{1,0},{2,3},{3,2},{4,5},{5,4},{6,7},{7,6},{8,9},{9,8},{10,11... | collective-permute-start | bytes 73736 | tf_op jit(solution)/shard_map/ppermute | solution.py:212
  6.0 0.7 %collective-permute-done.2.b_ref.refs_2_ = bf16[16,768]{1,0:T(8,128)(2,1)S(1)} collective-permute-done((bf16[16,768]{1,0:T(8,128)(2,1)S(1)}, bf16[16,768]{1,0:T(8,128)(2,1)S(1)}, u32[]{:S(2)}, u32[]{:S(2)}) %collective-permute-start.2) | collective-permute-done | bytes 24608 | tf_op jit(solution)/shard_map/ppermute | solution.py:219
  6.7 0.9 %collective-permute-start.3 = (bf16[16,768]{1,0:T(8,128)(2,1)S(1)}, bf16[16,768]{1,0:T(8,128)(2,1)S(1)}, u32[]{:S(2)}, u32[]{:S(2)}) collective-permute-start(bf16[16,768]{1,0:T(8,128)(2,1)S(1)} %collective-permute-done.2.b_ref.refs_2_), channel_id=1, source_target_pairs={{0,4},{1,5},{2,6},{3,7},{4,0},{5,1},{6,2},{7,3},{8,12},{9,13},{10,... | collective-permute-start | bytes 73736 | tf_op jit(solution)/shard_map/ppermute | solution.py:212
  7.7 1.2 %collective-permute-start.4 = (bf16[32,768]{1,0:T(8,128)(2,1)S(1)}, bf16[32,768]{1,0:T(8,128)(2,1)S(1)}, u32[]{:S(2)}, u32[]{:S(2)}) collective-permute-start(bf16[32,768]{1,0:T(8,128)(2,1)S(1)} %shard_map.39), channel_id=1, source_target_pairs={{0,12},{1,13},{2,14},{3,15},{4,8},{5,9},{6,10},{7,11},{8,4},{9,5},... | collective-permute-start | bytes 147464 | tf_op jit(solution)/shard_map/ppermute | solution.py:212
  8.8 0.3 %collective-permute-done.1.a_ref.refs_1_ = bf16[16,768]{1,0:T(8,128)(2,1)S(1)} collective-permute-done((bf16[16,768]{1,0:T(8,128)(2,1)S(1)}, bf16[16,768]{1,0:T(8,128)(2,1)S(1)}, u32[]{:S(2)}, u32[]{:S(2)}) %collective-permute-start.1) | collective-permute-done | bytes 24608 | tf_op jit(solution)/shard_map/ppermute | solution.py:212
  9.1 1.3 %collective-permute-start.5 = (bf16[32,768]{1,0:T(8,128)(2,1)S(1)}, bf16[32,768]{1,0:T(8,128)(2,1)S(1)}, u32[]{:S(2)}, u32[]{:S(2)}) collective-permute-start(bf16[32,768]{1,0:T(8,128)(2,1)S(1)} %shard_map.40), channel_id=1, source_target_pairs={{0,12},{1,13},{2,14},{3,15},{4,8},{5,9},{6,10},{7,11},{8,4},{9,5},... | collective-permute-start | bytes 147464 | tf_op jit(solution)/shard_map/ppermute | solution.py:212
  10.4 1.1 %collective-permute-done.4.refs_4_ = bf16[32,768]{1,0:T(8,128)(2,1)S(1)} collective-permute-done((bf16[32,768]{1,0:T(8,128)(2,1)S(1)}, bf16[32,768]{1,0:T(8,128)(2,1)S(1)}, u32[]{:S(2)}, u32[]{:S(2)}) %collective-permute-start.4) | collective-permute-done | bytes 49184 | tf_op jit(solution)/shard_map/ppermute | solution.py:212
  11.6 1.4 %collective-permute-done.5.refs_5_ = bf16[32,768]{1,0:T(8,128)(2,1)S(1)} collective-permute-done((bf16[32,768]{1,0:T(8,128)(2,1)S(1)}, bf16[32,768]{1,0:T(8,128)(2,1)S(1)}, u32[]{:S(2)}, u32[]{:S(2)}) %collective-permute-start.5) | collective-permute-done | bytes 49184 | tf_op jit(solution)/shard_map/ppermute | solution.py:212
  13.0 2.4 %shard_map.41 = (bf16[32,1024]{1,0:T(8,128)(2,1)S(1)}, bf16[32,1024]{1,0:T(8,128)(2,1)S(1)}, f32[32,1024]{1,0:T(8,128)S(1)}, f32[32,1024]{1,0:T(8,128)S(1)}) custom-call(bf16[16,768]{1,0:T(8,128)(2,1)S(1)} %shard_map.38.a_ref.refs_0_, bf16[16,768]{1,0:T(8,128)(2,1)S(1)} %collective-permute-done.1.a_ref.refs_1_, ...), custom_call_target="tpu_custom_call" | custom-call | flops 926941184 | bytes 7241728 | tf_op jit(solution)/shard_map/pallas_call | solution.py:27
  15.4 0.2 collective-permute-start.8
  15.6 0.4 %collective-permute-start.6 = (bf16[32,1024]{1,0:T(8,128)(2,1)S(1)}, bf16[32,1024]{1,0:T(8,128)(2,1)S(1)}, u32[]{:S(2)}, u32[]{:S(2)}) collective-permute-start(bf16[32,1024]{1,0:T(8,128)(2,1)S(1)} %get-tuple-element.12), channel_id=1, source_target_pairs={{0,4},{1,5},{2,6},{3,7},{4,0},{5,1},{6,2},{7,3},{8,12},{9,13},{10,... | collective-permute-start | bytes 196616 | tf_op jit(solution)/shard_map/ppermute | solution.py:212
  16.0 0.7 %collective-permute-done.8.other_ref = bf16[32,1024]{1,0:T(8,128)(2,1)S(1)} collective-permute-done((bf16[32,1024]{1,0:T(8,128)(2,1)S(1)}, bf16[32,1024]{1,0:T(8,128)(2,1)S(1)}, u32[]{:S(2)}, u32[]{:S(2)}) %collective-permute-start.8) | collective-permute-done | bytes 65568 | tf_op jit(solution)/shard_map/ppermute | solution.py:212
  16.7 0.1 shard_map.46
  16.9 1.3 %collective-permute-start.9 = (bf16[16,1024]{1,0:T(8,128)(2,1)S(1)}, bf16[16,1024]{1,0:T(8,128)(2,1)S(1)}, u32[]{:S(2)}, u32[]{:S(2)}) collective-permute-start(bf16[16,1024]{1,0:T(8,128)(2,1)S(1)} %shard_map.46), channel_id=1, source_target_pairs={{0,12},{1,13},{2,14},{3,15},{4,8},{5,9},{6,10},{7,11},{8,4},{9,5},... | collective-permute-start | bytes 98312 | tf_op jit(solution)/shard_map/ppermute | solution.py:212
  18.2 0.1 shard_map.43
  18.3 0.6 %collective-permute-start.7 = (bf16[16,1024]{1,0:T(8,128)(2,1)S(1)}, bf16[16,1024]{1,0:T(8,128)(2,1)S(1)}, u32[]{:S(2)}, u32[]{:S(2)}) collective-permute-start(bf16[16,1024]{1,0:T(8,128)(2,1)S(1)} %shard_map.43), channel_id=1, source_target_pairs={{0,12},{1,13},{2,14},{3,15},{4,8},{5,9},{6,10},{7,11},{8,4},{9,5},... | collective-permute-start | bytes 98312 | tf_op jit(solution)/shard_map/ppermute | solution.py:212
  18.9 0.1 shard_map.45.mine_ref
  19.0 1.3 %collective-permute-done.9.other_ref = bf16[16,1024]{1,0:T(8,128)(2,1)S(1)} collective-permute-done((bf16[16,1024]{1,0:T(8,128)(2,1)S(1)}, bf16[16,1024]{1,0:T(8,128)(2,1)S(1)}, u32[]{:S(2)}, u32[]{:S(2)}) %collective-permute-start.9) | collective-permute-done | bytes 32800 | tf_op jit(solution)/shard_map/ppermute | solution.py:212
  20.3 0.1 shard_map.47
  20.4 1.8 %collective-permute-start.10 = (bf16[16,1024]{1,0:T(8,128)(2,1)S(1)}, bf16[16,1024]{1,0:T(8,128)(2,1)S(1)}, u32[]{:S(2)}, u32[]{:S(2)}) collective-permute-start(bf16[16,1024]{1,0:T(8,128)(2,1)S(1)} %shard_map.47), channel_id=1, source_target_pairs={{0,6},{1,2},{2,1},{3,5},{4,7},{5,3},{6,0},{7,4},{8,14},{9,10},{10,... | collective-permute-start | bytes 98312 | tf_op jit(solution)/shard_map/ppermute | solution.py:219
  22.2 0.1 shard_map.42.mine_ref
  22.3 0.1 shard_map.44
  22.4 0.7 %collective-permute-start.11 = (bf16[8,1024]{1,0:T(8,128)(2,1)S(1)}, bf16[8,1024]{1,0:T(8,128)(2,1)S(1)}, u32[]{:S(2)}, u32[]{:S(2)}) collective-permute-start(bf16[8,1024]{1,0:T(8,128)(2,1)S(1)} %get-tuple-element.16), channel_id=1, source_target_pairs={{0,1},{1,0},{2,3},{3,2},{4,5},{5,4},{6,7},{7,6},{8,9},{9,8},{10,11... | collective-permute-start | bytes 49160 | tf_op jit(solution)/shard_map/ppermute | solution.py:212
  23.1 1.9 %collective-permute-done.10.far_ref.a_ref = bf16[16,1024]{1,0:T(8,128)(2,1)S(1)} collective-permute-done((bf16[16,1024]{1,0:T(8,128)(2,1)S(1)}, bf16[16,1024]{1,0:T(8,128)(2,1)S(1)}, u32[]{:S(2)}, u32[]{:S(2)}) %collective-permute-start.10) | collective-permute-done | bytes 32800 | tf_op jit(solution)/shard_map/ppermute | solution.py:219
  25.0 0.4 %collective-permute-start.12 = (bf16[8,1024]{1,0:T(8,128)(2,1)S(1)}, bf16[8,1024]{1,0:T(8,128)(2,1)S(1)}, u32[]{:S(2)}, u32[]{:S(2)}) collective-permute-start(bf16[8,1024]{1,0:T(8,128)(2,1)S(1)} %shard_map.49), channel_id=1, source_target_pairs={{0,4},{1,5},{2,6},{3,7},{4,0},{5,1},{6,2},{7,3},{8,12},{9,13},{10,... | collective-permute-start | bytes 49160 | tf_op jit(solution)/shard_map/ppermute | solution.py:212
  25.5 0.1 shard_map.48.own_ref
  25.6 0.7 %collective-permute-done.11.near_ref = bf16[8,1024]{1,0:T(8,128)(2,1)S(1)} collective-permute-done((bf16[8,1024]{1,0:T(8,128)(2,1)S(1)}, bf16[8,1024]{1,0:T(8,128)(2,1)S(1)}, u32[]{:S(2)}, u32[]{:S(2)}) %collective-permute-start.11) | collective-permute-done | bytes 16416 | tf_op jit(solution)/shard_map/ppermute | solution.py:212
  26.3 0.7 %shard_map.50 = f32[8,1000]{1,0:T(8,128)} custom-call(f32[8,1024]{1,0:T(8,128)S(1)} %shard_map.48.own_ref, bf16[8,1024]{1,0:T(8,128)(2,1)S(1)} %collective-permute-done.11.near_ref, bf16[8,1024]{1,0:T(8,128)(2,1)S(1)} %collective-permute-done.12.across_ref), custom_call_target="tpu_custom_call" | custom-call | tf_op jit(solution)/shard_map/pallas_call | solution.py:27
  (14 shorter events, 0.1 us)
Async XLA Ops:
  0.0 1.5 %collective-permute-start = (bf16[8,768]{1,0:T(8,128)(2,1)}, bf16[8,768]{1,0:T(8,128)(2,1)S(1)}, u32[]{:S(2)}, u32[]{:S(2)}) collective-permute-start(bf16[8,768]{1,0:T(8,128)(2,1)} %a_ref.1), channel_id=1, source_target_pairs={{0,4},{1,5},{2,6},{3,7},{4,0},{5,1},{6,2},{7,3},{8,12},{9,13},{10,... | collective-permute-start | bytes 36872 | tf_op jit(solution)/shard_map/ppermute | solution.py:212
  0.5 0.7 %copy-start.2 = (bf16[8,768]{1,0:T(8,128)(2,1)S(1)}, bf16[8,768]{1,0:T(8,128)(2,1)}, u32[]{:S(2)}) copy-start(bf16[8,768]{1,0:T(8,128)(2,1)} %a_ref.1) | copy-start | bytes 36868
  1.5 5.2 %collective-permute-start.2 = (bf16[16,768]{1,0:T(8,128)(2,1)S(1)}, bf16[16,768]{1,0:T(8,128)(2,1)S(1)}, u32[]{:S(2)}, u32[]{:S(2)}) collective-permute-start(bf16[16,768]{1,0:T(8,128)(2,1)S(1)} %shard_map.38.a_ref.refs_0_), channel_id=1, source_target_pairs={{0,6},{1,2},{2,1},{3,5},{4,7},{5,3},{6,0},{7,4},{8,14},{9,10},{10,... | collective-permute-start | bytes 73736 | tf_op jit(solution)/shard_map/ppermute | solution.py:219
  5.2 3.9 %collective-permute-start.1 = (bf16[16,768]{1,0:T(8,128)(2,1)S(1)}, bf16[16,768]{1,0:T(8,128)(2,1)S(1)}, u32[]{:S(2)}, u32[]{:S(2)}) collective-permute-start(bf16[16,768]{1,0:T(8,128)(2,1)S(1)} %shard_map.38.a_ref.refs_0_), channel_id=1, source_target_pairs={{0,1},{1,0},{2,3},{3,2},{4,5},{5,4},{6,7},{7,6},{8,9},{9,8},{10,11... | collective-permute-start | bytes 73736 | tf_op jit(solution)/shard_map/ppermute | solution.py:212
  6.7 2.4 %collective-permute-start.3 = (bf16[16,768]{1,0:T(8,128)(2,1)S(1)}, bf16[16,768]{1,0:T(8,128)(2,1)S(1)}, u32[]{:S(2)}, u32[]{:S(2)}) collective-permute-start(bf16[16,768]{1,0:T(8,128)(2,1)S(1)} %collective-permute-done.2.b_ref.refs_2_), channel_id=1, source_target_pairs={{0,4},{1,5},{2,6},{3,7},{4,0},{5,1},{6,2},{7,3},{8,12},{9,13},{10,... | collective-permute-start | bytes 73736 | tf_op jit(solution)/shard_map/ppermute | solution.py:212
  7.7 5.3 %copy-start = (bf16[2048,1000]{0,1:T(8,128)(2,1)S(1)}, bf16[2048,1000]{0,1:T(8,128)(2,1)}, u32[]{:S(2)}) copy-start(bf16[2048,1000]{0,1:T(8,128)(2,1)} %param.5) | copy-start | bytes 12288004
  7.7 5.3 %copy-start.1 = (bf16[2048,768]{1,0:T(8,128)(2,1)S(1)}, bf16[2048,768]{1,0:T(8,128)(2,1)}, u32[]{:S(2)}) copy-start(bf16[2048,768]{1,0:T(8,128)(2,1)} %refs_6_.1) | copy-start | bytes 9437188
  7.7 3.9 %collective-permute-start.4 = (bf16[32,768]{1,0:T(8,128)(2,1)S(1)}, bf16[32,768]{1,0:T(8,128)(2,1)S(1)}, u32[]{:S(2)}, u32[]{:S(2)}) collective-permute-start(bf16[32,768]{1,0:T(8,128)(2,1)S(1)} %shard_map.39), channel_id=1, source_target_pairs={{0,12},{1,13},{2,14},{3,15},{4,8},{5,9},{6,10},{7,11},{8,4},{9,5},... | collective-permute-start | bytes 147464 | tf_op jit(solution)/shard_map/ppermute | solution.py:212
  9.1 3.8 %collective-permute-start.5 = (bf16[32,768]{1,0:T(8,128)(2,1)S(1)}, bf16[32,768]{1,0:T(8,128)(2,1)S(1)}, u32[]{:S(2)}, u32[]{:S(2)}) collective-permute-start(bf16[32,768]{1,0:T(8,128)(2,1)S(1)} %shard_map.40), channel_id=1, source_target_pairs={{0,12},{1,13},{2,14},{3,15},{4,8},{5,9},{6,10},{7,11},{8,4},{9,5},... | collective-permute-start | bytes 147464 | tf_op jit(solution)/shard_map/ppermute | solution.py:212
  15.4 1.3 %collective-permute-start.8 = (bf16[32,1024]{1,0:T(8,128)(2,1)S(1)}, bf16[32,1024]{1,0:T(8,128)(2,1)S(1)}, u32[]{:S(2)}, u32[]{:S(2)}) collective-permute-start(bf16[32,1024]{1,0:T(8,128)(2,1)S(1)} %get-tuple-element.15), channel_id=1, source_target_pairs={{0,4},{1,5},{2,6},{3,7},{4,0},{5,1},{6,2},{7,3},{8,12},{9,13},{10,... | collective-permute-start | bytes 196616 | tf_op jit(solution)/shard_map/ppermute | solution.py:212
  15.6 2.6 %collective-permute-start.6 = (bf16[32,1024]{1,0:T(8,128)(2,1)S(1)}, bf16[32,1024]{1,0:T(8,128)(2,1)S(1)}, u32[]{:S(2)}, u32[]{:S(2)}) collective-permute-start(bf16[32,1024]{1,0:T(8,128)(2,1)S(1)} %get-tuple-element.12), channel_id=1, source_target_pairs={{0,4},{1,5},{2,6},{3,7},{4,0},{5,1},{6,2},{7,3},{8,12},{9,13},{10,... | collective-permute-start | bytes 196616 | tf_op jit(solution)/shard_map/ppermute | solution.py:212
  16.9 3.4 %collective-permute-start.9 = (bf16[16,1024]{1,0:T(8,128)(2,1)S(1)}, bf16[16,1024]{1,0:T(8,128)(2,1)S(1)}, u32[]{:S(2)}, u32[]{:S(2)}) collective-permute-start(bf16[16,1024]{1,0:T(8,128)(2,1)S(1)} %shard_map.46), channel_id=1, source_target_pairs={{0,12},{1,13},{2,14},{3,15},{4,8},{5,9},{6,10},{7,11},{8,4},{9,5},... | collective-permute-start | bytes 98312 | tf_op jit(solution)/shard_map/ppermute | solution.py:212
  18.3 4.0 %collective-permute-start.7 = (bf16[16,1024]{1,0:T(8,128)(2,1)S(1)}, bf16[16,1024]{1,0:T(8,128)(2,1)S(1)}, u32[]{:S(2)}, u32[]{:S(2)}) collective-permute-start(bf16[16,1024]{1,0:T(8,128)(2,1)S(1)} %shard_map.43), channel_id=1, source_target_pairs={{0,12},{1,13},{2,14},{3,15},{4,8},{5,9},{6,10},{7,11},{8,4},{9,5},... | collective-permute-start | bytes 98312 | tf_op jit(solution)/shard_map/ppermute | solution.py:212
  20.4 4.6 %collective-permute-start.10 = (bf16[16,1024]{1,0:T(8,128)(2,1)S(1)}, bf16[16,1024]{1,0:T(8,128)(2,1)S(1)}, u32[]{:S(2)}, u32[]{:S(2)}) collective-permute-start(bf16[16,1024]{1,0:T(8,128)(2,1)S(1)} %shard_map.47), channel_id=1, source_target_pairs={{0,6},{1,2},{2,1},{3,5},{4,7},{5,3},{6,0},{7,4},{8,14},{9,10},{10,... | collective-permute-start | bytes 98312 | tf_op jit(solution)/shard_map/ppermute | solution.py:219
  22.4 3.8 %collective-permute-start.11 = (bf16[8,1024]{1,0:T(8,128)(2,1)S(1)}, bf16[8,1024]{1,0:T(8,128)(2,1)S(1)}, u32[]{:S(2)}, u32[]{:S(2)}) collective-permute-start(bf16[8,1024]{1,0:T(8,128)(2,1)S(1)} %get-tuple-element.16), channel_id=1, source_target_pairs={{0,1},{1,0},{2,3},{3,2},{4,5},{5,4},{6,7},{7,6},{8,9},{9,8},{10,11... | collective-permute-start | bytes 49160 | tf_op jit(solution)/shard_map/ppermute | solution.py:212
  25.0 1.3 %collective-permute-start.12 = (bf16[8,1024]{1,0:T(8,128)(2,1)S(1)}, bf16[8,1024]{1,0:T(8,128)(2,1)S(1)}, u32[]{:S(2)}, u32[]{:S(2)}) collective-permute-start(bf16[8,1024]{1,0:T(8,128)(2,1)S(1)} %shard_map.49), channel_id=1, source_target_pairs={{0,4},{1,5},{2,6},{3,7},{4,0},{5,1},{6,2},{7,3},{8,12},{9,13},{10,... | collective-permute-start | bytes 49160 | tf_op jit(solution)/shard_map/ppermute | solution.py:212
